TPU v7x, 32 devices: a whole 2x2x4 slice. The times are simulated.
32 devices in a mesh: seq: 2 (over y), ctx: 4 (over x, core), fsdp: 4 (over z).
Axes of the slice: x: 2, y: 2, z: 4, core: 2. Of those that a mesh axis runs over, the one named last changes fastest.
Arguments:
- layer_input: bfloat16 [8, 768, 2048], P(('seq', 'fsdp'), 'ctx'), may hold values from -48 to 48
- document_ids: int32 [8, 768], P(('seq', 'fsdp')), may hold values from 0 to 5, as said below
- cotangent: bfloat16 [8, 768, 2048], P(('seq', 'fsdp'), 'ctx'), may hold values from -6 to 6
- attention_gain: bfloat16 [2048], P(('ctx', 'fsdp')), may hold values from 0.5 to 1.5
- query_weight: bfloat16 [2048, 2048], P(('ctx', 'fsdp')), may hold values from -0.125 to 0.125
- key_weight: bfloat16 [2048, 2048], P(('ctx', 'fsdp')), may hold values from -0.125 to 0.125
- value_weight: bfloat16 [2048, 2048], P(('ctx', 'fsdp')), may hold values from -0.125 to 0.125
- output_weight: bfloat16 [2048, 2048], P(('ctx', 'fsdp')), may hold values from -0.375 to 0.375
- feedforward_gain: bfloat16 [2048], P(('ctx', 'fsdp')), may hold values from 0.5 to 1.5
- gate_weight: bfloat16 [2048, 8192], P(('ctx', 'fsdp')), may hold values from -0.125 to 0.125
- up_weight: bfloat16 [2048, 8192], P(('ctx', 'fsdp')), may hold values from -0.125 to 0.125
- down_weight: bfloat16 [8192, 2048], P(('ctx', 'fsdp')), may hold values from -0.0625 to 0.0625
Outputs:
- layer_output: bfloat16 [8, 768, 2048], P(('seq', 'fsdp'), 'ctx')
- input_grad: bfloat16 [8, 768, 2048], P(('seq', 'fsdp'), 'ctx')
- attention_gain_grad: float32 [2048], P(('ctx', 'fsdp'))
- query_weight_grad: float32 [2048, 2048], P(('ctx', 'fsdp'))
- key_weight_grad: float32 [2048, 2048], P(('ctx', 'fsdp'))
- value_weight_grad: float32 [2048, 2048], P(('ctx', 'fsdp'))
- output_weight_grad: float32 [2048, 2048], P(('ctx', 'fsdp'))
- feedforward_gain_grad: float32 [2048], P(('ctx', 'fsdp'))
- gate_weight_grad: float32 [2048, 8192], P(('ctx', 'fsdp'))
- up_weight_grad: float32 [2048, 8192], P(('ctx', 'fsdp'))
- down_weight_grad: float32 [8192, 2048], P(('ctx', 'fsdp'))
Inputs may be any that keep to these rules, and one draw needn't show every extreme that they name: `document_ids`: along each sequence the ids never fall; document 0 covers at least the first half of the sequence.
All inputs are finite; a program needn't handle non-finite values.
Results may differ from a plain program's by a relative error of at most 0.02.
Values may be sent and summed in bfloat16 or wider, within the bound.
No kernel may reach another device: no remote copies, remote signals or barrier semaphores. Data moves between devices by JAX's collectives and lax.ppermute only.
A program may use at most 576 MiB of HBM per device.

v0:
```python
import math

import jax
import jax.numpy as jnp
from jax import lax
from jax.sharding import PartitionSpec as P

HEADS = 32
HEAD_DIM = 64


epsilon = 1e-05
rotary_base = 130000.0
masked_score = -1e30


def norm_scale(values, gain):
    inverse = lax.rsqrt(jnp.mean(values * values, axis=-1, keepdims=True) + epsilon)
    return values * inverse * gain


def rotation(positions, head_size):
    half_dim = head_size // 2
    frequency = rotary_base ** (-(jnp.arange(half_dim, dtype=jnp.float32) * 2.0) / head_size)
    angles = positions.astype(jnp.float32)[:, None] * frequency[None, :]
    return (jnp.cos(angles), jnp.sin(angles))


def rotate(values, cosine, sine_table):
    half_dim = values.shape[-1] // 2
    front_part = values[..., :half_dim]
    second = values[..., half_dim:]
    cos_wide = cosine[:, None, :]
    sin_wide = sine_table[:, None, :]
    return jnp.concatenate(
        [front_part * cos_wide - second * sin_wide, second * cos_wide + front_part * sin_wide],
        axis=-1,
    )


def place(holder, offset, block_rows, ctx_count):
    return jnp.where(
        offset < block_rows,
        holder * block_rows + offset,
        (2 * ctx_count - 1 - holder) * block_rows + offset - block_rows,
    )


def per_device(
    layer_input,
    document_ids,
    cotangent,
    attention_gain,
    query_weight,
    key_weight,
    value_weight,
    output_weight,
    feedforward_gain,
    gate_weight,
    up_weight,
    down_weight,
):
    ctx_count = lax.axis_size("ctx")
    device = lax.axis_index("ctx")
    inputs = layer_input[0].astype(jnp.float32)
    upstream = cotangent[0]
    tok_count = inputs.shape[0]
    model_width = inputs.shape[1]
    block_rows = tok_count // 2
    group_heads = math.gcd(8, HEADS)
    group_count = HEADS // group_heads
    group_width = group_heads * HEAD_DIM
    key_count = ctx_count * tok_count
    local_pos = place(device, jnp.arange(tok_count, dtype=jnp.int32), block_rows, ctx_count)
    key_index = jnp.arange(key_count, dtype=jnp.int32)
    key_pos = place(key_index // tok_count, key_index % tok_count, block_rows, ctx_count)
    documents = document_ids[0]
    same_doc = jnp.take(documents, local_pos)[:, None] == jnp.take(documents, key_pos)[None, :]
    allowed = (key_pos[None, :] <= local_pos[:, None]) & same_doc
    cosine, sine_table = rotation(local_pos, HEAD_DIM)
    attention_set = (
        lax.all_gather(attention_gain, ("ctx", "fsdp"), axis=0, tiled=True),
        lax.all_gather(query_weight, ("ctx", "fsdp"), axis=0, tiled=True),
        lax.all_gather(key_weight, ("ctx", "fsdp"), axis=0, tiled=True),
        lax.all_gather(value_weight, ("ctx", "fsdp"), axis=0, tiled=True),
        lax.all_gather(output_weight, ("ctx", "fsdp"), axis=0, tiled=True),
    )
    attn_gain_full = attention_set[0].astype(jnp.float32)
    normed_low = norm_scale(inputs, attn_gain_full).astype(jnp.bfloat16)
    query_pre = jnp.dot(normed_low, attention_set[1], preferred_element_type=jnp.float32)
    key_pre = jnp.dot(normed_low, attention_set[2], preferred_element_type=jnp.float32)
    value_pre = jnp.dot(normed_low, attention_set[3], preferred_element_type=jnp.float32)
    queries = (
        rotate(query_pre.reshape(tok_count, HEADS, HEAD_DIM), cosine, sine_table)
        .reshape(tok_count, model_width)
        .astype(jnp.bfloat16)
    )
    keys_local = (
        rotate(key_pre.reshape(tok_count, HEADS, HEAD_DIM), cosine, sine_table)
        .reshape(tok_count, model_width)
        .astype(jnp.bfloat16)
    )
    values_local = value_pre.astype(jnp.bfloat16)
    all_keys, all_values = (
        lax.all_gather(keys_local, "ctx", axis=0, tiled=True),
        lax.all_gather(values_local, "ctx", axis=0, tiled=True),
    )

    def group_parts(group_index):
        column_start = group_index * group_width
        query_part = lax.dynamic_slice_in_dim(queries, column_start, group_width, 1).reshape(
            tok_count, group_heads, HEAD_DIM
        )
        key_part = lax.dynamic_slice_in_dim(all_keys, column_start, group_width, 1).reshape(
            key_count, group_heads, HEAD_DIM
        )
        value_part = lax.dynamic_slice_in_dim(all_values, column_start, group_width, 1).reshape(
            key_count, group_heads, HEAD_DIM
        )
        scores = (
            jnp.einsum("qhd,khd->hqk", query_part, key_part, preferred_element_type=jnp.float32)
            * 0.125
        )
        scores = jnp.where(allowed[None], scores, masked_score)
        return (query_part, key_part, value_part, scores)

    def group_forward(group_index):
        query_part, key_part, value_part, scores = group_parts(group_index)
        row_peak = jnp.max(scores, axis=-1, keepdims=True)
        exponent = jnp.exp(scores - row_peak)
        row_total = jnp.sum(exponent, axis=-1, keepdims=True)
        softmax_weights = exponent / row_total
        log_total = row_peak[..., 0] + jnp.log(row_total[..., 0])
        attended = jnp.einsum(
            "hqk,khd->qhd",
            softmax_weights.astype(jnp.bfloat16),
            value_part,
            preferred_element_type=jnp.float32,
        )
        return (attended.reshape(tok_count, group_width), log_total)

    group_index_all = jnp.arange(group_count, dtype=jnp.int32)
    attended_groups, log_totals = lax.map(group_forward, group_index_all)
    attended_low = (
        jnp.transpose(attended_groups, (1, 0, 2))
        .reshape(tok_count, model_width)
        .astype(jnp.bfloat16)
    )
    hidden = inputs + jnp.dot(attended_low, attention_set[4], preferred_element_type=jnp.float32)
    feedforward_set = (
        lax.all_gather(feedforward_gain, ("ctx", "fsdp"), axis=0, tiled=True),
        lax.all_gather(gate_weight, ("ctx", "fsdp"), axis=0, tiled=True),
        lax.all_gather(up_weight, ("ctx", "fsdp"), axis=0, tiled=True),
        lax.all_gather(down_weight, ("ctx", "fsdp"), axis=0, tiled=True),
    )
    mlp_low = norm_scale(hidden, feedforward_set[0].astype(jnp.float32)).astype(jnp.bfloat16)
    gate_pre = jnp.dot(mlp_low, feedforward_set[1], preferred_element_type=jnp.float32)
    up_pre = jnp.dot(mlp_low, feedforward_set[2], preferred_element_type=jnp.float32)
    product_low = (jax.nn.silu(gate_pre) * up_pre).astype(jnp.bfloat16)
    layer_output = (
        hidden + jnp.dot(product_low, feedforward_set[3], preferred_element_type=jnp.float32)
    ).astype(jnp.bfloat16)
    feedforward_back = (
        lax.all_gather(feedforward_gain, ("ctx", "fsdp"), axis=0, tiled=True),
        lax.all_gather(gate_weight, ("ctx", "fsdp"), axis=0, tiled=True),
        lax.all_gather(up_weight, ("ctx", "fsdp"), axis=0, tiled=True),
        lax.all_gather(down_weight, ("ctx", "fsdp"), axis=0, tiled=True),
    )
    attention_back = (
        lax.all_gather(attention_gain, ("ctx", "fsdp"), axis=0, tiled=True),
        lax.all_gather(query_weight, ("ctx", "fsdp"), axis=0, tiled=True),
        lax.all_gather(key_weight, ("ctx", "fsdp"), axis=0, tiled=True),
        lax.all_gather(value_weight, ("ctx", "fsdp"), axis=0, tiled=True),
        lax.all_gather(output_weight, ("ctx", "fsdp"), axis=0, tiled=True),
    )
    piece = product_low
    down_shard = lax.psum_scatter(
        jnp.einsum("tf,td->fd", piece, upstream, preferred_element_type=jnp.float32),
        ("ctx", "fsdp"),
        scatter_dimension=0,
        tiled=True,
    )
    product_grad = jnp.einsum(
        "td,fd->tf", upstream, feedforward_back[3], preferred_element_type=jnp.float32
    )
    silu_out, silu_pullback = jax.vjp(
        lambda gate_in, up_in: jax.nn.silu(gate_in) * up_in, gate_pre, up_pre
    )
    gate_grad, up_grad = silu_pullback(product_grad)
    gate_grad_low = gate_grad.astype(jnp.bfloat16)
    up_grad_low = up_grad.astype(jnp.bfloat16)
    joined_grads = jnp.concatenate([gate_grad_low, up_grad_low], axis=1)
    piece = mlp_low
    joined_shard = lax.psum_scatter(
        jnp.einsum("td,tf->df", piece, joined_grads, preferred_element_type=jnp.float32),
        ("ctx", "fsdp"),
        scatter_dimension=0,
        tiled=True,
    )
    ff_width = gate_weight.shape[1]
    gate_shard = joined_shard[:, :ff_width]
    up_shard = joined_shard[:, ff_width:]
    mlp_normed_grad = jnp.einsum(
        "tf,df->td", gate_grad_low, feedforward_back[1], preferred_element_type=jnp.float32
    )
    mlp_normed_grad = mlp_normed_grad + jnp.einsum(
        "tf,df->td", up_grad_low, feedforward_back[2], preferred_element_type=jnp.float32
    )
    mlp_norm_out, mlp_norm_pullback = jax.vjp(
        norm_scale, hidden, feedforward_back[0].astype(jnp.float32)
    )
    hidden_from_norm, ff_gain_term = mlp_norm_pullback(mlp_normed_grad)
    hidden_grad = upstream.astype(jnp.float32) + hidden_from_norm
    hidden_low = hidden_grad.astype(jnp.bfloat16)
    output_term = jnp.einsum(
        "td,te->de", attended_low, hidden_low, preferred_element_type=jnp.float32
    )
    attended_grad_low = jnp.einsum(
        "te,de->td", hidden_low, attention_back[4], preferred_element_type=jnp.float32
    ).astype(jnp.bfloat16)

    def group_backward(operands):
        group_index, log_total = operands
        query_part, key_part, value_part, scores = group_parts(group_index)
        softmax_weights = jnp.exp(scores - log_total[:, :, None])
        column_start = group_index * group_width
        grad_part = lax.dynamic_slice_in_dim(
            attended_grad_low, column_start, group_width, 1
        ).reshape(tok_count, group_heads, HEAD_DIM)
        value_grad = jnp.einsum(
            "hqk,qhd->khd",
            softmax_weights.astype(jnp.bfloat16),
            grad_part,
            preferred_element_type=jnp.float32,
        )
        weight_grad = jnp.einsum(
            "qhd,khd->hqk", grad_part, value_part, preferred_element_type=jnp.float32
        )
        row_inner = jnp.sum(weight_grad * softmax_weights, axis=-1, keepdims=True)
        score_grad = (softmax_weights * (weight_grad - row_inner)).astype(jnp.bfloat16)
        query_grad = (
            jnp.einsum("hqk,khd->qhd", score_grad, key_part, preferred_element_type=jnp.float32)
            * 0.125
        )
        key_grad = (
            jnp.einsum("hqk,qhd->khd", score_grad, query_part, preferred_element_type=jnp.float32)
            * 0.125
        )
        return (
            query_grad.reshape(tok_count, group_width),
            key_grad.reshape(key_count, group_width),
            value_grad.reshape(key_count, group_width),
        )

    query_groups, key_groups, value_groups = lax.map(group_backward, (group_index_all, log_totals))
    query_grad_all = jnp.transpose(query_groups, (1, 0, 2)).reshape(tok_count, model_width)
    key_grad_all = jnp.transpose(key_groups, (1, 0, 2)).reshape(key_count, model_width)
    value_grad_all = jnp.transpose(value_groups, (1, 0, 2)).reshape(key_count, model_width)
    key_grad_local, value_grad_local = (
        lax.psum_scatter(
            key_grad_all.astype(jnp.bfloat16), "ctx", scatter_dimension=0, tiled=True
        ).astype(jnp.float32),
        lax.psum_scatter(
            value_grad_all.astype(jnp.bfloat16), "ctx", scatter_dimension=0, tiled=True
        ).astype(jnp.float32),
    )
    negative_sine = -sine_table
    query_pre_grad = (
        rotate(query_grad_all.reshape(tok_count, HEADS, HEAD_DIM), cosine, negative_sine)
        .reshape(tok_count, model_width)
        .astype(jnp.bfloat16)
    )
    key_pre_grad = (
        rotate(key_grad_local.reshape(tok_count, HEADS, HEAD_DIM), cosine, negative_sine)
        .reshape(tok_count, model_width)
        .astype(jnp.bfloat16)
    )
    value_pre_grad = value_grad_local.astype(jnp.bfloat16)
    query_term = jnp.einsum(
        "td,te->de", normed_low, query_pre_grad, preferred_element_type=jnp.float32
    )
    key_term = jnp.einsum("td,te->de", normed_low, key_pre_grad, preferred_element_type=jnp.float32)
    value_term = jnp.einsum(
        "td,te->de", normed_low, value_pre_grad, preferred_element_type=jnp.float32
    )
    attn_normed_grad = jnp.einsum(
        "te,de->td", query_pre_grad, attention_back[1], preferred_element_type=jnp.float32
    )
    attn_normed_grad = attn_normed_grad + jnp.einsum(
        "te,de->td", key_pre_grad, attention_back[2], preferred_element_type=jnp.float32
    )
    attn_normed_grad = attn_normed_grad + jnp.einsum(
        "te,de->td", value_pre_grad, attention_back[3], preferred_element_type=jnp.float32
    )
    attn_norm_out, attn_norm_pullback = jax.vjp(
        norm_scale, inputs, attention_back[0].astype(jnp.float32)
    )
    inputs_from_norm, attn_gain_term = attn_norm_pullback(attn_normed_grad)
    input_grad = (hidden_grad + inputs_from_norm).astype(jnp.bfloat16)
    attn_shards = (
        lax.psum_scatter(attn_gain_term, ("ctx", "fsdp"), scatter_dimension=0, tiled=True),
        lax.psum_scatter(ff_gain_term, ("ctx", "fsdp"), scatter_dimension=0, tiled=True),
        lax.psum_scatter(query_term, ("ctx", "fsdp"), scatter_dimension=0, tiled=True),
        lax.psum_scatter(key_term, ("ctx", "fsdp"), scatter_dimension=0, tiled=True),
        lax.psum_scatter(value_term, ("ctx", "fsdp"), scatter_dimension=0, tiled=True),
        lax.psum_scatter(output_term, ("ctx", "fsdp"), scatter_dimension=0, tiled=True),
    )
    summed = (
        lax.psum(attn_shards[0].astype(jnp.bfloat16), "seq").astype(jnp.float32),
        lax.psum(attn_shards[2].astype(jnp.bfloat16), "seq").astype(jnp.float32),
        lax.psum(attn_shards[3].astype(jnp.bfloat16), "seq").astype(jnp.float32),
        lax.psum(attn_shards[4].astype(jnp.bfloat16), "seq").astype(jnp.float32),
        lax.psum(attn_shards[5].astype(jnp.bfloat16), "seq").astype(jnp.float32),
        lax.psum(attn_shards[1].astype(jnp.bfloat16), "seq").astype(jnp.float32),
        lax.psum(gate_shard.astype(jnp.bfloat16), "seq").astype(jnp.float32),
        lax.psum(up_shard.astype(jnp.bfloat16), "seq").astype(jnp.float32),
        lax.psum(down_shard.astype(jnp.bfloat16), "seq").astype(jnp.float32),
    )
    return (
        layer_output[None],
        input_grad[None],
        summed[0],
        summed[1],
        summed[2],
        summed[3],
        summed[4],
        summed[5],
        summed[6],
        summed[7],
        summed[8],
    )


def solution(mesh):
    return jax.shard_map(
        per_device,
        mesh=mesh,
        in_specs=(
            P(("seq", "fsdp"), "ctx", None),
            P(("seq", "fsdp"), None),
            P(("seq", "fsdp"), "ctx", None),
            P(("ctx", "fsdp")),
            P(("ctx", "fsdp"), None),
            P(("ctx", "fsdp"), None),
            P(("ctx", "fsdp"), None),
            P(("ctx", "fsdp"), None),
            P(("ctx", "fsdp")),
            P(("ctx", "fsdp"), None),
            P(("ctx", "fsdp"), None),
            P(("ctx", "fsdp"), None),
        ),
        out_specs=(
            P(("seq", "fsdp"), "ctx", None),
            P(("seq", "fsdp"), "ctx", None),
            P(("ctx", "fsdp")),
            P(("ctx", "fsdp"), None),
            P(("ctx", "fsdp"), None),
            P(("ctx", "fsdp"), None),
            P(("ctx", "fsdp"), None),
            P(("ctx", "fsdp")),
            P(("ctx", "fsdp"), None),
            P(("ctx", "fsdp"), None),
            P(("ctx", "fsdp"), None),
        ),
        check_vma=False,
    )
```

profile of v0, /device:TPU:0, one launch (start us, length us, event | category | flops | bytes accessed | tf_op | source)
XLA Modules:
  0.0 3979.2 jit_solution(18401472366280901864)
XLA Ops:
  9.5 34.1 all-gather
  45.0 43.0 %all-gather.12.cloned.1.call-done = bf16[2048,2048]{1,0:T(8,128)(2,1)} async-done(((bf16[128,2048]{1,0:T(8,128)(2,1)}), bf16[2048,2048]{1,0:T(8,128)(2,1)}) %all-gather.12.cloned.1.call-update) | async-done | bytes 8388624 | tf_op jit(solution)/shard_map/all_gather | solution.py:85
  88.0 6.4 convolution_convert_fusion.1
  95.3 68.1 %all-gather.18.cloned.1.call-done = bf16[2048,2048]{1,0:T(8,128)(2,1)} async-done(((bf16[128,2048]{1,0:T(8,128)(2,1)}), bf16[2048,2048]{1,0:T(8,128)(2,1)}) %all-gather.18.cloned.1.call-update) | async-done | bytes 8388624 | tf_op jit(solution)/shard_map/all_gather | solution.py:84
  163.4 12.4 copy.34
  175.8 63.0 %all-gather.16.cloned.1.call-done = bf16[2048,2048]{1,0:T(8,128)(2,1)} async-done(((bf16[128,2048]{1,0:T(8,128)(2,1)}), bf16[2048,2048]{1,0:T(8,128)(2,1)}) %all-gather.16.cloned.1.call-update) | async-done | bytes 8388624 | tf_op jit(solution)/shard_map/all_gather | solution.py:83
  238.8 12.5 copy.33
  251.3 6.2 fusion.48
  270.6 29.9 all-gather.1
  301.9 4.6 copy.36
  306.5 4.8 copy.37
  311.3 28.0 while.30
  339.3 35.9 all-gather.22.cloned.1.call-done
  375.2 5.3 multiply_reduce_fusion.3
  380.8 172.2 %all-gather.24.cloned.1.call-done = bf16[2048,8192]{1,0:T(8,128)(2,1)} async-done(((bf16[128,8192]{1,0:T(8,128)(2,1)}), bf16[2048,8192]{1,0:T(8,128)(2,1)}) %all-gather.24.cloned.1.call-update) | async-done | bytes 33554448 | tf_op jit(solution)/shard_map/all_gather | solution.py:152
  552.9 17.4 fusion.86
  570.4 162.1 %all-gather.26.cloned.1.call-done = bf16[2048,8192]{1,0:T(8,128)(2,1)} async-done(((bf16[128,8192]{1,0:T(8,128)(2,1)}), bf16[2048,8192]{1,0:T(8,128)(2,1)}) %all-gather.26.cloned.1.call-update) | async-done | bytes 33554448 | tf_op jit(solution)/shard_map/all_gather | solution.py:153
  732.4 17.7 fusion.87
  750.2 161.8 %all-gather.28.cloned.1.call-done = bf16[8192,2048]{1,0:T(8,128)(2,1)} async-done(((bf16[512,2048]{1,0:T(8,128)(2,1)}), bf16[8192,2048]{1,0:T(8,128)(2,1)}) %all-gather.28.cloned.1.call-update) | async-done | bytes 33554448 | tf_op jit(solution)/shard_map/all_gather | solution.py:154
  912.0 21.1 multiply_convert_fusion.1
  933.1 18.3 fusion.88
  951.4 19.6 multiply_reduce_fusion.1
  973.4 7.8 convolution_convert_fusion
  981.1 79.2 %while.31 = (s32[]{:T(128)}, f32[4,192,512]{1,2,0:T(8,128)}, bf16[4,768,512]{1,2,0:T(8,128)(2,1)}, bf16[4,768,512]{1,2,0:T(8,128)(2,1)}, s32[4]{0:T(128)S(1)}, /...) while((s32[]{:T(128)}, f32[4,192,512]{1,2,0:T(8,128)}, ...), condition=%wide.region_9.10_spmd.clone.clone, body=%wide.region_7.9_spmd.clone.sunk.clone | while | flops 773995008 | bytes 63686424 | solution.py:255
  990.0 4.5 multiply_reduce_fusion.6
  1009.8 4.5 multiply_reduce_fusion.6
  1060.3 4.6 copy.41
  1065.1 4.6 copy.43
  1071.2 8.2 fusion.56
  1079.5 23.6 reduce-scatter.25.cloned.1.call-done
  1108.2 9.6 fusion.54
  1120.2 8.6 fusion.52
  1128.8 15.6 reduce-scatter.27.cloned.1.call-done
  1144.4 9.8 fusion.59
  1156.2 32.0 fusion.44
  1189.3 47.8 %fusion.21 = f32[2048,16384]{1,0:T(8,128)} fusion(bf16[192,2048]{1,0:T(8,128)(2,1)S(1)} %copy-done.20, bf16[192,8192]{1,0:T(8,128)(2,1)} %get-tuple-element.328, bf16[192,8192]{1,0:T(8,128)(2,1)} %copy-done.22), kind=kOutput, calls=%fused_computation.44 | convolution fusion | flops 12897484800 | bytes 141295616 | tf_op jit(solution)/shard_map/td,tf->df/dot_general | solution.py:195
  1237.2 89.8 %reduce-scatter.19.cloned.1.call-done = f32[128,2048]{1,0:T(8,128)} async-done(((f32[2048,2048]{1,0:T(8,128)}), f32[128,2048]{1,0:T(8,128)}) %reduce-scatter.19.cloned.1.call-update) | async-done | bytes 1048592 | tf_op jit(solution)/shard_map/reduce_scatter | solution.py:306
  1329.1 179.6 %reduce-scatter.13.cloned.1.call-done = f32[128,2048]{1,0:T(8,128)} async-done(((f32[2048,2048]{1,0:T(8,128)}), f32[128,2048]{1,0:T(8,128)}) %reduce-scatter.13.cloned.1.call-update) | async-done | bytes 1048592 | tf_op jit(solution)/shard_map/reduce_scatter | solution.py:303
  1510.8 179.5 %reduce-scatter.15.cloned.1.call-done = f32[128,2048]{1,0:T(8,128)} async-done(((f32[2048,2048]{1,0:T(8,128)}), f32[128,2048]{1,0:T(8,128)}) %reduce-scatter.15.cloned.1.call-update) | async-done | bytes 1048592 | tf_op jit(solution)/shard_map/reduce_scatter | solution.py:304
  1692.4 179.5 %reduce-scatter.17.cloned.1.call-done = f32[128,2048]{1,0:T(8,128)} async-done(((f32[2048,2048]{1,0:T(8,128)}), f32[128,2048]{1,0:T(8,128)}) %reduce-scatter.17.cloned.1.call-update) | async-done | bytes 1048592 | tf_op jit(solution)/shard_map/reduce_scatter | solution.py:305
  1874.0 638.2 %reduce-scatter.23.cloned.1.call-done = f32[512,2048]{1,0:T(8,128)} async-done(((f32[8192,2048]{1,0:T(8,128)}), f32[512,2048]{1,0:T(8,128)}) %reduce-scatter.23.cloned.1.call-update) | async-done | bytes 4194320 | tf_op jit(solution)/shard_map/reduce_scatter | solution.py:177
  2516.0 1235.6 %reduce-scatter.21.cloned.1.call-done = f32[128,16384]{1,0:T(8,128)} async-done(((f32[2048,16384]{1,0:T(8,128)}), f32[128,16384]{1,0:T(8,128)}) %reduce-scatter.21.cloned.1.call-update) | async-done | bytes 8388624 | tf_op jit(solution)/shard_map/reduce_scatter | solution.py:194
  3759.7 17.0 fusion.27
  3776.7 6.4 fusion.89
  3783.2 6.5 convolution_add_fusion.1
  3794.2 59.9 %all-reduce.2 = (bf16[2048]{0:T(1024)(128)(2,1)S(1)}, bf16[2048]{0:T(1024)(128)(2,1)S(1)}) all-reduce(f32[2048]{0:T(1024)S(1)} %get-tuple-element.257, f32[2048]{0:T(1024)S(1)} %copy-done.42), channel_id=4, replica_groups=mesh['seq'=2,'ctx'=4,'fsdp'=4] {'ctx','fsdp'}, use_global_device_ids=true, to_apply=%region_14.15.clone | all-reduce | flops 4096 | bytes 24576
  3854.3 4.9 all-reduce.3
  3863.0 95.2 %all-reduce.7.cloned.1.call-done = (bf16[128,2048]{1,0:T(8,128)(2,1)}, bf16[128,2048]{1,0:T(8,128)(2,1)}, bf16[128,2048]{1,0:T(8,128)(2,1)}, bf16[128,2048]{1,0:...) async-done(((bf16[128,2048]{1,0:T(8,128)(2,1)}, bf16[128,2048]{1,0:T(8,128)(2,1)}, bf16[128,2048]{1,0:T(8,128)(2,1)}, ...) | async-done | bytes 8388624 | tf_op jit(solution)/shard_map/psum | solution.py:310
  (310 shorter events, 167.9 us)
Async XLA Ops:
  7.2 258.9 %copy-start = (s32[1,768]{1,0:T(1,128)S(1)}, s32[1,768]{1,0:T(1,128)}, u32[]{:S(2)}) copy-start(s32[1,768]{1,0:T(1,128)} %param.17) | copy-start | bytes 9220
  7.2 80.8 %all-gather.12.cloned.1.call-start = ((), (), s32[]{:S(2)}) async-start(), calls=%async_computation.8 | async-start | bytes 8912896 | tf_op jit(solution)/shard_map/all_gather | solution.py:85
  7.9 155.4 %all-gather.18.cloned.1.call-start = ((), (), s32[]{:S(2)}) async-start(), calls=%async_computation.11 | async-start | bytes 8912896 | tf_op jit(solution)/shard_map/all_gather | solution.py:84
  8.7 230.1 %all-gather.16.cloned.1.call-start = ((), (), s32[]{:S(2)}) async-start(), calls=%async_computation.10 | async-start | bytes 8912896 | tf_op jit(solution)/shard_map/all_gather | solution.py:83
  9.4 292.4 %all-gather.14.cloned.1.call-start = ((), (), s32[]{:S(2)}) async-start(), calls=%async_computation.9 | async-start | bytes 3932160 | tf_op jit(solution)/shard_map/all_gather | solution.py:106
  43.6 213.9 %copy-start.31 = (f32[16,1,128]{2,1,0:T(1,128)}, f32[16,1,128]{2,1,0:T(1,128)S(1)}, u32[]{:S(2)}) copy-start(f32[16,1,128]{2,1,0:T(1,128)S(1)} %convert_element_type.242) | copy-start | bytes 24580
  44.9 49.4 %copy-start.40 = (f32[192]{0:T(256)}, f32[192]{0:T(256)S(1)}, u32[]{:S(2)}) copy-start(f32[192]{0:T(256)S(1)} %fusion.36) | copy-start | bytes 2308
  45.0 212.5 %copy-start.37 = (f32[192]{0:T(256)}, f32[192]{0:T(256)S(1)}, u32[]{:S(2)}) copy-start(f32[192]{0:T(256)S(1)} %fusion.76) | copy-start | bytes 2308
  94.4 212.1 %all-gather.20.cloned.1.call-start = ((), (), s32[]{:S(2)}) async-start(), calls=%async_computation.12 | async-start | bytes 3932160 | tf_op jit(solution)/shard_map/all_gather | solution.py:105
  95.3 164.9 %copy-start.34 = (f32[192,32]{0,1:T(8,128)}, f32[192,32]{0,1:T(8,128)S(1)}, u32[]{:S(2)}) copy-start(f32[192,32]{0,1:T(8,128)S(1)} %get-tuple-element.347) | copy-start | bytes 73732
  238.8 12.5 copy-start.2
  251.3 6.2 copy-start.14
  263.2 112.0 %all-gather.22.cloned.1.call-start = ((), (), s32[]{:S(2)}) async-start(), calls=%async_computation.13 | async-start | bytes 8912896 | tf_op jit(solution)/shard_map/all_gather | solution.py:86
  263.7 289.2 %all-gather.24.cloned.1.call-start = ((), (), s32[]{:S(2)}) async-start(), calls=%async_computation.14 | async-start | bytes 35651584 | tf_op jit(solution)/shard_map/all_gather | solution.py:152
  264.5 468.0 %all-gather.26.cloned.1.call-start = ((), (), s32[]{:S(2)}) async-start(), calls=%async_computation.15 | async-start | bytes 35651584 | tf_op jit(solution)/shard_map/all_gather | solution.py:153
  265.2 646.7 %all-gather.28.cloned.1.call-start = ((), (), s32[]{:S(2)}) async-start(), calls=%async_computation.16 | async-start | bytes 35651584 | tf_op jit(solution)/shard_map/all_gather | solution.py:154
  266.0 4.6 copy-start.43
  266.0 837.1 %reduce-scatter.25.cloned.1.call-start = ((), (), s32[]{:S(2)}) async-start(), calls=%async_computation.23 | async-start | bytes 3932160
  339.2 35.9 copy-start.9
  339.3 41.2 %copy-start.10 = (bf16[4,192,512]{1,2,0:T(8,128)(2,1)}, bf16[4,192,512]{1,2,0:T(8,128)(2,1)S(1)}, u32[]{:S(2)}) copy-start(bf16[4,192,512]{1,2,0:T(8,128)(2,1)S(1)} %get-tuple-element.113) | copy-start | bytes 2359300
  380.5 570.9 %copy-start.7 = (f32[192,2048]{1,0:T(8,128)}, f32[192,2048]{1,0:T(8,128)S(1)}, u32[]{:S(2)}) copy-start(f32[192,2048]{1,0:T(8,128)S(1)} %get-tuple-element.349) | copy-start | bytes 4718596
  380.7 351.7 %copy-start.19 = (bf16[192,2048]{1,0:T(8,128)(2,1)}, bf16[192,2048]{1,0:T(8,128)(2,1)S(1)}, u32[]{:S(2)}) copy-start(bf16[192,2048]{1,0:T(8,128)(2,1)S(1)} %multiply_convert_fusion.3) | copy-start | bytes 2359300
  570.4 341.6 %copy-start.18 = (bf16[1,192,2048]{2,1,0:T(8,128)(2,1)S(1)}, bf16[1,192,2048]{2,1,0:T(8,128)(2,1)}, u32[]{:S(2)}) copy-start(bf16[1,192,2048]{2,1,0:T(8,128)(2,1)} %param.18) | copy-start | bytes 2359300
  933.1 18.3 copy-start.22
  973.4 96.4 %copy-start.5 = (f32[192,2048]{1,0:T(8,128)}, f32[192,2048]{1,0:T(8,128)S(1)}, u32[]{:S(2)}) copy-start(f32[192,2048]{1,0:T(8,128)S(1)} %fusion.40) | copy-start | bytes 4718596
  1065.0 79.4 %reduce-scatter.27.cloned.1.call-start = ((), (), s32[]{:S(2)}) async-start(), calls=%async_computation.24 | async-start | bytes 3932160
  1069.7 257.3 %reduce-scatter.19.cloned.1.call-start = ((), (), s32[]{:S(2)}) async-start(), calls=%async_computation.20 | async-start | bytes 17825792 | tf_op jit(solution)/shard_map/reduce_scatter | solution.py:306
  1079.4 25.8 copy-start.23
  1079.5 25.8 copy-start.35
  1079.5 25.8 copy-start.36
  1079.5 429.3 %reduce-scatter.13.cloned.1.call-start = ((), (), s32[]{:S(2)}) async-start(), calls=%async_computation.17 | async-start | bytes 17825792 | tf_op jit(solution)/shard_map/reduce_scatter | solution.py:303
  1117.8 572.5 %reduce-scatter.15.cloned.1.call-start = ((), (), s32[]{:S(2)}) async-start(), calls=%async_computation.18 | async-start | bytes 17825792 | tf_op jit(solution)/shard_map/reduce_scatter | solution.py:304
  1128.8 743.1 %reduce-scatter.17.cloned.1.call-start = ((), (), s32[]{:S(2)}) async-start(), calls=%async_computation.19 | async-start | bytes 17825792 | tf_op jit(solution)/shard_map/reduce_scatter | solution.py:305
  1154.3 1357.9 %reduce-scatter.23.cloned.1.call-start = ((), (), s32[]{:S(2)}) async-start(), calls=%async_computation.22 | async-start | bytes 71303168 | tf_op jit(solution)/shard_map/reduce_scatter | solution.py:177
  1188.2 2563.4 %reduce-scatter.21.cloned.1.call-start = ((), (), s32[]{:S(2)}) async-start(), calls=%async_computation.21 | async-start | bytes 142606336 | tf_op jit(solution)/shard_map/reduce_scatter | solution.py:194
  1237.2 2721.1 %all-reduce.7.cloned.1.call-start = ((), (), s32[]{:S(2)}) async-start(), calls=%async_computation.25 | async-start | bytes 16777216 | tf_op jit(solution)/shard_map/psum | solution.py:310
  3759.7 17.0 copy-start.17
  3776.7 6.5 copy-start.13
  3776.7 13.0 slice-start.2
  3783.1 6.6 copy-start.4
  3783.2 6.6 slice-start.3
  3783.2 6.6 copy-start.21
  3783.2 6.6 copy-start.33
  3783.2 6.6 copy-start.39
  3789.8 70.4 %copy-start.41 = (f32[192]{0:T(256)S(1)}, f32[192]{0:T(256)}, u32[]{:S(2)}) copy-start(f32[192]{0:T(256)} %copy-done.40) | copy-start | bytes 2308
  3789.8 70.4 %copy-start.6 = (f32[192,2048]{1,0:T(8,128)S(1)}, f32[192,2048]{1,0:T(8,128)}, u32[]{:S(2)}) copy-start(f32[192,2048]{1,0:T(8,128)} %copy-done.5) | copy-start | bytes 4718596
  3958.2 5.5 copy-start.29
  3958.2 6.5 copy-start.26
  (25 other events, 72.2 us)
Sparse Core Ops, SparseCore 0:
  10.2 77.6 all-gather.11
  90.2 73.1 all-gather.17
  165.6 73.1 all-gather.15
  240.8 26.7 all-gather.13
  269.6 28.5 all-gather.19
  300.2 74.9 all-gather.21
  376.7 176.1 all-gather.23
  554.5 177.9 all-gather.25
  734.0 177.9 all-gather.27
  1065.1 37.9 reduce-scatter.24
  1106.4 37.9 reduce-scatter.26
  1148.4 178.5 reduce-scatter.18
  1331.1 177.5 reduce-scatter.12
  1512.7 177.5 reduce-scatter.14
  1694.3 177.5 reduce-scatter.16
  1876.0 636.1 reduce-scatter.22
  2516.3 1235.2 reduce-scatter.20
  3758.0 200.2 all-reduce.6
where the time goes:
time: 3990 us; the launch traced here: 3980 us
  waiting for transfers between devices  3350 us (84%)
  matrix products  325 us (8%)
  blocking collectives  129 us (3%)
  local copies, waits for them, and re-layouts  99.8 us (3%)
  other arithmetic  56.2 us (1%)
    reduce_scatter x1, waiting for transfers between devices, per_device(): lax.psum_scatter(jnp.einsum('td,tf->df', piece, joined_grads, preferred_e...  1240 us
    reduce_scatter x1, waiting for transfers between devices, per_device(): lax.psum_scatter(jnp.einsum('tf,td->fd', piece, upstream, preferred_eleme...  638 us
    reduce_scatter x1, waiting for transfers between devices, per_device(): lax.psum_scatter(query_term, ('ctx', 'fsdp'), scatter_dimension=0, tiled=...  180 us
    reduce_scatter x1, waiting for transfers between devices, per_device(): lax.psum_scatter(value_term, ('ctx', 'fsdp'), scatter_dimension=0, tiled=...  180 us
    reduce_scatter x1, waiting for transfers between devices, per_device(): lax.psum_scatter(key_term, ('ctx', 'fsdp'), scatter_dimension=0, tiled=True)  179 us
    all_gather x1, waiting for transfers between devices, per_device(): lax.all_gather(gate_weight, ('ctx', 'fsdp'), axis=0, tiled=True)  172 us
    all_gather x1, waiting for transfers between devices, per_device(): lax.all_gather(up_weight, ('ctx', 'fsdp'), axis=0, tiled=True)  162 us
    all_gather x1, waiting for transfers between devices, per_device(): lax.all_gather(down_weight, ('ctx', 'fsdp'), axis=0, tiled=True)  162 us
  transfers between devices with their start and end apart: 18, of which 16 were waited for; matrix products, arithmetic and copies ran while one was open for 8% of the time, Pallas kernels for 0%

commit v1 on v0

--- a/solution.py
+++ b/solution.py
@@ -1,9 +1,12 @@
+import functools
 import math
 
 import jax
 import jax.numpy as jnp
 from jax import lax
-from jax.sharding import PartitionSpec as P
+from jax.experimental import pallas as pl
+from jax.experimental.pallas import tpu as pltpu
+from jax.sharding import Mesh, PartitionSpec as P
 
 HEADS = 32
 HEAD_DIM = 64
@@ -38,7 +41,7 @@
     )
 
 
-def place(holder, offset, block_rows, ctx_count):
+def place_of(holder, offset, block_rows, ctx_count):
     return jnp.where(
         offset < block_rows,
         holder * block_rows + offset,
@@ -71,9 +74,9 @@
     group_count = HEADS // group_heads
     group_width = group_heads * HEAD_DIM
     key_count = ctx_count * tok_count
-    local_pos = place(device, jnp.arange(tok_count, dtype=jnp.int32), block_rows, ctx_count)
+    local_pos = place_of(device, jnp.arange(tok_count, dtype=jnp.int32), block_rows, ctx_count)
     key_index = jnp.arange(key_count, dtype=jnp.int32)
-    key_pos = place(key_index // tok_count, key_index % tok_count, block_rows, ctx_count)
+    key_pos = place_of(key_index // tok_count, key_index % tok_count, block_rows, ctx_count)
     documents = document_ids[0]
     same_doc = jnp.take(documents, local_pos)[:, None] == jnp.take(documents, key_pos)[None, :]
     allowed = (key_pos[None, :] <= local_pos[:, None]) & same_doc
@@ -331,7 +334,7 @@
     )
 
 
-def solution(mesh):
+def gathered(mesh):
     return jax.shard_map(
         per_device,
         mesh=mesh,
@@ -364,3 +367,553 @@
         ),
         check_vma=False,
     )
+
+
+BIG = pltpu.CompilerParams(vmem_limit_bytes=56 * 1024 * 1024)
+BF16 = jnp.bfloat16
+F32 = jnp.float32
+
+
+def swap(value, axis):
+    return lax.ppermute(value, axis, [(0, 1), (1, 0)])
+
+
+def swap_both(value, first, second):
+    return lax.ppermute(value, (first, second), [(0, 3), (1, 2), (2, 1), (3, 0)])
+
+
+def after(value, *earlier):
+    return lax.optimization_barrier((value, *earlier))[0]
+
+
+def gather_square(block):
+    half = block.shape[0] // 2
+    along_x = swap(block, "x")
+    along_seq = swap(block, "seq")
+    upper = swap(along_seq[:half], "x")
+    lower = swap(along_x[half:], "seq")
+    return [block, along_x, along_seq, jnp.concatenate([upper, lower], axis=0)]
+
+
+def gather_blocks(block):
+    across = swap(block, "zl")
+    return gather_square(block) + gather_square(across)
+
+
+def add_low(first, *others):
+    total = first.astype(F32)
+    for other in others:
+        total = total + other.astype(F32)
+    return total
+
+
+def scatter_square(own, to_x, to_seq, opposite):
+    half = own.shape[0] // 2
+    by_x = swap(opposite[:half], "x")
+    by_seq = swap(opposite[half:], "seq")
+    to_seq = jnp.concatenate([add_low(to_seq[:half], by_x).astype(BF16), to_seq[half:]], axis=0)
+    to_x = jnp.concatenate([to_x[:half], add_low(to_x[half:], by_seq).astype(BF16)], axis=0)
+    return add_low(own, swap(to_x, "x"), swap(to_seq, "seq"))
+
+
+def scatter_blocks(terms):
+    blocks = [terms[i * (terms.shape[0] // 8) : (i + 1) * (terms.shape[0] // 8)] for i in range(8)]
+    across = scatter_square(*blocks[4:]).astype(BF16)
+    near = scatter_square(*blocks[:4])
+    return near + swap(across, "zl").astype(F32)
+
+
+def copies_kernel(plan, table_ref, *refs):
+    sources, target, sems = refs[:-2], refs[-2], refs[-1]
+    copies = []
+    for i, (source, from_index, to_index) in enumerate(plan):
+        copy = pltpu.make_async_copy(
+            sources[source].at[from_index(table_ref)], target.at[to_index(table_ref)], sems.at[i]
+        )
+        copy.start()
+        copies.append(copy)
+    for copy in copies:
+        copy.wait()
+
+
+def copies(plan, table, out_shape, *sources):
+    moved = 2 * math.prod(out_shape) * 2
+    return pl.pallas_call(
+        functools.partial(copies_kernel, plan),
+        out_shape=jax.ShapeDtypeStruct(out_shape, BF16),
+        in_specs=[pl.BlockSpec(memory_space=pltpu.SMEM)] + [pl.BlockSpec(memory_space=pl.ANY)] * len(sources),
+        out_specs=pl.BlockSpec(memory_space=pl.ANY),
+        scratch_shapes=[pltpu.SemaphoreType.DMA((len(plan),))],
+        cost_estimate=pl.CostEstimate(flops=0, bytes_accessed=moved, transcendentals=0),
+        name="place_blocks",
+    )(table, *sources)
+
+
+class Place:
+    def __init__(self):
+        self.seq = lax.axis_index("seq")
+        self.x = lax.axis_index("x")
+        self.core = lax.axis_index("core")
+        self.zh = lax.axis_index("zh")
+        self.zl = lax.axis_index("zl")
+
+    def block(self, x, core, zh, zl):
+        return ((x * 2 + core) * 2 + zh) * 2 + zl
+
+
+def column_slices(place, weights, width):
+    rows = weights[0].shape[0]
+    table = jnp.stack(
+        [
+            place.block(place.x ^ dx, core, place.seq, place.zl ^ dz)
+            for dx in range(2)
+            for dz in range(2)
+            for core in range(2)
+        ]
+    ).astype(jnp.int32)
+    plan = []
+    for target in range(4):
+        for w in range(len(weights)):
+            for core in range(2):
+
+                def from_index(ref, entry=target * 2 + core):
+                    return (slice(None), pl.ds(pl.multiple_of(ref[entry] * width, width), width))
+
+                def to_index(ref, target=target, start=(w * 2 + core) * width):
+                    return (target, slice(None), pl.ds(start, width))
+
+                plan.append((w, from_index, to_index))
+    return copies(plan, table, (4, rows, 2 * width * len(weights)), *weights)
+
+
+def chip_columns(place, weights, width):
+    slices = column_slices(place, weights, width)
+    near = jnp.stack(
+        [slices[0], swap(slices[1], "zl"), swap(slices[2], "x"), swap_both(slices[3], "x", "zl")]
+    )
+    far = swap(near, "zh")
+    near_other = swap(near, "core")
+    far_other = swap(far, "core")
+    table = jnp.stack(
+        [
+            place.block(place.x ^ dx, place.core ^ dc, place.zh ^ dh, place.zl ^ dz)
+            for dc in range(2)
+            for dh in range(2)
+            for dx in range(2)
+            for dz in range(2)
+        ]
+    ).astype(jnp.int32)
+    plan = []
+    for part in range(4):
+        for i in range(4):
+
+            def from_index(ref, i=i):
+                return (i,)
+
+            def to_index(ref, entry=part * 4 + i):
+                return (ref[entry],)
+
+            plan.append((part, from_index, to_index))
+    rows, wide = near.shape[1:]
+    whole = copies(plan, table, (16, rows, wide), near, far, near_other, far_other)
+    return whole.reshape(16 * rows, wide)
+
+
+def chip_rows(place, weight):
+    moved = lax.ppermute(weight, ("seq", "zh"), [(0, 1), (3, 2)])
+    own = jnp.where(place.zh == place.seq, weight, moved)
+    other = swap(own, "core")
+    first = place.core == 0
+    return jnp.concatenate([jnp.where(first, own, other), jnp.where(first, other, own)], axis=0)
+
+
+def sum_rows(place, terms):
+    rows = terms.shape[0] // 2
+    parts = terms.reshape(2, rows, terms.shape[1])
+    received = swap(lax.dynamic_index_in_dim(parts, 1 - place.core, 0, False), "core")
+    own = add_low(lax.dynamic_index_in_dim(parts, place.core, 0, False), received)
+    far = lax.ppermute(own.astype(BF16), ("seq", "zh"), [(1, 0), (2, 3)])
+    total = (own + far.astype(F32)).astype(BF16)
+    copied = lax.ppermute(total, ("seq", "zh"), [(0, 2), (3, 1)])
+    return jnp.where(place.zh == place.seq, total, copied).astype(F32)
+
+
+def sum_columns(place, terms):
+    rows, wide = terms.shape[0] // 16, terms.shape[1]
+    parts = terms.reshape(2, 2, 2, 2, rows, wide)
+    received = swap(lax.dynamic_index_in_dim(parts, 1 - place.core, 1, False), "core")
+    own = add_low(lax.dynamic_index_in_dim(parts, place.core, 1, False), received).astype(BF16)
+    received = swap(lax.dynamic_index_in_dim(own, 1 - place.zh, 1, False), "zh")
+    own = add_low(lax.dynamic_index_in_dim(own, place.zh, 1, False), received).astype(BF16)
+
+    def piece(dx, dz):
+        return lax.dynamic_slice(own, (place.x ^ dx, place.zl ^ dz, 0, 0), (1, 1, rows, wide))[0, 0]
+
+    near = jnp.stack(
+        [piece(0, 0), swap(piece(0, 1), "zl"), swap(piece(1, 0), "x"), swap_both(piece(1, 1), "x", "zl")]
+    )
+    return near, swap(near, "seq")
+
+
+def finish_kernel(count, choice_ref, dy_ref, *refs):
+    near, far, weights, outs = refs[: 2 * count][0::2], refs[: 2 * count][1::2], refs[2 * count : 3 * count], refs[3 * count :]
+    j = pl.program_id(0)
+    use_near = dy_ref[j] == 0
+    total = None
+    for i in range(count):
+        grad = jnp.where(use_near, near[i][0].astype(F32), far[i][0].astype(F32))
+        outs[i][...] = grad
+        term = grad * weights[i][...].astype(F32)
+        total = term if total is None else total + term
+
+    @pl.when(j == 0)
+    def _():
+        outs[count][...] = jnp.zeros_like(outs[count])
+
+    outs[count][...] += total
+
+
+def finish_columns(place, near, far, weights, width):
+    count, rows = len(weights), weights[0].shape[0]
+    chips, picks = [], []
+    for x in range(2):
+        for core in range(2):
+            for zh in range(2):
+                for zl in range(2):
+                    chips.append((place.x ^ x) * 2 + (place.zl ^ zl))
+                    picks.append(place.seq ^ zh)
+    choice = jnp.stack(chips).astype(jnp.int32)
+    pick = jnp.stack(picks).astype(jnp.int32)
+
+    def piece_spec(w):
+        return pl.BlockSpec((1, rows, width), lambda j, choice, pick: (choice[j], 0, 2 * w + (j // 4) % 2))
+
+    column_spec = pl.BlockSpec((rows, width), lambda j, choice, pick: (0, j))
+    in_specs, operands = [], []
+    for w in range(count):
+        in_specs += [piece_spec(w), piece_spec(w)]
+        operands += [near, far]
+    outs = pl.pallas_call(
+        functools.partial(finish_kernel, count),
+        grid_spec=pltpu.PrefetchScalarGridSpec(
+            num_scalar_prefetch=2,
+            grid=(16,),
+            in_specs=in_specs + [column_spec] * count,
+            out_specs=[column_spec] * count + [pl.BlockSpec((rows, width), lambda j, choice, pick: (0, 0))],
+        ),
+        out_shape=[jax.ShapeDtypeStruct((rows, 16 * width), F32)] * count + [jax.ShapeDtypeStruct((rows, width), F32)],
+        compiler_params=BIG,
+        cost_estimate=pl.CostEstimate(flops=0, bytes_accessed=12 * count * rows * 16 * width, transcendentals=0),
+        name="finish_columns",
+    )(choice, pick, *operands, *weights)
+    return outs[:count], jnp.sum(outs[count], axis=1)
+
+
+def turn(value, cosine, sine):
+    lane = lax.broadcasted_iota(jnp.int32, value.shape, 1)
+    partner = jnp.where(lane % HEAD_DIM < HEAD_DIM // 2, pltpu.roll(value, 96, 1), pltpu.roll(value, 32, 1))
+    return value * cosine + partner * sine
+
+
+def project_kernel(x_ref, w_ref, gain_ref, cos_ref, sin_ref, a_ref, q_ref, k_ref, v_ref):
+    x = x_ref[...].astype(F32)
+    inverse = lax.rsqrt(jnp.mean(x * x, axis=-1, keepdims=True) + epsilon)
+    a = (x * inverse * gain_ref[...].astype(F32)).astype(BF16)
+    a_ref[...] = a
+    joined = jnp.dot(a, w_ref[...], preferred_element_type=F32)
+    wide = q_ref.shape[1]
+    cosine, sine = cos_ref[...], sin_ref[...]
+    for i in range(wide // 128):
+        at = slice(i * 128, (i + 1) * 128)
+        q_ref[:, at] = turn(joined[:, at], cosine, sine).astype(BF16)
+        k_ref[:, at] = turn(joined[:, wide + i * 128 : wide + (i + 1) * 128], cosine, sine).astype(BF16)
+    v_ref[...] = joined[:, 2 * wide :].astype(BF16)
+
+
+def project(x_all, weight, gain, cosine, sine):
+    tokens, model = x_all.shape
+    wide = weight.shape[1] // 3
+    tile = cosine.shape[0]
+    whole = lambda shape: pl.BlockSpec(shape, lambda i: (0, 0))
+    by_tile = lambda columns: pl.BlockSpec((tile, columns), lambda i: (i, 0))
+    return pl.pallas_call(
+        project_kernel,
+        grid=(tokens // tile,),
+        in_specs=[by_tile(model), whole(weight.shape), whole((1, model)), whole(cosine.shape), whole(sine.shape)],
+        out_specs=[by_tile(model), by_tile(wide), by_tile(wide), by_tile(wide)],
+        out_shape=[jax.ShapeDtypeStruct((tokens, model), BF16)] + [jax.ShapeDtypeStruct((tokens, wide), BF16)] * 3,
+        compiler_params=BIG,
+        cost_estimate=pl.CostEstimate(
+            flops=2 * tokens * model * 3 * wide, bytes_accessed=4 * tokens * model, transcendentals=0
+        ),
+        name="norm_project",
+    )(x_all, weight, gain, cosine, sine)
+
+
+def head_lanes(value, odd):
+    lane = lax.broadcasted_iota(jnp.int32, value.shape, 1)
+    return jnp.where((lane >= HEAD_DIM) == odd, value, jnp.zeros_like(value))
+
+
+def probabilities(query, key, mask):
+    scores = lax.dot_general(query, key, (((1,), (1,)), ((), ())), preferred_element_type=F32) * 0.125
+    scores = jnp.where(mask, scores, masked_score)
+    weights = jnp.exp(scores - jnp.max(scores, axis=-1, keepdims=True))
+    return weights * (1.0 / jnp.sum(weights, axis=-1, keepdims=True))
+
+
+def allowed_keys(qpos_ref, start_ref, kpos_ref):
+    kpos = kpos_ref[...]
+    return (kpos <= qpos_ref[...]) & (kpos >= start_ref[0])
+
+
+def attend_kernel(q_ref, k_ref, k2_ref, v_ref, v2_ref, qpos_ref, start_ref, kpos_ref, o_ref):
+    mask = allowed_keys(qpos_ref, start_ref, kpos_ref)
+    for pair in range(q_ref.shape[1] // 128):
+        at = slice(pair * 128, (pair + 1) * 128)
+        query = q_ref[:, at]
+        key = jnp.concatenate([k_ref[:, at], k2_ref[:, at]], axis=0)
+        value = jnp.concatenate([v_ref[:, at], v2_ref[:, at]], axis=0)
+        total = None
+        for odd in (False, True):
+            weights = probabilities(head_lanes(query, odd), key, mask).astype(BF16)
+            term = jnp.dot(weights, head_lanes(value, odd), preferred_element_type=F32)
+            total = term if total is None else total + term
+        o_ref[:, at] = total.astype(BF16)
+
+
+def attend_back_kernel(
+    q_ref, k_ref, k2_ref, v_ref, v2_ref, do_ref, qpos_ref, start_ref, kpos_ref, cos_ref, sin_ref,
+    dq_ref, dk_ref, dk2_ref, dv_ref, dv2_ref,
+):
+    mask = allowed_keys(qpos_ref, start_ref, kpos_ref)
+    rows = q_ref.shape[0]
+    for pair in range(q_ref.shape[1] // 128):
+        at = slice(pair * 128, (pair + 1) * 128)
+        query, grad = q_ref[:, at], do_ref[:, at]
+        key = jnp.concatenate([k_ref[:, at], k2_ref[:, at]], axis=0)
+        value = jnp.concatenate([v_ref[:, at], v2_ref[:, at]], axis=0)
+        dq = dk = dv = 0.0
+        for odd in (False, True):
+            query_one, grad_one = head_lanes(query, odd), head_lanes(grad, odd)
+            weights = probabilities(query_one, key, mask)
+            dp = lax.dot_general(grad_one, value, (((1,), (1,)), ((), ())), preferred_element_type=F32)
+            inner = jnp.sum(dp * weights, axis=-1, keepdims=True)
+            ds = (weights * (dp - inner)).astype(BF16)
+            low = weights.astype(BF16)
+            dq = dq + jnp.dot(ds, head_lanes(key, odd), preferred_element_type=F32)
+            dk = dk + lax.dot_general(ds, query_one, (((0,), (0,)), ((), ())), preferred_element_type=F32)
+            dv = dv + lax.dot_general(low, grad_one, (((0,), (0,)), ((), ())), preferred_element_type=F32)
+        dq_ref[:, at] = turn(dq * 0.125, cos_ref[...], -sin_ref[...]).astype(BF16)
+        dk_ref[:, at] = dk[:rows] * 0.125
+        dk2_ref[:, at] = (dk[rows:] * 0.125).astype(BF16)
+        dv_ref[:, at] = dv[:rows]
+        dv2_ref[:, at] = dv[rows:].astype(BF16)
+
+
+def join_kernel(dq_ref, dk_ref, dk2_ref, dv_ref, dv2_ref, cos_ref, sin_ref, out_ref):
+    wide = dq_ref.shape[1]
+    out_ref[:, :wide] = dq_ref[...]
+    for i in range(wide // 128):
+        at = slice(i * 128, (i + 1) * 128)
+        dk = dk_ref[:, at] + dk2_ref[:, at].astype(F32)
+        out_ref[:, wide + i * 128 : wide + (i + 1) * 128] = turn(dk, cos_ref[...], -sin_ref[...]).astype(BF16)
+    out_ref[:, 2 * wide :] = (dv_ref[...] + dv2_ref[...].astype(F32)).astype(BF16)
+
+
+def by_sequence(kernel, name, operands, outs, flops):
+    rows = next(a.shape[0] for a, kind in operands if kind == "rows") // 4
+
+    def spec(shape, kind):
+        if kind == "rows":
+            return pl.BlockSpec((rows, shape[1]), lambda i: (i, 0))
+        if kind == "one":
+            return pl.BlockSpec((1,) + shape[1:], lambda i: (i,) + (0,) * (len(shape) - 1))
+        return pl.BlockSpec(shape, lambda i: (0,) * len(shape))
+
+    return pl.pallas_call(
+        kernel,
+        grid=(4,),
+        in_specs=[spec(a.shape, kind) for a, kind in operands],
+        out_specs=[spec(s.shape, "rows") for s in outs],
+        out_shape=outs,
+        compiler_params=BIG,
+        cost_estimate=pl.CostEstimate(flops=flops, bytes_accessed=8_000_000, transcendentals=0),
+        name=name,
+    )(*[a for a, _ in operands])
+
+
+def hidden_kernel(b_ref, dy_ref, w_ref, down_ref, z_ref, d_ref):
+    width = z_ref.shape[1]
+    chunk = math.gcd(width, 512)
+    b, dy = b_ref[...], dy_ref[...]
+    for i in range(width // chunk):
+        at = slice(i * chunk, (i + 1) * chunk)
+        up_at = slice(width + i * chunk, width + (i + 1) * chunk)
+        gate = jnp.dot(b, w_ref[:, at], preferred_element_type=F32)
+        up = jnp.dot(b, w_ref[:, up_at], preferred_element_type=F32)
+        dz = lax.dot_general(dy, down_ref[at, :], (((1,), (1,)), ((), ())), preferred_element_type=F32)
+        sig = jax.nn.sigmoid(gate)
+        silu = gate * sig
+        z_ref[:, at] = (silu * up).astype(BF16)
+        d_ref[:, at] = (dz * up * sig * (1.0 + gate * (1.0 - sig))).astype(BF16)
+        d_ref[:, up_at] = (dz * silu).astype(BF16)
+
+
+def hidden_units(b_all, dy_all, weight, down):
+    tokens, model = b_all.shape
+    width = down.shape[0]
+    tile = math.gcd(tokens, 256)
+    whole = lambda shape: pl.BlockSpec(shape, lambda i: (0, 0))
+    by_tile = lambda columns: pl.BlockSpec((tile, columns), lambda i: (i, 0))
+    return pl.pallas_call(
+        hidden_kernel,
+        grid=(tokens // tile,),
+        in_specs=[by_tile(model), by_tile(model), whole(weight.shape), whole(down.shape)],
+        out_specs=[by_tile(width), by_tile(2 * width)],
+        out_shape=[jax.ShapeDtypeStruct((tokens, width), BF16), jax.ShapeDtypeStruct((tokens, 2 * width), BF16)],
+        compiler_params=BIG,
+        cost_estimate=pl.CostEstimate(
+            flops=6 * tokens * model * width, bytes_accessed=8 * tokens * model, transcendentals=0
+        ),
+        name="hidden_units",
+    )(b_all, dy_all, weight, down)
+
+
+def norm_back(values, grad, gain):
+    inverse = lax.rsqrt(jnp.mean(values * values, axis=-1, keepdims=True) + epsilon)
+    normed = values * inverse
+    scaled = grad * gain
+    return inverse * (scaled - normed * jnp.mean(scaled * normed, axis=-1, keepdims=True))
+
+
+def dot_low(left, right, left_dim, right_dim):
+    return lax.dot_general(
+        left, right, (((left_dim,), (right_dim,)), ((), ())), preferred_element_type=F32
+    ).astype(BF16)
+
+
+def paired_device(
+    layer_input, document_ids, cotangent, attention_gain, query_weight, key_weight, value_weight, output_weight,
+    feedforward_gain, gate_weight, up_weight, down_weight,
+):
+    place = Place()
+    x_own, dy_own = layer_input[0], cotangent[0]
+    tok_count, model = x_own.shape
+    block_rows = tok_count // 2
+    length = document_ids.shape[1]
+    block_count = length // block_rows
+    rows = query_weight.shape[0]
+    hidden_rows = down_weight.shape[0]
+
+    def positions(dx, dc):
+        holder = (place.x ^ dx) * 2 + (place.core ^ dc)
+        return place_of(holder, jnp.arange(tok_count, dtype=jnp.int32), block_rows, block_count // 2)
+
+    qpos = jnp.concatenate([positions(0, 0), positions(1, 0)])
+    kpos = jnp.concatenate([positions(0, 0), positions(1, 0), positions(0, 1), positions(1, 1)])
+    cosine, sine = rotation(qpos, HEAD_DIM)
+    cosine = jnp.concatenate([cosine] * 4, axis=1)
+    sine = jnp.concatenate([-sine, sine] * 2, axis=1)
+    documents = document_ids[0]
+    first = jnp.sum((documents[None, :] < documents[:, None]).astype(jnp.int32), axis=1)
+    firsts = jnp.stack([first, swap(first, "seq")])
+    firsts = jnp.concatenate([firsts, swap(firsts, "zl")]).reshape(4, block_count, block_rows)
+    starts = []
+    for dx in range(2):
+        holder = (place.x ^ dx) * 2 + place.core
+        for index in (holder, block_count - 1 - holder):
+            starts.append(lax.dynamic_index_in_dim(firsts, index, 1, False))
+    start = jnp.concatenate(starts, axis=1)[:, :, None]
+    qpos, kpos = qpos[:, None], kpos[None, :]
+
+    gains = lax.all_gather(
+        jnp.stack([attention_gain, feedforward_gain]), ("x", "core", "zh", "zl"), axis=1, tiled=True
+    )
+    attn_gain, ff_gain = gains[:1], gains[1:].astype(F32)
+
+    qkv_weight = chip_columns(place, [query_weight, key_weight, value_weight], rows)
+    x_all = jnp.concatenate(gather_blocks(x_own), axis=0)
+    x_all = after(x_all, qkv_weight)
+    gate_weight, up_weight, down_weight, output_weight, dy_start, _ = lax.optimization_barrier(
+        (gate_weight, up_weight, down_weight, output_weight, dy_own, x_all)
+    )
+    out_rows = chip_rows(place, output_weight)
+    gate_up = chip_columns(place, [gate_weight, up_weight], hidden_rows)
+    down_rows = chip_rows(place, down_weight)
+    dy_all = jnp.concatenate(gather_blocks(dy_start), axis=0)
+
+    a_all, q_all, k_all, v_all = project(x_all, qkv_weight, attn_gain, cosine, sine)
+    k_other, v_other = swap(k_all, "core"), swap(v_all, "core")
+    common = [(q_all, "rows"), (k_all, "rows"), (k_other, "rows"), (v_all, "rows"), (v_other, "rows")]
+    where = [(qpos, "whole"), (start, "one"), (kpos, "whole")]
+    token_total = q_all.shape[0]
+    wide = q_all.shape[1]
+    score_flops = 2 * token_total * length * wide
+    (o_all,) = by_sequence(
+        attend_kernel, "attend", common + where, [jax.ShapeDtypeStruct((token_total, wide), BF16)], 2 * score_flops
+    )
+    hidden = x_own.astype(F32) + scatter_blocks(dot_low(o_all, out_rows, 1, 0))
+    inverse = lax.rsqrt(jnp.mean(hidden * hidden, axis=-1, keepdims=True) + epsilon)
+    b_own = (hidden * inverse * ff_gain).astype(BF16)
+    b_all = jnp.concatenate(gather_blocks(b_own), axis=0)
+
+    z_all, d_all = hidden_units(b_all, dy_all, gate_up, down_rows)
+    db = scatter_blocks(dot_low(d_all, gate_up, 1, 1))
+    z_late = after(z_all, db)
+    layer_output = (hidden + scatter_blocks(dot_low(z_late, down_rows, 1, 0))).astype(BF16)
+    dh = dy_own.astype(F32) + norm_back(hidden, db, ff_gain)
+    dh_all = jnp.concatenate(gather_blocks(dh.astype(BF16)), axis=0)
+
+    gate_up_near, gate_up_far = sum_columns(place, dot_low(b_all, d_all, 0, 0))
+    (gate_grad, up_grad), ff_sum = finish_columns(
+        place, gate_up_near, gate_up_far, [gate_weight, up_weight], hidden_rows
+    )
+    down_grad = sum_rows(place, dot_low(z_all, dy_all, 0, 0))
+    output_grad = sum_rows(place, dot_low(o_all, dh_all, 0, 0))
+
+    do_all = dot_low(dh_all, out_rows, 1, 1)
+    low = jax.ShapeDtypeStruct((token_total, wide), BF16)
+    high = jax.ShapeDtypeStruct((token_total, wide), F32)
+    tables = [(cosine, "whole"), (sine, "whole")]
+    dq, dk, dk_other, dv, dv_other = by_sequence(
+        attend_back_kernel, "attend_back", common + [(do_all, "rows")] + where + tables,
+        [low, high, low, high, low], 5 * score_flops,
+    )
+    dk_other, dv_other = swap(dk_other, "core"), swap(dv_other, "core")
+    (d_qkv,) = by_sequence(
+        join_kernel, "join_grads",
+        [(dq, "rows"), (dk, "rows"), (dk_other, "rows"), (dv, "rows"), (dv_other, "rows")] + tables,
+        [jax.ShapeDtypeStruct((token_total, 3 * wide), BF16)], 0,
+    )
+    da = scatter_blocks(dot_low(d_qkv, qkv_weight, 1, 1))
+    qkv_near, qkv_far = sum_columns(place, dot_low(a_all, d_qkv, 0, 0))
+    (query_grad, key_grad, value_grad), attn_sum = finish_columns(
+        place, qkv_near, qkv_far, [query_weight, key_weight, value_weight], rows
+    )
+    input_grad = (dh + norm_back(x_own.astype(F32), da, attn_gain.astype(F32))).astype(BF16)
+    attn_gain_grad = attn_sum / attention_gain.astype(F32)
+    ff_gain_grad = ff_sum / feedforward_gain.astype(F32)
+    return (
+        layer_output[None], input_grad[None], attn_gain_grad, query_grad, key_grad, value_grad, output_grad,
+        ff_gain_grad, gate_grad, up_grad, down_grad,
+    )
+
+
+def paired(mesh):
+    fine = Mesh(mesh.devices.reshape(2, 2, 2, 2, 2), ("seq", "x", "core", "zh", "zl"))
+    tokens = P(("seq", "zh", "zl"), ("x", "core"), None)
+    matrix, vector = P(("x", "core", "zh", "zl"), None), P(("x", "core", "zh", "zl"))
+    return jax.shard_map(
+        paired_device,
+        mesh=fine,
+        in_specs=(tokens, P(("seq", "zh", "zl"), None), tokens, vector) + (matrix,) * 4 + (vector,) + (matrix,) * 3,
+        out_specs=(tokens, tokens, vector) + (matrix,) * 4 + (vector,) + (matrix,) * 3,
+        check_vma=False,
+    )
+
+
+def solution(mesh):
+    if tuple(mesh.shape[axis] for axis in ("seq", "ctx", "fsdp")) == (2, 4, 4):
+        return paired(mesh)
+    return gathered(mesh)

time: 3990 us -> 1480 us (0.37)
  waiting for transfers between devices: 3350 us -> 493 us
  Pallas kernels: 0 us -> 550 us
  matrix products: 325 us -> 76.1 us
  starting transfers between devices: 0.72 us -> 193 us
  blocking collectives: 129 us -> 31.1 us
    reduce_scatter x6 -> x0, waiting for transfers between devices: 2500 us -> none  [the longest x1 1240 us: per_device(): lax.psum_scatter(jnp.einsum('td,tf->df', piece, joined_grads, preferred_e...]
    all_gather x9 -> x0, waiting for transfers between devices: 706 us -> none  [the longest x1 172 us: per_device(): lax.all_gather(gate_weight, ('ctx', 'fsdp'), axis=0, tiled=True)]
    pallas_call x0 -> x11, Pallas kernels: none -> 550 us  [the longest x4 445 us: copies(): pl.pallas_call(functools.partial(copies_kernel, plan), out_shape=jax.Shap...]
    ppermute x0 -> x112, waiting for transfers between devices: none -> 493 us  [the longest x102 316 us: swap(): return lax.ppermute(value, axis, [(0, 1), (1, 0)])]
    dot_general x48 -> x9, matrix products: 325 us -> 76.1 us  [dot_low(): lax.dot_general(left, right, (((left_dim,), (right_dim,)), ((), ())), pre...]
    ppermute x0 -> x112, starting transfers between devices: none -> 193 us  [the longest x102 175 us: swap(): return lax.ppermute(value, axis, [(0, 1), (1, 0)])]
    psum x1 -> x0, waiting for transfers between devices: 95.2 us -> none  [per_device(): lax.psum(attn_shards[2].astype(jnp.bfloat16), 'seq').astype(jnp.float32)]
    unnamed x1 -> x0, blocking collectives: 59.9 us -> none
  transfers between devices with their start and end apart: 18 -> 112, of which waited for: 16 -> 41; matrix products, arithmetic and copies ran while one was open for 8% -> 11% of each run, Pallas kernels for 0% -> 34%
where the time goes in v1:
time: 1480 us; the launch traced here: 1470 us
  Pallas kernels  550 us (37%)
  waiting for transfers between devices  493 us (33%)
  starting transfers between devices  193 us (13%)
  matrix products  76.1 us (5%)
  local copies, waits for them, and re-layouts  69.1 us (5%)
  other arithmetic  59.3 us (4%)
  blocking collectives  31.1 us (2%)
    pallas_call x4, Pallas kernels, copies(): pl.pallas_call(functools.partial(copies_kernel, plan), out_shape=jax.Shap...  445 us
    ppermute x102, waiting for transfers between devices, swap(): return lax.ppermute(value, axis, [(0, 1), (1, 0)])  316 us
    ppermute x102, starting transfers between devices, swap(): return lax.ppermute(value, axis, [(0, 1), (1, 0)])  175 us
    ppermute x2, waiting for transfers between devices, sum_rows(): far = lax.ppermute(own.astype(BF16), ('seq', 'zh'), [(1, 0), (2, 3)])  111 us
    dot_general x9, matrix products, dot_low(): lax.dot_general(left, right, (((left_dim,), (right_dim,)), ((), ())), pre...  76.1 us
    ppermute x2, waiting for transfers between devices, sum_rows(): copied = lax.ppermute(total, ('seq', 'zh'), [(0, 2), (3, 1)])  48.3 us
    pallas_call x3, Pallas kernels, by_sequence(): pl.pallas_call(kernel, grid=(4,), in_specs=[spec(a.shape, kind) for a, ki...  41.4 us
    unnamed x140, local copies, waits for them, and re-layouts  33.1 us
  transfers between devices with their start and end apart: 112, of which 41 were waited for; matrix products, arithmetic and copies ran while one was open for 11% of the time, Pallas kernels for 34%

profile of v1, /device:TPU:0, one launch (start us, length us, event | category | flops | bytes accessed | tf_op | source)
XLA Modules:
  0.0 1474.9 jit_solution(10746864002354529664)
XLA Ops:
  9.1 25.9 %place_blocks.4 = bf16[4,128,768]{2,1,0:T(8,128)(2,1)} custom-call(s32[8]{0:T(128)} %stack.137.table_ref, bf16[128,2048]{1,0:T(8,128)(2,1)} %refs_6_.1, bf16[128,2048]{1,0:T(8,128)(2,1)} %refs_7_.1, bf16[128,2048]{1,0:T(8,128)(2,1)} %refs_8_.1), custom_call_target="tpu_custom_call" | custom-call | bytes 1572864 | tf_op jit(solution)/shard_map/place_blocks/pallas_call | solution.py:441
  37.4 31.1 %all_gather.3 = bf16[2,2048]{1,0:T(2,128)(2,1)S(1)} all-gather(bf16[2,128]{1,0:T(2,128)(2,1)S(1)} %pad_maximum_fusion.26), channel_id=1, replica_groups=mesh['seq'=2,'x'=2,'core'=2,'zh'=2,'zl'=2] {'x','core','zh','zl'}, dimensions={1}, use_global_device_ids=true | all-gather | bytes 8704 | tf_op jit(solution)/shard_map/all_gather | solution.py:830
  93.0 24.2 %collective-permute-done.12.refs_1_ = bf16[4,128,768]{2,1,0:T(8,128)(2,1)} collective-permute-done((bf16[4,128,768]{2,1,0:T(8,128)(2,1)S(1)}, bf16[4,128,768]{2,1,0:T(8,128)(2,1)}, u32[]{:S(2)}, u32[]{:S(2)}) %collective-permute-start.12) | collective-permute-done | bytes 786464 | tf_op jit(solution)/shard_map/ppermute | solution.py:378
  129.1 97.2 %place_blocks.5 = bf16[16,128,768]{2,1,0:T(8,128)(2,1)} custom-call(s32[16]{0:T(128)} %stack.128.table_ref, bf16[4,128,768]{2,1,0:T(8,128)(2,1)} %copy-done.24, bf16[4,128,768]{2,1,0:T(8,128)(2,1)} %collective-permute-done.12.refs_1_, bf16[4,128,768]{2,1,0:T(8,128)(2,1)} %copy-done.33, bf16[4,128,768]{2,1,0:T(8,128)(2,1)} %copy-done.34), custom_call_target="tpu_custom_call" | custom-call | bytes 6291456 | tf_op jit(solution)/shard_map/place_blocks/pallas_call | solution.py:441
  230.5 65.4 %place_blocks.6 = bf16[4,128,2048]{2,1,0:T(8,128)(2,1)} custom-call(s32[8]{0:T(128)} %stack.137.table_ref, bf16[128,8192]{1,0:T(8,128)(2,1)} %refs_4_, bf16[128,8192]{1,0:T(8,128)(2,1)} %refs_5_), custom_call_target="tpu_custom_call" | custom-call | bytes 4194304 | tf_op jit(solution)/shard_map/place_blocks/pallas_call | solution.py:441
  305.0 11.4 norm_project.1
  317.9 8.2 collective-permute-done.49
  332.8 9.9 collective-permute-done.39
  342.8 13.7 attend.1
  372.6 7.8 collective-permute-done.23
  383.2 5.6 collective-permute-done.41
  391.8 13.9 collective-permute-done.26
  405.7 17.5 %collective-permute-done.28 = bf16[192,2048]{1,0:T(8,128)(2,1)S(1)} collective-permute-done((bf16[192,2048]{1,0:T(8,128)(2,1)S(1)}, bf16[192,2048]{1,0:T(8,128)(2,1)S(1)}, u32[]{:S(2)}, u32[]{:S(2)}) %collective-permute-start.28) | collective-permute-done | bytes 786464 | tf_op jit(solution)/shard_map/ppermute | solution.py:378
  428.8 10.0 collective-permute-done.24
  438.8 67.7 %collective-permute-start.47 = (bf16[96,2048]{1,0:T(8,128)(2,1)S(1)}, bf16[96,2048]{1,0:T(8,128)(2,1)S(1)}, u32[]{:S(2)}, u32[]{:S(2)}) collective-permute-start(bf16[96,2048]{1,0:T(8,128)(2,1)S(1)} %slice.431), channel_id=1, source_target_pairs={{0,16},{16,0},{1,17},{17,1},{2,18},{18,2},{3,19},{19,3},{4,20},{20... | collective-permute-start | bytes 1179656 | tf_op jit(solution)/shard_map/ppermute | solution.py:378
  510.4 6.1 collective-permute-done.47
  518.1 13.9 collective-permute-done.31
  535.6 6.3 collective-permute-done.32
  541.9 24.7 %collective-permute-start.36 = (bf16[192,2048]{1,0:T(8,128)(2,1)S(1)}, bf16[192,2048]{1,0:T(8,128)(2,1)S(1)}, u32[]{:S(2)}, u32[]{:S(2)}) collective-permute-start(bf16[192,2048]{1,0:T(8,128)(2,1)S(1)} %collective-permute-done.34), channel_id=1, source_target_pairs={{0,16},{16,0},{1,17},{17,1},{2,18},{18,2},{3,19},{19,3},{4,20},{20... | collective-permute-start | bytes 2359304 | tf_op jit(solution)/shard_map/ppermute | solution.py:378
  574.2 10.5 collective-permute-done.36
  591.2 256.0 %place_blocks.7 = bf16[16,128,2048]{2,1,0:T(8,128)(2,1)} custom-call(s32[16]{0:T(128)} %stack.128.table_ref, bf16[4,128,2048]{2,1,0:T(8,128)(2,1)} %copy-done.7, bf16[4,128,2048]{2,1,0:T(8,128)(2,1)} %copy-done.27, bf16[4,128,2048]{2,1,0:T(8,128)(2,1)} %copy-done.28, bf16[4,128,2048]{2,1,0:T(8,128)(2,1)} %collective-permute-done.53.refs_3_), custom_call_target="tpu_custom_call" | custom-call | bytes 16777216 | tf_op jit(solution)/shard_map/place_blocks/pallas_call | solution.py:441
  848.9 28.2 %hidden_units.1 = (bf16[1536,1024]{1,0:T(8,128)(2,1)}, bf16[1536,2048]{1,0:T(8,128)(2,1)}) custom-call(bf16[1536,2048]{1,0:T(8,128)(2,1)} %constant_dynamic-update-slice_fusion.13.b_ref, bf16[1536,2048]{1,0:T(8,128)(2,1)} %constant_dynamic-update-slice_fusion.23.dy_ref, bf16[2048,2048]{1,0:T(8,128)(2,1)} %bitcast.163, ...), custom_call_target="tpu_custom_call" | custom-call | flops 19327352832 | bytes 25165824 | tf_op jit(solution)/shard_map/hidden_units/pallas_call | solution.py:769
  877.1 17.4 %convolution_convert_fusion.4 = bf16[1536,2048]{1,0:T(8,128)(2,1)S(1)} fusion(bf16[1536,2048]{1,0:T(8,128)(2,1)} %get-tuple-element.46, bf16[2048,2048]{1,0:T(8,128)(2,1)} %bitcast.164), kind=kOutput, calls=%fused_computation.6 | convolution fusion | flops 12888047616 | bytes 20971520 | tf_op jit(solution)/shard_map/dot_general | solution.py:791
  902.8 7.1 collective-permute-done.62
  910.7 5.8 collective-permute-done.58
  921.3 19.8 %convolution_convert_fusion.2 = bf16[2048,2048]{1,0:T(8,128)(2,1)} fusion(bf16[1536,2048]{1,0:T(8,128)(2,1)} %constant_dynamic-update-slice_fusion.13.b_ref, bf16[1536,2048]{1,0:T(8,128)(2,1)} %get-tuple-element.46), kind=kOutput, calls=%fused_computation.4 | convolution fusion | flops 12889096192 | bytes 20971520 | tf_op jit(solution)/shard_map/dot_general | solution.py:791
  946.1 9.3 convolution_convert_fusion.5
  957.1 7.1 constant_dynamic-slice_fusion.1
  970.1 7.1 convolution_convert_fusion.3
  1002.7 12.2 collective-permute-done.75
  1019.5 21.6 %collective-permute-done.76 = bf16[96,2048]{1,0:T(8,128)(2,1)S(1)} collective-permute-done((bf16[96,2048]{1,0:T(8,128)(2,1)S(1)}, bf16[96,2048]{1,0:T(8,128)(2,1)S(1)}, u32[]{:S(2)}, u32[]{:S(2)}) %collective-permute-start.76) | collective-permute-done | bytes 393248 | tf_op jit(solution)/shard_map/ppermute | solution.py:378
  1045.6 13.3 collective-permute-done.80
  1061.7 6.3 collective-permute-done.81
  1075.0 22.0 %attend_back.1 = (bf16[1536,256]{1,0:T(8,128)(2,1)}, f32[1536,256]{1,0:T(8,128)}, bf16[1536,256]{1,0:T(8,128)(2,1)}, f32[1536,256]{1,0:T(8,128)}, bf16[1536,256]{1,0:T(8,128)(2,1)}) custom-call(bf16[1536,256]{1,0:T(8,128)(2,1)} %get-tuple-element.37.q_ref, bf16[1536,256]{1,0:T(8,128)(2,1)} %get-tuple-element.38.k_ref, ...), custom_call_target="tpu_custom_call" | custom-call | flops 3019898880 | bytes 8000000 | tf_op jit(solution)/shard_map/attend_back/pallas_call | solution.py:734
  1097.6 5.9 fusion
  1106.7 87.5 %collective-permute-done.110 = bf16[512,2048]{1,0:T(8,128)(2,1)} collective-permute-done((bf16[512,2048]{1,0:T(8,128)(2,1)}, bf16[512,2048]{1,0:T(8,128)(2,1)}, u32[]{:S(2)}, u32[]{:S(2)}) %collective-permute-start.110) | collective-permute-done | bytes 2097184 | tf_op jit(solution)/shard_map/ppermute | solution.py:535
  1200.6 5.7 join_grads.1
  1206.2 7.6 convolution_convert_fusion
  1213.9 8.6 convolution_convert_fusion.6
  1225.3 23.4 %collective-permute-done.101 = bf16[128,2048]{1,0:T(8,128)(2,1)} collective-permute-done((bf16[128,2048]{1,0:T(8,128)(2,1)}, bf16[128,2048]{1,0:T(8,128)(2,1)}, u32[]{:S(2)}, u32[]{:S(2)}) %collective-permute-start.101) | collective-permute-done | bytes 524320 | tf_op jit(solution)/shard_map/ppermute | solution.py:535
  1266.3 48.2 %collective-permute-done.102 = bf16[128,2048]{1,0:T(8,128)(2,1)S(1)} collective-permute-done((bf16[128,2048]{1,0:T(8,128)(2,1)S(1)}, bf16[128,2048]{1,0:T(8,128)(2,1)S(1)}, u32[]{:S(2)}, u32[]{:S(2)}) %collective-permute-start.102) | collective-permute-done | bytes 524320 | tf_op jit(solution)/shard_map/ppermute | solution.py:537
  1315.7 13.4 collective-permute-done.92
  1336.8 27.5 %collective-permute-done.95 = bf16[2,2,128,768]{3,2,1,0:T(8,128)(2,1)S(1)} collective-permute-done((bf16[2,2,128,768]{3,2,1,0:T(8,128)(2,1)S(1)}, bf16[2,2,128,768]{3,2,1,0:T(8,128)(2,1)S(1)}, u32[]{:S(2)}, u32[]{:S(2)}) %collective-permute-start.95) | collective-permute-done | bytes 786464 | tf_op jit(solution)/shard_map/ppermute | solution.py:378
  1372.6 18.6 %collective-permute-done.98 = bf16[128,768]{1,0:T(8,128)(2,1)S(1)} collective-permute-done((bf16[128,768]{1,0:T(8,128)(2,1)S(1)}, bf16[128,768]{1,0:T(8,128)(2,1)S(1)}, u32[]{:S(2)}, u32[]{:S(2)}) %collective-permute-start.98) | collective-permute-done | bytes 196640 | tf_op jit(solution)/shard_map/ppermute | solution.py:382
  1397.2 5.4 collective-permute-done.96
  1407.1 38.7 %collective-permute-done.99.refs_1_.refs_3_.refs_5_ = bf16[4,128,768]{2,1,0:T(8,128)(2,1)S(1)} collective-permute-done((bf16[4,128,768]{2,1,0:T(8,128)(2,1)S(1)}, bf16[4,128,768]{2,1,0:T(8,128)(2,1)S(1)}, u32[]{:S(2)}, u32[]{:S(2)}) %collective-permute-start.99) | collective-permute-done | bytes 786464 | tf_op jit(solution)/shard_map/ppermute | solution.py:378
  1446.7 10.5 finish_columns.2
  1458.7 14.2 finish_columns.3
  (458 shorter events, 253.0 us)
Async XLA Ops:
  0.7 86.2 %collective-permute-start.1 = (bf16[192,2048]{1,0:T(8,128)(2,1)}, bf16[192,2048]{1,0:T(8,128)(2,1)S(1)}, u32[]{:S(2)}, u32[]{:S(2)}) collective-permute-start(bf16[192,2048]{1,0:T(8,128)(2,1)} %bitcast.157), channel_id=1, source_target_pairs={{0,16},{16,0},{1,17},{17,1},{2,18},{18,2},{3,19},{19,3},{4,20},{20... | collective-permute-start | bytes 2359304 | tf_op jit(solution)/shard_map/ppermute | solution.py:378
  3.7 84.4 %collective-permute-start = (bf16[192,2048]{1,0:T(8,128)(2,1)}, bf16[192,2048]{1,0:T(8,128)(2,1)S(1)}, u32[]{:S(2)}, u32[]{:S(2)}) collective-permute-start(bf16[192,2048]{1,0:T(8,128)(2,1)} %bitcast.158), channel_id=1, source_target_pairs={{0,8},{8,0},{1,9},{9,1},{2,10},{10,2},{3,11},{11,3},{4,12},{12,4},... | collective-permute-start | bytes 2359304 | tf_op jit(solution)/shard_map/ppermute | solution.py:378
  5.2 84.5 %collective-permute-start.4 = (bf16[192,2048]{1,0:T(8,128)(2,1)}, bf16[192,2048]{1,0:T(8,128)(2,1)}, u32[]{:S(2)}, u32[]{:S(2)}) collective-permute-start(bf16[192,2048]{1,0:T(8,128)(2,1)} %bitcast.159), channel_id=1, source_target_pairs={{0,1},{1,0},{2,3},{3,2},{4,5},{5,4},{6,7},{7,6},{8,9},{9,8},{10,11... | collective-permute-start | bytes 2359304 | tf_op jit(solution)/shard_map/ppermute | solution.py:378
  7.8 66.8 %collective-permute-start.17 = (s32[768]{0:T(1024)S(1)}, s32[768]{0:T(1024)S(1)}, u32[]{:S(2)}, u32[]{:S(2)}) collective-permute-start(s32[768]{0:T(1024)S(1)} %convert_reduce_fusion), channel_id=1, source_target_pairs={{0,16},{16,0},{1,17},{17,1},{2,18},{18,2},{3,19},{19,3},{4,20},{20... | collective-permute-start | bytes 9224 | tf_op jit(solution)/shard_map/ppermute | solution.py:378
  36.3 38.8 %collective-permute-start.11 = (bf16[128,768]{1,0:T(8,128)(2,1)S(1)}, bf16[128,768]{1,0:T(8,128)(2,1)S(1)}, u32[]{:S(2)}, u32[]{:S(2)}) collective-permute-start(bf16[128,768]{1,0:T(8,128)(2,1)S(1)} %get-tuple-element.141), channel_id=1, source_target_pairs={{0,9},{1,8},{8,1},{9,0},{2,11},{3,10},{10,3},{11,2},{4,13},{5,12},... | collective-permute-start | bytes 589832 | tf_op jit(solution)/shard_map/ppermute | solution.py:382
  82.8 34.4 %collective-permute-start.12 = (bf16[4,128,768]{2,1,0:T(8,128)(2,1)S(1)}, bf16[4,128,768]{2,1,0:T(8,128)(2,1)}, u32[]{:S(2)}, u32[]{:S(2)}) collective-permute-start(bf16[4,128,768]{2,1,0:T(8,128)(2,1)S(1)} %pad_maximum_fusion.4.refs_0_), channel_id=1, source_target_pairs={{0,2},{2,0},{1,3},{3,1},{4,6},{6,4},{5,7},{7,5},{8,10},{10,8},{9,1... | collective-permute-start | bytes 2359304 | tf_op jit(solution)/shard_map/ppermute | solution.py:378
  122.2 104.2 %collective-permute-start.7 = (bf16[96,2048]{1,0:T(8,128)(2,1)}, bf16[96,2048]{1,0:T(8,128)(2,1)S(1)}, u32[]{:S(2)}, u32[]{:S(2)}) collective-permute-start(bf16[96,2048]{1,0:T(8,128)(2,1)} %slice.402), channel_id=1, source_target_pairs={{0,8},{8,0},{1,9},{9,1},{2,10},{10,2},{3,11},{11,3},{4,12},{12,4},... | collective-permute-start | bytes 1179656 | tf_op jit(solution)/shard_map/ppermute | solution.py:378
  123.9 103.3 %collective-permute-start.8 = (bf16[96,2048]{1,0:T(8,128)(2,1)}, bf16[96,2048]{1,0:T(8,128)(2,1)}, u32[]{:S(2)}, u32[]{:S(2)}) collective-permute-start(bf16[96,2048]{1,0:T(8,128)(2,1)} %slice.403), channel_id=1, source_target_pairs={{0,16},{16,0},{1,17},{17,1},{2,18},{18,2},{3,19},{19,3},{4,20},{20... | collective-permute-start | bytes 1179656 | tf_op jit(solution)/shard_map/ppermute | solution.py:378
  229.0 87.5 %collective-permute-start.19 = (bf16[128,2048]{1,0:T(8,128)(2,1)}, bf16[128,2048]{1,0:T(8,128)(2,1)S(1)}, u32[]{:S(2)}, u32[]{:S(2)}) collective-permute-start(bf16[128,2048]{1,0:T(8,128)(2,1)} %param.19), channel_id=1, source_target_pairs={{0,2},{18,16},{1,3},{19,17},{4,6},{22,20},{5,7},{23,21},{8,10},{26... | collective-permute-start | bytes 1572872 | tf_op jit(solution)/shard_map/ppermute | solution.py:523
  330.0 35.9 %collective-permute-start.43 = (bf16[192,2048]{1,0:T(8,128)(2,1)S(1)}, bf16[192,2048]{1,0:T(8,128)(2,1)S(1)}, u32[]{:S(2)}, u32[]{:S(2)}) collective-permute-start(bf16[192,2048]{1,0:T(8,128)(2,1)S(1)} %bitcast.169), channel_id=1, source_target_pairs={{0,1},{1,0},{2,3},{3,2},{4,5},{5,4},{6,7},{7,6},{8,9},{9,8},{10,11... | collective-permute-start | bytes 2359304 | tf_op jit(solution)/shard_map/ppermute | solution.py:378
  365.9 61.2 %collective-permute-start.54 = (bf16[512,2048]{1,0:T(8,128)(2,1)S(1)}, bf16[512,2048]{1,0:T(8,128)(2,1)S(1)}, u32[]{:S(2)}, u32[]{:S(2)}) collective-permute-start(bf16[512,2048]{1,0:T(8,128)(2,1)S(1)} %copy-done.26), channel_id=1, source_target_pairs={{0,2},{18,16},{1,3},{19,17},{4,6},{22,20},{5,7},{23,21},{8,10},{26... | collective-permute-start | bytes 6291464 | tf_op jit(solution)/shard_map/ppermute | solution.py:523
  380.4 44.6 %collective-permute-start.45 = (bf16[192,2048]{1,0:T(8,128)(2,1)S(1)}, bf16[192,2048]{1,0:T(8,128)(2,1)S(1)}, u32[]{:S(2)}, u32[]{:S(2)}) collective-permute-start(bf16[192,2048]{1,0:T(8,128)(2,1)S(1)} %collective-permute-done.43), channel_id=1, source_target_pairs={{0,16},{16,0},{1,17},{17,1},{2,18},{18,2},{3,19},{19,3},{4,20},{20... | collective-permute-start | bytes 2359304 | tf_op jit(solution)/shard_map/ppermute | solution.py:378
  388.8 34.4 %collective-permute-start.28 = (bf16[192,2048]{1,0:T(8,128)(2,1)S(1)}, bf16[192,2048]{1,0:T(8,128)(2,1)S(1)}, u32[]{:S(2)}, u32[]{:S(2)}) collective-permute-start(bf16[192,2048]{1,0:T(8,128)(2,1)S(1)} %pad_maximum_fusion.8), channel_id=1, source_target_pairs={{0,16},{16,0},{1,17},{17,1},{2,18},{18,2},{3,19},{19,3},{4,20},{20... | collective-permute-start | bytes 2359304 | tf_op jit(solution)/shard_map/ppermute | solution.py:378
  389.6 37.4 %collective-permute-start.44 = (bf16[192,2048]{1,0:T(8,128)(2,1)S(1)}, bf16[192,2048]{1,0:T(8,128)(2,1)S(1)}, u32[]{:S(2)}, u32[]{:S(2)}) collective-permute-start(bf16[192,2048]{1,0:T(8,128)(2,1)S(1)} %collective-permute-done.43), channel_id=1, source_target_pairs={{0,8},{8,0},{1,9},{9,1},{2,10},{10,2},{3,11},{11,3},{4,12},{12,4},... | collective-permute-start | bytes 2359304 | tf_op jit(solution)/shard_map/ppermute | solution.py:378
  423.2 83.3 %collective-permute-start.22 = (bf16[192,2048]{1,0:T(8,128)(2,1)S(1)}, bf16[192,2048]{1,0:T(8,128)(2,1)S(1)}, u32[]{:S(2)}, u32[]{:S(2)}) collective-permute-start(bf16[192,2048]{1,0:T(8,128)(2,1)S(1)} %pad_maximum_fusion.5), channel_id=1, source_target_pairs={{0,8},{8,0},{1,9},{9,1},{2,10},{10,2},{3,11},{11,3},{4,12},{12,4},... | collective-permute-start | bytes 2359304 | tf_op jit(solution)/shard_map/ppermute | solution.py:378
  425.0 81.5 %collective-permute-start.29 = (bf16[192,2048]{1,0:T(8,128)(2,1)S(1)}, bf16[192,2048]{1,0:T(8,128)(2,1)S(1)}, u32[]{:S(2)}, u32[]{:S(2)}) collective-permute-start(bf16[192,2048]{1,0:T(8,128)(2,1)S(1)} %add_convert_fusion.5), channel_id=1, source_target_pairs={{0,1},{1,0},{2,3},{3,2},{4,5},{5,4},{6,7},{7,6},{8,9},{9,8},{10,11... | collective-permute-start | bytes 2359304 | tf_op jit(solution)/shard_map/ppermute | solution.py:378
  427.0 108.0 %collective-permute-start.51 = (bf16[4,128,2048]{2,1,0:T(8,128)(2,1)S(1)}, bf16[4,128,2048]{2,1,0:T(8,128)(2,1)S(1)}, u32[]{:S(2)}, u32[]{:S(2)}) collective-permute-start(bf16[4,128,2048]{2,1,0:T(8,128)(2,1)S(1)} %pad_maximum_fusion.1.refs_0_), channel_id=1, source_target_pairs={{0,2},{2,0},{1,3},{3,1},{4,6},{6,4},{5,7},{7,5},{8,10},{10,8},{9,1... | collective-permute-start | bytes 6291464 | tf_op jit(solution)/shard_map/ppermute | solution.py:378
  427.1 80.6 %collective-permute-start.46 = (bf16[96,2048]{1,0:T(8,128)(2,1)S(1)}, bf16[96,2048]{1,0:T(8,128)(2,1)S(1)}, u32[]{:S(2)}, u32[]{:S(2)}) collective-permute-start(bf16[96,2048]{1,0:T(8,128)(2,1)S(1)} %slice.430), channel_id=1, source_target_pairs={{0,8},{8,0},{1,9},{9,1},{2,10},{10,2},{3,11},{11,3},{4,12},{12,4},... | collective-permute-start | bytes 1179656 | tf_op jit(solution)/shard_map/ppermute | solution.py:378
  438.8 77.8 %collective-permute-start.47 = (bf16[96,2048]{1,0:T(8,128)(2,1)S(1)}, bf16[96,2048]{1,0:T(8,128)(2,1)S(1)}, u32[]{:S(2)}, u32[]{:S(2)}) collective-permute-start(bf16[96,2048]{1,0:T(8,128)(2,1)S(1)} %slice.431), channel_id=1, source_target_pairs={{0,16},{16,0},{1,17},{17,1},{2,18},{18,2},{3,19},{19,3},{4,20},{20... | collective-permute-start | bytes 1179656 | tf_op jit(solution)/shard_map/ppermute | solution.py:378
  506.5 64.1 %collective-permute-start.55 = (bf16[512,2048]{1,0:T(8,128)(2,1)S(1)}, bf16[512,2048]{1,0:T(8,128)(2,1)S(1)}, u32[]{:S(2)}, u32[]{:S(2)}) collective-permute-start(bf16[512,2048]{1,0:T(8,128)(2,1)S(1)} %broadcast_select_fusion), channel_id=1, source_target_pairs={{0,4},{4,0},{1,5},{5,1},{2,6},{6,2},{3,7},{7,3},{8,12},{12,8},{9,1... | collective-permute-start | bytes 6291464 | tf_op jit(solution)/shard_map/ppermute | solution.py:378
  533.1 33.5 %collective-permute-start.33 = (bf16[96,2048]{1,0:T(8,128)(2,1)S(1)}, bf16[96,2048]{1,0:T(8,128)(2,1)S(1)}, u32[]{:S(2)}, u32[]{:S(2)}) collective-permute-start(bf16[96,2048]{1,0:T(8,128)(2,1)S(1)} %slice.425), channel_id=1, source_target_pairs={{0,16},{16,0},{1,17},{17,1},{2,18},{18,2},{3,19},{19,3},{4,20},{20... | collective-permute-start | bytes 1179656 | tf_op jit(solution)/shard_map/ppermute | solution.py:378
  535.0 54.9 %collective-permute-start.52 = (bf16[4,128,2048]{2,1,0:T(8,128)(2,1)S(1)}, bf16[4,128,2048]{2,1,0:T(8,128)(2,1)S(1)}, u32[]{:S(2)}, u32[]{:S(2)}) collective-permute-start(bf16[4,128,2048]{2,1,0:T(8,128)(2,1)S(1)} %pad_maximum_fusion.1.refs_0_), channel_id=1, source_target_pairs={{0,4},{4,0},{1,5},{5,1},{2,6},{6,2},{3,7},{7,3},{8,12},{12,8},{9,1... | collective-permute-start | bytes 6291464 | tf_op jit(solution)/shard_map/ppermute | solution.py:378
  535.1 56.1 %collective-permute-start.53 = (bf16[4,128,2048]{2,1,0:T(8,128)(2,1)S(1)}, bf16[4,128,2048]{2,1,0:T(8,128)(2,1)}, u32[]{:S(2)}, u32[]{:S(2)}) collective-permute-start(bf16[4,128,2048]{2,1,0:T(8,128)(2,1)S(1)} %collective-permute-done.51.refs_1_), channel_id=1, source_target_pairs={{0,4},{4,0},{1,5},{5,1},{2,6},{6,2},{3,7},{7,3},{8,12},{12,8},{9,1... | collective-permute-start | bytes 6291464 | tf_op jit(solution)/shard_map/ppermute | solution.py:378
  541.9 42.9 %collective-permute-start.36 = (bf16[192,2048]{1,0:T(8,128)(2,1)S(1)}, bf16[192,2048]{1,0:T(8,128)(2,1)S(1)}, u32[]{:S(2)}, u32[]{:S(2)}) collective-permute-start(bf16[192,2048]{1,0:T(8,128)(2,1)S(1)} %collective-permute-done.34), channel_id=1, source_target_pairs={{0,16},{16,0},{1,17},{17,1},{2,18},{18,2},{3,19},{19,3},{4,20},{20... | collective-permute-start | bytes 2359304 | tf_op jit(solution)/shard_map/ppermute | solution.py:378
  584.8 262.5 %collective-permute-start.37 = (bf16[96,2048]{1,0:T(8,128)(2,1)S(1)}, bf16[96,2048]{1,0:T(8,128)(2,1)S(1)}, u32[]{:S(2)}, u32[]{:S(2)}) collective-permute-start(bf16[96,2048]{1,0:T(8,128)(2,1)S(1)} %slice.426), channel_id=1, source_target_pairs={{0,8},{8,0},{1,9},{9,1},{2,10},{10,2},{3,11},{11,3},{4,12},{12,4},... | collective-permute-start | bytes 1179656 | tf_op jit(solution)/shard_map/ppermute | solution.py:378
  586.4 261.7 %collective-permute-start.38 = (bf16[96,2048]{1,0:T(8,128)(2,1)S(1)}, bf16[96,2048]{1,0:T(8,128)(2,1)S(1)}, u32[]{:S(2)}, u32[]{:S(2)}) collective-permute-start(bf16[96,2048]{1,0:T(8,128)(2,1)S(1)} %slice.427), channel_id=1, source_target_pairs={{0,16},{16,0},{1,17},{17,1},{2,18},{18,2},{3,19},{19,3},{4,20},{20... | collective-permute-start | bytes 1179656 | tf_op jit(solution)/shard_map/ppermute | solution.py:378
  966.7 131.0 %collective-permute-start.103 = (bf16[2,2,2,128,2048]{4,3,2,0,1:T(8,128)(2,1)}, bf16[2,2,2,128,2048]{4,3,2,0,1:T(8,128)(2,1)}, u32[]{:S(2)}, u32[]{:S(2)}) collective-permute-start(bf16[2,2,2,128,2048]{4,3,2,0,1:T(8,128)(2,1)} %bitcast.155), channel_id=1, source_target_pairs={{0,4},{4,0},{1,5},{5,1},{2,6},{6,2},{3,7},{7,3},{8,12},{12,8},{9,1... | collective-permute-start | bytes 12582920 | tf_op jit(solution)/shard_map/ppermute | solution.py:378
  999.8 43.2 %collective-permute-start.70 = (bf16[192,2048]{1,0:T(8,128)(2,1)S(1)}, bf16[192,2048]{1,0:T(8,128)(2,1)S(1)}, u32[]{:S(2)}, u32[]{:S(2)}) collective-permute-start(bf16[192,2048]{1,0:T(8,128)(2,1)S(1)} %pad_maximum_fusion.15), channel_id=1, source_target_pairs={{0,8},{8,0},{1,9},{9,1},{2,10},{10,2},{3,11},{11,3},{4,12},{12,4},... | collective-permute-start | bytes 2359304 | tf_op jit(solution)/shard_map/ppermute | solution.py:378
  1043.0 151.2 %collective-permute-start.110 = (bf16[512,2048]{1,0:T(8,128)(2,1)}, bf16[512,2048]{1,0:T(8,128)(2,1)}, u32[]{:S(2)}, u32[]{:S(2)}) collective-permute-start(bf16[512,2048]{1,0:T(8,128)(2,1)} %fusion.2), channel_id=1, source_target_pairs={{2,0},{16,18},{3,1},{17,19},{6,4},{20,22},{7,5},{21,23},{10,8},{24... | collective-permute-start | bytes 6291464 | tf_op jit(solution)/shard_map/ppermute | solution.py:535
  1072.2 126.1 %collective-permute-start.100 = (bf16[128,2048]{1,0:T(8,128)(2,1)}, bf16[128,2048]{1,0:T(8,128)(2,1)S(1)}, u32[]{:S(2)}, u32[]{:S(2)}) collective-permute-start(bf16[128,2048]{1,0:T(8,128)(2,1)} %dynamic-slice_bitcast_fusion.7), channel_id=1, source_target_pairs={{0,4},{4,0},{1,5},{5,1},{2,6},{6,2},{3,7},{7,3},{8,12},{12,8},{9,1... | collective-permute-start | bytes 1572872 | tf_op jit(solution)/shard_map/ppermute | solution.py:378
  1097.0 103.6 %collective-permute-start.83 = (bf16[1536,256]{1,0:T(8,128)(2,1)}, bf16[1536,256]{1,0:T(8,128)(2,1)}, u32[]{:S(2)}, u32[]{:S(2)}) collective-permute-start(bf16[1536,256]{1,0:T(8,128)(2,1)} %get-tuple-element.50), channel_id=1, source_target_pairs={{0,4},{4,0},{1,5},{5,1},{2,6},{6,2},{3,7},{7,3},{8,12},{12,8},{9,1... | collective-permute-start | bytes 2359304 | tf_op jit(solution)/shard_map/ppermute | solution.py:378
  1097.5 103.0 %collective-permute-start.84 = (bf16[1536,256]{1,0:T(8,128)(2,1)}, bf16[1536,256]{1,0:T(8,128)(2,1)}, u32[]{:S(2)}, u32[]{:S(2)}) collective-permute-start(bf16[1536,256]{1,0:T(8,128)(2,1)} %get-tuple-element.52), channel_id=1, source_target_pairs={{0,4},{4,0},{1,5},{5,1},{2,6},{6,2},{3,7},{7,3},{8,12},{12,8},{9,1... | collective-permute-start | bytes 2359304 | tf_op jit(solution)/shard_map/ppermute | solution.py:378
  1105.1 155.4 %collective-permute-start.104 = (bf16[2,2,128,2048]{3,2,1,0:T(8,128)(2,1)}, bf16[2,2,128,2048]{3,2,1,0:T(8,128)(2,1)}, u32[]{:S(2)}, u32[]{:S(2)}) collective-permute-start(bf16[2,2,128,2048]{3,2,1,0:T(8,128)(2,1)} %dynamic-slice_bitcast_fusion.1), channel_id=1, source_target_pairs={{0,2},{2,0},{1,3},{3,1},{4,6},{6,4},{5,7},{7,5},{8,10},{10,8},{9,1... | collective-permute-start | bytes 6291464 | tf_op jit(solution)/shard_map/ppermute | solution.py:378
  1199.3 49.5 %collective-permute-start.101 = (bf16[128,2048]{1,0:T(8,128)(2,1)}, bf16[128,2048]{1,0:T(8,128)(2,1)}, u32[]{:S(2)}, u32[]{:S(2)}) collective-permute-start(bf16[128,2048]{1,0:T(8,128)(2,1)} %fusion.13), channel_id=1, source_target_pairs={{2,0},{16,18},{3,1},{17,19},{6,4},{20,22},{7,5},{21,23},{10,8},{24... | collective-permute-start | bytes 1572872 | tf_op jit(solution)/shard_map/ppermute | solution.py:535
  1250.1 116.8 %collective-permute-start.111 = (bf16[512,2048]{1,0:T(8,128)(2,1)S(1)}, bf16[512,2048]{1,0:T(8,128)(2,1)S(1)}, u32[]{:S(2)}, u32[]{:S(2)}) collective-permute-start(bf16[512,2048]{1,0:T(8,128)(2,1)S(1)} %copy-done.10), channel_id=1, source_target_pairs={{0,16},{18,2},{1,17},{19,3},{4,20},{22,6},{5,21},{23,7},{8,24},{26... | collective-permute-start | bytes 6291464 | tf_op jit(solution)/shard_map/ppermute | solution.py:537
  1254.2 60.3 %collective-permute-start.102 = (bf16[128,2048]{1,0:T(8,128)(2,1)S(1)}, bf16[128,2048]{1,0:T(8,128)(2,1)S(1)}, u32[]{:S(2)}, u32[]{:S(2)}) collective-permute-start(bf16[128,2048]{1,0:T(8,128)(2,1)S(1)} %add_convert_fusion.6), channel_id=1, source_target_pairs={{0,16},{18,2},{1,17},{19,3},{4,20},{22,6},{5,21},{23,7},{8,24},{26... | collective-permute-start | bytes 1572872 | tf_op jit(solution)/shard_map/ppermute | solution.py:537
  1259.0 56.7 %collective-permute-start.90 = (bf16[192,2048]{1,0:T(8,128)(2,1)S(1)}, bf16[192,2048]{1,0:T(8,128)(2,1)S(1)}, u32[]{:S(2)}, u32[]{:S(2)}) collective-permute-start(bf16[192,2048]{1,0:T(8,128)(2,1)S(1)} %pad_maximum_fusion.19), channel_id=1, source_target_pairs={{0,8},{8,0},{1,9},{9,1},{2,10},{10,2},{3,11},{11,3},{4,12},{12,4},... | collective-permute-start | bytes 2359304 | tf_op jit(solution)/shard_map/ppermute | solution.py:378
  1260.5 68.6 %collective-permute-start.92 = (bf16[192,2048]{1,0:T(8,128)(2,1)S(1)}, bf16[192,2048]{1,0:T(8,128)(2,1)S(1)}, u32[]{:S(2)}, u32[]{:S(2)}) collective-permute-start(bf16[192,2048]{1,0:T(8,128)(2,1)S(1)} %pad_maximum_fusion.20), channel_id=1, source_target_pairs={{0,16},{16,0},{1,17},{17,1},{2,18},{18,2},{3,19},{19,3},{4,20},{20... | collective-permute-start | bytes 2359304 | tf_op jit(solution)/shard_map/ppermute | solution.py:378
  1265.6 65.6 %collective-permute-start.107 = (bf16[128,2048]{1,0:T(8,128)(2,1)S(1)}, bf16[128,2048]{1,0:T(8,128)(2,1)S(1)}, u32[]{:S(2)}, u32[]{:S(2)}) collective-permute-start(bf16[128,2048]{1,0:T(8,128)(2,1)S(1)} %get-tuple-element.124), channel_id=1, source_target_pairs={{0,9},{1,8},{8,1},{9,0},{2,11},{3,10},{10,3},{11,2},{4,13},{5,12},... | collective-permute-start | bytes 1572872 | tf_op jit(solution)/shard_map/ppermute | solution.py:382
  1329.1 35.2 %collective-permute-start.95 = (bf16[2,2,128,768]{3,2,1,0:T(8,128)(2,1)S(1)}, bf16[2,2,128,768]{3,2,1,0:T(8,128)(2,1)S(1)}, u32[]{:S(2)}, u32[]{:S(2)}) collective-permute-start(bf16[2,2,128,768]{3,2,1,0:T(8,128)(2,1)S(1)} %dynamic-slice_bitcast_fusion.2), channel_id=1, source_target_pairs={{0,2},{2,0},{1,3},{3,1},{4,6},{6,4},{5,7},{7,5},{8,10},{10,8},{9,1... | collective-permute-start | bytes 2359304 | tf_op jit(solution)/shard_map/ppermute | solution.py:378
  1331.3 35.4 %collective-permute-start.88 = (bf16[192,2048]{1,0:T(8,128)(2,1)S(1)}, bf16[192,2048]{1,0:T(8,128)(2,1)S(1)}, u32[]{:S(2)}, u32[]{:S(2)}) collective-permute-start(bf16[192,2048]{1,0:T(8,128)(2,1)S(1)} %pad_maximum_fusion.18), channel_id=1, source_target_pairs={{0,16},{16,0},{1,17},{17,1},{2,18},{18,2},{3,19},{19,3},{4,20},{20... | collective-permute-start | bytes 2359304 | tf_op jit(solution)/shard_map/ppermute | solution.py:378
  1332.1 34.7 %collective-permute-start.86 = (bf16[192,2048]{1,0:T(8,128)(2,1)S(1)}, bf16[192,2048]{1,0:T(8,128)(2,1)S(1)}, u32[]{:S(2)}, u32[]{:S(2)}) collective-permute-start(bf16[192,2048]{1,0:T(8,128)(2,1)S(1)} %pad_maximum_fusion.17), channel_id=1, source_target_pairs={{0,8},{8,0},{1,9},{9,1},{2,10},{10,2},{3,11},{11,3},{4,12},{12,4},... | collective-permute-start | bytes 2359304 | tf_op jit(solution)/shard_map/ppermute | solution.py:378
  1333.3 34.7 %collective-permute-start.93 = (bf16[192,2048]{1,0:T(8,128)(2,1)S(1)}, bf16[192,2048]{1,0:T(8,128)(2,1)S(1)}, u32[]{:S(2)}, u32[]{:S(2)}) collective-permute-start(bf16[192,2048]{1,0:T(8,128)(2,1)S(1)} %add_convert_fusion.1), channel_id=1, source_target_pairs={{0,1},{1,0},{2,3},{3,2},{4,5},{5,4},{6,7},{7,6},{8,9},{9,8},{10,11... | collective-permute-start | bytes 2359304 | tf_op jit(solution)/shard_map/ppermute | solution.py:378
  1364.3 38.8 %collective-permute-start.68 = (bf16[192,2048]{1,0:T(8,128)(2,1)S(1)}, bf16[192,2048]{1,0:T(8,128)(2,1)S(1)}, u32[]{:S(2)}, u32[]{:S(2)}) collective-permute-start(bf16[192,2048]{1,0:T(8,128)(2,1)S(1)} %copy-done.36), channel_id=1, source_target_pairs={{0,16},{16,0},{1,17},{17,1},{2,18},{18,2},{3,19},{19,3},{4,20},{20... | collective-permute-start | bytes 2359304 | tf_op jit(solution)/shard_map/ppermute | solution.py:378
  1366.7 36.4 %collective-permute-start.66 = (bf16[192,2048]{1,0:T(8,128)(2,1)S(1)}, bf16[192,2048]{1,0:T(8,128)(2,1)S(1)}, u32[]{:S(2)}, u32[]{:S(2)}) collective-permute-start(bf16[192,2048]{1,0:T(8,128)(2,1)S(1)} %copy-done.35), channel_id=1, source_target_pairs={{0,8},{8,0},{1,9},{9,1},{2,10},{10,2},{3,11},{11,3},{4,12},{12,4},... | collective-permute-start | bytes 2359304 | tf_op jit(solution)/shard_map/ppermute | solution.py:378
  1366.8 36.3 %collective-permute-start.73 = (bf16[192,2048]{1,0:T(8,128)(2,1)S(1)}, bf16[192,2048]{1,0:T(8,128)(2,1)S(1)}, u32[]{:S(2)}, u32[]{:S(2)}) collective-permute-start(bf16[192,2048]{1,0:T(8,128)(2,1)S(1)} %copy-done.37), channel_id=1, source_target_pairs={{0,1},{1,0},{2,3},{3,2},{4,5},{5,4},{6,7},{7,6},{8,9},{9,8},{10,11... | collective-permute-start | bytes 2359304 | tf_op jit(solution)/shard_map/ppermute | solution.py:378
  1366.9 91.9 %collective-permute-start.108 = (bf16[4,128,2048]{2,1,0:T(8,128)(2,1)}, bf16[4,128,2048]{2,1,0:T(8,128)(2,1)}, u32[]{:S(2)}, u32[]{:S(2)}) collective-permute-start(bf16[4,128,2048]{2,1,0:T(8,128)(2,1)} %pad_maximum_fusion.2.refs_0_.refs_2_), channel_id=1, source_target_pairs={{0,16},{16,0},{1,17},{17,1},{2,18},{18,2},{3,19},{19,3},{4,20},{20... | collective-permute-start | bytes 6291464 | tf_op jit(solution)/shard_map/ppermute | solution.py:378
  1402.7 43.1 %collective-permute-start.99 = (bf16[4,128,768]{2,1,0:T(8,128)(2,1)S(1)}, bf16[4,128,768]{2,1,0:T(8,128)(2,1)S(1)}, u32[]{:S(2)}, u32[]{:S(2)}) collective-permute-start(bf16[4,128,768]{2,1,0:T(8,128)(2,1)S(1)} %pad_maximum_fusion.21.refs_0_.refs_2_.refs_4_), channel_id=1, source_target_pairs={{0,16},{16,0},{1,17},{17,1},{2,18},{18,2},{3,19},{19,3},{4,20},{20... | collective-permute-start | bytes 2359304 | tf_op jit(solution)/shard_map/ppermute | solution.py:378
  (116 other events, 2369.9 us)

commit v2 on v0

--- a/solution.py
+++ b/solution.py
@@ -1,9 +1,12 @@
+import functools
 import math
 
 import jax
 import jax.numpy as jnp
 from jax import lax
-from jax.sharding import PartitionSpec as P
+from jax.experimental import pallas as pl
+from jax.experimental.pallas import tpu as pltpu
+from jax.sharding import Mesh, PartitionSpec as P
 
 HEADS = 32
 HEAD_DIM = 64
@@ -38,7 +41,7 @@
     )
 
 
-def place(holder, offset, block_rows, ctx_count):
+def place_of(holder, offset, block_rows, ctx_count):
     return jnp.where(
         offset < block_rows,
         holder * block_rows + offset,
@@ -71,9 +74,9 @@
     group_count = HEADS // group_heads
     group_width = group_heads * HEAD_DIM
     key_count = ctx_count * tok_count
-    local_pos = place(device, jnp.arange(tok_count, dtype=jnp.int32), block_rows, ctx_count)
+    local_pos = place_of(device, jnp.arange(tok_count, dtype=jnp.int32), block_rows, ctx_count)
     key_index = jnp.arange(key_count, dtype=jnp.int32)
-    key_pos = place(key_index // tok_count, key_index % tok_count, block_rows, ctx_count)
+    key_pos = place_of(key_index // tok_count, key_index % tok_count, block_rows, ctx_count)
     documents = document_ids[0]
     same_doc = jnp.take(documents, local_pos)[:, None] == jnp.take(documents, key_pos)[None, :]
     allowed = (key_pos[None, :] <= local_pos[:, None]) & same_doc
@@ -331,7 +334,7 @@
     )
 
 
-def solution(mesh):
+def gathered(mesh):
     return jax.shard_map(
         per_device,
         mesh=mesh,
@@ -364,3 +367,787 @@
         ),
         check_vma=False,
     )
+
+
+HIDDEN_PIECES = 2
+BIG = pltpu.CompilerParams(vmem_limit_bytes=56 * 1024 * 1024)
+BF16 = jnp.bfloat16
+F32 = jnp.float32
+
+
+def swap(value, axis):
+    return lax.ppermute(value, axis, [(0, 1), (1, 0)])
+
+
+def fence(late, early):
+    return list(lax.optimization_barrier((tuple(late), tuple(early)))[0])
+
+
+def opposite(along_x, along_seq):
+    half = along_x.shape[0] // 2
+    return [swap(along_seq[:half], "x"), swap(along_x[half:], "seq")]
+
+
+def along(block):
+    return [swap(block, "x"), swap(block, "seq")]
+
+
+def add_low(first, *others):
+    total = first.astype(F32)
+    for other in others:
+        total = total + other.astype(F32)
+    return total
+
+
+def return_halves(upper, lower):
+    return [swap(upper, "x"), swap(lower, "seq")]
+
+
+def return_along(to_x, to_seq, by_x, by_seq):
+    half = to_x.shape[0] // 2
+    to_seq = jnp.concatenate([add_low(to_seq[:half], by_x).astype(BF16), to_seq[half:]], axis=0)
+    to_x = jnp.concatenate([to_x[:half], add_low(to_x[half:], by_seq).astype(BF16)], axis=0)
+    return [swap(to_x, "x"), swap(to_seq, "seq")]
+
+
+def return_across(own, by_x, by_seq):
+    return swap(add_low(own, by_x, by_seq).astype(BF16), "zl")
+
+
+def in_order(mine, other, place):
+    first = place == 0
+    return jnp.stack([jnp.where(first, mine, other), jnp.where(first, other, mine)])
+
+
+def pair_up(mine, axis):
+    return in_order(mine, swap(mine, axis), lax.axis_index(axis))
+
+
+def slot(count, blocks, joined, w, block):
+    return block * count + w if joined else w * blocks + block
+
+
+def slices_kernel(count, blocks, joined, table_ref, *refs):
+    gain, out = refs[-2][...], refs[-1]
+    width = refs[0].shape[1]
+    for w in range(count):
+        for block in range(blocks):
+            at = slot(count, blocks, joined, w, block) * width
+            out[0, :, at : at + width] = (refs[blocks * w + block][...].astype(F32) * gain).astype(BF16)
+
+
+def column_slices(table, chips, blocks, column, weights, gain, width, joined):
+    rows = weights[0].shape[0]
+
+    def column_spec(block):
+        return pl.BlockSpec((rows, width), lambda t, table: (0, column(t, block, table)))
+
+    wide = blocks * width * len(weights)
+    return pl.pallas_call(
+        functools.partial(slices_kernel, len(weights), blocks, joined),
+        grid_spec=pltpu.PrefetchScalarGridSpec(
+            num_scalar_prefetch=1,
+            grid=(chips,),
+            in_specs=[column_spec(block) for _ in weights for block in range(blocks)]
+            + [pl.BlockSpec((rows, 1), lambda t, table: (0, 0))],
+            out_specs=pl.BlockSpec((1, rows, wide), lambda t, table: (t, 0, 0)),
+        ),
+        out_shape=jax.ShapeDtypeStruct((chips, rows, wide), BF16),
+        compiler_params=BIG,
+        cost_estimate=pl.CostEstimate(flops=0, bytes_accessed=1_000_000, transcendentals=0),
+        name="column_slices",
+    )(table, *[w for w in weights for _ in range(blocks)], gain)
+
+
+def hidden_slices(place, weights, gain, width):
+    def column(t, zh, table):
+        return (((t % 2) * 2 + table[0]) * 2 + zh) * 2 + t // 2
+
+    table = jnp.stack([place.seq]).astype(jnp.int32)
+    return column_slices(table, 4, 2, column, weights, gain, width, True)
+
+
+def head_slices(place, weights, gain, width):
+    def column(t, z, table):
+        return ((table[1] + t - 2 * table[1] * t) * 2 + table[0]) * 4 + z
+
+    table = jnp.stack([place.seq, place.x]).astype(jnp.int32)
+    return column_slices(table, 2, 4, column, weights, gain, width, False)
+
+
+def share_columns(slices):
+    return lax.all_to_all(slices, ("zl", "x"), split_axis=0, concat_axis=0, tiled=True)
+
+
+def chip_half(place, weight):
+    half = weight.shape[0] // 2
+    moved = lax.ppermute(
+        lax.dynamic_slice_in_dim(weight, (1 - place.core) * half, half, 0), ("seq", "core"), [(0, 1), (3, 2)]
+    )
+    own = lax.dynamic_slice_in_dim(weight, place.core * half, half, 0)
+    return jnp.where(place.core == place.seq, own, moved)
+
+
+def chip_rows(place, mine, other):
+    first = place.core == 0
+    halves = jnp.stack([jnp.where(first, mine, other), jnp.where(first, other, mine)], axis=1)
+    return halves.reshape(-1, mine.shape[-1])
+
+
+def add_core(place, parts, axis):
+    received = swap(lax.dynamic_index_in_dim(parts, 1 - place.core, axis, False), "core")
+    return add_low(lax.dynamic_index_in_dim(parts, place.core, axis, False), received).astype(BF16)
+
+
+def to_far(place, sums):
+    return lax.dynamic_index_in_dim(sums, 1 - place.zh, 0, False)
+
+
+def add_far(place, sums, received):
+    return add_low(lax.dynamic_index_in_dim(sums, place.zh, 0, False), received).astype(BF16)
+
+
+def own_rows(place, total, other):
+    mine = place.core == place.seq
+    received = swap(jnp.where(mine, other, total), "core")
+    kept = jnp.where(mine, total, other)
+    first = place.core == 0
+    return jnp.concatenate([jnp.where(first, kept, received), jnp.where(first, received, kept)]).astype(F32)
+
+
+def finish_kernel(count, *refs):
+    grads, weights, gain, outs = refs[:count], refs[count : 2 * count], refs[2 * count], refs[2 * count + 1 :]
+    j = pl.program_id(0)
+    total = None
+    for i in range(count):
+        grad = grads[i][0, 0].astype(F32)
+        outs[i][...] = grad * gain[...]
+        term = grad * weights[i][...].astype(F32)
+        total = term if total is None else total + term
+
+    @pl.when(j == 0)
+    def _():
+        outs[count][...] = jnp.zeros_like(outs[count])
+
+    outs[count][...] += total
+
+
+def finish_columns(pieces, weights, gain, width, joined):
+    count, rows = len(weights), weights[0].shape[0]
+
+    def piece_spec(w):
+        def index(j):
+            x, seq, zh, zl = j // 8, (j // 4) % 2, (j // 2) % 2, j % 2
+            if joined:
+                return seq, zl * 2 + x, 0, slot(count, 2, joined, w, zh)
+            return seq, x, 0, slot(count, 4, joined, w, zh * 2 + zl)
+
+        return pl.BlockSpec((1, 1, rows, width), index)
+
+    column_spec = pl.BlockSpec((rows, width), lambda j: (0, j))
+    outs = pl.pallas_call(
+        functools.partial(finish_kernel, count),
+        grid=(16,),
+        in_specs=[piece_spec(w) for w in range(count)]
+        + [column_spec] * count
+        + [pl.BlockSpec((rows, 1), lambda j: (0, 0))],
+        out_specs=[column_spec] * count + [pl.BlockSpec((rows, width), lambda j: (0, 0))],
+        out_shape=[jax.ShapeDtypeStruct((rows, 16 * width), F32)] * count + [jax.ShapeDtypeStruct((rows, width), F32)],
+        compiler_params=BIG,
+        cost_estimate=pl.CostEstimate(flops=0, bytes_accessed=1_000_000, transcendentals=0),
+        name="finish_columns",
+    )(*[pieces] * count, *weights, gain)
+    return outs[:count], jnp.sum(outs[count], axis=1)
+
+
+class Place:
+    def __init__(self):
+        self.seq = lax.axis_index("seq")
+        self.x = lax.axis_index("x")
+        self.core = lax.axis_index("core")
+        self.zh = lax.axis_index("zh")
+        self.zl = lax.axis_index("zl")
+
+
+def block_columns(value, source):
+    wide = value.shape[1] // 16
+    return jnp.concatenate([value[:, i * wide : (i + 1) * wide] for i in source], axis=1)
+
+
+def to_inner(value):
+    return block_columns(value, [x * 8 + z for z in range(8) for x in (0, 1)])
+
+
+def to_outer(value):
+    return block_columns(value, [z * 2 + x for x in (0, 1) for z in range(8)])
+
+
+def turn(value, cosine, sine):
+    lane = lax.broadcasted_iota(jnp.int32, value.shape, 1)
+    partner = jnp.where(lane % HEAD_DIM < HEAD_DIM // 2, pltpu.roll(value, 96, 1), pltpu.roll(value, 32, 1))
+    return value * cosine + partner * sine
+
+
+def project_kernel(a_ref, w_ref, cos_ref, sin_ref, q_ref, kv_ref):
+    joined = jnp.dot(a_ref[...], w_ref[...], preferred_element_type=F32)
+    wide = q_ref.shape[1]
+    cosine, sine = cos_ref[...], sin_ref[...]
+    for i in range(wide // 128):
+        at = slice(i * 128, (i + 1) * 128)
+        q_ref[:, at] = turn(joined[:, at], cosine, sine).astype(BF16)
+        kv_ref[:, at] = turn(joined[:, wide + i * 128 : wide + (i + 1) * 128], cosine, sine).astype(BF16)
+    kv_ref[:, wide:] = joined[:, 2 * wide :].astype(BF16)
+
+
+def whole_spec(array):
+    return pl.BlockSpec(array.shape, lambda i: (0,) * array.ndim)
+
+
+def project(a_all, weight, cosine, sine):
+    tokens, model = a_all.shape
+    wide = weight.shape[1] // 3
+    tile = cosine.shape[0]
+    by_tile = lambda columns: pl.BlockSpec((tile, columns), lambda i: (i, 0))
+    return pl.pallas_call(
+        project_kernel,
+        grid=(tokens // tile,),
+        in_specs=[by_tile(model), whole_spec(weight), whole_spec(cosine), whole_spec(sine)],
+        out_specs=[by_tile(wide), by_tile(2 * wide)],
+        out_shape=[jax.ShapeDtypeStruct((tokens, columns), BF16) for columns in (wide, 2 * wide)],
+        compiler_params=BIG,
+        cost_estimate=pl.CostEstimate(flops=0, bytes_accessed=1_000_000, transcendentals=0),
+        name="project",
+    )(a_all, weight, cosine, sine)
+
+
+def head_lanes(value, odd):
+    lane = lax.broadcasted_iota(jnp.int32, value.shape, 1)
+    return jnp.where((lane >= HEAD_DIM) == odd, value, jnp.zeros_like(value))
+
+
+def probabilities(query, key, mask):
+    scores = lax.dot_general(query, key, (((1,), (1,)), ((), ())), preferred_element_type=F32) * 0.125
+    scores = jnp.where(mask, scores, masked_score)
+    weights = jnp.exp(scores - jnp.max(scores, axis=-1, keepdims=True))
+    return weights * (1.0 / jnp.sum(weights, axis=-1, keepdims=True))
+
+
+def allowed_keys(qpos_ref, start_ref, kpos_ref):
+    kpos = kpos_ref[...]
+    return (kpos <= qpos_ref[...]) & (kpos >= start_ref[0])
+
+
+def attend_kernel(q_ref, kv_ref, kv2_ref, out_ref, qpos_ref, start_ref, kpos_ref, o_ref, *term_refs):
+    mask = allowed_keys(qpos_ref, start_ref, kpos_ref)
+    wide = q_ref.shape[1]
+    for pair in range(wide // 128):
+        at = slice(pair * 128, (pair + 1) * 128)
+        value_at = slice(wide + pair * 128, wide + (pair + 1) * 128)
+        query = q_ref[:, at]
+        key = jnp.concatenate([kv_ref[:, at], kv2_ref[:, at]], axis=0)
+        value = jnp.concatenate([kv_ref[:, value_at], kv2_ref[:, value_at]], axis=0)
+        total = None
+        for odd in (False, True):
+            weights = probabilities(head_lanes(query, odd), key, mask).astype(BF16)
+            term = jnp.dot(weights, head_lanes(value, odd), preferred_element_type=F32)
+            total = term if total is None else total + term
+        o_ref[:, at] = total.astype(BF16)
+    spill(term_refs, jnp.dot(o_ref[...], out_ref[...], preferred_element_type=F32).astype(BF16))
+
+
+def fill(refs, target):
+    at = 0
+    for ref in refs:
+        target[at : at + ref.shape[0]] = ref[...]
+        at += ref.shape[0]
+
+
+def spill(refs, value):
+    at = 0
+    for ref in refs:
+        ref[...] = value[at : at + ref.shape[0]]
+        at += ref.shape[0]
+
+
+def at_step(step, action, refs, value):
+    for k, group in enumerate((refs[:2], refs[2:])):
+
+        @pl.when(step == k)
+        def _(group=group):
+            action(group, value)
+
+
+def square_shapes(half, model):
+    return [(half, model)] * 3 + [(half // 2, model)] * 2
+
+
+def whole_shape(shape, **options):
+    return pl.BlockSpec(shape, lambda i: (0, 0), **options)
+
+
+def square_specs(half, model, **options):
+    return [whole_shape(shape, **options) for shape in square_shapes(half, model)]
+
+
+def sequence_shapes(sequence, half, model):
+    return square_shapes(half, model)[2 * sequence : 2 + 3 * sequence]
+
+
+def attend(sequence, q_all, kv_all, kv_other, out_rows, where, o_all):
+    (tokens, wide), model = q_all.shape, out_rows.shape[1]
+    rows = tokens // 2
+    qpos, start, kpos = where
+    at = lambda i: (sequence, 0)
+    in_specs = [
+        pl.BlockSpec((rows, wide), at),
+        pl.BlockSpec((rows, 2 * wide), at),
+        pl.BlockSpec((rows, 2 * wide), at),
+        whole_spec(out_rows),
+        whole_spec(qpos),
+        pl.BlockSpec((1, rows, 1), lambda i: (sequence, 0, 0)),
+        whole_spec(kpos),
+    ]
+    shapes = sequence_shapes(sequence, rows // 2, model)
+    return into(
+        attend_kernel, "attend", [q_all, kv_all, kv_other, out_rows, qpos, start, kpos], in_specs,
+        [(tokens, wide)] + shapes, [pl.BlockSpec((rows, wide), at)] + [whole_shape(shape) for shape in shapes],
+        [o_all], (1,),
+    )
+
+
+def into(kernel, name, operands, in_specs, shapes, out_specs, buffers, grid, types=None):
+    count = len(operands)
+    given = [b for b in buffers if b is not None]
+    types = types or [BF16] * len(shapes)
+
+    def body(*refs):
+        return kernel(*refs[:count], *refs[count + len(given) :])
+
+    return pl.pallas_call(
+        body,
+        grid=grid,
+        in_specs=in_specs + [pl.BlockSpec(memory_space=pl.ANY)] * len(given),
+        out_specs=out_specs,
+        out_shape=[jax.ShapeDtypeStruct(shape, kind) for shape, kind in zip(shapes, types)],
+        input_output_aliases={count + i: i for i in range(len(given))},
+        compiler_params=BIG,
+        cost_estimate=pl.CostEstimate(flops=0, bytes_accessed=1_000_000, transcendentals=0),
+        name=name,
+    )(*operands, *given)
+
+
+def hidden_kernel(*refs):
+    b_refs, dy_refs, (w_ref, down_ref, z_ref, d_ref, b_ref, dy_ref) = refs[:5], refs[5:10], refs[10:16]
+    db_refs, y_refs = refs[16:21], refs[21:]
+    step = pl.program_id(0)
+    at_step(step, fill, b_refs, b_ref)
+    at_step(step, fill, dy_refs, dy_ref)
+    piece = z_ref.shape[1] // HIDDEN_PIECES
+    for i in range(HIDDEN_PIECES):
+        at = slice(i * piece, (i + 1) * piece)
+        gate_at, up_at = slice(2 * i * piece, (2 * i + 1) * piece), slice((2 * i + 1) * piece, (2 * i + 2) * piece)
+        both = jnp.dot(b_ref[...], w_ref[:, 2 * i * piece : 2 * (i + 1) * piece], preferred_element_type=F32)
+        gate, up = both[:, :piece], both[:, piece:]
+        dz = lax.dot_general(dy_ref[...], down_ref[at, :], (((1,), (1,)), ((), ())), preferred_element_type=F32)
+        sig = jax.nn.sigmoid(gate)
+        silu = gate * sig
+        z_ref[:, at] = (silu * up).astype(BF16)
+        d_ref[:, gate_at] = (dz * up * sig * (1.0 + gate * (1.0 - sig))).astype(BF16)
+        d_ref[:, up_at] = (dz * silu).astype(BF16)
+    db = lax.dot_general(d_ref[...], w_ref[...], (((1,), (1,)), ((), ())), preferred_element_type=F32).astype(BF16)
+    y = jnp.dot(z_ref[...], down_ref[...], preferred_element_type=F32).astype(BF16)
+
+    at_step(step, spill, db_refs, db)
+    at_step(step, spill, y_refs, y)
+
+
+def hidden_units(square, b_blocks, dy_blocks, weight, down, buffers):
+    half, model = b_blocks[0].shape
+    rows, width = 2 * half, down.shape[0]
+    once = dict(pipeline_mode=pl.Buffered(1))
+    by_sequence = lambda columns: pl.BlockSpec((rows, columns), lambda i: (2 * square + i, 0))
+    return into(
+        hidden_kernel, "hidden_units", [*b_blocks, *dy_blocks, weight, down],
+        square_specs(half, model, **once) * 2 + [pl.BlockSpec(a.shape, lambda i: (0, 0), **once) for a in (weight, down)],
+        [(4 * rows, width), (4 * rows, 2 * width), (4 * rows, model), (4 * rows, model)] + square_shapes(half, model) * 2,
+        [by_sequence(width), by_sequence(2 * width), by_sequence(model), by_sequence(model)]
+        + square_specs(half, model) * 2,
+        buffers, (2,),
+    )
+
+
+def attend_back_kernel(count, *refs):
+    out_ref, q_ref, kv_ref, kv2_ref, qpos_ref, start_ref, kpos_ref, cos_ref, sin_ref = refs[count : count + 9]
+    dh_ref, dq_ref, dkv_ref, dkv2_ref = refs[count + 9 :]
+    mask = allowed_keys(qpos_ref, start_ref, kpos_ref)
+    rows, wide = q_ref.shape
+    fill(refs[:count], dh_ref)
+    do = lax.dot_general(
+        dh_ref[...], out_ref[...], (((1,), (1,)), ((), ())), preferred_element_type=F32
+    ).astype(BF16)
+    for pair in range(wide // 128):
+        at = slice(pair * 128, (pair + 1) * 128)
+        value_at = slice(wide + pair * 128, wide + (pair + 1) * 128)
+        query, grad = q_ref[:, at], do[:, at]
+        key = jnp.concatenate([kv_ref[:, at], kv2_ref[:, at]], axis=0)
+        value = jnp.concatenate([kv_ref[:, value_at], kv2_ref[:, value_at]], axis=0)
+        dq = dk = dv = 0.0
+        for odd in (False, True):
+            query_one, grad_one = head_lanes(query, odd), head_lanes(grad, odd)
+            weights = probabilities(query_one, key, mask)
+            dp = lax.dot_general(grad_one, value, (((1,), (1,)), ((), ())), preferred_element_type=F32)
+            inner = jnp.sum(dp * weights, axis=-1, keepdims=True)
+            ds = (weights * (dp - inner)).astype(BF16)
+            low = weights.astype(BF16)
+            dq = dq + jnp.dot(ds, head_lanes(key, odd), preferred_element_type=F32)
+            dk = dk + lax.dot_general(ds, query_one, (((0,), (0,)), ((), ())), preferred_element_type=F32)
+            dv = dv + lax.dot_general(low, grad_one, (((0,), (0,)), ((), ())), preferred_element_type=F32)
+        dq_ref[:, at] = turn(dq * 0.125, cos_ref[...], -sin_ref[...]).astype(BF16)
+        dkv_ref[:, at] = dk[:rows] * 0.125
+        dkv2_ref[:, at] = (dk[rows:] * 0.125).astype(BF16)
+        dkv_ref[:, value_at] = dv[:rows]
+        dkv2_ref[:, value_at] = dv[rows:].astype(BF16)
+
+
+def attend_back(sequence, dh_blocks, out_rows, q_all, kv_all, kv_other, where, tables, dh_all):
+    model, (tokens, wide) = dh_blocks[0].shape[1], q_all.shape
+    rows = tokens // 2
+    qpos, start, kpos = where
+    at = lambda i: (sequence, 0)
+    in_specs = [whole_spec(block) for block in dh_blocks] + [
+        whole_spec(out_rows),
+        pl.BlockSpec((rows, wide), at),
+        pl.BlockSpec((rows, 2 * wide), at),
+        pl.BlockSpec((rows, 2 * wide), at),
+        whole_spec(qpos),
+        pl.BlockSpec((1, rows, 1), lambda i: (sequence, 0, 0)),
+        whole_spec(kpos), whole_spec(tables[0]), whole_spec(tables[1]),
+    ]
+    return into(
+        functools.partial(attend_back_kernel, len(dh_blocks)), "attend_back",
+        [*dh_blocks, out_rows, q_all, kv_all, kv_other, qpos, start, kpos, *tables],
+        in_specs, [(tokens, model), (rows, wide), (rows, 2 * wide), (rows, 2 * wide)],
+        [pl.BlockSpec((rows, model), at)] + [whole_shape((rows, n * wide)) for n in (1, 2, 2)],
+        [dh_all], (1,), types=[BF16, BF16, F32, BF16],
+    )
+
+
+def join_kernel(dq_ref, dkv_ref, dkv2_ref, w_ref, cos_ref, sin_ref, out_ref, *term_refs):
+    wide = dq_ref.shape[1]
+    out_ref[:, :wide] = dq_ref[...]
+    for i in range(wide // 128):
+        at = slice(i * 128, (i + 1) * 128)
+        dk = dkv_ref[:, at] + dkv2_ref[:, at].astype(F32)
+        out_ref[:, wide + i * 128 : wide + (i + 1) * 128] = turn(dk, cos_ref[...], -sin_ref[...]).astype(BF16)
+    out_ref[:, 2 * wide :] = (dkv_ref[:, wide:] + dkv2_ref[:, wide:].astype(F32)).astype(BF16)
+    term = lax.dot_general(out_ref[...], w_ref[...], (((1,), (1,)), ((), ())), preferred_element_type=F32)
+    spill(term_refs, term.astype(BF16))
+
+
+def join_grads(sequence, dq, dkv, dkv_other, weight, tables, d_qkv):
+    (rows, wide), model = dq.shape, weight.shape[0]
+    operands = [dq, dkv, dkv_other, weight, *tables]
+    shapes = sequence_shapes(sequence, rows // 2, model)
+    return into(
+        join_kernel, "join_grads", operands, [whole_spec(a) for a in operands],
+        [(2 * rows, 3 * wide)] + shapes,
+        [pl.BlockSpec((rows, 3 * wide), lambda i: (sequence, 0))] + [whole_shape(shape) for shape in shapes],
+        [d_qkv], (1,),
+    )
+
+
+def on_rows(kernel, name, operands, types):
+    rows, model = operands[0].shape
+    tile = pl.BlockSpec((rows // 3, model), lambda i: (i, 0))
+    return pl.pallas_call(
+        kernel,
+        grid=(3,),
+        in_specs=[tile] * len(operands),
+        out_specs=[tile] * len(types),
+        out_shape=[jax.ShapeDtypeStruct((rows, model), kind) for kind in types],
+        compiler_params=BIG,
+        cost_estimate=pl.CostEstimate(flops=0, bytes_accessed=1_000_000, transcendentals=0),
+        name=name,
+    )(*operands)
+
+
+def total_of(refs):
+    return add_low(*[ref[...] for ref in refs])
+
+
+def open_kernel(x_ref, a_ref):
+    x = x_ref[...].astype(F32)
+    inverse = lax.rsqrt(jnp.mean(x * x, axis=-1, keepdims=True) + epsilon)
+    a_ref[...] = to_inner((x * inverse).astype(BF16))
+
+
+def close_attention_kernel(x_ref, *refs):
+    hidden_ref, b_ref = refs[-2:]
+    hidden = x_ref[...].astype(F32) + total_of(refs[:-2])
+    hidden_ref[...] = hidden
+    inverse = lax.rsqrt(jnp.mean(hidden * hidden, axis=-1, keepdims=True) + epsilon)
+    b_ref[...] = to_inner((hidden * inverse).astype(BF16))
+
+
+def close_hidden_kernel(dy_ref, hidden_ref, *refs):
+    dh_ref, low_ref = refs[-2:]
+    dh = dy_ref[...].astype(F32) + norm_back(hidden_ref[...], to_outer(total_of(refs[:-2])))
+    dh_ref[...] = dh
+    low_ref[...] = dh.astype(BF16)
+
+
+def close_input_kernel(x_ref, dh_ref, *refs):
+    out_ref = refs[-1]
+    out_ref[...] = (dh_ref[...] + norm_back(x_ref[...].astype(F32), to_outer(total_of(refs[:-1])))).astype(BF16)
+
+
+def norm_back(values, scaled):
+    inverse = lax.rsqrt(jnp.mean(values * values, axis=-1, keepdims=True) + epsilon)
+    normed = values * inverse
+    return inverse * (scaled - normed * jnp.mean(scaled * normed, axis=-1, keepdims=True))
+
+
+def dot_low(left, right, left_dim, right_dim):
+    return lax.dot_general(
+        left, right, (((left_dim,), (right_dim,)), ((), ())), preferred_element_type=F32
+    ).astype(BF16)
+
+
+def paired_device(
+    layer_input, document_ids, cotangent, attention_gain, query_weight, key_weight, value_weight, output_weight,
+    feedforward_gain, gate_weight, up_weight, down_weight,
+):
+    place = Place()
+    x_own, dy_own = layer_input[0], cotangent[0]
+    tok_count, model = x_own.shape
+    block_rows = tok_count // 2
+    length = document_ids.shape[1]
+    block_count = length // block_rows
+    rows = query_weight.shape[0]
+    hidden_rows = down_weight.shape[0]
+
+    attn_gain = attention_gain.astype(F32)[:, None]
+    ff_gain = feedforward_gain.astype(F32)[:, None]
+
+    mine, sent = head_slices(place, [query_weight, key_weight, value_weight], attn_gain, rows)
+    (a_own,) = on_rows(open_kernel, "open_layer", [x_own], [BF16])
+    received = swap(sent, "x")
+    a_x, a_s = along(a_own)
+    gate_up = hidden_slices(place, [gate_weight, up_weight], ff_gain, hidden_rows)
+    qkv = in_order(mine, received, place.x)
+    a_x, a_s, qkv, gate_up, out_late, dy_late, document_ids = fence(
+        [a_x, a_s, qkv, gate_up, output_weight, dy_own, document_ids], []
+    )
+
+    by_zh, by_zl = swap(qkv, "zh"), swap(qkv, "zl")
+    a_o = opposite(a_x, a_s)
+    gate_up = share_columns(gate_up)
+    dy_x, dy_s = along(dy_late)
+    documents = document_ids[0]
+    first = jnp.sum((documents[None, :] < documents[:, None]).astype(jnp.int32), axis=1)
+    out_half = chip_half(place, out_late)
+    a_all = jnp.concatenate([a_own, a_x, a_s, *a_o], axis=0)
+    by_zh, by_zl, a_all, out_half, first, dy_x, dy_s, dy_late, gate_up = fence(
+        [by_zh, by_zl, a_all, out_half, first, dy_x, dy_s, dy_late, gate_up], []
+    )
+
+    gate_up = lax.all_gather(gate_up, ("core", "zh"), axis=0, tiled=True).reshape(model, -1)
+    by_both = swap(by_zh, "zl")
+    qkv = in_order(in_order(qkv, by_zl, place.zl), in_order(by_zh, by_both, place.zl), place.zh)
+    dy_o = opposite(dy_x, dy_s)
+    out_zh, out_zl = swap(out_half, "zh"), swap(out_half, "zl")
+    first = jnp.stack([first, swap(first, "seq")])
+
+    def positions(dx, dc):
+        holder = (place.x ^ dx) * 2 + (place.core ^ dc)
+        return place_of(holder, jnp.arange(tok_count, dtype=jnp.int32), block_rows, block_count // 2)
+
+    qpos = jnp.concatenate([positions(0, 0), positions(1, 0)])
+    kpos = jnp.concatenate([positions(0, 0), positions(1, 0), positions(0, 1), positions(1, 1)])
+    cosine, sine = rotation(qpos, HEAD_DIM)
+    cosine = jnp.concatenate([cosine] * 4, axis=1)
+    sine = jnp.concatenate([-sine, sine] * 2, axis=1)
+    firsts = first.reshape(2, block_count, block_rows)
+    starts = []
+    for dx in range(2):
+        holder = (place.x ^ dx) * 2 + place.core
+        for index in (holder, block_count - 1 - holder):
+            starts.append(lax.dynamic_index_in_dim(firsts, index, 1, False))
+    start = jnp.concatenate(starts, axis=1)[:, :, None]
+    where = (qpos[:, None], start, kpos[None, :])
+    tables = (cosine, sine)
+    qkv, out_zh, out_zl, dy_late, where, tables = fence([qkv, out_zh, out_zl, dy_late, where, tables], dy_o)
+
+    qkv = in_order(qkv, swap(qkv, "core"), place.core).reshape(model, -1)
+    dy_l = swap(dy_late, "zl")
+    out_both = swap(out_zh, "zl")
+    out_half = in_order(
+        in_order(out_half, out_zl, place.zl), in_order(out_zh, out_both, place.zl), place.zh
+    ).reshape(4, -1, model)
+    qkv, out_half, down_late = fence([qkv, out_half, down_weight], [])
+
+    q_all, kv_all = project(a_all, qkv, *tables)
+    out_rows = chip_rows(place, out_half, swap(out_half, "core"))
+    down_half = chip_half(place, down_late)
+    quarter = down_half.shape[0] // 2
+    q_all, kv_all, out_rows, dy_l, down_half = fence([q_all, kv_all, out_rows, dy_l, down_half], [])
+
+    kv_other = swap(kv_all, "core")
+    o_all, term_s, *term_o = attend(1, q_all, kv_all, kv_other, out_rows, where, None)
+    dy_lx, dy_ls = along(dy_l)
+    term_s, term_o, o_all, dy_lx, dy_ls = fence([term_s, term_o, o_all, dy_lx, dy_ls], [])
+
+    o_all, own, term_x = attend(0, q_all, kv_all, kv_other, out_rows, where, o_all)
+    halves = return_halves(*term_o)
+    dy_lo = opposite(dy_lx, dy_ls)
+    own, term_x, halves, down_half = fence([own, term_x, halves, down_half], dy_lo)
+
+    down_far = [swap(down_half[:quarter], "zh")]
+    sums = return_along(term_x, term_s, *halves)
+    hidden, b_own = on_rows(close_attention_kernel, "close_attention", [x_own, own, *sums], [F32, BF16])
+    b_own, down_half = fence([b_own, down_half], [])
+
+    b_x, b_s = along(b_own)
+    b_l = swap(b_own, "zl")
+    b_x, b_s, b_l, down_half = fence([b_x, b_s, b_l, down_half], down_far)
+
+    down_far += [swap(down_half[quarter:], "zh")]
+    b_o = opposite(b_x, b_s)
+    (b_l,) = fence([b_l], b_o)
+
+    b_lx, b_ls = along(b_l)
+    down_half = in_order(down_half, jnp.concatenate(down_far), place.zh)
+    down_rows = chip_rows(place, down_half, swap(down_half, "core"))
+    *buffers, d0, d1, d2, d3, d4, y0, y1, y2, y3, y4 = hidden_units(
+        0, [b_own, b_x, b_s, *b_o], [dy_own, dy_x, dy_s, *dy_o], gate_up, down_rows, [None] * 4
+    )
+    b_lo = opposite(b_lx, b_ls)
+    near, near_y = [d0, d1, d2, d3, d4], [y0, y1, y2, y3, y4]
+    near, b_lx = fence([near, b_lx], b_lo)
+
+    *buffers, d0, d1, d2, d3, d4, y0, y1, y2, y3, y4 = hidden_units(
+        1, [b_l, b_lx, b_ls, *b_lo], [dy_l, dy_lx, dy_ls, *dy_lo], gate_up, down_rows, buffers
+    )
+    z_all, d_all, b_all, dy_all = buffers
+    far, far_y = [d0, d1, d2, d3, d4], [y0, y1, y2, y3, y4]
+    near_halves = return_halves(*near[3:])
+    near_along = return_along(near[1], near[2], *near_halves)
+    far, d_all = fence([far, d_all], near_along)
+
+    far_halves = return_halves(*far[3:])
+    gate_up_terms = dot_low(b_all, d_all, 0, 0)
+    z_all, gate_up_terms, far_halves = fence([z_all, gate_up_terms, far_halves], [])
+
+    far_along = return_along(far[1], far[2], *far_halves)
+    gate_up_sums = add_core(place, gate_up_terms.reshape(2, 2, 4, rows, -1), 0)
+    down_terms = dot_low(z_all, dy_all, 0, 0)
+    gate_up_sums, down_terms, near_y, near0, far_along = fence(
+        [gate_up_sums, down_terms, near_y, near[0], far_along], []
+    )
+
+    across = return_across(far[0], *far_along)
+    near_y_halves = return_halves(*near_y[3:])
+    gate_up_near = lax.psum_scatter(gate_up_sums, "zh", scatter_dimension=0, tiled=True)[0]
+    down_sums = add_core(place, down_terms.reshape(2, 2, -1, model), 1)
+    dh, dh_low = on_rows(
+        close_hidden_kernel, "close_hidden", [dy_own, hidden, near0, *near_along, across], [F32, BF16]
+    )
+    dh_low, down_sums, near_y_halves = fence([dh_low, down_sums, near_y_halves], [])
+
+    dh_x, dh_s = along(dh_low)
+    down_to_zh = to_far(place, down_sums)
+    dh_x, dh_s, down_to_zh, near_y, far_y = fence([dh_x, dh_s, down_to_zh, near_y, far_y], [])
+
+    dh_o = opposite(dh_x, dh_s)
+    dh_all, dq0, dkv0, dkv_other0 = attend_back(
+        0, [dh_low, dh_x], out_rows, q_all, kv_all, kv_other, where, tables, None
+    )
+    near_y_along = return_along(near_y[1], near_y[2], *near_y_halves)
+    down_far = [swap(down_to_zh[:quarter], "zh")]
+    dkv_other0, dh_s, far_y, down_to_zh = fence([dkv_other0, dh_s, far_y, down_to_zh], dh_o)
+
+    dkv_other0 = swap(dkv_other0, "core")
+    dh_all, dq1, dkv1, dkv_other1 = attend_back(
+        1, [dh_s, *dh_o], out_rows, q_all, kv_all, kv_other, where, tables, dh_all
+    )
+    far_y_halves = return_halves(*far_y[3:])
+    dkv0, dkv_other0, dkv_other1, dh_all, down_to_zh = fence(
+        [dkv0, dkv_other0, dkv_other1, dh_all, down_to_zh], [*near_y_along, *far_y_halves, *down_far]
+    )
+
+    dkv_other1 = swap(dkv_other1, "core")
+    d_qkv, own, term_x = join_grads(0, dq0, dkv0, dkv_other0, qkv, tables, None)
+    d_qkv, term_s, *term_o = join_grads(1, dq1, dkv1, dkv_other1, qkv, tables, d_qkv)
+    down_far += [swap(down_to_zh[quarter:], "zh")]
+    far_y_along = return_along(far_y[1], far_y[2], *far_y_halves)
+    out_terms = dot_low(o_all, dh_all, 0, 0)
+    own, term_x, term_s, term_o, d_qkv, out_terms = fence(
+        [own, term_x, term_s, term_o, d_qkv, out_terms], far_y_along
+    )
+
+    halves = return_halves(*term_o)
+    qkv_terms = dot_low(a_all, d_qkv, 0, 0)
+    out_sums = add_core(place, out_terms.reshape(4, 2, -1, model), 1).reshape(2, 2, -1, model)
+    y_across = return_across(far_y[0], *far_y_along)
+    qkv_terms, halves, out_sums = fence([qkv_terms, halves, out_sums], down_far)
+
+    sums = return_along(term_x, term_s, *halves)
+    qkv_sums = add_core(place, qkv_terms.reshape(2, 2, 2, 2 * rows, -1), 0)
+    qkv_sums, out_sums, sums, gate_up_near = fence([qkv_sums, out_sums, sums, gate_up_near], [y_across])
+
+    def part(sums, zh, zl):
+        return lax.dynamic_slice(sums, (place.zh ^ zh, place.zl ^ zl, 0, 0), (1, 1, *sums.shape[2:]))[0, 0]
+
+    qkv_zl, out_zl = swap(part(qkv_sums, 1, 1), "zl"), swap(part(out_sums, 1, 1), "zl")
+    gate_up_near = share_columns(gate_up_near)
+    (input_grad,) = on_rows(close_input_kernel, "close_input", [x_own, dh, own, *sums], [BF16])
+    down_total = add_far(place, down_sums, jnp.concatenate(down_far))
+    down_other = swap(down_total, "seq")
+    qkv_zl, out_zl, input_grad = fence([qkv_zl, out_zl, input_grad], [])
+
+    qkv_zh = swap(add_low(part(qkv_sums, 1, 0), qkv_zl).astype(BF16), "zh")
+    out_zh = swap(add_low(part(out_sums, 1, 0), out_zl).astype(BF16), "zh")
+    qkv_zl, out_zl = swap(part(qkv_sums, 0, 1), "zl"), swap(part(out_sums, 0, 1), "zl")
+    gate_up_far = swap(gate_up_near, "seq")
+    layer_output = add_low(hidden, near_y[0], *near_y_along, y_across).astype(BF16)
+    down_grad = own_rows(place, down_total, down_other)
+    qkv_zh, out_zh, qkv_zl, out_zl = fence([qkv_zh, out_zh, qkv_zl, out_zl], [layer_output, down_grad])
+
+    qkv_total = add_low(part(qkv_sums, 0, 0), qkv_zl, qkv_zh).astype(BF16).reshape(2, rows, -1)
+    out_total = add_low(part(out_sums, 0, 0), out_zl, out_zh).astype(BF16)
+    received = swap(lax.dynamic_index_in_dim(qkv_total, 1 - place.x, 0, False), "x")
+    out_other = swap(out_total, "seq")
+    qkv_near = in_order(lax.dynamic_index_in_dim(qkv_total, place.x, 0, False), received, place.x)
+    qkv_near, out_other, gate_up_far = fence([qkv_near, out_other, gate_up_far], [])
+
+    qkv_far = swap(qkv_near, "seq")
+    (gate_grad, up_grad), ff_gain_grad = finish_columns(
+        in_order(gate_up_near, gate_up_far, place.seq), [gate_weight, up_weight], ff_gain, hidden_rows, True
+    )
+    output_grad = own_rows(place, out_total, out_other)
+    (query_grad, key_grad, value_grad), attn_gain_grad = finish_columns(
+        in_order(qkv_near, qkv_far, place.seq), [query_weight, key_weight, value_weight], attn_gain, rows, False
+    )
+    return (
+        layer_output[None], input_grad[None], attn_gain_grad, query_grad, key_grad, value_grad, output_grad,
+        ff_gain_grad, gate_grad, up_grad, down_grad,
+    )
+
+
+def paired(mesh):
+    fine = Mesh(mesh.devices.reshape(2, 2, 2, 2, 2), ("seq", "x", "core", "zh", "zl"))
+    tokens = P(("seq", "zh", "zl"), ("x", "core"), None)
+    matrix, vector = P(("x", "core", "zh", "zl"), None), P(("x", "core", "zh", "zl"))
+    return jax.shard_map(
+        paired_device,
+        mesh=fine,
+        in_specs=(tokens, P(("seq", "zh", "zl"), None), tokens, vector) + (matrix,) * 4 + (vector,) + (matrix,) * 3,
+        out_specs=(tokens, tokens, vector) + (matrix,) * 4 + (vector,) + (matrix,) * 3,
+        check_vma=False,
+    )
+
+
+def solution(mesh):
+    if tuple(mesh.shape[axis] for axis in ("seq", "ctx", "fsdp")) == (2, 4, 4):
+        return paired(mesh)
+    return gathered(mesh)

time: 3990 us -> 872 us (0.22)
  waiting for transfers between devices: 3350 us -> 381 us
  matrix products: 325 us -> 36.5 us
  Pallas kernels: 0 us -> 186 us
  blocking collectives: 129 us -> 0 us
  starting transfers between devices: 0.72 us -> 104 us
  local copies, waits for them, and re-layouts: 99.8 us -> 53.1 us
    reduce_scatter x6 -> x1, waiting for transfers between devices: 2500 us -> 0.01 us  [paired_device(): lax.psum_scatter(gate_up_sums, 'zh', scatter_dimension=0, tiled=True)[0]]
    all_gather x9 -> x1, waiting for transfers between devices: 706 us -> 0.01 us  [paired_device(): lax.all_gather(gate_up, ('core', 'zh'), axis=0, tiled=True)]
    ppermute x0 -> x89, waiting for transfers between devices: none -> 381 us  [the longest x87 381 us: swap(): return lax.ppermute(value, axis, [(0, 1), (1, 0)])]
    dot_general x48 -> x4, matrix products: 325 us -> 36.5 us  [dot_low(): lax.dot_general(left, right, (((left_dim,), (right_dim,)), ((), ())), pre...]
    pallas_call x0 -> x17, Pallas kernels: none -> 186 us  [the longest x8 129 us: into(): pl.pallas_call(body, grid=grid, in_specs=in_specs + [pl.BlockSpec(memory_...]
    ppermute x0 -> x89, starting transfers between devices: none -> 95.5 us  [the longest x87 90.2 us: swap(): return lax.ppermute(value, axis, [(0, 1), (1, 0)])]
    psum x1 -> x0, waiting for transfers between devices: 95.2 us -> none  [per_device(): lax.psum(attn_shards[2].astype(jnp.bfloat16), 'seq').astype(jnp.float32)]
    all_gather x2 -> x0, blocking collectives: 64 us -> none  [the longest x1 34.1 us: per_device(): lax.all_gather(attention_gain, ('ctx', 'fsdp'), axis=0, tiled=True)]
  transfers between devices with their start and end apart: 18 -> 93, of which waited for: 16 -> 36; matrix products, arithmetic and copies ran while one was open for 8% -> 18% of each run, Pallas kernels for 0% -> 20%
where the time goes in v2:
time: 872 us; the launch traced here: 862 us
  waiting for transfers between devices  381 us (44%)
  Pallas kernels  186 us (21%)
  starting transfers between devices  104 us (12%)
  other arithmetic  85.5 us (10%)
  local copies, waits for them, and re-layouts  53.1 us (6%)
  matrix products  36.5 us (4%)
  between operations  15.8 us (2%)
    ppermute x87, waiting for transfers between devices, swap(): return lax.ppermute(value, axis, [(0, 1), (1, 0)])  381 us
    pallas_call x8, Pallas kernels, into(): pl.pallas_call(body, grid=grid, in_specs=in_specs + [pl.BlockSpec(memory_...  129 us
    ppermute x87, starting transfers between devices, swap(): return lax.ppermute(value, axis, [(0, 1), (1, 0)])  90.2 us
    dot_general x4, matrix products, dot_low(): lax.dot_general(left, right, (((left_dim,), (right_dim,)), ((), ())), pre...  36.5 us
    pallas_call x2, Pallas kernels, finish_columns(): pl.pallas_call(functools.partial(finish_kernel, count), grid=(16,), in_sp...  22.7 us
    another operation x18, other arithmetic, in_order(): jnp.stack([jnp.where(first, mine, other), jnp.where(first, other, mine)])  20.3 us
    unnamed x151, local copies, waits for them, and re-layouts  19 us
    pallas_call x4, Pallas kernels, on_rows(): pl.pallas_call(kernel, grid=(3,), in_specs=[tile] * len(operands), out_sp...  17.5 us
  transfers between devices with their start and end apart: 93, of which 36 were waited for; matrix products, arithmetic and copies ran while one was open for 18% of the time, Pallas kernels for 20%

profile of v2, /device:TPU:0, one launch (start us, length us, event | category | flops | bytes accessed | tf_op | source)
XLA Modules:
  0.0 862.1 jit_solution(27696984935700955)
XLA Ops:
  22.1 4.2 column_slices.3
  27.3 15.0 %collective-permute-done = bf16[192,2048]{1,0:T(8,128)(2,1)S(1)} collective-permute-done((bf16[192,2048]{1,0:T(8,128)(2,1)}, bf16[192,2048]{1,0:T(8,128)(2,1)S(1)}, u32[]{:S(2)}, u32[]{:S(2)}) %collective-permute-start) | collective-permute-done | bytes 786464 | tf_op jit(solution)/shard_map/ppermute | solution.py:379
  43.4 4.0 all-to-all-start
  66.8 14.2 %collective-permute-done.5 = bf16[96,2048]{1,0:T(8,128)(2,1)S(1)} collective-permute-done((bf16[96,2048]{1,0:T(8,128)(2,1)}, bf16[96,2048]{1,0:T(8,128)(2,1)S(1)}, u32[]{:S(2)}, u32[]{:S(2)}) %collective-permute-start.5) | collective-permute-done | bytes 393248 | tf_op jit(solution)/shard_map/ppermute | solution.py:379
  86.0 8.4 collective-permute-done.6
  95.1 10.3 %collective-permute-done.4 = bf16[2,128,1536]{2,1,0:T(8,128)(2,1)} collective-permute-done((bf16[2,128,1536]{2,1,0:T(8,128)(2,1)}, bf16[2,128,1536]{2,1,0:T(8,128)(2,1)}, u32[]{:S(2)}, u32[]{:S(2)}) %collective-permute-start.4) | collective-permute-done | bytes 786464 | tf_op jit(solution)/shard_map/ppermute | solution.py:379
  121.8 9.9 %collective-permute-done.10 = bf16[2,128,1536]{2,1,0:T(8,128)(2,1)} collective-permute-done((bf16[2,128,1536]{2,1,0:T(8,128)(2,1)}, bf16[2,128,1536]{2,1,0:T(8,128)(2,1)}, u32[]{:S(2)}, u32[]{:S(2)}) %collective-permute-start.10) | collective-permute-done | bytes 786464 | tf_op jit(solution)/shard_map/ppermute | solution.py:379
  136.2 7.4 collective-permute-done.17
  157.2 9.6 %project.1 = (bf16[768,512]{1,0:T(8,128)(2,1)}, bf16[768,1024]{1,0:T(8,128)(2,1)}) custom-call(bf16[768,2048]{1,0:T(8,128)(2,1)} %constant_dynamic-update-slice_fusion.a_ref, bf16[2048,1536]{1,0:T(8,128)(2,1)} %bitcast.156, f32[384,128]{1,0:T(8,128)} %pad_maximum_fusion.26.cos_ref.refs_9_.refs_10_.refs_4_, ...), custom_call_target="tpu_custom_call" | custom-call | bytes 1000000 | tf_op jit(solution)/shard_map/project/pallas_call | solution.py:611
  171.9 19.2 %collective-permute-done.19.refs_5_ = bf16[192,2048]{1,0:T(8,128)(2,1)} collective-permute-done((bf16[192,2048]{1,0:T(8,128)(2,1)S(1)}, bf16[192,2048]{1,0:T(8,128)(2,1)}, u32[]{:S(2)}, u32[]{:S(2)}) %collective-permute-start.19) | collective-permute-done | bytes 786464 | tf_op jit(solution)/shard_map/ppermute | solution.py:379
  196.5 8.9 %attend.2 = (bf16[768,512]{1,0:T(8,128)(2,1)}, bf16[192,2048]{1,0:T(8,128)(2,1)}, bf16[96,2048]{1,0:T(8,128)(2,1)}, bf16[96,2048]{1,0:T(8,128)(2,1)}) custom-call(bf16[768,512]{1,0:T(8,128)(2,1)} %get-tuple-element.231.refs_0_.refs_3_.refs_4_, bf16[768,1024]{1,0:T(8,128)(2,1)} %get-tuple-element.232.refs_1_.refs_4_.refs_5_, bf16[768,1024]{1,0:T(8,128)(2,1)} %copy-done.1, ...), custom_call_target="tpu_custom_call" | custom-call | bytes 1000000 | tf_op jit(solution)/shard_map/attend/pallas_call | solution.py:726
  205.4 6.0 collective-permute-done.22.refs_6_
  219.8 9.5 %attend.3 = (bf16[768,512]{1,0:T(8,128)(2,1)}, bf16[192,2048]{1,0:T(8,128)(2,1)}, bf16[192,2048]{1,0:T(8,128)(2,1)}) custom-call(bf16[768,512]{1,0:T(8,128)(2,1)} %get-tuple-element.231.refs_0_.refs_3_.refs_4_, bf16[768,1024]{1,0:T(8,128)(2,1)} %get-tuple-element.232.refs_1_.refs_4_.refs_5_, ...), custom_call_target="tpu_custom_call", output_to_operand_aliasing={{0}: (7, {})} | custom-call | bytes 1000000 | tf_op jit(solution)/shard_map/attend/pallas_call | solution.py:726
  236.2 15.7 %collective-permute-done.29.refs_2_ = bf16[192,2048]{1,0:T(8,128)(2,1)S(1)} collective-permute-done((bf16[192,2048]{1,0:T(8,128)(2,1)S(1)}, bf16[192,2048]{1,0:T(8,128)(2,1)S(1)}, u32[]{:S(2)}, u32[]{:S(2)}) %collective-permute-start.29) | collective-permute-done | bytes 786464 | tf_op jit(solution)/shard_map/ppermute | solution.py:379
  253.7 4.2 close_attention.1
  264.8 23.0 %collective-permute-done.33 = bf16[128,2048]{1,0:T(8,128)(2,1)S(1)} collective-permute-done((bf16[128,2048]{1,0:T(8,128)(2,1)S(1)}, bf16[128,2048]{1,0:T(8,128)(2,1)S(1)}, u32[]{:S(2)}, u32[]{:S(2)}) %collective-permute-start.33) | collective-permute-done | bytes 524320 | tf_op jit(solution)/shard_map/ppermute | solution.py:379
  291.4 22.5 %collective-permute-done.36 = bf16[128,2048]{1,0:T(8,128)(2,1)S(1)} collective-permute-done((bf16[128,2048]{1,0:T(8,128)(2,1)S(1)}, bf16[128,2048]{1,0:T(8,128)(2,1)S(1)}, u32[]{:S(2)}, u32[]{:S(2)}) %collective-permute-start.36) | collective-permute-done | bytes 524320 | tf_op jit(solution)/shard_map/ppermute | solution.py:379
  316.4 9.6 %collective-permute-done.34.refs_3_ = bf16[96,2048]{1,0:T(8,128)(2,1)S(1)} collective-permute-done((bf16[96,2048]{1,0:T(8,128)(2,1)S(1)}, bf16[96,2048]{1,0:T(8,128)(2,1)S(1)}, u32[]{:S(2)}, u32[]{:S(2)}) %collective-permute-start.34) | collective-permute-done | bytes 393248 | tf_op jit(solution)/shard_map/ppermute | solution.py:379
  329.0 16.4 %collective-permute-done.39.refs_2_ = bf16[192,2048]{1,0:T(8,128)(2,1)S(1)} collective-permute-done((bf16[192,2048]{1,0:T(8,128)(2,1)S(1)}, bf16[192,2048]{1,0:T(8,128)(2,1)S(1)}, u32[]{:S(2)}, u32[]{:S(2)}) %collective-permute-start.39) | collective-permute-done | bytes 786464 | tf_op jit(solution)/shard_map/ppermute | solution.py:379
  351.0 32.6 %hidden_units.2 = (bf16[1536,1024]{1,0:T(8,128)(2,1)}, bf16[1536,2048]{1,0:T(8,128)(2,1)}, bf16[1536,2048]{1,0:T(8,128)(2,1)}, bf16[1536,2048]{1,0:T(8,128)(2,1)...) custom-call(bf16[192,2048]{1,0:T(8,128)(2,1)} %get-tuple-element.258, ...), custom_call_target="tpu_custom_call" | custom-call | bytes 1000000 | tf_op jit(solution)/shard_map/hidden_units/pallas_call | solution.py:726
  387.6 5.3 collective-permute-done.44
  397.3 32.8 %hidden_units.3 = (bf16[1536,1024]{1,0:T(8,128)(2,1)}, bf16[1536,2048]{1,0:T(8,128)(2,1)}, bf16[1536,2048]{1,0:T(8,128)(2,1)}, bf16[1536,2048]{1,0:T(8,128)(2,1)...) custom-call(bf16[192,2048]{1,0:T(8,128)(2,1)} %copy-done.49, ...), custom_call_target="tpu_custom_call", output_to_operand_aliasing={{0}: (12, {}), {1}: (13, {}), {2}: (14, {}), {3}: (15, {})} | custom-call | bytes 1000000 | tf_op jit(solution)/shard_map/hidden_units/pallas_call | solution.py:726
  431.4 17.5 %convolution_convert_fusion.1 = bf16[2048,2048]{1,0:T(8,128)(2,1)S(1)} fusion(bf16[1536,2048]{1,0:T(8,128)(2,1)} %get-tuple-element.277, bf16[1536,2048]{1,0:T(8,128)(2,1)} %get-tuple-element.288), kind=kOutput, calls=%fused_computation.3 | convolution fusion | flops 12889096192 | bytes 20971520 | tf_op jit(solution)/shard_map/dot_general | solution.py:911
  462.9 8.5 convolution_convert_fusion.2
  471.4 6.1 fusion
  487.6 17.3 %collective-permute-done.51.refs_3_ = bf16[192,2048]{1,0:T(8,128)(2,1)S(1)} collective-permute-done((bf16[192,2048]{1,0:T(8,128)(2,1)S(1)}, bf16[192,2048]{1,0:T(8,128)(2,1)S(1)}, u32[]{:S(2)}, u32[]{:S(2)}) %collective-permute-start.51) | collective-permute-done | bytes 786464 | tf_op jit(solution)/shard_map/ppermute | solution.py:379
  505.8 6.0 close_hidden.1
  517.6 16.8 %collective-permute-done.55.refs_1_ = bf16[192,2048]{1,0:T(8,128)(2,1)} collective-permute-done((bf16[192,2048]{1,0:T(8,128)(2,1)}, bf16[192,2048]{1,0:T(8,128)(2,1)}, u32[]{:S(2)}, u32[]{:S(2)}) %collective-permute-start.55) | collective-permute-done | bytes 786464 | tf_op jit(solution)/shard_map/ppermute | solution.py:379
  541.6 14.6 %attend_back.2 = (bf16[768,2048]{1,0:T(8,128)(2,1)}, bf16[384,512]{1,0:T(8,128)(2,1)}, f32[384,1024]{1,0:T(8,128)}, bf16[384,1024]{1,0:T(8,128)(2,1)}) custom-call(bf16[192,2048]{1,0:T(8,128)(2,1)} %get-tuple-element.312.refs_0_, bf16[192,2048]{1,0:T(8,128)(2,1)} %collective-permute-done.55.refs_1_, bf16[512,2048]{1,0:T(8,128)(2,1)} %bitcast.161, ...), custom_call_target="tpu_custom_call" | custom-call | bytes 1000000 | tf_op jit(solution)/shard_map/attend_back/pallas_call | solution.py:726
  558.9 14.5 %attend_back.3 = (bf16[768,2048]{1,0:T(8,128)(2,1)}, bf16[384,512]{1,0:T(8,128)(2,1)}, f32[384,1024]{1,0:T(8,128)}, bf16[384,1024]{1,0:T(8,128)(2,1)}) custom-call(bf16[192,2048]{1,0:T(8,128)(2,1)} %copy-done.23, bf16[96,2048]{1,0:T(8,128)(2,1)} %copy-done.55, bf16[96,2048]{1,0:T(8,128)(2,1)} %collective-permute-done.60.refs_2_, ...), custom_call_target="tpu_custom_call", output_to_operand_aliasing={{0}: (12, {})} | custom-call | bytes 1000000 | tf_op jit(solution)/shard_map/attend_back/pallas_call | solution.py:726
  576.8 9.1 %collective-permute-done.63 = bf16[96,2048]{1,0:T(8,128)(2,1)S(1)} collective-permute-done((bf16[96,2048]{1,0:T(8,128)(2,1)}, bf16[96,2048]{1,0:T(8,128)(2,1)S(1)}, u32[]{:S(2)}, u32[]{:S(2)}) %collective-permute-start.63) | collective-permute-done | bytes 393248 | tf_op jit(solution)/shard_map/ppermute | solution.py:379
  586.4 18.9 %collective-permute-done.67 = bf16[128,2048]{1,0:T(8,128)(2,1)} collective-permute-done((bf16[128,2048]{1,0:T(8,128)(2,1)S(1)}, bf16[128,2048]{1,0:T(8,128)(2,1)}, u32[]{:S(2)}, u32[]{:S(2)}) %collective-permute-start.67) | collective-permute-done | bytes 524320 | tf_op jit(solution)/shard_map/ppermute | solution.py:379
  608.2 8.0 join_grads.2
  619.4 7.6 join_grads.3
  628.6 7.3 convolution_convert_fusion
  639.5 19.0 %collective-permute-done.72 = bf16[128,2048]{1,0:T(8,128)(2,1)S(1)} collective-permute-done((bf16[128,2048]{1,0:T(8,128)(2,1)S(1)}, bf16[128,2048]{1,0:T(8,128)(2,1)S(1)}, u32[]{:S(2)}, u32[]{:S(2)}) %collective-permute-start.72) | collective-permute-done | bytes 524320 | tf_op jit(solution)/shard_map/ppermute | solution.py:379
  672.3 3.7 fusion.1
  676.0 8.1 collective-permute-done.65
  684.2 25.0 %collective-permute-done.75.refs_2_ = bf16[192,2048]{1,0:T(8,128)(2,1)} collective-permute-done((bf16[192,2048]{1,0:T(8,128)(2,1)}, bf16[192,2048]{1,0:T(8,128)(2,1)}, u32[]{:S(2)}, u32[]{:S(2)}) %collective-permute-start.75) | collective-permute-done | bytes 786464 | tf_op jit(solution)/shard_map/ppermute | solution.py:379
  709.2 4.7 all-to-all-start.1
  728.1 4.3 close_input.1
  732.4 30.4 %collective-permute-done.77 = bf16[64,2048]{1,0:T(8,128)(2,1)} collective-permute-done((bf16[64,2048]{1,0:T(8,128)(2,1)}, bf16[64,2048]{1,0:T(8,128)(2,1)}, u32[]{:S(2)}, u32[]{:S(2)}) %collective-permute-start.77) | collective-permute-done | bytes 262176 | tf_op jit(solution)/shard_map/ppermute | solution.py:379
  769.9 4.1 maximum_convert_fusion
  774.0 29.0 %collective-permute-done.81 = bf16[64,2048]{1,0:T(8,128)(2,1)S(1)} collective-permute-done((bf16[64,2048]{1,0:T(8,128)(2,1)}, bf16[64,2048]{1,0:T(8,128)(2,1)S(1)}, u32[]{:S(2)}, u32[]{:S(2)}) %collective-permute-start.81) | collective-permute-done | bytes 262176 | tf_op jit(solution)/shard_map/ppermute | solution.py:379
  803.1 6.8 collective-permute-done.79
  815.8 3.7 collective-permute-done.84
  826.6 12.6 %finish_columns.3 = (f32[128,8192]{1,0:T(8,128)}, f32[128,8192]{1,0:T(8,128)}, f32[128,512]{1,0:T(8,128)}) custom-call(bf16[2,4,128,2048]{3,2,1,0:T(8,128)(2,1)} %pad_maximum_fusion.2.refs_0_.refs_1_, bf16[2,4,128,2048]{3,2,1,0:T(8,128)(2,1)} %pad_maximum_fusion.2.refs_0_.refs_1_, bf16[128,8192]{1,0:T(8,128)(2,1)} %refs_2_.5, bf16[128,8192]{1,0:T(8,128)(2,1)} %refs_3_.7, ...), custom_call_target="tpu_custom_call" | custom-call | bytes 1000000 | tf_op jit(solution)/shard_map/finish_columns/pallas_call | solution.py:548
  843.3 10.1 %finish_columns.2 = (f32[128,2048]{1,0:T(8,128)}, f32[128,2048]{1,0:T(8,128)}, f32[128,2048]{1,0:T(8,128)}, f32[128,128]{1,0:T(8,128)}) custom-call(bf16[2,2,128,1536]{3,2,1,0:T(8,128)(2,1)} %pad_maximum_fusion.8.refs_0_.refs_1_.refs_2_, bf16[2,2,128,1536]{3,2,1,0:T(8,128)(2,1)} %pad_maximum_fusion.8.refs_0_.refs_1_.refs_2_, ...), custom_call_target="tpu_custom_call" | custom-call | bytes 1000000 | tf_op jit(solution)/shard_map/finish_columns/pallas_call | solution.py:548
  (448 shorter events, 243.6 us)
Async XLA Ops:
  19.3 23.0 %collective-permute-start = (bf16[192,2048]{1,0:T(8,128)(2,1)}, bf16[192,2048]{1,0:T(8,128)(2,1)S(1)}, u32[]{:S(2)}, u32[]{:S(2)}) collective-permute-start(bf16[192,2048]{1,0:T(8,128)(2,1)} %open_layer.1), channel_id=1, source_target_pairs={{0,8},{8,0},{1,9},{9,1},{2,10},{10,2},{3,11},{11,3},{4,12},{12,4},... | collective-permute-start | bytes 2359304 | tf_op jit(solution)/shard_map/ppermute | solution.py:379
  19.3 22.9 %collective-permute-start.1 = (bf16[192,2048]{1,0:T(8,128)(2,1)}, bf16[192,2048]{1,0:T(8,128)(2,1)S(1)}, u32[]{:S(2)}, u32[]{:S(2)}) collective-permute-start(bf16[192,2048]{1,0:T(8,128)(2,1)} %open_layer.1), channel_id=1, source_target_pairs={{0,16},{16,0},{1,17},{17,1},{2,18},{18,2},{3,19},{19,3},{4,20},{20... | collective-permute-start | bytes 2359304 | tf_op jit(solution)/shard_map/ppermute | solution.py:379
  43.4 62.0 %all-to-all-start = ((bf16[4,128,2048]{2,1,0:T(8,128)(2,1)}), bf16[4,128,2048]{2,1,0:T(8,128)(2,1)S(1)}, u32[]{:S(2)}, u32[]{:S(2)}) async-start(bf16[4,128,2048]{2,1,0:T(8,128)(2,1)} %column_slices.3), calls=%async_computation | async-start | bytes 4194304 | tf_op jit(solution)/shard_map/all_to_all | solution.py:479
  47.4 303.6 %all-gather.2.cloned.1.call-start = ((), (), s32[]{:S(2)}) async-start(), calls=%async_computation.3 | async-start | bytes 10485760 | tf_op jit(solution)/shard_map/all_gather | solution.py:954
  52.2 42.9 %collective-permute-start.3 = (bf16[2,128,1536]{2,1,0:T(8,128)(2,1)}, bf16[2,128,1536]{2,1,0:T(8,128)(2,1)}, u32[]{:S(2)}, u32[]{:S(2)}) collective-permute-start(bf16[2,128,1536]{2,1,0:T(8,128)(2,1)} %pad_maximum_fusion.10), channel_id=1, source_target_pairs={{0,2},{2,0},{1,3},{3,1},{4,6},{6,4},{5,7},{7,5},{8,10},{10,8},{9,1... | collective-permute-start | bytes 2359304 | tf_op jit(solution)/shard_map/ppermute | solution.py:379
  54.8 50.6 %collective-permute-start.4 = (bf16[2,128,1536]{2,1,0:T(8,128)(2,1)}, bf16[2,128,1536]{2,1,0:T(8,128)(2,1)}, u32[]{:S(2)}, u32[]{:S(2)}) collective-permute-start(bf16[2,128,1536]{2,1,0:T(8,128)(2,1)} %pad_maximum_fusion.10), channel_id=1, source_target_pairs={{0,1},{1,0},{2,3},{3,2},{4,5},{5,4},{6,7},{7,6},{8,9},{9,8},{10,11... | collective-permute-start | bytes 2359304 | tf_op jit(solution)/shard_map/ppermute | solution.py:379
  57.6 23.4 %collective-permute-start.5 = (bf16[96,2048]{1,0:T(8,128)(2,1)}, bf16[96,2048]{1,0:T(8,128)(2,1)S(1)}, u32[]{:S(2)}, u32[]{:S(2)}) collective-permute-start(bf16[96,2048]{1,0:T(8,128)(2,1)} %slice.120), channel_id=1, source_target_pairs={{0,8},{8,0},{1,9},{9,1},{2,10},{10,2},{3,11},{11,3},{4,12},{12,4},... | collective-permute-start | bytes 1179656 | tf_op jit(solution)/shard_map/ppermute | solution.py:379
  62.8 42.6 %collective-permute-start.8 = (bf16[192,2048]{1,0:T(8,128)(2,1)S(1)}, bf16[192,2048]{1,0:T(8,128)(2,1)}, u32[]{:S(2)}, u32[]{:S(2)}) collective-permute-start(bf16[192,2048]{1,0:T(8,128)(2,1)S(1)} %bitcast.185), channel_id=1, source_target_pairs={{0,8},{8,0},{1,9},{9,1},{2,10},{10,2},{3,11},{11,3},{4,12},{12,4},... | collective-permute-start | bytes 2359304 | tf_op jit(solution)/shard_map/ppermute | solution.py:379
  65.9 39.6 %collective-permute-start.9 = (bf16[192,2048]{1,0:T(8,128)(2,1)S(1)}, bf16[192,2048]{1,0:T(8,128)(2,1)}, u32[]{:S(2)}, u32[]{:S(2)}) collective-permute-start(bf16[192,2048]{1,0:T(8,128)(2,1)S(1)} %bitcast.186), channel_id=1, source_target_pairs={{0,16},{16,0},{1,17},{17,1},{2,18},{18,2},{3,19},{19,3},{4,20},{20... | collective-permute-start | bytes 2359304 | tf_op jit(solution)/shard_map/ppermute | solution.py:379
  105.4 26.2 %collective-permute-start.10 = (bf16[2,128,1536]{2,1,0:T(8,128)(2,1)}, bf16[2,128,1536]{2,1,0:T(8,128)(2,1)}, u32[]{:S(2)}, u32[]{:S(2)}) collective-permute-start(bf16[2,128,1536]{2,1,0:T(8,128)(2,1)} %collective-permute-done.3), channel_id=1, source_target_pairs={{0,1},{1,0},{2,3},{3,2},{4,5},{5,4},{6,7},{7,6},{8,9},{9,8},{10,11... | collective-permute-start | bytes 2359304 | tf_op jit(solution)/shard_map/ppermute | solution.py:379
  107.9 25.9 %collective-permute-start.11 = (bf16[64,2048]{1,0:T(8,128)(2,1)S(1)}, bf16[64,2048]{1,0:T(8,128)(2,1)}, u32[]{:S(2)}, u32[]{:S(2)}) collective-permute-start(bf16[64,2048]{1,0:T(8,128)(2,1)S(1)} %dynamic-slice_select_fusion.1), channel_id=1, source_target_pairs={{0,2},{2,0},{1,3},{3,1},{4,6},{6,4},{5,7},{7,5},{8,10},{10,8},{9,1... | collective-permute-start | bytes 786440 | tf_op jit(solution)/shard_map/ppermute | solution.py:379
  110.4 24.1 %collective-permute-start.12 = (bf16[64,2048]{1,0:T(8,128)(2,1)S(1)}, bf16[64,2048]{1,0:T(8,128)(2,1)}, u32[]{:S(2)}, u32[]{:S(2)}) collective-permute-start(bf16[64,2048]{1,0:T(8,128)(2,1)S(1)} %dynamic-slice_select_fusion.1), channel_id=1, source_target_pairs={{0,1},{1,0},{2,3},{3,2},{4,5},{5,4},{6,7},{7,6},{8,9},{9,8},{10,11... | collective-permute-start | bytes 786440 | tf_op jit(solution)/shard_map/ppermute | solution.py:379
  134.5 574.7 %reduce-scatter.2.cloned.1.call-start = ((), (), s32[]{:S(2)}) async-start(), calls=%async_computation.4 | async-start | bytes 6291456 | tf_op jit(solution)/shard_map/reduce_scatter | solution.py:1050
  156.5 34.6 %collective-permute-start.19 = (bf16[192,2048]{1,0:T(8,128)(2,1)S(1)}, bf16[192,2048]{1,0:T(8,128)(2,1)}, u32[]{:S(2)}, u32[]{:S(2)}) collective-permute-start(bf16[192,2048]{1,0:T(8,128)(2,1)S(1)} %bitcast.187), channel_id=1, source_target_pairs={{0,1},{1,0},{2,3},{3,2},{4,5},{5,4},{6,7},{7,6},{8,9},{9,8},{10,11... | collective-permute-start | bytes 2359304 | tf_op jit(solution)/shard_map/ppermute | solution.py:379
  257.9 29.9 %collective-permute-start.30 = (bf16[192,2048]{1,0:T(8,128)(2,1)}, bf16[192,2048]{1,0:T(8,128)(2,1)S(1)}, u32[]{:S(2)}, u32[]{:S(2)}) collective-permute-start(bf16[192,2048]{1,0:T(8,128)(2,1)} %get-tuple-element.258.refs_0_), channel_id=1, source_target_pairs={{0,8},{8,0},{1,9},{9,1},{2,10},{10,2},{3,11},{11,3},{4,12},{12,4},... | collective-permute-start | bytes 2359304 | tf_op jit(solution)/shard_map/ppermute | solution.py:379
  259.3 28.5 %collective-permute-start.31 = (bf16[192,2048]{1,0:T(8,128)(2,1)}, bf16[192,2048]{1,0:T(8,128)(2,1)S(1)}, u32[]{:S(2)}, u32[]{:S(2)}) collective-permute-start(bf16[192,2048]{1,0:T(8,128)(2,1)} %get-tuple-element.258.refs_0_), channel_id=1, source_target_pairs={{0,16},{16,0},{1,17},{17,1},{2,18},{18,2},{3,19},{19,3},{4,20},{20... | collective-permute-start | bytes 2359304 | tf_op jit(solution)/shard_map/ppermute | solution.py:379
  260.5 28.1 %collective-permute-start.32 = (bf16[192,2048]{1,0:T(8,128)(2,1)}, bf16[192,2048]{1,0:T(8,128)(2,1)S(1)}, u32[]{:S(2)}, u32[]{:S(2)}) collective-permute-start(bf16[192,2048]{1,0:T(8,128)(2,1)} %get-tuple-element.258.refs_0_), channel_id=1, source_target_pairs={{0,1},{1,0},{2,3},{3,2},{4,5},{5,4},{6,7},{7,6},{8,9},{9,8},{10,11... | collective-permute-start | bytes 2359304 | tf_op jit(solution)/shard_map/ppermute | solution.py:379
  263.0 24.8 %collective-permute-start.33 = (bf16[128,2048]{1,0:T(8,128)(2,1)S(1)}, bf16[128,2048]{1,0:T(8,128)(2,1)S(1)}, u32[]{:S(2)}, u32[]{:S(2)}) collective-permute-start(bf16[128,2048]{1,0:T(8,128)(2,1)S(1)} %slice.130), channel_id=1, source_target_pairs={{0,2},{2,0},{1,3},{3,1},{4,6},{6,4},{5,7},{7,5},{8,10},{10,8},{9,1... | collective-permute-start | bytes 1572872 | tf_op jit(solution)/shard_map/ppermute | solution.py:379
  288.6 25.3 %collective-permute-start.36 = (bf16[128,2048]{1,0:T(8,128)(2,1)S(1)}, bf16[128,2048]{1,0:T(8,128)(2,1)S(1)}, u32[]{:S(2)}, u32[]{:S(2)}) collective-permute-start(bf16[128,2048]{1,0:T(8,128)(2,1)S(1)} %slice.133), channel_id=1, source_target_pairs={{0,2},{2,0},{1,3},{3,1},{4,6},{6,4},{5,7},{7,5},{8,10},{10,8},{9,1... | collective-permute-start | bytes 1572872 | tf_op jit(solution)/shard_map/ppermute | solution.py:379
  314.3 33.7 %collective-permute-start.37 = (bf16[2,256,2048]{2,1,0:T(8,128)(2,1)S(1)}, bf16[2,256,2048]{2,1,0:T(8,128)(2,1)S(1)}, u32[]{:S(2)}, u32[]{:S(2)}) collective-permute-start(bf16[2,256,2048]{2,1,0:T(8,128)(2,1)S(1)} %pad_maximum_fusion.5), channel_id=1, source_target_pairs={{0,4},{4,0},{1,5},{5,1},{2,6},{6,2},{3,7},{7,3},{8,12},{12,8},{9,1... | collective-permute-start | bytes 6291464 | tf_op jit(solution)/shard_map/ppermute | solution.py:379
  345.3 38.3 %collective-permute-start.40 = (bf16[96,2048]{1,0:T(8,128)(2,1)S(1)}, bf16[96,2048]{1,0:T(8,128)(2,1)S(1)}, u32[]{:S(2)}, u32[]{:S(2)}) collective-permute-start(bf16[96,2048]{1,0:T(8,128)(2,1)S(1)} %slice.160), channel_id=1, source_target_pairs={{0,8},{8,0},{1,9},{9,1},{2,10},{10,2},{3,11},{11,3},{4,12},{12,4},... | collective-permute-start | bytes 1179656 | tf_op jit(solution)/shard_map/ppermute | solution.py:379
  346.8 36.9 %collective-permute-start.41 = (bf16[96,2048]{1,0:T(8,128)(2,1)S(1)}, bf16[96,2048]{1,0:T(8,128)(2,1)S(1)}, u32[]{:S(2)}, u32[]{:S(2)}) collective-permute-start(bf16[96,2048]{1,0:T(8,128)(2,1)S(1)} %slice.161), channel_id=1, source_target_pairs={{0,16},{16,0},{1,17},{17,1},{2,18},{18,2},{3,19},{19,3},{4,20},{20... | collective-permute-start | bytes 1179656 | tf_op jit(solution)/shard_map/ppermute | solution.py:379
  394.1 36.0 %collective-permute-start.45 = (bf16[192,2048]{1,0:T(8,128)(2,1)S(1)}, bf16[192,2048]{1,0:T(8,128)(2,1)S(1)}, u32[]{:S(2)}, u32[]{:S(2)}) collective-permute-start(bf16[192,2048]{1,0:T(8,128)(2,1)S(1)} %pad_maximum_fusion.14), channel_id=1, source_target_pairs={{0,16},{16,0},{1,17},{17,1},{2,18},{18,2},{3,19},{19,3},{4,20},{20... | collective-permute-start | bytes 2359304 | tf_op jit(solution)/shard_map/ppermute | solution.py:379
  395.3 34.8 %collective-permute-start.43 = (bf16[192,2048]{1,0:T(8,128)(2,1)S(1)}, bf16[192,2048]{1,0:T(8,128)(2,1)S(1)}, u32[]{:S(2)}, u32[]{:S(2)}) collective-permute-start(bf16[192,2048]{1,0:T(8,128)(2,1)S(1)} %pad_maximum_fusion.13), channel_id=1, source_target_pairs={{0,8},{8,0},{1,9},{9,1},{2,10},{10,2},{3,11},{11,3},{4,12},{12,4},... | collective-permute-start | bytes 2359304 | tf_op jit(solution)/shard_map/ppermute | solution.py:379
  483.0 28.7 %collective-permute-start.52 = (bf16[2,256,2048]{2,1,0:T(8,128)(2,1)S(1)}, bf16[2,256,2048]{2,1,0:T(8,128)(2,1)}, u32[]{:S(2)}, u32[]{:S(2)}) collective-permute-start(bf16[2,256,2048]{2,1,0:T(8,128)(2,1)S(1)} %dynamic-slice_bitcast_fusion.2), channel_id=1, source_target_pairs={{0,4},{4,0},{1,5},{5,1},{2,6},{6,2},{3,7},{7,3},{8,12},{12,8},{9,1... | collective-permute-start | bytes 6291464 | tf_op jit(solution)/shard_map/ppermute | solution.py:379
  485.0 29.2 %collective-permute-start.53 = (bf16[96,2048]{1,0:T(8,128)(2,1)}, bf16[96,2048]{1,0:T(8,128)(2,1)S(1)}, u32[]{:S(2)}, u32[]{:S(2)}) collective-permute-start(bf16[96,2048]{1,0:T(8,128)(2,1)} %get-tuple-element.310), channel_id=1, source_target_pairs={{0,8},{8,0},{1,9},{9,1},{2,10},{10,2},{3,11},{11,3},{4,12},{12,4},... | collective-permute-start | bytes 1179656 | tf_op jit(solution)/shard_map/ppermute | solution.py:379
  486.8 27.4 %collective-permute-start.54 = (bf16[96,2048]{1,0:T(8,128)(2,1)}, bf16[96,2048]{1,0:T(8,128)(2,1)S(1)}, u32[]{:S(2)}, u32[]{:S(2)}) collective-permute-start(bf16[96,2048]{1,0:T(8,128)(2,1)} %get-tuple-element.311), channel_id=1, source_target_pairs={{0,16},{16,0},{1,17},{17,1},{2,18},{18,2},{3,19},{19,3},{4,20},{20... | collective-permute-start | bytes 1179656 | tf_op jit(solution)/shard_map/ppermute | solution.py:379
  539.8 65.5 %collective-permute-start.57 = (bf16[192,2048]{1,0:T(8,128)(2,1)S(1)}, bf16[192,2048]{1,0:T(8,128)(2,1)}, u32[]{:S(2)}, u32[]{:S(2)}) collective-permute-start(bf16[192,2048]{1,0:T(8,128)(2,1)S(1)} %pad_maximum_fusion.17), channel_id=1, source_target_pairs={{0,8},{8,0},{1,9},{9,1},{2,10},{10,2},{3,11},{11,3},{4,12},{12,4},... | collective-permute-start | bytes 2359304 | tf_op jit(solution)/shard_map/ppermute | solution.py:379
  557.9 47.4 %collective-permute-start.58 = (bf16[192,2048]{1,0:T(8,128)(2,1)S(1)}, bf16[192,2048]{1,0:T(8,128)(2,1)}, u32[]{:S(2)}, u32[]{:S(2)}) collective-permute-start(bf16[192,2048]{1,0:T(8,128)(2,1)S(1)} %pad_maximum_fusion.18), channel_id=1, source_target_pairs={{0,16},{16,0},{1,17},{17,1},{2,18},{18,2},{3,19},{19,3},{4,20},{20... | collective-permute-start | bytes 2359304 | tf_op jit(solution)/shard_map/ppermute | solution.py:379
  558.8 46.5 %collective-permute-start.67 = (bf16[128,2048]{1,0:T(8,128)(2,1)S(1)}, bf16[128,2048]{1,0:T(8,128)(2,1)}, u32[]{:S(2)}, u32[]{:S(2)}) collective-permute-start(bf16[128,2048]{1,0:T(8,128)(2,1)S(1)} %slice.154), channel_id=1, source_target_pairs={{0,2},{2,0},{1,3},{3,1},{4,6},{6,4},{5,7},{7,5},{8,10},{10,8},{9,1... | collective-permute-start | bytes 1572872 | tf_op jit(solution)/shard_map/ppermute | solution.py:379
  558.8 46.5 %collective-permute-start.66 = (bf16[384,1024]{1,0:T(8,128)(2,1)}, bf16[384,1024]{1,0:T(8,128)(2,1)S(1)}, u32[]{:S(2)}, u32[]{:S(2)}) collective-permute-start(bf16[384,1024]{1,0:T(8,128)(2,1)} %get-tuple-element.343), channel_id=1, source_target_pairs={{0,4},{4,0},{1,5},{5,1},{2,6},{6,2},{3,7},{7,3},{8,12},{12,8},{9,1... | collective-permute-start | bytes 2359304 | tf_op jit(solution)/shard_map/ppermute | solution.py:379
  585.9 41.1 %collective-permute-start.62 = (bf16[192,2048]{1,0:T(8,128)(2,1)}, bf16[192,2048]{1,0:T(8,128)(2,1)}, u32[]{:S(2)}, u32[]{:S(2)}) collective-permute-start(bf16[192,2048]{1,0:T(8,128)(2,1)} %pad_maximum_fusion.19), channel_id=1, source_target_pairs={{0,8},{8,0},{1,9},{9,1},{2,10},{10,2},{3,11},{11,3},{4,12},{12,4},... | collective-permute-start | bytes 2359304 | tf_op jit(solution)/shard_map/ppermute | solution.py:379
  606.5 20.5 %collective-permute-start.64 = (bf16[192,2048]{1,0:T(8,128)(2,1)}, bf16[192,2048]{1,0:T(8,128)(2,1)}, u32[]{:S(2)}, u32[]{:S(2)}) collective-permute-start(bf16[192,2048]{1,0:T(8,128)(2,1)} %pad_maximum_fusion.20), channel_id=1, source_target_pairs={{0,16},{16,0},{1,17},{17,1},{2,18},{18,2},{3,19},{19,3},{4,20},{20... | collective-permute-start | bytes 2359304 | tf_op jit(solution)/shard_map/ppermute | solution.py:379
  627.3 31.2 %collective-permute-start.72 = (bf16[128,2048]{1,0:T(8,128)(2,1)S(1)}, bf16[128,2048]{1,0:T(8,128)(2,1)S(1)}, u32[]{:S(2)}, u32[]{:S(2)}) collective-permute-start(bf16[128,2048]{1,0:T(8,128)(2,1)S(1)} %slice.155), channel_id=1, source_target_pairs={{0,2},{2,0},{1,3},{3,1},{4,6},{6,4},{5,7},{7,5},{8,10},{10,8},{9,1... | collective-permute-start | bytes 1572872 | tf_op jit(solution)/shard_map/ppermute | solution.py:379
  636.0 22.5 %collective-permute-start.69 = (bf16[96,2048]{1,0:T(8,128)(2,1)S(1)}, bf16[96,2048]{1,0:T(8,128)(2,1)S(1)}, u32[]{:S(2)}, u32[]{:S(2)}) collective-permute-start(bf16[96,2048]{1,0:T(8,128)(2,1)S(1)} %copy-done.69), channel_id=1, source_target_pairs={{0,8},{8,0},{1,9},{9,1},{2,10},{10,2},{3,11},{11,3},{4,12},{12,4},... | collective-permute-start | bytes 1179656 | tf_op jit(solution)/shard_map/ppermute | solution.py:379
  637.5 21.0 %collective-permute-start.70 = (bf16[96,2048]{1,0:T(8,128)(2,1)S(1)}, bf16[96,2048]{1,0:T(8,128)(2,1)S(1)}, u32[]{:S(2)}, u32[]{:S(2)}) collective-permute-start(bf16[96,2048]{1,0:T(8,128)(2,1)S(1)} %copy-done.68), channel_id=1, source_target_pairs={{0,16},{16,0},{1,17},{17,1},{2,18},{18,2},{3,19},{19,3},{4,20},{20... | collective-permute-start | bytes 1179656 | tf_op jit(solution)/shard_map/ppermute | solution.py:379
  666.6 47.4 %collective-permute-start.82 = (bf16[256,2048]{1,0:T(8,128)(2,1)}, bf16[256,2048]{1,0:T(8,128)(2,1)}, u32[]{:S(2)}, u32[]{:S(2)}) collective-permute-start(bf16[256,2048]{1,0:T(8,128)(2,1)} %fusion.3), channel_id=1, source_target_pairs={{0,16},{16,0},{1,17},{17,1},{2,18},{18,2},{3,19},{19,3},{4,20},{20... | collective-permute-start | bytes 3145736 | tf_op jit(solution)/shard_map/ppermute | solution.py:379
  669.2 40.0 %collective-permute-start.75 = (bf16[192,2048]{1,0:T(8,128)(2,1)}, bf16[192,2048]{1,0:T(8,128)(2,1)}, u32[]{:S(2)}, u32[]{:S(2)}) collective-permute-start(bf16[192,2048]{1,0:T(8,128)(2,1)} %pad_maximum_fusion.22), channel_id=1, source_target_pairs={{0,16},{16,0},{1,17},{17,1},{2,18},{18,2},{3,19},{19,3},{4,20},{20... | collective-permute-start | bytes 2359304 | tf_op jit(solution)/shard_map/ppermute | solution.py:379
  670.8 38.4 %collective-permute-start.74 = (bf16[192,2048]{1,0:T(8,128)(2,1)}, bf16[192,2048]{1,0:T(8,128)(2,1)}, u32[]{:S(2)}, u32[]{:S(2)}) collective-permute-start(bf16[192,2048]{1,0:T(8,128)(2,1)} %pad_maximum_fusion.21), channel_id=1, source_target_pairs={{0,8},{8,0},{1,9},{9,1},{2,10},{10,2},{3,11},{11,3},{4,12},{12,4},... | collective-permute-start | bytes 2359304 | tf_op jit(solution)/shard_map/ppermute | solution.py:379
  709.2 59.2 %all-to-all-start.1 = ((bf16[4,128,2048]{2,1,0:T(8,128)(2,1)}), bf16[4,128,2048]{2,1,0:T(8,128)(2,1)}, u32[]{:S(2)}, u32[]{:S(2)}) async-start(bf16[4,128,2048]{2,1,0:T(8,128)(2,1)} %bitcast.190), calls=%async_computation.2 | async-start | bytes 4194304 | tf_op jit(solution)/shard_map/all_to_all | solution.py:479
  719.9 42.8 %collective-permute-start.76 = (bf16[256,1536]{1,0:T(8,128)(2,1)S(1)}, bf16[256,1536]{1,0:T(8,128)(2,1)S(1)}, u32[]{:S(2)}, u32[]{:S(2)}) collective-permute-start(bf16[256,1536]{1,0:T(8,128)(2,1)S(1)} %get-tuple-element.408), channel_id=1, source_target_pairs={{0,1},{1,0},{2,3},{3,2},{4,5},{5,4},{6,7},{7,6},{8,9},{9,8},{10,11... | collective-permute-start | bytes 2359304 | tf_op jit(solution)/shard_map/ppermute | solution.py:379
  722.8 40.0 %collective-permute-start.77 = (bf16[64,2048]{1,0:T(8,128)(2,1)}, bf16[64,2048]{1,0:T(8,128)(2,1)}, u32[]{:S(2)}, u32[]{:S(2)}) collective-permute-start(bf16[64,2048]{1,0:T(8,128)(2,1)} %get-tuple-element.426), channel_id=1, source_target_pairs={{0,1},{1,0},{2,3},{3,2},{4,5},{5,4},{6,7},{7,6},{8,9},{9,8},{10,11... | collective-permute-start | bytes 786440 | tf_op jit(solution)/shard_map/ppermute | solution.py:379
  726.0 77.0 %collective-permute-start.80 = (bf16[256,1536]{1,0:T(8,128)(2,1)}, bf16[256,1536]{1,0:T(8,128)(2,1)}, u32[]{:S(2)}, u32[]{:S(2)}) collective-permute-start(bf16[256,1536]{1,0:T(8,128)(2,1)} %get-tuple-element.407), channel_id=1, source_target_pairs={{0,1},{1,0},{2,3},{3,2},{4,5},{5,4},{6,7},{7,6},{8,9},{9,8},{10,11... | collective-permute-start | bytes 2359304 | tf_op jit(solution)/shard_map/ppermute | solution.py:379
  727.5 75.5 %collective-permute-start.81 = (bf16[64,2048]{1,0:T(8,128)(2,1)}, bf16[64,2048]{1,0:T(8,128)(2,1)S(1)}, u32[]{:S(2)}, u32[]{:S(2)}) collective-permute-start(bf16[64,2048]{1,0:T(8,128)(2,1)} %get-tuple-element.425), channel_id=1, source_target_pairs={{0,1},{1,0},{2,3},{3,2},{4,5},{5,4},{6,7},{7,6},{8,9},{9,8},{10,11... | collective-permute-start | bytes 786440 | tf_op jit(solution)/shard_map/ppermute | solution.py:379
  763.8 46.1 %collective-permute-start.78 = (bf16[256,1536]{1,0:T(8,128)(2,1)}, bf16[256,1536]{1,0:T(8,128)(2,1)}, u32[]{:S(2)}, u32[]{:S(2)}) collective-permute-start(bf16[256,1536]{1,0:T(8,128)(2,1)} %fusion.5), channel_id=1, source_target_pairs={{0,2},{2,0},{1,3},{3,1},{4,6},{6,4},{5,7},{7,5},{8,10},{10,8},{9,1... | collective-permute-start | bytes 2359304 | tf_op jit(solution)/shard_map/ppermute | solution.py:379
  766.9 43.0 %collective-permute-start.79 = (bf16[64,2048]{1,0:T(8,128)(2,1)}, bf16[64,2048]{1,0:T(8,128)(2,1)}, u32[]{:S(2)}, u32[]{:S(2)}) collective-permute-start(bf16[64,2048]{1,0:T(8,128)(2,1)} %fusion.10), channel_id=1, source_target_pairs={{0,2},{2,0},{1,3},{3,1},{4,6},{6,4},{5,7},{7,5},{8,10},{10,8},{9,1... | collective-permute-start | bytes 786440 | tf_op jit(solution)/shard_map/ppermute | solution.py:379
  768.5 52.2 %collective-permute-start.86 = (bf16[4,128,2048]{2,1,0:T(8,128)(2,1)}, bf16[4,128,2048]{2,1,0:T(8,128)(2,1)S(1)}, u32[]{:S(2)}, u32[]{:S(2)}) collective-permute-start(bf16[4,128,2048]{2,1,0:T(8,128)(2,1)} %all-to-all-done.1), channel_id=1, source_target_pairs={{0,16},{16,0},{1,17},{17,1},{2,18},{18,2},{3,19},{19,3},{4,20},{20... | collective-permute-start | bytes 6291464 | tf_op jit(solution)/shard_map/ppermute | solution.py:379
  820.8 21.1 %collective-permute-start.87 = (bf16[2,128,1536]{2,1,0:T(8,128)(2,1)S(1)}, bf16[2,128,1536]{2,1,0:T(8,128)(2,1)S(1)}, u32[]{:S(2)}, u32[]{:S(2)}) collective-permute-start(bf16[2,128,1536]{2,1,0:T(8,128)(2,1)S(1)} %pad_maximum_fusion.23), channel_id=1, source_target_pairs={{0,16},{16,0},{1,17},{17,1},{2,18},{18,2},{3,19},{19,3},{4,20},{20... | collective-permute-start | bytes 2359304 | tf_op jit(solution)/shard_map/ppermute | solution.py:379
  (118 other events, 1296.7 us)
Sparse Core Ops, SparseCore 0:
  134.6 104.3 all-gather.1
  517.6 136.5 reduce-scatter.1

commit v3 on v2

--- a/solution.py
+++ b/solution.py
@@ -588,8 +588,9 @@
     return value * cosine + partner * sine
 
 
-def project_kernel(a_ref, w_ref, cos_ref, sin_ref, q_ref, kv_ref):
+def project_kernel(core_ref, a_ref, a2_ref, w_ref, w2_ref, cos_ref, sin_ref, q_ref, kv_ref):
     joined = jnp.dot(a_ref[...], w_ref[...], preferred_element_type=F32)
+    joined = joined + jnp.dot(a2_ref[...], w2_ref[...], preferred_element_type=F32)
     wide = q_ref.shape[1]
     cosine, sine = cos_ref[...], sin_ref[...]
     for i in range(wide // 128):
@@ -603,21 +604,29 @@
     return pl.BlockSpec(array.shape, lambda i: (0,) * array.ndim)
 
 
-def project(a_all, weight, cosine, sine):
+def project(core, a_all, weight, weight_other, cosine, sine):
     tokens, model = a_all.shape
     wide = weight.shape[1] // 3
-    tile = cosine.shape[0]
-    by_tile = lambda columns: pl.BlockSpec((tile, columns), lambda i: (i, 0))
+    tile, half = cosine.shape[0], model // 2
+    by_tile = lambda columns: pl.BlockSpec((tile, columns), lambda i, core: (i, 0))
+    whole = lambda array: pl.BlockSpec(array.shape, lambda i, core: (0, 0))
     return pl.pallas_call(
         project_kernel,
-        grid=(tokens // tile,),
-        in_specs=[by_tile(model), whole_spec(weight), whole_spec(cosine), whole_spec(sine)],
-        out_specs=[by_tile(wide), by_tile(2 * wide)],
+        grid_spec=pltpu.PrefetchScalarGridSpec(
+            num_scalar_prefetch=1,
+            grid=(tokens // tile,),
+            in_specs=[
+                pl.BlockSpec((tile, half), lambda i, core: (i, core[0])),
+                pl.BlockSpec((tile, half), lambda i, core: (i, 1 - core[0])),
+                whole(weight), whole(weight_other), whole(cosine), whole(sine),
+            ],
+            out_specs=[by_tile(wide), by_tile(2 * wide)],
+        ),
         out_shape=[jax.ShapeDtypeStruct((tokens, columns), BF16) for columns in (wide, 2 * wide)],
         compiler_params=BIG,
         cost_estimate=pl.CostEstimate(flops=0, bytes_accessed=1_000_000, transcendentals=0),
         name="project",
-    )(a_all, weight, cosine, sine)
+    )(core, a_all, a_all, weight, weight_other, cosine, sine)
 
 
 def head_lanes(value, odd):
@@ -736,12 +745,14 @@
     )(*operands, *given)
 
 
-def hidden_kernel(*refs):
-    b_refs, dy_refs, (w_ref, down_ref, z_ref, d_ref, b_ref, dy_ref) = refs[:5], refs[5:10], refs[10:16]
-    db_refs, y_refs = refs[16:21], refs[21:]
-    step = pl.program_id(0)
-    at_step(step, fill, b_refs, b_ref)
-    at_step(step, fill, dy_refs, dy_ref)
+def hidden_kernel(count, *refs):
+    (b_refs, dy_refs), (w_ref, down_ref, z_ref, d_ref, b_ref, dy_ref) = (
+        (refs[:count], refs[count : 2 * count]),
+        refs[2 * count : 2 * count + 6],
+    )
+    db_refs, y_refs = refs[2 * count + 6 : 3 * count + 6], refs[3 * count + 6 :]
+    fill(b_refs, b_ref)
+    fill(dy_refs, dy_ref)
     piece = z_ref.shape[1] // HIDDEN_PIECES
     for i in range(HIDDEN_PIECES):
         at = slice(i * piece, (i + 1) * piece)
@@ -757,23 +768,25 @@
     db = lax.dot_general(d_ref[...], w_ref[...], (((1,), (1,)), ((), ())), preferred_element_type=F32).astype(BF16)
     y = jnp.dot(z_ref[...], down_ref[...], preferred_element_type=F32).astype(BF16)
 
-    at_step(step, spill, db_refs, db)
-    at_step(step, spill, y_refs, y)
-
-
-def hidden_units(square, b_blocks, dy_blocks, weight, down, buffers):
-    half, model = b_blocks[0].shape
-    rows, width = 2 * half, down.shape[0]
+    spill(db_refs, db)
+    spill(y_refs, y)
+
+
+def hidden_units(index, b_blocks, dy_blocks, weight, down, buffers):
+    model, width = weight.shape[0], down.shape[0]
+    shapes = [block.shape for block in b_blocks]
+    rows = sum(shape[0] for shape in shapes)
     once = dict(pipeline_mode=pl.Buffered(1))
-    by_sequence = lambda columns: pl.BlockSpec((rows, columns), lambda i: (2 * square + i, 0))
-    return into(
-        hidden_kernel, "hidden_units", [*b_blocks, *dy_blocks, weight, down],
-        square_specs(half, model, **once) * 2 + [pl.BlockSpec(a.shape, lambda i: (0, 0), **once) for a in (weight, down)],
-        [(4 * rows, width), (4 * rows, 2 * width), (4 * rows, model), (4 * rows, model)] + square_shapes(half, model) * 2,
-        [by_sequence(width), by_sequence(2 * width), by_sequence(model), by_sequence(model)]
-        + square_specs(half, model) * 2,
-        buffers, (2,),
-    )
+    own = lambda columns: pl.BlockSpec((rows, columns), lambda i: (index, 0))
+    operands = [*b_blocks, *dy_blocks, weight, down]
+    out = into(
+        functools.partial(hidden_kernel, len(shapes)), "hidden_units", operands,
+        [whole_shape(a.shape, **once) for a in operands],
+        [(4 * rows, width), (4 * rows, 2 * width), (4 * rows, model), (4 * rows, model)] + shapes * 2,
+        [own(width), own(2 * width), own(model), own(model)] + [whole_shape(shape) for shape in shapes * 2],
+        buffers, (1,),
+    )
+    return list(out[:4]), list(out[4 : 4 + len(shapes)]), list(out[4 + len(shapes) :])
 
 
 def attend_back_kernel(count, *refs):
@@ -832,7 +845,7 @@
     )
 
 
-def join_kernel(dq_ref, dkv_ref, dkv2_ref, w_ref, cos_ref, sin_ref, out_ref, *term_refs):
+def join_kernel(dq_ref, dkv_ref, dkv2_ref, cos_ref, sin_ref, out_ref):
     wide = dq_ref.shape[1]
     out_ref[:, :wide] = dq_ref[...]
     for i in range(wide // 128):
@@ -840,19 +853,36 @@
         dk = dkv_ref[:, at] + dkv2_ref[:, at].astype(F32)
         out_ref[:, wide + i * 128 : wide + (i + 1) * 128] = turn(dk, cos_ref[...], -sin_ref[...]).astype(BF16)
     out_ref[:, 2 * wide :] = (dkv_ref[:, wide:] + dkv2_ref[:, wide:].astype(F32)).astype(BF16)
-    term = lax.dot_general(out_ref[...], w_ref[...], (((1,), (1,)), ((), ())), preferred_element_type=F32)
-    spill(term_refs, term.astype(BF16))
-
-
-def join_grads(sequence, dq, dkv, dkv_other, weight, tables, d_qkv):
-    (rows, wide), model = dq.shape, weight.shape[0]
-    operands = [dq, dkv, dkv_other, weight, *tables]
-    shapes = sequence_shapes(sequence, rows // 2, model)
+
+
+def join_grads(sequence, dq, dkv, dkv_other, tables, d_qkv):
+    rows, wide = dq.shape
+    operands = [dq, dkv, dkv_other, *tables]
+    (d_qkv,) = into(
+        join_kernel, "join_grads", operands, [whole_spec(a) for a in operands],
+        [(2 * rows, 3 * wide)], [pl.BlockSpec((rows, 3 * wide), lambda i: (sequence, 0))], [d_qkv], (1,),
+    )
+    return d_qkv
+
+
+def input_terms_kernel(d_ref, w_ref, w2_ref, core_ref, *term_refs):
+    mine, other = (
+        lax.dot_general(d_ref[...], ref[...], (((1,), (1,)), ((), ())), preferred_element_type=F32).astype(BF16)
+        for ref in (w_ref, w2_ref)
+    )
+    first = core_ref[0] == 0
+    terms = jnp.concatenate([jnp.where(first, mine, other), jnp.where(first, other, mine)], axis=1)
+    at_step(pl.program_id(0), spill, term_refs, terms)
+
+
+def input_terms(core, d_qkv, weights):
+    tokens, wide = d_qkv.shape
+    model = 2 * weights[0].shape[0]
     return into(
-        join_kernel, "join_grads", operands, [whole_spec(a) for a in operands],
-        [(2 * rows, 3 * wide)] + shapes,
-        [pl.BlockSpec((rows, 3 * wide), lambda i: (sequence, 0))] + [whole_shape(shape) for shape in shapes],
-        [d_qkv], (1,),
+        input_terms_kernel, "input_terms", [d_qkv, *weights, core],
+        [pl.BlockSpec((tokens // 2, wide), lambda i: (i, 0)), whole_spec(weights[0]), whole_spec(weights[1]),
+         pl.BlockSpec(memory_space=pltpu.SMEM)],
+        square_shapes(tokens // 4, model), square_specs(tokens // 4, model), [], (2,),
     )
 
 
@@ -930,33 +960,42 @@
     ff_gain = feedforward_gain.astype(F32)[:, None]
 
     mine, sent = head_slices(place, [query_weight, key_weight, value_weight], attn_gain, rows)
+    out_half = chip_half(place, output_weight)
     (a_own,) = on_rows(open_kernel, "open_layer", [x_own], [BF16])
+    dy_l = swap(dy_own, "zl")
+    mine, sent, out_half, a_own, down_late, gate_late, up_late = fence(
+        [mine, sent, out_half, a_own, down_weight, gate_weight, up_weight], []
+    )
+
     received = swap(sent, "x")
-    a_x, a_s = along(a_own)
-    gate_up = hidden_slices(place, [gate_weight, up_weight], ff_gain, hidden_rows)
+    out_zh, out_zl = swap(out_half, "zh"), swap(out_half, "zl")
     qkv = in_order(mine, received, place.x)
-    a_x, a_s, qkv, gate_up, out_late, dy_late, document_ids = fence(
-        [a_x, a_s, qkv, gate_up, output_weight, dy_own, document_ids], []
-    )
-
+    down_half = chip_half(place, down_late)
+    quarter = down_half.shape[0] // 2
+    qkv, a_late, out_zh, out_zl, dy_late, down_half, dy_l = fence(
+        [qkv, a_own, out_zh, out_zl, dy_own, down_half, dy_l], []
+    )
+
+    gate_up = hidden_slices(place, [gate_late, up_late], ff_gain, hidden_rows)
     by_zh, by_zl = swap(qkv, "zh"), swap(qkv, "zl")
+    a_x, a_s = along(a_late)
+    out_both = swap(out_zh, "zl")
+    by_zh, by_zl, a_x, a_s, dy_late, out_both, gate_up, document_ids, down_half = fence(
+        [by_zh, by_zl, a_x, a_s, dy_late, out_both, gate_up, document_ids, down_half], []
+    )
+
+    by_both = swap(by_zh, "zl")
+    dy_x, dy_s = along(dy_late)
     a_o = opposite(a_x, a_s)
-    gate_up = share_columns(gate_up)
-    dy_x, dy_s = along(dy_late)
+    out_half = in_order(
+        in_order(out_half, out_zl, place.zl), in_order(out_zh, out_both, place.zl), place.zh
+    ).reshape(4, -1, model)
     documents = document_ids[0]
     first = jnp.sum((documents[None, :] < documents[:, None]).astype(jnp.int32), axis=1)
-    out_half = chip_half(place, out_late)
+    qkv = in_order(in_order(qkv, by_zl, place.zl), in_order(by_zh, by_both, place.zl), place.zh)
+    first = jnp.stack([first, swap(first, "seq")])
+    down_far = [swap(down_half[:quarter], "zh")]
     a_all = jnp.concatenate([a_own, a_x, a_s, *a_o], axis=0)
-    by_zh, by_zl, a_all, out_half, first, dy_x, dy_s, dy_late, gate_up = fence(
-        [by_zh, by_zl, a_all, out_half, first, dy_x, dy_s, dy_late, gate_up], []
-    )
-
-    gate_up = lax.all_gather(gate_up, ("core", "zh"), axis=0, tiled=True).reshape(model, -1)
-    by_both = swap(by_zh, "zl")
-    qkv = in_order(in_order(qkv, by_zl, place.zl), in_order(by_zh, by_both, place.zl), place.zh)
-    dy_o = opposite(dy_x, dy_s)
-    out_zh, out_zl = swap(out_half, "zh"), swap(out_half, "zl")
-    first = jnp.stack([first, swap(first, "seq")])
 
     def positions(dx, dc):
         holder = (place.x ^ dx) * 2 + (place.core ^ dc)
@@ -976,157 +1015,158 @@
     start = jnp.concatenate(starts, axis=1)[:, :, None]
     where = (qpos[:, None], start, kpos[None, :])
     tables = (cosine, sine)
-    qkv, out_zh, out_zl, dy_late, where, tables = fence([qkv, out_zh, out_zl, dy_late, where, tables], dy_o)
-
-    qkv = in_order(qkv, swap(qkv, "core"), place.core).reshape(model, -1)
-    dy_l = swap(dy_late, "zl")
-    out_both = swap(out_zh, "zl")
-    out_half = in_order(
-        in_order(out_half, out_zl, place.zl), in_order(out_zh, out_both, place.zl), place.zh
-    ).reshape(4, -1, model)
-    qkv, out_half, down_late = fence([qkv, out_half, down_weight], [])
-
-    q_all, kv_all = project(a_all, qkv, *tables)
+    qkv, dy_x, dy_s, dy_l, tables, a_all, down_half, out_half, down_far, gate_up = fence(
+        [qkv, dy_x, dy_s, dy_l, tables, a_all, down_half, out_half, down_far, gate_up], []
+    )
+
+    qkv = qkv.reshape(model // 2, -1)
+    qkv_other = swap(qkv, "core")
+    gate_up = share_columns(gate_up)
+    dy_ls = swap(dy_l, "seq")
+    dy_o = opposite(dy_x, dy_s)
     out_rows = chip_rows(place, out_half, swap(out_half, "core"))
-    down_half = chip_half(place, down_late)
-    quarter = down_half.shape[0] // 2
-    q_all, kv_all, out_rows, dy_l, down_half = fence([q_all, kv_all, out_rows, dy_l, down_half], [])
-
+    core = jnp.stack([place.core]).astype(jnp.int32)
+    down_far += [swap(down_half[quarter:], "zh")]
+    qkv, qkv_other, core, dy_l = fence([qkv, qkv_other, core, dy_l], [])
+
+    q_all, kv_all = project(core, a_all, qkv, qkv_other, *tables)
+    q_all, kv_all, down_half, down_far, dy_o, dy_ls, dy_l, where, gate_up = fence(
+        [q_all, kv_all, down_half, down_far, dy_o, dy_ls, dy_l, where, gate_up], [out_rows]
+    )
+
+    gate_up = lax.all_gather(gate_up, ("core", "zh"), axis=0, tiled=True).reshape(model, -1)
+    dy_lx = swap(dy_l, "x")
     kv_other = swap(kv_all, "core")
     o_all, term_s, *term_o = attend(1, q_all, kv_all, kv_other, out_rows, where, None)
-    dy_lx, dy_ls = along(dy_l)
-    term_s, term_o, o_all, dy_lx, dy_ls = fence([term_s, term_o, o_all, dy_lx, dy_ls], [])
+    down_half = in_order(down_half, jnp.concatenate(down_far), place.zh)
+    down_rows = chip_rows(place, down_half, swap(down_half, "core"))
+    term_s, term_o, o_all, down_rows, dy_lx = fence([term_s, term_o, o_all, down_rows, dy_lx], [])
 
     o_all, own, term_x = attend(0, q_all, kv_all, kv_other, out_rows, where, o_all)
     halves = return_halves(*term_o)
-    dy_lo = opposite(dy_lx, dy_ls)
-    own, term_x, halves, down_half = fence([own, term_x, halves, down_half], dy_lo)
-
-    down_far = [swap(down_half[:quarter], "zh")]
+    own, term_x, halves, dy_lx, dy_ls = fence([own, term_x, halves, dy_lx, dy_ls], [])
+
     sums = return_along(term_x, term_s, *halves)
     hidden, b_own = on_rows(close_attention_kernel, "close_attention", [x_own, own, *sums], [F32, BF16])
-    b_own, down_half = fence([b_own, down_half], [])
+    b_own, dy_lx, dy_ls = fence([b_own, dy_lx, dy_ls], [])
 
     b_x, b_s = along(b_own)
     b_l = swap(b_own, "zl")
-    b_x, b_s, b_l, down_half = fence([b_x, b_s, b_l, down_half], down_far)
-
-    down_far += [swap(down_half[quarter:], "zh")]
+    dy_lo = opposite(dy_lx, dy_ls)
+    b_x, b_s = fence([b_x, b_s], dy_lo)
+
     b_o = opposite(b_x, b_s)
-    (b_l,) = fence([b_l], b_o)
+    buffers, db0, y0 = hidden_units(0, [b_own, b_x], [dy_own, dy_x], gate_up, down_rows, [None] * 4)
+    buffers, b_o, b_l = fence([buffers, b_o, b_l], [])
 
     b_lx, b_ls = along(b_l)
-    down_half = in_order(down_half, jnp.concatenate(down_far), place.zh)
-    down_rows = chip_rows(place, down_half, swap(down_half, "core"))
-    *buffers, d0, d1, d2, d3, d4, y0, y1, y2, y3, y4 = hidden_units(
-        0, [b_own, b_x, b_s, *b_o], [dy_own, dy_x, dy_s, *dy_o], gate_up, down_rows, [None] * 4
-    )
+    buffers, db1, y1 = hidden_units(1, [b_s, *b_o], [dy_s, *dy_o], gate_up, down_rows, buffers)
+    buffers, b_lx, b_ls, db1 = fence([buffers, b_lx, b_ls, db1], [])
+
     b_lo = opposite(b_lx, b_ls)
-    near, near_y = [d0, d1, d2, d3, d4], [y0, y1, y2, y3, y4]
-    near, b_lx = fence([near, b_lx], b_lo)
-
-    *buffers, d0, d1, d2, d3, d4, y0, y1, y2, y3, y4 = hidden_units(
-        1, [b_l, b_lx, b_ls, *b_lo], [dy_l, dy_lx, dy_ls, *dy_lo], gate_up, down_rows, buffers
-    )
+    near_halves = return_halves(*db1[1:])
+    buffers, db2, y2 = hidden_units(2, [b_l, b_lx], [dy_l, dy_lx], gate_up, down_rows, buffers)
+    buffers, b_lo, near_halves = fence([buffers, b_lo, near_halves], [])
+
+    near_along = return_along(db0[1], db1[0], *near_halves)
+    buffers, db3, y3 = hidden_units(3, [b_ls, *b_lo], [dy_ls, *dy_lo], gate_up, down_rows, buffers)
     z_all, d_all, b_all, dy_all = buffers
-    far, far_y = [d0, d1, d2, d3, d4], [y0, y1, y2, y3, y4]
-    near_halves = return_halves(*near[3:])
-    near_along = return_along(near[1], near[2], *near_halves)
-    far, d_all = fence([far, d_all], near_along)
-
-    far_halves = return_halves(*far[3:])
+    db3, z_all, d_all, near_along = fence([db3, z_all, d_all, near_along], [])
+
+    far_halves = return_halves(*db3[1:])
+    down_terms = dot_low(z_all, dy_all, 0, 0)
+    d_all, down_terms, far_halves = fence([d_all, down_terms, far_halves], [])
+
+    far_along = return_along(db2[1], db3[0], *far_halves)
     gate_up_terms = dot_low(b_all, d_all, 0, 0)
-    z_all, gate_up_terms, far_halves = fence([z_all, gate_up_terms, far_halves], [])
-
-    far_along = return_along(far[1], far[2], *far_halves)
+    down_sums = add_core(place, down_terms.reshape(2, 2, -1, model), 1)
+    gate_up_terms, down_sums, y1, near0, far_along = fence([gate_up_terms, down_sums, y1, db0[0], far_along], [])
+
+    down_total = lax.psum_scatter(down_sums, "zh", scatter_dimension=0, tiled=True)[0]
+    across = return_across(db2[0], *far_along)
+    near_y_halves = return_halves(*y1[1:])
     gate_up_sums = add_core(place, gate_up_terms.reshape(2, 2, 4, rows, -1), 0)
-    down_terms = dot_low(z_all, dy_all, 0, 0)
-    gate_up_sums, down_terms, near_y, near0, far_along = fence(
-        [gate_up_sums, down_terms, near_y, near[0], far_along], []
-    )
-
-    across = return_across(far[0], *far_along)
-    near_y_halves = return_halves(*near_y[3:])
-    gate_up_near = lax.psum_scatter(gate_up_sums, "zh", scatter_dimension=0, tiled=True)[0]
-    down_sums = add_core(place, down_terms.reshape(2, 2, -1, model), 1)
     dh, dh_low = on_rows(
         close_hidden_kernel, "close_hidden", [dy_own, hidden, near0, *near_along, across], [F32, BF16]
     )
-    dh_low, down_sums, near_y_halves = fence([dh_low, down_sums, near_y_halves], [])
-
+    dh_low, gate_up_sums, near_y_halves = fence([dh_low, gate_up_sums, near_y_halves], [])
+
+    gate_up_near = lax.psum_scatter(gate_up_sums, "zh", scatter_dimension=0, tiled=True)[0]
     dh_x, dh_s = along(dh_low)
-    down_to_zh = to_far(place, down_sums)
-    dh_x, dh_s, down_to_zh, near_y, far_y = fence([dh_x, dh_s, down_to_zh, near_y, far_y], [])
+    dh_x, dh_s, y0, y1, y3 = fence([dh_x, dh_s, y0, y1, y3], [])
 
     dh_o = opposite(dh_x, dh_s)
     dh_all, dq0, dkv0, dkv_other0 = attend_back(
         0, [dh_low, dh_x], out_rows, q_all, kv_all, kv_other, where, tables, None
     )
-    near_y_along = return_along(near_y[1], near_y[2], *near_y_halves)
-    down_far = [swap(down_to_zh[:quarter], "zh")]
-    dkv_other0, dh_s, far_y, down_to_zh = fence([dkv_other0, dh_s, far_y, down_to_zh], dh_o)
+    near_y_along = return_along(y0[1], y1[0], *near_y_halves)
+    dkv_other0, dh_s, y3 = fence([dkv_other0, dh_s, y3], dh_o)
 
     dkv_other0 = swap(dkv_other0, "core")
+    down_other = swap(down_total, "seq")
     dh_all, dq1, dkv1, dkv_other1 = attend_back(
         1, [dh_s, *dh_o], out_rows, q_all, kv_all, kv_other, where, tables, dh_all
     )
-    far_y_halves = return_halves(*far_y[3:])
-    dkv0, dkv_other0, dkv_other1, dh_all, down_to_zh = fence(
-        [dkv0, dkv_other0, dkv_other1, dh_all, down_to_zh], [*near_y_along, *far_y_halves, *down_far]
-    )
+    far_y_halves = return_halves(*y3[1:])
+    dkv_other1, dh_all = fence([dkv_other1, dh_all], near_y_along)
 
     dkv_other1 = swap(dkv_other1, "core")
-    d_qkv, own, term_x = join_grads(0, dq0, dkv0, dkv_other0, qkv, tables, None)
-    d_qkv, term_s, *term_o = join_grads(1, dq1, dkv1, dkv_other1, qkv, tables, d_qkv)
-    down_far += [swap(down_to_zh[quarter:], "zh")]
-    far_y_along = return_along(far_y[1], far_y[2], *far_y_halves)
+    d_qkv = join_grads(0, dq0, dkv0, dkv_other0, tables, None)
     out_terms = dot_low(o_all, dh_all, 0, 0)
-    own, term_x, term_s, term_o, d_qkv, out_terms = fence(
-        [own, term_x, term_s, term_o, d_qkv, out_terms], far_y_along
-    )
-
-    halves = return_halves(*term_o)
+    d_qkv, dkv_other1, out_terms, far_y_halves, down_other = fence(
+        [d_qkv, dkv_other1, out_terms, far_y_halves, down_other], []
+    )
+
+    d_qkv = join_grads(1, dq1, dkv1, dkv_other1, tables, d_qkv)
     qkv_terms = dot_low(a_all, d_qkv, 0, 0)
+    far_y_along = return_along(y2[1], y3[0], *far_y_halves)
     out_sums = add_core(place, out_terms.reshape(4, 2, -1, model), 1).reshape(2, 2, -1, model)
-    y_across = return_across(far_y[0], *far_y_along)
-    qkv_terms, halves, out_sums = fence([qkv_terms, halves, out_sums], down_far)
-
-    sums = return_along(term_x, term_s, *halves)
-    qkv_sums = add_core(place, qkv_terms.reshape(2, 2, 2, 2 * rows, -1), 0)
-    qkv_sums, out_sums, sums, gate_up_near = fence([qkv_sums, out_sums, sums, gate_up_near], [y_across])
+    qkv_terms, out_sums, d_qkv = fence([qkv_terms, out_sums, d_qkv], [])
 
     def part(sums, zh, zl):
         return lax.dynamic_slice(sums, (place.zh ^ zh, place.zl ^ zl, 0, 0), (1, 1, *sums.shape[2:]))[0, 0]
 
-    qkv_zl, out_zl = swap(part(qkv_sums, 1, 1), "zl"), swap(part(out_sums, 1, 1), "zl")
+    qkv_sums = add_core(place, qkv_terms.reshape(2, 2, 2, 2 * rows, -1), 0)
+    own, term_x, term_s, *term_o = input_terms(core, d_qkv, [qkv, qkv_other])
+    out_zl = swap(part(out_sums, 1, 1), "zl")
+    qkv_sums, out_sums, out_zl, term_o, far_y_along, gate_up_near = fence(
+        [qkv_sums, out_sums, out_zl, term_o, far_y_along, gate_up_near], []
+    )
+
+    qkv_zl = swap(part(qkv_sums, 1, 1), "zl")
     gate_up_near = share_columns(gate_up_near)
+    sums = return_along(term_x, term_s, *return_halves(*term_o))
+    out_zh = swap(add_low(part(out_sums, 1, 0), out_zl).astype(BF16), "zh")
+    out_zl = swap(part(out_sums, 0, 1), "zl")
+    down_grad = own_rows(place, down_total, down_other)
+    qkv_zl, gate_up_near, sums = fence([qkv_zl, gate_up_near, sums], [down_grad])
+
+    qkv_zh = swap(add_low(part(qkv_sums, 1, 0), qkv_zl).astype(BF16), "zh")
+    qkv_zl = swap(part(qkv_sums, 0, 1), "zl")
+    gate_up_far = swap(gate_up_near, "seq")
     (input_grad,) = on_rows(close_input_kernel, "close_input", [x_own, dh, own, *sums], [BF16])
-    down_total = add_far(place, down_sums, jnp.concatenate(down_far))
-    down_other = swap(down_total, "seq")
-    qkv_zl, out_zl, input_grad = fence([qkv_zl, out_zl, input_grad], [])
-
-    qkv_zh = swap(add_low(part(qkv_sums, 1, 0), qkv_zl).astype(BF16), "zh")
-    out_zh = swap(add_low(part(out_sums, 1, 0), out_zl).astype(BF16), "zh")
-    qkv_zl, out_zl = swap(part(qkv_sums, 0, 1), "zl"), swap(part(out_sums, 0, 1), "zl")
-    gate_up_far = swap(gate_up_near, "seq")
-    layer_output = add_low(hidden, near_y[0], *near_y_along, y_across).astype(BF16)
-    down_grad = own_rows(place, down_total, down_other)
-    qkv_zh, out_zh, qkv_zl, out_zl = fence([qkv_zh, out_zh, qkv_zl, out_zl], [layer_output, down_grad])
+    qkv_zh, qkv_zl, out_zh, out_zl = fence([qkv_zh, qkv_zl, out_zh, out_zl], [input_grad])
 
     qkv_total = add_low(part(qkv_sums, 0, 0), qkv_zl, qkv_zh).astype(BF16).reshape(2, rows, -1)
+    kept = lax.dynamic_index_in_dim(qkv_total, place.x, 0, False)
+    received = swap(lax.dynamic_index_in_dim(qkv_total, 1 - place.x, 0, False), "x")
+    kept_far, received_far = swap(kept, "seq"), swap(received, "seq")
+    y_across = return_across(y2[0], *far_y_along)
     out_total = add_low(part(out_sums, 0, 0), out_zl, out_zh).astype(BF16)
-    received = swap(lax.dynamic_index_in_dim(qkv_total, 1 - place.x, 0, False), "x")
+    kept, kept_far, received, received_far, gate_up_far, out_total = fence(
+        [kept, kept_far, received, received_far, gate_up_far, out_total], []
+    )
+
     out_other = swap(out_total, "seq")
-    qkv_near = in_order(lax.dynamic_index_in_dim(qkv_total, place.x, 0, False), received, place.x)
-    qkv_near, out_other, gate_up_far = fence([qkv_near, out_other, gate_up_far], [])
-
-    qkv_far = swap(qkv_near, "seq")
+    output_grad = own_rows(place, out_total, out_other)
+
+    layer_output = add_low(hidden, y0[0], *near_y_along, y_across).astype(BF16)
+    pieces = in_order(in_order(kept, received, place.x), in_order(kept_far, received_far, place.x), place.seq)
+    (query_grad, key_grad, value_grad), attn_gain_grad = finish_columns(
+        pieces, [query_weight, key_weight, value_weight], attn_gain, rows, False
+    )
     (gate_grad, up_grad), ff_gain_grad = finish_columns(
         in_order(gate_up_near, gate_up_far, place.seq), [gate_weight, up_weight], ff_gain, hidden_rows, True
-    )
-    output_grad = own_rows(place, out_total, out_other)
-    (query_grad, key_grad, value_grad), attn_gain_grad = finish_columns(
-        in_order(qkv_near, qkv_far, place.seq), [query_weight, key_weight, value_weight], attn_gain, rows, False
     )
     return (
         layer_output[None], input_grad[None], attn_gain_grad, query_grad, key_grad, value_grad, output_grad,

time: 872 us -> 763 us (0.88)
  waiting for transfers between devices: 381 us -> 307 us
  other arithmetic: 85.5 us -> 57.7 us
    ppermute x87 -> x86, waiting for transfers between devices: 381 us -> 297 us  [swap(): return lax.ppermute(value, axis, [(0, 1), (1, 0)])]
    another operation x18 -> x14, other arithmetic: 20.3 us -> 9.81 us  [in_order(): jnp.stack([jnp.where(first, mine, other), jnp.where(first, other, mine)])]
    all_gather x1, waiting for transfers between devices: 0.01 us -> 9.61 us  [paired_device(): lax.all_gather(gate_up, ('core', 'zh'), axis=0, tiled=True)]
    ppermute x87 -> x86, starting transfers between devices: 90.2 us -> 84.3 us  [swap(): return lax.ppermute(value, axis, [(0, 1), (1, 0)])]
    pallas_call x8 -> x11, Pallas kernels: 129 us -> 134 us  [into(): pl.pallas_call(body, grid=grid, in_specs=in_specs + [pl.BlockSpec(memory_...]
    unnamed x151 -> x181, local copies, waits for them, and re-layouts: 19 us -> 20.5 us
  transfers between devices with their start and end apart: 93 -> 93, of which waited for: 36 -> 36; matrix products, arithmetic and copies ran while one was open for 18% -> 15% of each run, Pallas kernels for 20% -> 24%
where the time goes in v3:
time: 763 us; the launch traced here: 753 us
  waiting for transfers between devices  307 us (40%)
  Pallas kernels  191 us (25%)
  starting transfers between devices  98.1 us (13%)
  other arithmetic  57.7 us (8%)
  local copies, waits for them, and re-layouts  46.9 us (6%)
  matrix products  37.6 us (5%)
  between operations  15.4 us (2%)
    ppermute x86, waiting for transfers between devices, swap(): return lax.ppermute(value, axis, [(0, 1), (1, 0)])  297 us
    pallas_call x11, Pallas kernels, into(): pl.pallas_call(body, grid=grid, in_specs=in_specs + [pl.BlockSpec(memory_...  134 us
    ppermute x86, starting transfers between devices, swap(): return lax.ppermute(value, axis, [(0, 1), (1, 0)])  84.3 us
    dot_general x4, matrix products, dot_low(): lax.dot_general(left, right, (((left_dim,), (right_dim,)), ((), ())), pre...  37.6 us
    pallas_call x2, Pallas kernels, finish_columns(): pl.pallas_call(functools.partial(finish_kernel, count), grid=(16,), in_sp...  22.8 us
    unnamed x181, local copies, waits for them, and re-layouts  20.5 us
    pallas_call x4, Pallas kernels, on_rows(): pl.pallas_call(kernel, grid=(3,), in_specs=[tile] * len(operands), out_sp...  16.8 us
  transfers between devices with their start and end apart: 93, of which 36 were waited for; matrix products, arithmetic and copies ran while one was open for 15% of the time, Pallas kernels for 24%

profile of v3, /device:TPU:0, one launch (start us, length us, event | category | flops | bytes accessed | tf_op | source)
XLA Modules:
  0.0 753.3 jit_solution(12495052847803324666)
XLA Ops:
  36.2 7.3 collective-permute-done.2
  51.1 4.3 column_slices.3
  56.6 29.2 %collective-permute-done.10 = bf16[64,2048]{1,0:T(8,128)(2,1)S(1)} collective-permute-done((bf16[64,2048]{1,0:T(8,128)(2,1)S(1)}, bf16[64,2048]{1,0:T(8,128)(2,1)S(1)}, u32[]{:S(2)}, u32[]{:S(2)}) %collective-permute-start.10) | collective-permute-done | bytes 262176 | tf_op jit(solution)/shard_map/ppermute | solution.py:379
  86.1 4.4 collective-permute-start.13
  96.3 15.8 %collective-permute-done.14 = bf16[96,2048]{1,0:T(8,128)(2,1)S(1)} collective-permute-done((bf16[96,2048]{1,0:T(8,128)(2,1)S(1)}, bf16[96,2048]{1,0:T(8,128)(2,1)S(1)}, u32[]{:S(2)}, u32[]{:S(2)}) %collective-permute-start.14) | collective-permute-done | bytes 393248 | tf_op jit(solution)/shard_map/ppermute | solution.py:379
  117.4 16.9 %collective-permute-done.16 = bf16[128,2048]{1,0:T(8,128)(2,1)S(1)} collective-permute-done((bf16[128,2048]{1,0:T(8,128)(2,1)S(1)}, bf16[128,2048]{1,0:T(8,128)(2,1)S(1)}, u32[]{:S(2)}, u32[]{:S(2)}) %collective-permute-start.16) | collective-permute-done | bytes 524320 | tf_op jit(solution)/shard_map/ppermute | solution.py:379
  135.7 4.5 all-to-all-start
  141.2 7.5 collective-permute-start.22
  159.6 9.5 %project.1 = (bf16[768,512]{1,0:T(8,128)(2,1)}, bf16[768,1024]{1,0:T(8,128)(2,1)}) custom-call(s32[1]{0:T(128)} %bitcast.20.core_ref.refs_3_, bf16[768,2048]{1,0:T(8,128)(2,1)} %constant_dynamic-update-slice_fusion.a_ref.a2_ref, bf16[768,2048]{1,0:T(8,128)(2,1)} %constant_dynamic-update-slice_fusion.a_ref.a2_ref, bf16[1024,1536]{1,0:T(8,128)(2,1)} %bitcast.157, ...), custom_call_target="tpu_custom_call" | custom-call | bytes 1000000 | tf_op jit(solution)/shard_map/project/pallas_call | solution.py:613
  169.1 5.2 collective-permute-done.19.refs_4_
  177.6 4.7 collective-permute-done.21.refs_3_
  188.6 3.7 collective-permute-done.24.refs_2_.refs_5_.refs_6_
  193.4 9.6 %attend.2 = (bf16[768,512]{1,0:T(8,128)(2,1)}, bf16[192,2048]{1,0:T(8,128)(2,1)}, bf16[96,2048]{1,0:T(8,128)(2,1)}, bf16[96,2048]{1,0:T(8,128)(2,1)}) custom-call(bf16[768,512]{1,0:T(8,128)(2,1)} %get-tuple-element.281.refs_0_.refs_3_.refs_4_, bf16[768,1024]{1,0:T(8,128)(2,1)} %get-tuple-element.282.refs_1_.refs_4_.refs_5_, bf16[768,1024]{1,0:T(8,128)(2,1)} %copy-done.4, ...), custom_call_target="tpu_custom_call" | custom-call | bytes 1000000 | tf_op jit(solution)/shard_map/attend/pallas_call | solution.py:735
  212.4 9.4 %attend.3 = (bf16[768,512]{1,0:T(8,128)(2,1)}, bf16[192,2048]{1,0:T(8,128)(2,1)}, bf16[192,2048]{1,0:T(8,128)(2,1)}) custom-call(bf16[768,512]{1,0:T(8,128)(2,1)} %get-tuple-element.281.refs_0_.refs_3_.refs_4_, bf16[768,1024]{1,0:T(8,128)(2,1)} %get-tuple-element.282.refs_1_.refs_4_.refs_5_, ...), custom_call_target="tpu_custom_call", output_to_operand_aliasing={{0}: (7, {})} | custom-call | bytes 1000000 | tf_op jit(solution)/shard_map/attend/pallas_call | solution.py:735
  224.1 16.7 %collective-permute-done.30.refs_2_ = bf16[192,2048]{1,0:T(8,128)(2,1)S(1)} collective-permute-done((bf16[192,2048]{1,0:T(8,128)(2,1)S(1)}, bf16[192,2048]{1,0:T(8,128)(2,1)S(1)}, u32[]{:S(2)}, u32[]{:S(2)}) %collective-permute-start.30) | collective-permute-done | bytes 786464 | tf_op jit(solution)/shard_map/ppermute | solution.py:379
  242.8 4.2 close_attention.1
  252.3 21.0 %collective-permute-done.33.refs_4_ = bf16[96,2048]{1,0:T(8,128)(2,1)S(1)} collective-permute-done((bf16[96,2048]{1,0:T(8,128)(2,1)S(1)}, bf16[96,2048]{1,0:T(8,128)(2,1)S(1)}, u32[]{:S(2)}, u32[]{:S(2)}) %collective-permute-start.33) | collective-permute-done | bytes 393248 | tf_op jit(solution)/shard_map/ppermute | solution.py:379
  277.6 9.6 %all-gather.2.cloned.1.call-done = bf16[16,128,2048]{2,1,0:T(8,128)(2,1)} async-done(((bf16[4,128,2048]{2,1,0:T(8,128)(2,1)}), bf16[16,128,2048]{2,1,0:T(8,128)(2,1)}) %all-gather.2.cloned.1.call-update) | async-done | bytes 8388624 | tf_op jit(solution)/shard_map/all_gather | solution.py:1037
  287.2 17.1 %hidden_units.4 = (bf16[1536,1024]{1,0:T(8,128)(2,1)}, bf16[1536,2048]{1,0:T(8,128)(2,1)}, bf16[1536,2048]{1,0:T(8,128)(2,1)}, bf16[1536,2048]{1,0:T(8,128)(2,1)...) custom-call(bf16[192,2048]{1,0:T(8,128)(2,1)} %get-tuple-element.310, ...), custom_call_target="tpu_custom_call" | custom-call | bytes 1000000 | tf_op jit(solution)/shard_map/hidden_units/pallas_call | solution.py:735
  307.4 17.2 %hidden_units.5 = (bf16[1536,1024]{1,0:T(8,128)(2,1)}, bf16[1536,2048]{1,0:T(8,128)(2,1)}, bf16[1536,2048]{1,0:T(8,128)(2,1)}, bf16[1536,2048]{1,0:T(8,128)(2,1)...) custom-call(bf16[192,2048]{1,0:T(8,128)(2,1)} %copy-done.30, ...), custom_call_target="tpu_custom_call", output_to_operand_aliasing={{0}: (8, {}), {1}: (9, {}), {2}: (10, {}), {3}: (11, {})} | custom-call | bytes 1000000 | tf_op jit(solution)/shard_map/hidden_units/pallas_call | solution.py:735
  329.7 17.3 %hidden_units.6 = (bf16[1536,1024]{1,0:T(8,128)(2,1)}, bf16[1536,2048]{1,0:T(8,128)(2,1)}, bf16[1536,2048]{1,0:T(8,128)(2,1)}, bf16[1536,2048]{1,0:T(8,128)(2,1)...) custom-call(bf16[192,2048]{1,0:T(8,128)(2,1)} %copy-done.62, ...), custom_call_target="tpu_custom_call", output_to_operand_aliasing={{0}: (6, {}), {1}: (7, {}), {2}: (8, {}), {3}: (9, {})} | custom-call | bytes 1000000 | tf_op jit(solution)/shard_map/hidden_units/pallas_call | solution.py:735
  350.3 17.0 %hidden_units.7 = (bf16[1536,1024]{1,0:T(8,128)(2,1)}, bf16[1536,2048]{1,0:T(8,128)(2,1)}, bf16[1536,2048]{1,0:T(8,128)(2,1)}, bf16[1536,2048]{1,0:T(8,128)(2,1)...) custom-call(bf16[192,2048]{1,0:T(8,128)(2,1)} %copy-done.29, ...), custom_call_target="tpu_custom_call", output_to_operand_aliasing={{0}: (8, {}), {1}: (9, {}), {2}: (10, {}), {3}: (11, {})} | custom-call | bytes 1000000 | tf_op jit(solution)/shard_map/hidden_units/pallas_call | solution.py:735
  369.4 10.4 %convolution_convert_fusion.2 = bf16[1024,2048]{1,0:T(8,128)(2,1)S(1)} fusion(bf16[1536,1024]{1,0:T(8,128)(2,1)} %get-tuple-element.366, bf16[1536,2048]{1,0:T(8,128)(2,1)} %get-tuple-element.367), kind=kOutput, calls=%fused_computation.11 | convolution fusion | flops 6444548096 | bytes 13631488 | tf_op jit(solution)/shard_map/dot_general | solution.py:941
  384.4 15.4 %convolution_convert_fusion.1 = bf16[2048,2048]{1,0:T(8,128)(2,1)} fusion(bf16[1536,2048]{1,0:T(8,128)(2,1)S(1)} %copy-done.1, bf16[1536,2048]{1,0:T(8,128)(2,1)S(1)} %copy-done), kind=kOutput, calls=%fused_computation.3 | convolution fusion | flops 12889096192 | bytes 20971520 | tf_op jit(solution)/shard_map/dot_general | solution.py:941
  402.0 4.8 dynamic-slice_bitcast_fusion
  409.5 31.8 %collective-permute-done.51.refs_3_ = bf16[192,2048]{1,0:T(8,128)(2,1)S(1)} collective-permute-done((bf16[192,2048]{1,0:T(8,128)(2,1)S(1)}, bf16[192,2048]{1,0:T(8,128)(2,1)S(1)}, u32[]{:S(2)}, u32[]{:S(2)}) %collective-permute-start.51) | collective-permute-done | bytes 786464 | tf_op jit(solution)/shard_map/ppermute | solution.py:379
  442.2 5.3 close_hidden.1
  447.5 7.8 %fusion = bf16[2,4,128,2048]{3,2,1,0:T(8,128)(2,1)} fusion(bf16[2,4,128,2048]{3,2,1,0:T(8,128)(2,1)} %collective-permute-done.52, bf16[2,2,4,128,2048]{4,3,2,1,0:T(8,128)(2,1)} %bitcast.162, s32[]{:T(128)S(6)} %select_n.375), kind=kLoop, calls=%fused_computation.1 | loop fusion | flops 8388608 | bytes 12582916 | tf_op jit(solution)/shard_map/convert_element_type | solution.py:499
  456.2 16.9 %collective-permute-done.55.refs_1_ = bf16[192,2048]{1,0:T(8,128)(2,1)S(1)} collective-permute-done((bf16[192,2048]{1,0:T(8,128)(2,1)S(1)}, bf16[192,2048]{1,0:T(8,128)(2,1)S(1)}, u32[]{:S(2)}, u32[]{:S(2)}) %collective-permute-start.55) | collective-permute-done | bytes 786464 | tf_op jit(solution)/shard_map/ppermute | solution.py:379
  480.7 14.7 %attend_back.2 = (bf16[768,2048]{1,0:T(8,128)(2,1)}, bf16[384,512]{1,0:T(8,128)(2,1)}, f32[384,1024]{1,0:T(8,128)}, bf16[384,1024]{1,0:T(8,128)(2,1)}) custom-call(bf16[192,2048]{1,0:T(8,128)(2,1)} %get-tuple-element.390.refs_0_, bf16[192,2048]{1,0:T(8,128)(2,1)} %copy-done.24, bf16[512,2048]{1,0:T(8,128)(2,1)} %bitcast.154, ...), custom_call_target="tpu_custom_call" | custom-call | bytes 1000000 | tf_op jit(solution)/shard_map/attend_back/pallas_call | solution.py:735
  495.5 5.3 collective-permute-done.59.refs_1_
  504.9 14.6 %attend_back.3 = (bf16[768,2048]{1,0:T(8,128)(2,1)}, bf16[384,512]{1,0:T(8,128)(2,1)}, f32[384,1024]{1,0:T(8,128)}, bf16[384,1024]{1,0:T(8,128)(2,1)}) custom-call(bf16[192,2048]{1,0:T(8,128)(2,1)} %copy-done.23, bf16[96,2048]{1,0:T(8,128)(2,1)} %copy-done.73, bf16[96,2048]{1,0:T(8,128)(2,1)} %copy-done.74, ...), custom_call_target="tpu_custom_call", output_to_operand_aliasing={{0}: (12, {})} | custom-call | bytes 1000000 | tf_op jit(solution)/shard_map/attend_back/pallas_call | solution.py:735
  521.1 4.3 convolution_convert_fusion.3
  532.9 3.7 join_grads.3.refs_0_
  536.6 7.5 convolution_convert_fusion
  549.2 10.4 %input_terms.1 = (bf16[192,2048]{1,0:T(8,128)(2,1)}, bf16[192,2048]{1,0:T(8,128)(2,1)}, bf16[192,2048]{1,0:T(8,128)(2,1)}, bf16[96,2048]{1,0:T(8,128)(2,1)}, bf16[96,2048]{1,0:T(8,128)(2,1)}) custom-call(bf16[768,1536]{1,0:T(8,128)(2,1)} %join_grads.3.refs_0_, bf16[1024,1536]{1,0:T(8,128)(2,1)} %bitcast.158, ...), custom_call_target="tpu_custom_call" | custom-call | bytes 1000000 | tf_op jit(solution)/shard_map/input_terms/pallas_call | solution.py:735
  561.2 3.8 fusion.1
  570.5 4.6 all-to-all-start.1
  581.0 12.2 %collective-permute-done.75 = bf16[96,2048]{1,0:T(8,128)(2,1)S(1)} collective-permute-done((bf16[96,2048]{1,0:T(8,128)(2,1)}, bf16[96,2048]{1,0:T(8,128)(2,1)S(1)}, u32[]{:S(2)}, u32[]{:S(2)}) %collective-permute-start.75) | collective-permute-done | bytes 393248 | tf_op jit(solution)/shard_map/ppermute | solution.py:379
  599.9 18.4 %collective-permute-done.72 = bf16[256,1536]{1,0:T(8,128)(2,1)S(1)} collective-permute-done((bf16[256,1536]{1,0:T(8,128)(2,1)S(1)}, bf16[256,1536]{1,0:T(8,128)(2,1)S(1)}, u32[]{:S(2)}, u32[]{:S(2)}) %collective-permute-start.72) | collective-permute-done | bytes 786464 | tf_op jit(solution)/shard_map/ppermute | solution.py:379
  631.4 38.9 %collective-permute-done.80 = bf16[64,2048]{1,0:T(8,128)(2,1)S(1)} collective-permute-done((bf16[64,2048]{1,0:T(8,128)(2,1)S(1)}, bf16[64,2048]{1,0:T(8,128)(2,1)S(1)}, u32[]{:S(2)}, u32[]{:S(2)}) %collective-permute-start.80) | collective-permute-done | bytes 262176 | tf_op jit(solution)/shard_map/ppermute | solution.py:379
  670.3 4.3 close_input.1
  677.3 10.8 %collective-permute-done.71 = bf16[192,2048]{1,0:T(8,128)(2,1)} collective-permute-done((bf16[192,2048]{1,0:T(8,128)(2,1)}, bf16[192,2048]{1,0:T(8,128)(2,1)}, u32[]{:S(2)}, u32[]{:S(2)}) %collective-permute-start.71) | collective-permute-done | bytes 786464 | tf_op jit(solution)/shard_map/ppermute | solution.py:379
  694.4 8.9 %collective-permute-done.82 = bf16[128,1536]{1,0:T(8,128)(2,1)S(1)} collective-permute-done((bf16[128,1536]{1,0:T(8,128)(2,1)S(1)}, bf16[128,1536]{1,0:T(8,128)(2,1)S(1)}, u32[]{:S(2)}, u32[]{:S(2)}) %collective-permute-start.82) | collective-permute-done | bytes 393248 | tf_op jit(solution)/shard_map/ppermute | solution.py:379
  703.3 4.6 collective-permute-done.84
  712.7 12.6 %finish_columns.3 = (f32[128,8192]{1,0:T(8,128)}, f32[128,8192]{1,0:T(8,128)}, f32[128,512]{1,0:T(8,128)}) custom-call(bf16[2,4,128,2048]{3,2,1,0:T(8,128)(2,1)} %pad_maximum_fusion.1.refs_0_.refs_1_, bf16[2,4,128,2048]{3,2,1,0:T(8,128)(2,1)} %pad_maximum_fusion.1.refs_0_.refs_1_, bf16[128,8192]{1,0:T(8,128)(2,1)} %refs_2_.4, bf16[128,8192]{1,0:T(8,128)(2,1)} %refs_3_.6, ...), custom_call_target="tpu_custom_call" | custom-call | bytes 1000000 | tf_op jit(solution)/shard_map/finish_columns/pallas_call | solution.py:548
  725.9 5.8 collective-permute-done.86
  733.2 10.2 %finish_columns.2 = (f32[128,2048]{1,0:T(8,128)}, f32[128,2048]{1,0:T(8,128)}, f32[128,2048]{1,0:T(8,128)}, f32[128,128]{1,0:T(8,128)}) custom-call(bf16[2,2,128,1536]{3,2,1,0:T(8,128)(2,1)} %pad_maximum_fusion.7.refs_0_.refs_1_.refs_2_, bf16[2,2,128,1536]{3,2,1,0:T(8,128)(2,1)} %pad_maximum_fusion.7.refs_0_.refs_1_.refs_2_, ...), custom_call_target="tpu_custom_call" | custom-call | bytes 1000000 | tf_op jit(solution)/shard_map/finish_columns/pallas_call | solution.py:548
  (477 shorter events, 197.9 us)
Async XLA Ops:
  11.2 33.3 %collective-permute-start.5 = (bf16[192,2048]{1,0:T(8,128)(2,1)}, bf16[192,2048]{1,0:T(8,128)(2,1)S(1)}, u32[]{:S(2)}, u32[]{:S(2)}) collective-permute-start(bf16[192,2048]{1,0:T(8,128)(2,1)} %bitcast.178), channel_id=1, source_target_pairs={{0,1},{1,0},{2,3},{3,2},{4,5},{5,4},{6,7},{7,6},{8,9},{9,8},{10,11... | collective-permute-start | bytes 2359304 | tf_op jit(solution)/shard_map/ppermute | solution.py:379
  44.5 41.3 %collective-permute-start.6 = (bf16[2,128,1536]{2,1,0:T(8,128)(2,1)S(1)}, bf16[2,128,1536]{2,1,0:T(8,128)(2,1)S(1)}, u32[]{:S(2)}, u32[]{:S(2)}) collective-permute-start(bf16[2,128,1536]{2,1,0:T(8,128)(2,1)S(1)} %pad_maximum_fusion.9), channel_id=1, source_target_pairs={{0,2},{2,0},{1,3},{3,1},{4,6},{6,4},{5,7},{7,5},{8,10},{10,8},{9,1... | collective-permute-start | bytes 2359304 | tf_op jit(solution)/shard_map/ppermute | solution.py:379
  44.6 41.2 %collective-permute-start.7 = (bf16[2,128,1536]{2,1,0:T(8,128)(2,1)S(1)}, bf16[2,128,1536]{2,1,0:T(8,128)(2,1)S(1)}, u32[]{:S(2)}, u32[]{:S(2)}) collective-permute-start(bf16[2,128,1536]{2,1,0:T(8,128)(2,1)S(1)} %pad_maximum_fusion.9), channel_id=1, source_target_pairs={{0,1},{1,0},{2,3},{3,2},{4,5},{5,4},{6,7},{7,6},{8,9},{9,8},{10,11... | collective-permute-start | bytes 2359304 | tf_op jit(solution)/shard_map/ppermute | solution.py:379
  46.6 39.1 %collective-permute-start.8 = (bf16[192,2048]{1,0:T(8,128)(2,1)S(1)}, bf16[192,2048]{1,0:T(8,128)(2,1)S(1)}, u32[]{:S(2)}, u32[]{:S(2)}) collective-permute-start(bf16[192,2048]{1,0:T(8,128)(2,1)S(1)} %copy-done.19), channel_id=1, source_target_pairs={{0,8},{8,0},{1,9},{9,1},{2,10},{10,2},{3,11},{11,3},{4,12},{12,4},... | collective-permute-start | bytes 2359304 | tf_op jit(solution)/shard_map/ppermute | solution.py:379
  47.4 38.4 %collective-permute-start.9 = (bf16[192,2048]{1,0:T(8,128)(2,1)S(1)}, bf16[192,2048]{1,0:T(8,128)(2,1)S(1)}, u32[]{:S(2)}, u32[]{:S(2)}) collective-permute-start(bf16[192,2048]{1,0:T(8,128)(2,1)S(1)} %copy-done.19), channel_id=1, source_target_pairs={{0,16},{16,0},{1,17},{17,1},{2,18},{18,2},{3,19},{19,3},{4,20},{20... | collective-permute-start | bytes 2359304 | tf_op jit(solution)/shard_map/ppermute | solution.py:379
  56.3 29.5 %collective-permute-start.10 = (bf16[64,2048]{1,0:T(8,128)(2,1)S(1)}, bf16[64,2048]{1,0:T(8,128)(2,1)S(1)}, u32[]{:S(2)}, u32[]{:S(2)}) collective-permute-start(bf16[64,2048]{1,0:T(8,128)(2,1)S(1)} %copy-done.78), channel_id=1, source_target_pairs={{0,1},{1,0},{2,3},{3,2},{4,5},{5,4},{6,7},{7,6},{8,9},{9,8},{10,11... | collective-permute-start | bytes 786440 | tf_op jit(solution)/shard_map/ppermute | solution.py:379
  85.8 48.6 %collective-permute-start.12 = (bf16[192,2048]{1,0:T(8,128)(2,1)S(1)}, bf16[192,2048]{1,0:T(8,128)(2,1)S(1)}, u32[]{:S(2)}, u32[]{:S(2)}) collective-permute-start(bf16[192,2048]{1,0:T(8,128)(2,1)S(1)} %bitcast.181), channel_id=1, source_target_pairs={{0,8},{8,0},{1,9},{9,1},{2,10},{10,2},{3,11},{11,3},{4,12},{12,4},... | collective-permute-start | bytes 2359304 | tf_op jit(solution)/shard_map/ppermute | solution.py:379
  86.1 48.2 %collective-permute-start.13 = (bf16[192,2048]{1,0:T(8,128)(2,1)S(1)}, bf16[192,2048]{1,0:T(8,128)(2,1)S(1)}, u32[]{:S(2)}, u32[]{:S(2)}) collective-permute-start(bf16[192,2048]{1,0:T(8,128)(2,1)S(1)} %bitcast.182), channel_id=1, source_target_pairs={{0,16},{16,0},{1,17},{17,1},{2,18},{18,2},{3,19},{19,3},{4,20},{20... | collective-permute-start | bytes 2359304 | tf_op jit(solution)/shard_map/ppermute | solution.py:379
  90.6 21.5 %collective-permute-start.14 = (bf16[96,2048]{1,0:T(8,128)(2,1)S(1)}, bf16[96,2048]{1,0:T(8,128)(2,1)S(1)}, u32[]{:S(2)}, u32[]{:S(2)}) collective-permute-start(bf16[96,2048]{1,0:T(8,128)(2,1)S(1)} %slice.114), channel_id=1, source_target_pairs={{0,8},{8,0},{1,9},{9,1},{2,10},{10,2},{3,11},{11,3},{4,12},{12,4},... | collective-permute-start | bytes 1179656 | tf_op jit(solution)/shard_map/ppermute | solution.py:379
  92.7 23.9 %collective-permute-start.11 = (bf16[2,128,1536]{2,1,0:T(8,128)(2,1)S(1)}, bf16[2,128,1536]{2,1,0:T(8,128)(2,1)S(1)}, u32[]{:S(2)}, u32[]{:S(2)}) collective-permute-start(bf16[2,128,1536]{2,1,0:T(8,128)(2,1)S(1)} %collective-permute-done.6), channel_id=1, source_target_pairs={{0,1},{1,0},{2,3},{3,2},{4,5},{5,4},{6,7},{7,6},{8,9},{9,8},{10,11... | collective-permute-start | bytes 2359304 | tf_op jit(solution)/shard_map/ppermute | solution.py:379
  112.1 22.2 %collective-permute-start.16 = (bf16[128,2048]{1,0:T(8,128)(2,1)S(1)}, bf16[128,2048]{1,0:T(8,128)(2,1)S(1)}, u32[]{:S(2)}, u32[]{:S(2)}) collective-permute-start(bf16[128,2048]{1,0:T(8,128)(2,1)S(1)} %slice.116), channel_id=1, source_target_pairs={{0,2},{2,0},{1,3},{3,1},{4,6},{6,4},{5,7},{7,5},{8,10},{10,8},{9,1... | collective-permute-start | bytes 1572872 | tf_op jit(solution)/shard_map/ppermute | solution.py:379
  135.7 23.9 %collective-permute-start.17 = (bf16[1024,1536]{1,0:T(8,128)(2,1)S(1)}, bf16[1024,1536]{1,0:T(8,128)(2,1)}, u32[]{:S(2)}, u32[]{:S(2)}) collective-permute-start(bf16[1024,1536]{1,0:T(8,128)(2,1)S(1)} %bitcast.156), channel_id=1, source_target_pairs={{0,4},{4,0},{1,5},{5,1},{2,6},{6,2},{3,7},{7,3},{8,12},{12,8},{9,1... | collective-permute-start | bytes 9437192 | tf_op jit(solution)/shard_map/ppermute | solution.py:379
  135.7 46.5 %all-to-all-start = ((bf16[4,128,2048]{2,1,0:T(8,128)(2,1)}), bf16[4,128,2048]{2,1,0:T(8,128)(2,1)}, u32[]{:S(2)}, u32[]{:S(2)}) async-start(bf16[4,128,2048]{2,1,0:T(8,128)(2,1)} %column_slices.3), calls=%async_computation | async-start | bytes 4194304 | tf_op jit(solution)/shard_map/all_to_all | solution.py:479
  140.2 147.0 %all-gather.2.cloned.1.call-start = ((), (), s32[]{:S(2)}) async-start(), calls=%async_computation.4 | async-start | bytes 10485760 | tf_op jit(solution)/shard_map/all_gather | solution.py:1037
  151.7 25.9 %collective-permute-start.18 = (bf16[128,2048]{1,0:T(8,128)(2,1)S(1)}, bf16[128,2048]{1,0:T(8,128)(2,1)}, u32[]{:S(2)}, u32[]{:S(2)}) collective-permute-start(bf16[128,2048]{1,0:T(8,128)(2,1)S(1)} %slice.117), channel_id=1, source_target_pairs={{0,2},{2,0},{1,3},{3,1},{4,6},{6,4},{5,7},{7,5},{8,10},{10,8},{9,1... | collective-permute-start | bytes 1572872 | tf_op jit(solution)/shard_map/ppermute | solution.py:379
  152.8 21.5 %collective-permute-start.19 = (bf16[96,2048]{1,0:T(8,128)(2,1)S(1)}, bf16[96,2048]{1,0:T(8,128)(2,1)S(1)}, u32[]{:S(2)}, u32[]{:S(2)}) collective-permute-start(bf16[96,2048]{1,0:T(8,128)(2,1)S(1)} %slice.118), channel_id=1, source_target_pairs={{0,8},{8,0},{1,9},{9,1},{2,10},{10,2},{3,11},{11,3},{4,12},{12,4},... | collective-permute-start | bytes 1179656 | tf_op jit(solution)/shard_map/ppermute | solution.py:379
  156.6 25.6 %collective-permute-start.21 = (bf16[192,2048]{1,0:T(8,128)(2,1)S(1)}, bf16[192,2048]{1,0:T(8,128)(2,1)}, u32[]{:S(2)}, u32[]{:S(2)}) collective-permute-start(bf16[192,2048]{1,0:T(8,128)(2,1)S(1)} %copy-done.61), channel_id=1, source_target_pairs={{0,16},{16,0},{1,17},{17,1},{2,18},{18,2},{3,19},{19,3},{4,20},{20... | collective-permute-start | bytes 2359304 | tf_op jit(solution)/shard_map/ppermute | solution.py:379
  182.3 298.2 %reduce-scatter.3.cloned.1.call-start = ((), (), s32[]{:S(2)}) async-start(), calls=%async_computation.5 | async-start | bytes 3145728 | tf_op jit(solution)/shard_map/reduce_scatter | solution.py:1085
  247.0 26.5 %collective-permute-start.31 = (bf16[192,2048]{1,0:T(8,128)(2,1)}, bf16[192,2048]{1,0:T(8,128)(2,1)S(1)}, u32[]{:S(2)}, u32[]{:S(2)}) collective-permute-start(bf16[192,2048]{1,0:T(8,128)(2,1)} %get-tuple-element.310.refs_0_), channel_id=1, source_target_pairs={{0,8},{8,0},{1,9},{9,1},{2,10},{10,2},{3,11},{11,3},{4,12},{12,4},... | collective-permute-start | bytes 2359304 | tf_op jit(solution)/shard_map/ppermute | solution.py:379
  247.6 26.0 %collective-permute-start.32 = (bf16[192,2048]{1,0:T(8,128)(2,1)}, bf16[192,2048]{1,0:T(8,128)(2,1)S(1)}, u32[]{:S(2)}, u32[]{:S(2)}) collective-permute-start(bf16[192,2048]{1,0:T(8,128)(2,1)} %get-tuple-element.310.refs_0_), channel_id=1, source_target_pairs={{0,16},{16,0},{1,17},{17,1},{2,18},{18,2},{3,19},{19,3},{4,20},{20... | collective-permute-start | bytes 2359304 | tf_op jit(solution)/shard_map/ppermute | solution.py:379
  249.5 23.8 %collective-permute-start.33 = (bf16[96,2048]{1,0:T(8,128)(2,1)S(1)}, bf16[96,2048]{1,0:T(8,128)(2,1)S(1)}, u32[]{:S(2)}, u32[]{:S(2)}) collective-permute-start(bf16[96,2048]{1,0:T(8,128)(2,1)S(1)} %slice.124), channel_id=1, source_target_pairs={{0,8},{8,0},{1,9},{9,1},{2,10},{10,2},{3,11},{11,3},{4,12},{12,4},... | collective-permute-start | bytes 1179656 | tf_op jit(solution)/shard_map/ppermute | solution.py:379
  251.0 22.5 %collective-permute-start.34 = (bf16[96,2048]{1,0:T(8,128)(2,1)S(1)}, bf16[96,2048]{1,0:T(8,128)(2,1)S(1)}, u32[]{:S(2)}, u32[]{:S(2)}) collective-permute-start(bf16[96,2048]{1,0:T(8,128)(2,1)S(1)} %slice.125), channel_id=1, source_target_pairs={{0,16},{16,0},{1,17},{17,1},{2,18},{18,2},{3,19},{19,3},{4,20},{20... | collective-permute-start | bytes 1179656 | tf_op jit(solution)/shard_map/ppermute | solution.py:379
  252.2 52.0 %collective-permute-start.37 = (bf16[192,2048]{1,0:T(8,128)(2,1)}, bf16[192,2048]{1,0:T(8,128)(2,1)S(1)}, u32[]{:S(2)}, u32[]{:S(2)}) collective-permute-start(bf16[192,2048]{1,0:T(8,128)(2,1)} %get-tuple-element.310.refs_0_), channel_id=1, source_target_pairs={{0,1},{1,0},{2,3},{3,2},{4,5},{5,4},{6,7},{7,6},{8,9},{9,8},{10,11... | collective-permute-start | bytes 2359304 | tf_op jit(solution)/shard_map/ppermute | solution.py:379
  274.5 29.9 %collective-permute-start.35 = (bf16[96,2048]{1,0:T(8,128)(2,1)}, bf16[96,2048]{1,0:T(8,128)(2,1)S(1)}, u32[]{:S(2)}, u32[]{:S(2)}) collective-permute-start(bf16[96,2048]{1,0:T(8,128)(2,1)} %slice.126), channel_id=1, source_target_pairs={{0,8},{8,0},{1,9},{9,1},{2,10},{10,2},{3,11},{11,3},{4,12},{12,4},... | collective-permute-start | bytes 1179656 | tf_op jit(solution)/shard_map/ppermute | solution.py:379
  276.7 27.6 %collective-permute-start.36 = (bf16[96,2048]{1,0:T(8,128)(2,1)}, bf16[96,2048]{1,0:T(8,128)(2,1)}, u32[]{:S(2)}, u32[]{:S(2)}) collective-permute-start(bf16[96,2048]{1,0:T(8,128)(2,1)} %slice.127), channel_id=1, source_target_pairs={{0,16},{16,0},{1,17},{17,1},{2,18},{18,2},{3,19},{19,3},{4,20},{20... | collective-permute-start | bytes 1179656 | tf_op jit(solution)/shard_map/ppermute | solution.py:379
  325.3 21.6 %collective-permute-start.40 = (bf16[96,2048]{1,0:T(8,128)(2,1)S(1)}, bf16[96,2048]{1,0:T(8,128)(2,1)S(1)}, u32[]{:S(2)}, u32[]{:S(2)}) collective-permute-start(bf16[96,2048]{1,0:T(8,128)(2,1)S(1)} %slice.128), channel_id=1, source_target_pairs={{0,8},{8,0},{1,9},{9,1},{2,10},{10,2},{3,11},{11,3},{4,12},{12,4},... | collective-permute-start | bytes 1179656 | tf_op jit(solution)/shard_map/ppermute | solution.py:379
  380.1 21.8 %collective-permute-start.50 = (bf16[192,2048]{1,0:T(8,128)(2,1)S(1)}, bf16[192,2048]{1,0:T(8,128)(2,1)S(1)}, u32[]{:S(2)}, u32[]{:S(2)}) collective-permute-start(bf16[192,2048]{1,0:T(8,128)(2,1)S(1)} %pad_maximum_fusion.15), channel_id=1, source_target_pairs={{0,16},{16,0},{1,17},{17,1},{2,18},{18,2},{3,19},{19,3},{4,20},{20... | collective-permute-start | bytes 2359304 | tf_op jit(solution)/shard_map/ppermute | solution.py:379
  406.7 40.7 %collective-permute-start.52 = (bf16[2,4,128,2048]{3,2,1,0:T(8,128)(2,1)}, bf16[2,4,128,2048]{3,2,1,0:T(8,128)(2,1)}, u32[]{:S(2)}, u32[]{:S(2)}) collective-permute-start(bf16[2,4,128,2048]{3,2,1,0:T(8,128)(2,1)} %dynamic-slice_bitcast_fusion), channel_id=1, source_target_pairs={{0,4},{4,0},{1,5},{5,1},{2,6},{6,2},{3,7},{7,3},{8,12},{12,8},{9,1... | collective-permute-start | bytes 12582920 | tf_op jit(solution)/shard_map/ppermute | solution.py:379
  406.8 163.0 %reduce-scatter.5.cloned.1.call-start = ((), (), s32[]{:S(2)}) async-start(), calls=%async_computation.6 | async-start | bytes 6291456 | tf_op jit(solution)/shard_map/reduce_scatter | solution.py:1094
  408.3 33.0 %collective-permute-start.51 = (bf16[192,2048]{1,0:T(8,128)(2,1)S(1)}, bf16[192,2048]{1,0:T(8,128)(2,1)S(1)}, u32[]{:S(2)}, u32[]{:S(2)}) collective-permute-start(bf16[192,2048]{1,0:T(8,128)(2,1)S(1)} %add_convert_fusion.2), channel_id=1, source_target_pairs={{0,1},{1,0},{2,3},{3,2},{4,5},{5,4},{6,7},{7,6},{8,9},{9,8},{10,11... | collective-permute-start | bytes 2359304 | tf_op jit(solution)/shard_map/ppermute | solution.py:379
  408.4 47.0 %collective-permute-start.53 = (bf16[96,2048]{1,0:T(8,128)(2,1)}, bf16[96,2048]{1,0:T(8,128)(2,1)S(1)}, u32[]{:S(2)}, u32[]{:S(2)}) collective-permute-start(bf16[96,2048]{1,0:T(8,128)(2,1)} %get-tuple-element.388), channel_id=1, source_target_pairs={{0,8},{8,0},{1,9},{9,1},{2,10},{10,2},{3,11},{11,3},{4,12},{12,4},... | collective-permute-start | bytes 1179656 | tf_op jit(solution)/shard_map/ppermute | solution.py:379
  409.0 46.3 %collective-permute-start.54 = (bf16[96,2048]{1,0:T(8,128)(2,1)}, bf16[96,2048]{1,0:T(8,128)(2,1)S(1)}, u32[]{:S(2)}, u32[]{:S(2)}) collective-permute-start(bf16[96,2048]{1,0:T(8,128)(2,1)} %get-tuple-element.389), channel_id=1, source_target_pairs={{0,16},{16,0},{1,17},{17,1},{2,18},{18,2},{3,19},{19,3},{4,20},{20... | collective-permute-start | bytes 1179656 | tf_op jit(solution)/shard_map/ppermute | solution.py:379
  475.1 44.4 %collective-permute-start.58 = (bf16[192,2048]{1,0:T(8,128)(2,1)S(1)}, bf16[192,2048]{1,0:T(8,128)(2,1)}, u32[]{:S(2)}, u32[]{:S(2)}) collective-permute-start(bf16[192,2048]{1,0:T(8,128)(2,1)S(1)} %pad_maximum_fusion.17), channel_id=1, source_target_pairs={{0,16},{16,0},{1,17},{17,1},{2,18},{18,2},{3,19},{19,3},{4,20},{20... | collective-permute-start | bytes 2359304 | tf_op jit(solution)/shard_map/ppermute | solution.py:379
  475.7 43.8 %collective-permute-start.57 = (bf16[192,2048]{1,0:T(8,128)(2,1)S(1)}, bf16[192,2048]{1,0:T(8,128)(2,1)}, u32[]{:S(2)}, u32[]{:S(2)}) collective-permute-start(bf16[192,2048]{1,0:T(8,128)(2,1)S(1)} %pad_maximum_fusion.16), channel_id=1, source_target_pairs={{0,8},{8,0},{1,9},{9,1},{2,10},{10,2},{3,11},{11,3},{4,12},{12,4},... | collective-permute-start | bytes 2359304 | tf_op jit(solution)/shard_map/ppermute | solution.py:379
  477.0 23.8 %collective-permute-start.59 = (bf16[96,2048]{1,0:T(8,128)(2,1)S(1)}, bf16[96,2048]{1,0:T(8,128)(2,1)S(1)}, u32[]{:S(2)}, u32[]{:S(2)}) collective-permute-start(bf16[96,2048]{1,0:T(8,128)(2,1)S(1)} %slice.142), channel_id=1, source_target_pairs={{0,8},{8,0},{1,9},{9,1},{2,10},{10,2},{3,11},{11,3},{4,12},{12,4},... | collective-permute-start | bytes 1179656 | tf_op jit(solution)/shard_map/ppermute | solution.py:379
  478.7 25.4 %collective-permute-start.60 = (bf16[96,2048]{1,0:T(8,128)(2,1)}, bf16[96,2048]{1,0:T(8,128)(2,1)S(1)}, u32[]{:S(2)}, u32[]{:S(2)}) collective-permute-start(bf16[96,2048]{1,0:T(8,128)(2,1)} %slice.143), channel_id=1, source_target_pairs={{0,16},{16,0},{1,17},{17,1},{2,18},{18,2},{3,19},{19,3},{4,20},{20... | collective-permute-start | bytes 1179656 | tf_op jit(solution)/shard_map/ppermute | solution.py:379
  480.4 49.3 %collective-permute-start.65 = (bf16[256,2048]{1,0:T(8,128)(2,1)}, bf16[256,2048]{1,0:T(8,128)(2,1)S(1)}, u32[]{:S(2)}, u32[]{:S(2)}) collective-permute-start(bf16[256,2048]{1,0:T(8,128)(2,1)} %bitcast.176), channel_id=1, source_target_pairs={{0,16},{16,0},{1,17},{17,1},{2,18},{18,2},{3,19},{19,3},{4,20},{20... | collective-permute-start | bytes 3145736 | tf_op jit(solution)/shard_map/ppermute | solution.py:379
  504.1 21.3 %collective-permute-start.61 = (bf16[384,1024]{1,0:T(8,128)(2,1)}, bf16[384,1024]{1,0:T(8,128)(2,1)S(1)}, u32[]{:S(2)}, u32[]{:S(2)}) collective-permute-start(bf16[384,1024]{1,0:T(8,128)(2,1)} %get-tuple-element.415), channel_id=1, source_target_pairs={{0,4},{4,0},{1,5},{5,1},{2,6},{6,2},{3,7},{7,3},{8,12},{12,8},{9,1... | collective-permute-start | bytes 2359304 | tf_op jit(solution)/shard_map/ppermute | solution.py:379
  569.8 23.4 %collective-permute-start.75 = (bf16[96,2048]{1,0:T(8,128)(2,1)}, bf16[96,2048]{1,0:T(8,128)(2,1)S(1)}, u32[]{:S(2)}, u32[]{:S(2)}) collective-permute-start(bf16[96,2048]{1,0:T(8,128)(2,1)} %get-tuple-element.446), channel_id=1, source_target_pairs={{0,8},{8,0},{1,9},{9,1},{2,10},{10,2},{3,11},{11,3},{4,12},{12,4},... | collective-permute-start | bytes 1179656 | tf_op jit(solution)/shard_map/ppermute | solution.py:379
  570.5 49.8 %all-to-all-start.1 = ((bf16[4,128,2048]{2,1,0:T(8,128)(2,1)}), bf16[4,128,2048]{2,1,0:T(8,128)(2,1)}, u32[]{:S(2)}, u32[]{:S(2)}) async-start(bf16[4,128,2048]{2,1,0:T(8,128)(2,1)} %bitcast.183), calls=%async_computation.3 | async-start | bytes 4194304 | tf_op jit(solution)/shard_map/all_to_all | solution.py:479
  579.0 39.2 %collective-permute-start.72 = (bf16[256,1536]{1,0:T(8,128)(2,1)S(1)}, bf16[256,1536]{1,0:T(8,128)(2,1)S(1)}, u32[]{:S(2)}, u32[]{:S(2)}) collective-permute-start(bf16[256,1536]{1,0:T(8,128)(2,1)S(1)} %get-tuple-element.476), channel_id=1, source_target_pairs={{0,1},{1,0},{2,3},{3,2},{4,5},{5,4},{6,7},{7,6},{8,9},{9,8},{10,11... | collective-permute-start | bytes 2359304 | tf_op jit(solution)/shard_map/ppermute | solution.py:379
  593.4 24.8 %collective-permute-start.76 = (bf16[192,2048]{1,0:T(8,128)(2,1)S(1)}, bf16[192,2048]{1,0:T(8,128)(2,1)S(1)}, u32[]{:S(2)}, u32[]{:S(2)}) collective-permute-start(bf16[192,2048]{1,0:T(8,128)(2,1)S(1)} %pad_maximum_fusion.21), channel_id=1, source_target_pairs={{0,16},{16,0},{1,17},{17,1},{2,18},{18,2},{3,19},{19,3},{4,20},{20... | collective-permute-start | bytes 2359304 | tf_op jit(solution)/shard_map/ppermute | solution.py:379
  594.8 25.5 %collective-permute-start.74 = (bf16[192,2048]{1,0:T(8,128)(2,1)S(1)}, bf16[192,2048]{1,0:T(8,128)(2,1)}, u32[]{:S(2)}, u32[]{:S(2)}) collective-permute-start(bf16[192,2048]{1,0:T(8,128)(2,1)S(1)} %pad_maximum_fusion.20), channel_id=1, source_target_pairs={{0,8},{8,0},{1,9},{9,1},{2,10},{10,2},{3,11},{11,3},{4,12},{12,4},... | collective-permute-start | bytes 2359304 | tf_op jit(solution)/shard_map/ppermute | solution.py:379
  598.4 76.3 %collective-permute-start.79 = (bf16[256,1536]{1,0:T(8,128)(2,1)}, bf16[256,1536]{1,0:T(8,128)(2,1)}, u32[]{:S(2)}, u32[]{:S(2)}) collective-permute-start(bf16[256,1536]{1,0:T(8,128)(2,1)} %get-tuple-element.475), channel_id=1, source_target_pairs={{0,1},{1,0},{2,3},{3,2},{4,5},{5,4},{6,7},{7,6},{8,9},{9,8},{10,11... | collective-permute-start | bytes 2359304 | tf_op jit(solution)/shard_map/ppermute | solution.py:379
  622.7 52.0 %collective-permute-start.78 = (bf16[256,1536]{1,0:T(8,128)(2,1)}, bf16[256,1536]{1,0:T(8,128)(2,1)}, u32[]{:S(2)}, u32[]{:S(2)}) collective-permute-start(bf16[256,1536]{1,0:T(8,128)(2,1)} %fusion.4), channel_id=1, source_target_pairs={{0,2},{2,0},{1,3},{3,1},{4,6},{6,4},{5,7},{7,5},{8,10},{10,8},{9,1... | collective-permute-start | bytes 2359304 | tf_op jit(solution)/shard_map/ppermute | solution.py:379
  623.7 46.6 %collective-permute-start.80 = (bf16[64,2048]{1,0:T(8,128)(2,1)S(1)}, bf16[64,2048]{1,0:T(8,128)(2,1)S(1)}, u32[]{:S(2)}, u32[]{:S(2)}) collective-permute-start(bf16[64,2048]{1,0:T(8,128)(2,1)S(1)} %fusion.10), channel_id=1, source_target_pairs={{0,2},{2,0},{1,3},{3,1},{4,6},{6,4},{5,7},{7,5},{8,10},{10,8},{9,1... | collective-permute-start | bytes 786440 | tf_op jit(solution)/shard_map/ppermute | solution.py:379
  627.4 47.3 %collective-permute-start.81 = (bf16[64,2048]{1,0:T(8,128)(2,1)}, bf16[64,2048]{1,0:T(8,128)(2,1)}, u32[]{:S(2)}, u32[]{:S(2)}) collective-permute-start(bf16[64,2048]{1,0:T(8,128)(2,1)} %dynamic-slice_bitcast_fusion.8), channel_id=1, source_target_pairs={{0,1},{1,0},{2,3},{3,2},{4,5},{5,4},{6,7},{7,6},{8,9},{9,8},{10,11... | collective-permute-start | bytes 786440 | tf_op jit(solution)/shard_map/ppermute | solution.py:379
  629.2 78.7 %collective-permute-start.85 = (bf16[4,128,2048]{2,1,0:T(8,128)(2,1)}, bf16[4,128,2048]{2,1,0:T(8,128)(2,1)}, u32[]{:S(2)}, u32[]{:S(2)}) collective-permute-start(bf16[4,128,2048]{2,1,0:T(8,128)(2,1)} %all-to-all-done.1), channel_id=1, source_target_pairs={{0,16},{16,0},{1,17},{17,1},{2,18},{18,2},{3,19},{19,3},{4,20},{20... | collective-permute-start | bytes 6291464 | tf_op jit(solution)/shard_map/ppermute | solution.py:379
  (133 other events, 1456.4 us)
Sparse Core Ops, SparseCore 0:
  182.4 104.7 all-gather.1
  406.9 52.6 reduce-scatter.2
  462.5 99.1 reduce-scatter.4

commit v4 on v3

--- a/solution.py
+++ b/solution.py
@@ -515,12 +515,16 @@
     return jnp.concatenate([jnp.where(first, kept, received), jnp.where(first, received, kept)]).astype(F32)
 
 
-def finish_kernel(count, *refs):
-    grads, weights, gain, outs = refs[:count], refs[count : 2 * count], refs[2 * count], refs[2 * count + 1 :]
+def finish_kernel(count, seq_ref, *refs):
+    near, far, weights = refs[:count], refs[count : 2 * count], refs[2 * count : 3 * count]
+    gain, outs = refs[3 * count], refs[3 * count + 1 :]
     j = pl.program_id(0)
+    use_near = (j // 2) % 2 == seq_ref[0]
     total = None
     for i in range(count):
-        grad = grads[i][0, 0].astype(F32)
+        grad = jnp.where(use_near, near[i][...], far[i][...]).astype(F32)
+        pieces = [grad[k, 0] for k in range(2)] if grad.ndim == 4 else [grad[0]]
+        grad = jnp.concatenate(pieces, axis=1)
         outs[i][...] = grad * gain[...]
         term = grad * weights[i][...].astype(F32)
         total = term if total is None else total + term
@@ -532,31 +536,32 @@
     outs[count][...] += total
 
 
-def finish_columns(pieces, weights, gain, width, joined):
+def finish_columns(place, near, far, weights, gain, width, joined):
     count, rows = len(weights), weights[0].shape[0]
 
     def piece_spec(w):
-        def index(j):
-            x, seq, zh, zl = j // 8, (j // 4) % 2, (j // 2) % 2, j % 2
-            if joined:
-                return seq, zl * 2 + x, 0, slot(count, 2, joined, w, zh)
-            return seq, x, 0, slot(count, 4, joined, w, zh * 2 + zl)
-
-        return pl.BlockSpec((1, 1, rows, width), index)
-
-    column_spec = pl.BlockSpec((rows, width), lambda j: (0, j))
+        def index(j, seq):
+            x, zh = j // 4, j % 2
+            return (0, x, 0, slot(count, 2, joined, w, zh)) if joined else (x, 0, w * 2 + zh)
+
+        return pl.BlockSpec((2, 1, rows, width) if joined else (1, rows, 2 * width), index)
+
+    column_spec = pl.BlockSpec((rows, 2 * width), lambda j, seq: (0, j))
+    pieces = [piece_spec(w) for w in range(count)]
     outs = pl.pallas_call(
         functools.partial(finish_kernel, count),
-        grid=(16,),
-        in_specs=[piece_spec(w) for w in range(count)]
-        + [column_spec] * count
-        + [pl.BlockSpec((rows, 1), lambda j: (0, 0))],
-        out_specs=[column_spec] * count + [pl.BlockSpec((rows, width), lambda j: (0, 0))],
-        out_shape=[jax.ShapeDtypeStruct((rows, 16 * width), F32)] * count + [jax.ShapeDtypeStruct((rows, width), F32)],
+        grid_spec=pltpu.PrefetchScalarGridSpec(
+            num_scalar_prefetch=1,
+            grid=(8,),
+            in_specs=pieces * 2 + [column_spec] * count + [pl.BlockSpec((rows, 1), lambda j, seq: (0, 0))],
+            out_specs=[column_spec] * count + [pl.BlockSpec((rows, 2 * width), lambda j, seq: (0, 0))],
+        ),
+        out_shape=[jax.ShapeDtypeStruct((rows, 16 * width), F32)] * count
+        + [jax.ShapeDtypeStruct((rows, 2 * width), F32)],
         compiler_params=BIG,
         cost_estimate=pl.CostEstimate(flops=0, bytes_accessed=1_000_000, transcendentals=0),
         name="finish_columns",
-    )(*[pieces] * count, *weights, gain)
+    )(jnp.stack([place.seq]).astype(jnp.int32), *[near] * count, *[far] * count, *weights, gain)
     return outs[:count], jnp.sum(outs[count], axis=1)
 
 
@@ -959,29 +964,32 @@
     attn_gain = attention_gain.astype(F32)[:, None]
     ff_gain = feedforward_gain.astype(F32)[:, None]
 
+    documents = document_ids[0]
+    first = jnp.sum((documents[None, :] < documents[:, None]).astype(jnp.int32), axis=1)
     mine, sent = head_slices(place, [query_weight, key_weight, value_weight], attn_gain, rows)
     out_half = chip_half(place, output_weight)
-    (a_own,) = on_rows(open_kernel, "open_layer", [x_own], [BF16])
     dy_l = swap(dy_own, "zl")
-    mine, sent, out_half, a_own, down_late, gate_late, up_late = fence(
-        [mine, sent, out_half, a_own, down_weight, gate_weight, up_weight], []
-    )
+    first = jnp.stack([first, swap(first, "seq")])
+    mine, sent, out_half, x_late, down_late, gate_late, up_late = fence(
+        [mine, sent, out_half, x_own, down_weight, gate_weight, up_weight], []
+    )
+    (a_own,) = on_rows(open_kernel, "open_layer", [x_late], [BF16])
 
     received = swap(sent, "x")
     out_zh, out_zl = swap(out_half, "zh"), swap(out_half, "zl")
     qkv = in_order(mine, received, place.x)
     down_half = chip_half(place, down_late)
-    quarter = down_half.shape[0] // 2
-    qkv, a_late, out_zh, out_zl, dy_late, down_half, dy_l = fence(
-        [qkv, a_own, out_zh, out_zl, dy_own, down_half, dy_l], []
+    quarter = down_half.shape[0] * 3 // 4
+    qkv, a_own, out_zh, out_zl, dy_late, down_half, dy_l, first = fence(
+        [qkv, a_own, out_zh, out_zl, dy_own, down_half, dy_l, first], []
     )
 
     gate_up = hidden_slices(place, [gate_late, up_late], ff_gain, hidden_rows)
     by_zh, by_zl = swap(qkv, "zh"), swap(qkv, "zl")
-    a_x, a_s = along(a_late)
+    a_x, a_s = along(a_own)
     out_both = swap(out_zh, "zl")
-    by_zh, by_zl, a_x, a_s, dy_late, out_both, gate_up, document_ids, down_half = fence(
-        [by_zh, by_zl, a_x, a_s, dy_late, out_both, gate_up, document_ids, down_half], []
+    by_zh, by_zl, a_x, a_s, dy_late, out_both, gate_up, down_half = fence(
+        [by_zh, by_zl, a_x, a_s, dy_late, out_both, gate_up, down_half], []
     )
 
     by_both = swap(by_zh, "zl")
@@ -990,11 +998,7 @@
     out_half = in_order(
         in_order(out_half, out_zl, place.zl), in_order(out_zh, out_both, place.zl), place.zh
     ).reshape(4, -1, model)
-    documents = document_ids[0]
-    first = jnp.sum((documents[None, :] < documents[:, None]).astype(jnp.int32), axis=1)
     qkv = in_order(in_order(qkv, by_zl, place.zl), in_order(by_zh, by_both, place.zl), place.zh)
-    first = jnp.stack([first, swap(first, "seq")])
-    down_far = [swap(down_half[:quarter], "zh")]
     a_all = jnp.concatenate([a_own, a_x, a_s, *a_o], axis=0)
 
     def positions(dx, dc):
@@ -1015,49 +1019,51 @@
     start = jnp.concatenate(starts, axis=1)[:, :, None]
     where = (qpos[:, None], start, kpos[None, :])
     tables = (cosine, sine)
-    qkv, dy_x, dy_s, dy_l, tables, a_all, down_half, out_half, down_far, gate_up = fence(
-        [qkv, dy_x, dy_s, dy_l, tables, a_all, down_half, out_half, down_far, gate_up], []
+    qkv, dy_l, tables, a_all, down_half, out_half, gate_up = fence(
+        [qkv, dy_l, tables, a_all, down_half, out_half, gate_up], []
     )
 
     qkv = qkv.reshape(model // 2, -1)
     qkv_other = swap(qkv, "core")
     gate_up = share_columns(gate_up)
-    dy_ls = swap(dy_l, "seq")
-    dy_o = opposite(dy_x, dy_s)
+    down_far = [swap(down_half[:quarter], "zh")]
     out_rows = chip_rows(place, out_half, swap(out_half, "core"))
     core = jnp.stack([place.core]).astype(jnp.int32)
+    qkv, qkv_other, core, dy_l, down_half, down_far = fence(
+        [qkv, qkv_other, core, dy_l, down_half, down_far], []
+    )
+
+    q_all, kv_all = project(core, a_all, qkv, qkv_other, *tables)
     down_far += [swap(down_half[quarter:], "zh")]
-    qkv, qkv_other, core, dy_l = fence([qkv, qkv_other, core, dy_l], [])
-
-    q_all, kv_all = project(core, a_all, qkv, qkv_other, *tables)
-    q_all, kv_all, down_half, down_far, dy_o, dy_ls, dy_l, where, gate_up = fence(
-        [q_all, kv_all, down_half, down_far, dy_o, dy_ls, dy_l, where, gate_up], [out_rows]
+    q_all, kv_all, down_half, down_far, dy_x, dy_s, dy_l, where, gate_up = fence(
+        [q_all, kv_all, down_half, down_far, dy_x, dy_s, dy_l, where, gate_up], [out_rows]
     )
 
     gate_up = lax.all_gather(gate_up, ("core", "zh"), axis=0, tiled=True).reshape(model, -1)
-    dy_lx = swap(dy_l, "x")
+    dy_o = opposite(dy_x, dy_s)
     kv_other = swap(kv_all, "core")
     o_all, term_s, *term_o = attend(1, q_all, kv_all, kv_other, out_rows, where, None)
     down_half = in_order(down_half, jnp.concatenate(down_far), place.zh)
     down_rows = chip_rows(place, down_half, swap(down_half, "core"))
-    term_s, term_o, o_all, down_rows, dy_lx = fence([term_s, term_o, o_all, down_rows, dy_lx], [])
+    term_s, term_o, o_all, down_rows, dy_l = fence([term_s, term_o, o_all, down_rows, dy_l], dy_o)
 
     o_all, own, term_x = attend(0, q_all, kv_all, kv_other, out_rows, where, o_all)
     halves = return_halves(*term_o)
-    own, term_x, halves, dy_lx, dy_ls = fence([own, term_x, halves, dy_lx, dy_ls], [])
+    own, term_x, halves, dy_l = fence([own, term_x, halves, dy_l], [])
 
     sums = return_along(term_x, term_s, *halves)
     hidden, b_own = on_rows(close_attention_kernel, "close_attention", [x_own, own, *sums], [F32, BF16])
-    b_own, dy_lx, dy_ls = fence([b_own, dy_lx, dy_ls], [])
+    b_own, dy_l = fence([b_own, dy_l], [])
 
     b_x, b_s = along(b_own)
     b_l = swap(b_own, "zl")
-    dy_lo = opposite(dy_lx, dy_ls)
-    b_x, b_s = fence([b_x, b_s], dy_lo)
+    dy_lx, dy_ls = along(dy_l)
+    b_x, b_s, dy_lx, dy_ls = fence([b_x, b_s, dy_lx, dy_ls], [])
 
     b_o = opposite(b_x, b_s)
     buffers, db0, y0 = hidden_units(0, [b_own, b_x], [dy_own, dy_x], gate_up, down_rows, [None] * 4)
-    buffers, b_o, b_l = fence([buffers, b_o, b_l], [])
+    dy_lo = opposite(dy_lx, dy_ls)
+    buffers, b_o, b_l = fence([buffers, b_o, b_l], dy_lo)
 
     b_lx, b_ls = along(b_l)
     buffers, db1, y1 = hidden_units(1, [b_s, *b_o], [dy_s, *dy_o], gate_up, down_rows, buffers)
@@ -1080,26 +1086,27 @@
     far_along = return_along(db2[1], db3[0], *far_halves)
     gate_up_terms = dot_low(b_all, d_all, 0, 0)
     down_sums = add_core(place, down_terms.reshape(2, 2, -1, model), 1)
-    gate_up_terms, down_sums, y1, near0, far_along = fence([gate_up_terms, down_sums, y1, db0[0], far_along], [])
+    gate_up_terms, down_sums, y0, y1, near0, far_along = fence(
+        [gate_up_terms, down_sums, y0, y1, db0[0], far_along], []
+    )
 
     down_total = lax.psum_scatter(down_sums, "zh", scatter_dimension=0, tiled=True)[0]
     across = return_across(db2[0], *far_along)
-    near_y_halves = return_halves(*y1[1:])
+    near_y_along = return_along(y0[1], y1[0], *return_halves(*y1[1:]))
     gate_up_sums = add_core(place, gate_up_terms.reshape(2, 2, 4, rows, -1), 0)
     dh, dh_low = on_rows(
         close_hidden_kernel, "close_hidden", [dy_own, hidden, near0, *near_along, across], [F32, BF16]
     )
-    dh_low, gate_up_sums, near_y_halves = fence([dh_low, gate_up_sums, near_y_halves], [])
+    dh_low, gate_up_sums, near_y_along = fence([dh_low, gate_up_sums, near_y_along], [])
 
     gate_up_near = lax.psum_scatter(gate_up_sums, "zh", scatter_dimension=0, tiled=True)[0]
     dh_x, dh_s = along(dh_low)
-    dh_x, dh_s, y0, y1, y3 = fence([dh_x, dh_s, y0, y1, y3], [])
+    dh_x, dh_s, y3 = fence([dh_x, dh_s, y3], [])
 
     dh_o = opposite(dh_x, dh_s)
     dh_all, dq0, dkv0, dkv_other0 = attend_back(
         0, [dh_low, dh_x], out_rows, q_all, kv_all, kv_other, where, tables, None
     )
-    near_y_along = return_along(y0[1], y1[0], *near_y_halves)
     dkv_other0, dh_s, y3 = fence([dkv_other0, dh_s, y3], dh_o)
 
     dkv_other0 = swap(dkv_other0, "core")
@@ -1108,7 +1115,7 @@
         1, [dh_s, *dh_o], out_rows, q_all, kv_all, kv_other, where, tables, dh_all
     )
     far_y_halves = return_halves(*y3[1:])
-    dkv_other1, dh_all = fence([dkv_other1, dh_all], near_y_along)
+    dkv_other1, dh_all = fence([dkv_other1, dh_all], [])
 
     dkv_other1 = swap(dkv_other1, "core")
     d_qkv = join_grads(0, dq0, dkv0, dkv_other0, tables, None)
@@ -1136,38 +1143,39 @@
     qkv_zl = swap(part(qkv_sums, 1, 1), "zl")
     gate_up_near = share_columns(gate_up_near)
     sums = return_along(term_x, term_s, *return_halves(*term_o))
-    out_zh = swap(add_low(part(out_sums, 1, 0), out_zl).astype(BF16), "zh")
-    out_zl = swap(part(out_sums, 0, 1), "zl")
     down_grad = own_rows(place, down_total, down_other)
-    qkv_zl, gate_up_near, sums = fence([qkv_zl, gate_up_near, sums], [down_grad])
+    qkv_zl, gate_up_near, sums, out_zl = fence([qkv_zl, gate_up_near, sums, out_zl], [down_grad])
 
     qkv_zh = swap(add_low(part(qkv_sums, 1, 0), qkv_zl).astype(BF16), "zh")
     qkv_zl = swap(part(qkv_sums, 0, 1), "zl")
     gate_up_far = swap(gate_up_near, "seq")
     (input_grad,) = on_rows(close_input_kernel, "close_input", [x_own, dh, own, *sums], [BF16])
-    qkv_zh, qkv_zl, out_zh, out_zl = fence([qkv_zh, qkv_zl, out_zh, out_zl], [input_grad])
+    qkv_zh, qkv_zl, out_zl, out_sums = fence([qkv_zh, qkv_zl, out_zl, out_sums], [input_grad])
 
     qkv_total = add_low(part(qkv_sums, 0, 0), qkv_zl, qkv_zh).astype(BF16).reshape(2, rows, -1)
     kept = lax.dynamic_index_in_dim(qkv_total, place.x, 0, False)
     received = swap(lax.dynamic_index_in_dim(qkv_total, 1 - place.x, 0, False), "x")
     kept_far, received_far = swap(kept, "seq"), swap(received, "seq")
+    out_zh = swap(add_low(part(out_sums, 1, 0), out_zl).astype(BF16), "zh")
+    out_zl = swap(part(out_sums, 0, 1), "zl")
+    (gate_grad, up_grad), ff_gain_grad = finish_columns(
+        place, *[v.reshape(2, 2, rows, -1) for v in (gate_up_near, gate_up_far)], [gate_weight, up_weight], ff_gain,
+        hidden_rows, True,
+    )
+    kept, kept_far, received, received_far, out_zh, out_zl, far_y_along = fence(
+        [kept, kept_far, received, received_far, out_zh, out_zl, far_y_along], [ff_gain_grad]
+    )
+
     y_across = return_across(y2[0], *far_y_along)
     out_total = add_low(part(out_sums, 0, 0), out_zl, out_zh).astype(BF16)
-    kept, kept_far, received, received_far, gate_up_far, out_total = fence(
-        [kept, kept_far, received, received_far, gate_up_far, out_total], []
-    )
-
     out_other = swap(out_total, "seq")
     output_grad = own_rows(place, out_total, out_other)
 
+    (query_grad, key_grad, value_grad), attn_gain_grad = finish_columns(
+        place, in_order(kept, received, place.x), in_order(kept_far, received_far, place.x),
+        [query_weight, key_weight, value_weight], attn_gain, rows, False,
+    )
     layer_output = add_low(hidden, y0[0], *near_y_along, y_across).astype(BF16)
-    pieces = in_order(in_order(kept, received, place.x), in_order(kept_far, received_far, place.x), place.seq)
-    (query_grad, key_grad, value_grad), attn_gain_grad = finish_columns(
-        pieces, [query_weight, key_weight, value_weight], attn_gain, rows, False
-    )
-    (gate_grad, up_grad), ff_gain_grad = finish_columns(
-        in_order(gate_up_near, gate_up_far, place.seq), [gate_weight, up_weight], ff_gain, hidden_rows, True
-    )
     return (
         layer_output[None], input_grad[None], attn_gain_grad, query_grad, key_grad, value_grad, output_grad,
         ff_gain_grad, gate_grad, up_grad, down_grad,

time: 763 us -> 719 us (0.942)
  waiting for transfers between devices: 307 us -> 255 us
  other arithmetic: 57.7 us -> 66.1 us
    ppermute x86, waiting for transfers between devices: 297 us -> 255 us  [swap(): return lax.ppermute(value, axis, [(0, 1), (1, 0)])]
    all_gather x1, waiting for transfers between devices: 9.61 us -> 0.01 us  [paired_device(): lax.all_gather(gate_up, ('core', 'zh'), axis=0, tiled=True)]
    unnamed x181 -> x175, local copies, waits for them, and re-layouts: 20.5 us -> 20.9 us
  transfers between devices with their start and end apart: 93 -> 93, of which waited for: 36 -> 31; matrix products, arithmetic and copies ran while one was open for 15% -> 18% of each run, Pallas kernels for 24% -> 26%
where the time goes in v4:
time: 719 us; the launch traced here: 710 us
  waiting for transfers between devices  255 us (35%)
  Pallas kernels  185 us (26%)
  starting transfers between devices  98.5 us (14%)
  other arithmetic  66.1 us (9%)
  local copies, waits for them, and re-layouts  52 us (7%)
  matrix products  37.5 us (5%)
  between operations  15.4 us (2%)
    ppermute x86, waiting for transfers between devices, swap(): return lax.ppermute(value, axis, [(0, 1), (1, 0)])  255 us
    pallas_call x11, Pallas kernels, into(): pl.pallas_call(body, grid=grid, in_specs=in_specs + [pl.BlockSpec(memory_...  134 us
    ppermute x86, starting transfers between devices, swap(): return lax.ppermute(value, axis, [(0, 1), (1, 0)])  84.3 us
    dot_general x4, matrix products, dot_low(): lax.dot_general(left, right, (((left_dim,), (right_dim,)), ((), ())), pre...  37.5 us
    unnamed x175, local copies, waits for them, and re-layouts  20.9 us
    pallas_call x2, Pallas kernels, finish_columns(): pl.pallas_call(functools.partial(finish_kernel, count), grid_spec=pltpu.P...  17.4 us
    pallas_call x4, Pallas kernels, on_rows(): pl.pallas_call(kernel, grid=(3,), in_specs=[tile] * len(operands), out_sp...  16.8 us
    convert_element_type x4, other arithmetic, add_core(): add_low(lax.dynamic_index_in_dim(parts, place.core, axis, False), received)  14.8 us
  transfers between devices with their start and end apart: 93, of which 31 were waited for; matrix products, arithmetic and copies ran while one was open for 18% of the time, Pallas kernels for 26%

profile of v4, /device:TPU:0, one launch (start us, length us, event | category | flops | bytes accessed | tf_op | source)
XLA Modules:
  0.0 709.9 jit_solution(14610467873929736431)
XLA Ops:
  17.2 3.2 column_slices.2
  28.2 3.2 collective-permute-start.4
  44.2 4.8 collective-permute-done.2
  54.2 4.2 column_slices.3
  60.3 30.8 %collective-permute-done.11 = bf16[64,2048]{1,0:T(8,128)(2,1)S(1)} collective-permute-done((bf16[64,2048]{1,0:T(8,128)(2,1)S(1)}, bf16[64,2048]{1,0:T(8,128)(2,1)S(1)}, u32[]{:S(2)}, u32[]{:S(2)}) %collective-permute-start.11) | collective-permute-done | bytes 262176 | tf_op jit(solution)/shard_map/ppermute | solution.py:379
  91.8 3.1 collective-permute-start.14
  104.4 9.3 %collective-permute-done.12 = bf16[2,128,1536]{2,1,0:T(8,128)(2,1)S(1)} collective-permute-done((bf16[2,128,1536]{2,1,0:T(8,128)(2,1)S(1)}, bf16[2,128,1536]{2,1,0:T(8,128)(2,1)S(1)}, u32[]{:S(2)}, u32[]{:S(2)}) %collective-permute-start.12) | collective-permute-done | bytes 786464 | tf_op jit(solution)/shard_map/ppermute | solution.py:379
  116.0 4.5 all-to-all-start
  128.7 30.8 %collective-permute-done.16 = bf16[192,2048]{1,0:T(8,128)(2,1)} collective-permute-done((bf16[192,2048]{1,0:T(8,128)(2,1)}, bf16[192,2048]{1,0:T(8,128)(2,1)}, u32[]{:S(2)}, u32[]{:S(2)}) %collective-permute-start.16) | collective-permute-done | bytes 786464 | tf_op jit(solution)/shard_map/ppermute | solution.py:379
  160.5 3.4 collective-permute-start.17
  165.4 9.5 %project.1 = (bf16[768,512]{1,0:T(8,128)(2,1)}, bf16[768,1024]{1,0:T(8,128)(2,1)}) custom-call(s32[1]{0:T(128)} %bitcast.20.core_ref.refs_3_, bf16[768,2048]{1,0:T(8,128)(2,1)} %constant_dynamic-update-slice_fusion.a_ref.a2_ref, bf16[768,2048]{1,0:T(8,128)(2,1)} %constant_dynamic-update-slice_fusion.a_ref.a2_ref, bf16[1024,1536]{1,0:T(8,128)(2,1)} %bitcast.151, ...), custom_call_target="tpu_custom_call" | custom-call | bytes 1000000 | tf_op jit(solution)/shard_map/project/pallas_call | solution.py:618
  186.6 9.0 %attend.2 = (bf16[768,512]{1,0:T(8,128)(2,1)}, bf16[192,2048]{1,0:T(8,128)(2,1)}, bf16[96,2048]{1,0:T(8,128)(2,1)}, bf16[96,2048]{1,0:T(8,128)(2,1)}) custom-call(bf16[768,512]{1,0:T(8,128)(2,1)} %get-tuple-element.280.refs_0_.refs_3_.refs_4_, bf16[768,1024]{1,0:T(8,128)(2,1)} %get-tuple-element.281.refs_1_.refs_4_.refs_5_, bf16[768,1024]{1,0:T(8,128)(2,1)} %copy-done.4, ...), custom_call_target="tpu_custom_call" | custom-call | bytes 1000000 | tf_op jit(solution)/shard_map/attend/pallas_call | solution.py:740
  202.9 9.4 %attend.3 = (bf16[768,512]{1,0:T(8,128)(2,1)}, bf16[192,2048]{1,0:T(8,128)(2,1)}, bf16[192,2048]{1,0:T(8,128)(2,1)}) custom-call(bf16[768,512]{1,0:T(8,128)(2,1)} %get-tuple-element.280.refs_0_.refs_3_.refs_4_, bf16[768,1024]{1,0:T(8,128)(2,1)} %get-tuple-element.281.refs_1_.refs_4_.refs_5_, ...), custom_call_target="tpu_custom_call", output_to_operand_aliasing={{0}: (7, {})} | custom-call | bytes 1000000 | tf_op jit(solution)/shard_map/attend/pallas_call | solution.py:740
  215.3 16.2 %collective-permute-done.28.refs_2_ = bf16[192,2048]{1,0:T(8,128)(2,1)S(1)} collective-permute-done((bf16[192,2048]{1,0:T(8,128)(2,1)S(1)}, bf16[192,2048]{1,0:T(8,128)(2,1)S(1)}, u32[]{:S(2)}, u32[]{:S(2)}) %collective-permute-start.28) | collective-permute-done | bytes 786464 | tf_op jit(solution)/shard_map/ppermute | solution.py:379
  233.5 4.2 close_attention.1
  242.3 16.1 %collective-permute-done.29.refs_1_ = bf16[192,2048]{1,0:T(8,128)(2,1)S(1)} collective-permute-done((bf16[192,2048]{1,0:T(8,128)(2,1)}, bf16[192,2048]{1,0:T(8,128)(2,1)S(1)}, u32[]{:S(2)}, u32[]{:S(2)}) %collective-permute-start.29) | collective-permute-done | bytes 786464 | tf_op jit(solution)/shard_map/ppermute | solution.py:379
  259.5 12.8 %collective-permute-done.31.refs_3_ = bf16[192,2048]{1,0:T(8,128)(2,1)S(1)} collective-permute-done((bf16[192,2048]{1,0:T(8,128)(2,1)}, bf16[192,2048]{1,0:T(8,128)(2,1)S(1)}, u32[]{:S(2)}, u32[]{:S(2)}) %collective-permute-start.31) | collective-permute-done | bytes 786464 | tf_op jit(solution)/shard_map/ppermute | solution.py:379
  280.6 17.1 %hidden_units.4 = (bf16[1536,1024]{1,0:T(8,128)(2,1)}, bf16[1536,2048]{1,0:T(8,128)(2,1)}, bf16[1536,2048]{1,0:T(8,128)(2,1)}, bf16[1536,2048]{1,0:T(8,128)(2,1)...) custom-call(bf16[192,2048]{1,0:T(8,128)(2,1)} %get-tuple-element.309, ...), custom_call_target="tpu_custom_call" | custom-call | bytes 1000000 | tf_op jit(solution)/shard_map/hidden_units/pallas_call | solution.py:740
  299.7 17.1 %hidden_units.5 = (bf16[1536,1024]{1,0:T(8,128)(2,1)}, bf16[1536,2048]{1,0:T(8,128)(2,1)}, bf16[1536,2048]{1,0:T(8,128)(2,1)}, bf16[1536,2048]{1,0:T(8,128)(2,1)...) custom-call(bf16[192,2048]{1,0:T(8,128)(2,1)} %copy-done.25, ...), custom_call_target="tpu_custom_call", output_to_operand_aliasing={{0}: (8, {}), {1}: (9, {}), {2}: (10, {}), {3}: (11, {})} | custom-call | bytes 1000000 | tf_op jit(solution)/shard_map/hidden_units/pallas_call | solution.py:740
  321.2 17.3 %hidden_units.6 = (bf16[1536,1024]{1,0:T(8,128)(2,1)}, bf16[1536,2048]{1,0:T(8,128)(2,1)}, bf16[1536,2048]{1,0:T(8,128)(2,1)}, bf16[1536,2048]{1,0:T(8,128)(2,1)...) custom-call(bf16[192,2048]{1,0:T(8,128)(2,1)} %collective-permute-do, ...), custom_call_target="tpu_custom_call", output_to_operand_aliasing={{0}: (6, {}), {1}: (7, {}), {2}: (8, {}), {3}: (9, {})} | custom-call | bytes 1000000 | tf_op jit(solution)/shard_map/hidden_units/pallas_call | solution.py:740
  341.4 17.0 %hidden_units.7 = (bf16[1536,1024]{1,0:T(8,128)(2,1)}, bf16[1536,2048]{1,0:T(8,128)(2,1)}, bf16[1536,2048]{1,0:T(8,128)(2,1)}, bf16[1536,2048]{1,0:T(8,128)(2,1)...) custom-call(bf16[192,2048]{1,0:T(8,128)(2,1)} %copy-done.24, ...), custom_call_target="tpu_custom_call", output_to_operand_aliasing={{0}: (8, {}), {1}: (9, {}), {2}: (10, {}), {3}: (11, {})} | custom-call | bytes 1000000 | tf_op jit(solution)/shard_map/hidden_units/pallas_call | solution.py:740
  360.2 10.4 %convolution_convert_fusion.2 = bf16[1024,2048]{1,0:T(8,128)(2,1)S(1)} fusion(bf16[1536,1024]{1,0:T(8,128)(2,1)} %get-tuple-element.364, bf16[1536,2048]{1,0:T(8,128)(2,1)} %get-tuple-element.365), kind=kOutput, calls=%fused_computation.10 | convolution fusion | flops 6444548096 | bytes 13631488 | tf_op jit(solution)/shard_map/dot_general | solution.py:946
  375.2 15.4 %convolution_convert_fusion.1 = bf16[2048,2048]{1,0:T(8,128)(2,1)} fusion(bf16[1536,2048]{1,0:T(8,128)(2,1)S(1)} %copy-done.1, bf16[1536,2048]{1,0:T(8,128)(2,1)S(1)} %copy-done), kind=kOutput, calls=%fused_computation.3 | convolution fusion | flops 12889096192 | bytes 20971520 | tf_op jit(solution)/shard_map/dot_general | solution.py:946
  393.7 4.8 dynamic-slice_bitcast_fusion
  401.6 8.8 %collective-permute-done.55 = bf16[96,2048]{1,0:T(8,128)(2,1)S(1)} collective-permute-done((bf16[96,2048]{1,0:T(8,128)(2,1)}, bf16[96,2048]{1,0:T(8,128)(2,1)S(1)}, u32[]{:S(2)}, u32[]{:S(2)}) %collective-permute-start.55) | collective-permute-done | bytes 393248 | tf_op jit(solution)/shard_map/ppermute | solution.py:379
  412.5 22.0 %collective-permute-done.51.refs_3_ = bf16[192,2048]{1,0:T(8,128)(2,1)S(1)} collective-permute-done((bf16[192,2048]{1,0:T(8,128)(2,1)S(1)}, bf16[192,2048]{1,0:T(8,128)(2,1)S(1)}, u32[]{:S(2)}, u32[]{:S(2)}) %collective-permute-start.51) | collective-permute-done | bytes 786464 | tf_op jit(solution)/shard_map/ppermute | solution.py:379
  435.4 5.3 close_hidden.1
  440.7 7.8 %fusion = bf16[2,4,128,2048]{3,2,1,0:T(8,128)(2,1)} fusion(bf16[2,4,128,2048]{3,2,1,0:T(8,128)(2,1)} %collective-permute-done.52, bf16[2,2,4,128,2048]{4,3,2,1,0:T(8,128)(2,1)} %bitcast.158, s32[]{:T(128)S(6)} %select_n.339), kind=kLoop, calls=%fused_computation.1 | loop fusion | flops 8388608 | bytes 12582916 | tf_op jit(solution)/shard_map/convert_element_type | solution.py:499
  452.5 16.2 %collective-permute-done.57.refs_1_ = bf16[192,2048]{1,0:T(8,128)(2,1)S(1)} collective-permute-done((bf16[192,2048]{1,0:T(8,128)(2,1)S(1)}, bf16[192,2048]{1,0:T(8,128)(2,1)S(1)}, u32[]{:S(2)}, u32[]{:S(2)}) %collective-permute-start.57) | collective-permute-done | bytes 786464 | tf_op jit(solution)/shard_map/ppermute | solution.py:379
  472.7 14.7 %attend_back.2 = (bf16[768,2048]{1,0:T(8,128)(2,1)}, bf16[384,512]{1,0:T(8,128)(2,1)}, f32[384,1024]{1,0:T(8,128)}, bf16[384,1024]{1,0:T(8,128)(2,1)}) custom-call(bf16[192,2048]{1,0:T(8,128)(2,1)} %get-tuple-element.396.refs_0_, bf16[192,2048]{1,0:T(8,128)(2,1)} %copy-done.21, bf16[512,2048]{1,0:T(8,128)(2,1)} %bitcast.148, ...), custom_call_target="tpu_custom_call" | custom-call | bytes 1000000 | tf_op jit(solution)/shard_map/attend_back/pallas_call | solution.py:740
  488.3 14.6 %attend_back.3 = (bf16[768,2048]{1,0:T(8,128)(2,1)}, bf16[384,512]{1,0:T(8,128)(2,1)}, f32[384,1024]{1,0:T(8,128)}, bf16[384,1024]{1,0:T(8,128)(2,1)}) custom-call(bf16[192,2048]{1,0:T(8,128)(2,1)} %copy-done.20, bf16[96,2048]{1,0:T(8,128)(2,1)} %copy-done.66, bf16[96,2048]{1,0:T(8,128)(2,1)} %copy-done.67, ...), custom_call_target="tpu_custom_call", output_to_operand_aliasing={{0}: (12, {})} | custom-call | bytes 1000000 | tf_op jit(solution)/shard_map/attend_back/pallas_call | solution.py:740
  504.9 4.2 convolution_convert_fusion.3
  510.0 3.4 join_grads.2.refs_5_
  515.5 3.6 join_grads.3.refs_0_
  519.1 7.5 %convolution_convert_fusion = bf16[2048,1536]{1,0:T(8,128)(2,1)S(1)} fusion(bf16[768,2048]{1,0:T(8,128)(2,1)} %constant_dynamic-update-slice_fusion.a_ref.a2_ref, bf16[768,1536]{1,0:T(8,128)(2,1)} %join_grads.3.refs_0_), kind=kOutput, calls=%fused_computation.2 | convolution fusion | flops 4834983936 | bytes 11796480 | tf_op jit(solution)/shard_map/dot_general | solution.py:946
  536.6 10.8 %input_terms.1 = (bf16[192,2048]{1,0:T(8,128)(2,1)}, bf16[192,2048]{1,0:T(8,128)(2,1)}, bf16[192,2048]{1,0:T(8,128)(2,1)}, bf16[96,2048]{1,0:T(8,128)(2,1)}, bf16[96,2048]{1,0:T(8,128)(2,1)}) custom-call(bf16[768,1536]{1,0:T(8,128)(2,1)} %join_grads.3.refs_0_, bf16[1024,1536]{1,0:T(8,128)(2,1)} %bitcast.152, ...), custom_call_target="tpu_custom_call" | custom-call | bytes 1000000 | tf_op jit(solution)/shard_map/input_terms/pallas_call | solution.py:740
  548.3 4.5 fusion.1
  555.9 3.7 collective-permute-done.68
  561.0 3.8 all-to-all-start.1
  572.1 10.9 %collective-permute-done.74 = bf16[96,2048]{1,0:T(8,128)(2,1)S(1)} collective-permute-done((bf16[96,2048]{1,0:T(8,128)(2,1)}, bf16[96,2048]{1,0:T(8,128)(2,1)S(1)}, u32[]{:S(2)}, u32[]{:S(2)}) %collective-permute-start.74) | collective-permute-done | bytes 393248 | tf_op jit(solution)/shard_map/ppermute | solution.py:379
  589.2 18.7 %collective-permute-done.71 = bf16[256,1536]{1,0:T(8,128)(2,1)S(1)} collective-permute-done((bf16[256,1536]{1,0:T(8,128)(2,1)S(1)}, bf16[256,1536]{1,0:T(8,128)(2,1)S(1)}, u32[]{:S(2)}, u32[]{:S(2)}) %collective-permute-start.71) | collective-permute-done | bytes 786464 | tf_op jit(solution)/shard_map/ppermute | solution.py:379
  610.3 3.2 fusion.4
  614.9 4.3 close_input.1
  619.2 11.3 %collective-permute-done.78 = bf16[256,1536]{1,0:T(8,128)(2,1)} collective-permute-done((bf16[256,1536]{1,0:T(8,128)(2,1)}, bf16[256,1536]{1,0:T(8,128)(2,1)}, u32[]{:S(2)}, u32[]{:S(2)}) %collective-permute-start.78) | collective-permute-done | bytes 786464 | tf_op jit(solution)/shard_map/ppermute | solution.py:379
  630.6 19.6 %collective-permute-done.77 = bf16[256,1536]{1,0:T(8,128)(2,1)} collective-permute-done((bf16[256,1536]{1,0:T(8,128)(2,1)}, bf16[256,1536]{1,0:T(8,128)(2,1)}, u32[]{:S(2)}, u32[]{:S(2)}) %collective-permute-start.77) | collective-permute-done | bytes 786464 | tf_op jit(solution)/shard_map/ppermute | solution.py:379
  655.9 5.8 collective-permute-done.80
  665.8 10.4 %finish_columns.2 = (f32[128,8192]{1,0:T(8,128)}, f32[128,8192]{1,0:T(8,128)}, f32[128,1024]{1,0:T(8,128)}) custom-call(s32[1]{0:T(128)} %bitcast.1.table_ref.seq_ref, bf16[2,2,128,2048]{3,2,1,0:T(8,128)(2,1)} %bitcast.153, bf16[2,2,128,2048]{3,2,1,0:T(8,128)(2,1)} %bitcast.154, bf16[2,2,128,2048]{3,2,1,0:T(8,128)(2,1)} %bitcast.62.refs_2_.refs_3_, ...), custom_call_target="tpu_custom_call" | custom-call | bytes 1000000 | tf_op jit(solution)/shard_map/finish_columns/pallas_call | solution.py:551
  687.7 7.0 finish_columns.3
  (472 shorter events, 198.9 us)
Async XLA Ops:
  10.5 39.8 %collective-permute-start.5 = (bf16[192,2048]{1,0:T(8,128)(2,1)}, bf16[192,2048]{1,0:T(8,128)(2,1)}, u32[]{:S(2)}, u32[]{:S(2)}) collective-permute-start(bf16[192,2048]{1,0:T(8,128)(2,1)} %bitcast.176), channel_id=1, source_target_pairs={{0,1},{1,0},{2,3},{3,2},{4,5},{5,4},{6,7},{7,6},{8,9},{9,8},{10,11... | collective-permute-start | bytes 2359304 | tf_op jit(solution)/shard_map/ppermute | solution.py:379
  14.1 20.8 %collective-permute-start.6 = (s32[768]{0:T(1024)S(1)}, s32[768]{0:T(1024)}, u32[]{:S(2)}, u32[]{:S(2)}) collective-permute-start(s32[768]{0:T(1024)S(1)} %convert_reduce_fusion), channel_id=1, source_target_pairs={{0,16},{16,0},{1,17},{17,1},{2,18},{18,2},{3,19},{19,3},{4,20},{20... | collective-permute-start | bytes 9224 | tf_op jit(solution)/shard_map/ppermute | solution.py:379
  50.3 40.7 %collective-permute-start.7 = (bf16[2,128,1536]{2,1,0:T(8,128)(2,1)S(1)}, bf16[2,128,1536]{2,1,0:T(8,128)(2,1)S(1)}, u32[]{:S(2)}, u32[]{:S(2)}) collective-permute-start(bf16[2,128,1536]{2,1,0:T(8,128)(2,1)S(1)} %pad_maximum_fusion.7), channel_id=1, source_target_pairs={{0,2},{2,0},{1,3},{3,1},{4,6},{6,4},{5,7},{7,5},{8,10},{10,8},{9,1... | collective-permute-start | bytes 2359304 | tf_op jit(solution)/shard_map/ppermute | solution.py:379
  50.3 40.7 %collective-permute-start.8 = (bf16[2,128,1536]{2,1,0:T(8,128)(2,1)S(1)}, bf16[2,128,1536]{2,1,0:T(8,128)(2,1)S(1)}, u32[]{:S(2)}, u32[]{:S(2)}) collective-permute-start(bf16[2,128,1536]{2,1,0:T(8,128)(2,1)S(1)} %pad_maximum_fusion.7), channel_id=1, source_target_pairs={{0,1},{1,0},{2,3},{3,2},{4,5},{5,4},{6,7},{7,6},{8,9},{9,8},{10,11... | collective-permute-start | bytes 2359304 | tf_op jit(solution)/shard_map/ppermute | solution.py:379
  52.2 38.9 %collective-permute-start.10 = (bf16[192,2048]{1,0:T(8,128)(2,1)S(1)}, bf16[192,2048]{1,0:T(8,128)(2,1)S(1)}, u32[]{:S(2)}, u32[]{:S(2)}) collective-permute-start(bf16[192,2048]{1,0:T(8,128)(2,1)S(1)} %copy-done.17), channel_id=1, source_target_pairs={{0,16},{16,0},{1,17},{17,1},{2,18},{18,2},{3,19},{19,3},{4,20},{20... | collective-permute-start | bytes 2359304 | tf_op jit(solution)/shard_map/ppermute | solution.py:379
  52.8 38.2 %collective-permute-start.9 = (bf16[192,2048]{1,0:T(8,128)(2,1)S(1)}, bf16[192,2048]{1,0:T(8,128)(2,1)S(1)}, u32[]{:S(2)}, u32[]{:S(2)}) collective-permute-start(bf16[192,2048]{1,0:T(8,128)(2,1)S(1)} %copy-done.17), channel_id=1, source_target_pairs={{0,8},{8,0},{1,9},{9,1},{2,10},{10,2},{3,11},{11,3},{4,12},{12,4},... | collective-permute-start | bytes 2359304 | tf_op jit(solution)/shard_map/ppermute | solution.py:379
  58.5 32.6 %collective-permute-start.11 = (bf16[64,2048]{1,0:T(8,128)(2,1)S(1)}, bf16[64,2048]{1,0:T(8,128)(2,1)S(1)}, u32[]{:S(2)}, u32[]{:S(2)}) collective-permute-start(bf16[64,2048]{1,0:T(8,128)(2,1)S(1)} %copy-done.71), channel_id=1, source_target_pairs={{0,1},{1,0},{2,3},{3,2},{4,5},{5,4},{6,7},{7,6},{8,9},{9,8},{10,11... | collective-permute-start | bytes 786440 | tf_op jit(solution)/shard_map/ppermute | solution.py:379
  114.4 45.1 %collective-permute-start.15 = (bf16[1024,1536]{1,0:T(8,128)(2,1)S(1)}, bf16[1024,1536]{1,0:T(8,128)(2,1)}, u32[]{:S(2)}, u32[]{:S(2)}) collective-permute-start(bf16[1024,1536]{1,0:T(8,128)(2,1)S(1)} %bitcast.150), channel_id=1, source_target_pairs={{0,4},{4,0},{1,5},{5,1},{2,6},{6,2},{3,7},{7,3},{8,12},{12,8},{9,1... | collective-permute-start | bytes 9437192 | tf_op jit(solution)/shard_map/ppermute | solution.py:379
  116.0 58.9 %all-to-all-start = ((bf16[4,128,2048]{2,1,0:T(8,128)(2,1)}), bf16[4,128,2048]{2,1,0:T(8,128)(2,1)}, u32[]{:S(2)}, u32[]{:S(2)}) async-start(bf16[4,128,2048]{2,1,0:T(8,128)(2,1)} %column_slices.3), calls=%async_computation | async-start | bytes 4194304 | tf_op jit(solution)/shard_map/all_to_all | solution.py:479
  120.5 160.1 %all-gather.2.cloned.1.call-start = ((), (), s32[]{:S(2)}) async-start(), calls=%async_computation.4 | async-start | bytes 10485760 | tf_op jit(solution)/shard_map/all_gather | solution.py:1042
  122.8 36.7 %collective-permute-start.16 = (bf16[192,2048]{1,0:T(8,128)(2,1)}, bf16[192,2048]{1,0:T(8,128)(2,1)}, u32[]{:S(2)}, u32[]{:S(2)}) collective-permute-start(bf16[192,2048]{1,0:T(8,128)(2,1)} %slice.116), channel_id=1, source_target_pairs={{0,2},{2,0},{1,3},{3,1},{4,6},{6,4},{5,7},{7,5},{8,10},{10,8},{9,1... | collective-permute-start | bytes 2359304 | tf_op jit(solution)/shard_map/ppermute | solution.py:379
  124.9 50.0 %collective-permute-start.18 = (bf16[192,2048]{1,0:T(8,128)(2,1)}, bf16[192,2048]{1,0:T(8,128)(2,1)}, u32[]{:S(2)}, u32[]{:S(2)}) collective-permute-start(bf16[192,2048]{1,0:T(8,128)(2,1)} %bitcast.177), channel_id=1, source_target_pairs={{0,8},{8,0},{1,9},{9,1},{2,10},{10,2},{3,11},{11,3},{4,12},{12,4},... | collective-permute-start | bytes 2359304 | tf_op jit(solution)/shard_map/ppermute | solution.py:379
  126.8 48.2 %collective-permute-start.19 = (bf16[192,2048]{1,0:T(8,128)(2,1)}, bf16[192,2048]{1,0:T(8,128)(2,1)}, u32[]{:S(2)}, u32[]{:S(2)}) collective-permute-start(bf16[192,2048]{1,0:T(8,128)(2,1)} %bitcast.178), channel_id=1, source_target_pairs={{0,16},{16,0},{1,17},{17,1},{2,18},{18,2},{3,19},{19,3},{4,20},{20... | collective-permute-start | bytes 2359304 | tf_op jit(solution)/shard_map/ppermute | solution.py:379
  175.0 296.3 %reduce-scatter.3.cloned.1.call-start = ((), (), s32[]{:S(2)}) async-start(), calls=%async_computation.5 | async-start | bytes 3145728 | tf_op jit(solution)/shard_map/reduce_scatter | solution.py:1093
  237.7 20.7 %collective-permute-start.29 = (bf16[192,2048]{1,0:T(8,128)(2,1)}, bf16[192,2048]{1,0:T(8,128)(2,1)S(1)}, u32[]{:S(2)}, u32[]{:S(2)}) collective-permute-start(bf16[192,2048]{1,0:T(8,128)(2,1)} %get-tuple-element.309.refs_0_), channel_id=1, source_target_pairs={{0,8},{8,0},{1,9},{9,1},{2,10},{10,2},{3,11},{11,3},{4,12},{12,4},... | collective-permute-start | bytes 2359304 | tf_op jit(solution)/shard_map/ppermute | solution.py:379
  238.8 20.7 %collective-permute-start.30 = (bf16[192,2048]{1,0:T(8,128)(2,1)}, bf16[192,2048]{1,0:T(8,128)(2,1)S(1)}, u32[]{:S(2)}, u32[]{:S(2)}) collective-permute-start(bf16[192,2048]{1,0:T(8,128)(2,1)} %get-tuple-element.309.refs_0_), channel_id=1, source_target_pairs={{0,16},{16,0},{1,17},{17,1},{2,18},{18,2},{3,19},{19,3},{4,20},{20... | collective-permute-start | bytes 2359304 | tf_op jit(solution)/shard_map/ppermute | solution.py:379
  239.7 32.7 %collective-permute-start.31 = (bf16[192,2048]{1,0:T(8,128)(2,1)}, bf16[192,2048]{1,0:T(8,128)(2,1)S(1)}, u32[]{:S(2)}, u32[]{:S(2)}) collective-permute-start(bf16[192,2048]{1,0:T(8,128)(2,1)} %collective-permute-done.5.refs_2_), channel_id=1, source_target_pairs={{0,8},{8,0},{1,9},{9,1},{2,10},{10,2},{3,11},{11,3},{4,12},{12,4},... | collective-permute-start | bytes 2359304 | tf_op jit(solution)/shard_map/ppermute | solution.py:379
  240.8 32.6 %collective-permute-start.32 = (bf16[192,2048]{1,0:T(8,128)(2,1)}, bf16[192,2048]{1,0:T(8,128)(2,1)S(1)}, u32[]{:S(2)}, u32[]{:S(2)}) collective-permute-start(bf16[192,2048]{1,0:T(8,128)(2,1)} %collective-permute-done.5.refs_2_), channel_id=1, source_target_pairs={{0,16},{16,0},{1,17},{17,1},{2,18},{18,2},{3,19},{19,3},{4,20},{20... | collective-permute-start | bytes 2359304 | tf_op jit(solution)/shard_map/ppermute | solution.py:379
  241.7 56.0 %collective-permute-start.35 = (bf16[192,2048]{1,0:T(8,128)(2,1)}, bf16[192,2048]{1,0:T(8,128)(2,1)}, u32[]{:S(2)}, u32[]{:S(2)}) collective-permute-start(bf16[192,2048]{1,0:T(8,128)(2,1)} %get-tuple-element.309.refs_0_), channel_id=1, source_target_pairs={{0,1},{1,0},{2,3},{3,2},{4,5},{5,4},{6,7},{7,6},{8,9},{9,8},{10,11... | collective-permute-start | bytes 2359304 | tf_op jit(solution)/shard_map/ppermute | solution.py:379
  274.2 23.5 %collective-permute-start.33 = (bf16[96,2048]{1,0:T(8,128)(2,1)}, bf16[96,2048]{1,0:T(8,128)(2,1)}, u32[]{:S(2)}, u32[]{:S(2)}) collective-permute-start(bf16[96,2048]{1,0:T(8,128)(2,1)} %slice.124), channel_id=1, source_target_pairs={{0,8},{8,0},{1,9},{9,1},{2,10},{10,2},{3,11},{11,3},{4,12},{12,4},... | collective-permute-start | bytes 1179656 | tf_op jit(solution)/shard_map/ppermute | solution.py:379
  275.7 22.0 %collective-permute-start.34 = (bf16[96,2048]{1,0:T(8,128)(2,1)}, bf16[96,2048]{1,0:T(8,128)(2,1)}, u32[]{:S(2)}, u32[]{:S(2)}) collective-permute-start(bf16[96,2048]{1,0:T(8,128)(2,1)} %slice.125), channel_id=1, source_target_pairs={{0,16},{16,0},{1,17},{17,1},{2,18},{18,2},{3,19},{19,3},{4,20},{20... | collective-permute-start | bytes 1179656 | tf_op jit(solution)/shard_map/ppermute | solution.py:379
  277.6 20.2 %collective-permute-start.36 = (bf16[96,2048]{1,0:T(8,128)(2,1)}, bf16[96,2048]{1,0:T(8,128)(2,1)S(1)}, u32[]{:S(2)}, u32[]{:S(2)}) collective-permute-start(bf16[96,2048]{1,0:T(8,128)(2,1)} %slice.126), channel_id=1, source_target_pairs={{0,8},{8,0},{1,9},{9,1},{2,10},{10,2},{3,11},{11,3},{4,12},{12,4},... | collective-permute-start | bytes 1179656 | tf_op jit(solution)/shard_map/ppermute | solution.py:379
  297.8 19.0 %collective-permute-start.38 = (bf16[192,2048]{1,0:T(8,128)(2,1)}, bf16[192,2048]{1,0:T(8,128)(2,1)S(1)}, u32[]{:S(2)}, u32[]{:S(2)}) collective-permute-start(bf16[192,2048]{1,0:T(8,128)(2,1)} %collective-permute-done.35.refs_0_), channel_id=1, source_target_pairs={{0,8},{8,0},{1,9},{9,1},{2,10},{10,2},{3,11},{11,3},{4,12},{12,4},... | collective-permute-start | bytes 2359304 | tf_op jit(solution)/shard_map/ppermute | solution.py:379
  316.9 21.6 %collective-permute-start.40 = (bf16[96,2048]{1,0:T(8,128)(2,1)S(1)}, bf16[96,2048]{1,0:T(8,128)(2,1)S(1)}, u32[]{:S(2)}, u32[]{:S(2)}) collective-permute-start(bf16[96,2048]{1,0:T(8,128)(2,1)S(1)} %slice.128), channel_id=1, source_target_pairs={{0,8},{8,0},{1,9},{9,1},{2,10},{10,2},{3,11},{11,3},{4,12},{12,4},... | collective-permute-start | bytes 1179656 | tf_op jit(solution)/shard_map/ppermute | solution.py:379
  318.1 20.4 %collective-permute-start.41 = (bf16[96,2048]{1,0:T(8,128)(2,1)S(1)}, bf16[96,2048]{1,0:T(8,128)(2,1)S(1)}, u32[]{:S(2)}, u32[]{:S(2)}) collective-permute-start(bf16[96,2048]{1,0:T(8,128)(2,1)S(1)} %slice.129), channel_id=1, source_target_pairs={{0,16},{16,0},{1,17},{17,1},{2,18},{18,2},{3,19},{19,3},{4,20},{20... | collective-permute-start | bytes 1179656 | tf_op jit(solution)/shard_map/ppermute | solution.py:379
  319.3 19.2 %collective-permute-start.42 = (bf16[96,2048]{1,0:T(8,128)(2,1)}, bf16[96,2048]{1,0:T(8,128)(2,1)S(1)}, u32[]{:S(2)}, u32[]{:S(2)}) collective-permute-start(bf16[96,2048]{1,0:T(8,128)(2,1)} %get-tuple-element.345), channel_id=1, source_target_pairs={{0,8},{8,0},{1,9},{9,1},{2,10},{10,2},{3,11},{11,3},{4,12},{12,4},... | collective-permute-start | bytes 1179656 | tf_op jit(solution)/shard_map/ppermute | solution.py:379
  338.7 19.6 %collective-permute-start.45 = (bf16[192,2048]{1,0:T(8,128)(2,1)S(1)}, bf16[192,2048]{1,0:T(8,128)(2,1)S(1)}, u32[]{:S(2)}, u32[]{:S(2)}) collective-permute-start(bf16[192,2048]{1,0:T(8,128)(2,1)S(1)} %pad_maximum_fusion.11), channel_id=1, source_target_pairs={{0,16},{16,0},{1,17},{17,1},{2,18},{18,2},{3,19},{19,3},{4,20},{20... | collective-permute-start | bytes 2359304 | tf_op jit(solution)/shard_map/ppermute | solution.py:379
  370.9 21.8 %collective-permute-start.50 = (bf16[192,2048]{1,0:T(8,128)(2,1)S(1)}, bf16[192,2048]{1,0:T(8,128)(2,1)S(1)}, u32[]{:S(2)}, u32[]{:S(2)}) collective-permute-start(bf16[192,2048]{1,0:T(8,128)(2,1)S(1)} %pad_maximum_fusion.13), channel_id=1, source_target_pairs={{0,16},{16,0},{1,17},{17,1},{2,18},{18,2},{3,19},{19,3},{4,20},{20... | collective-permute-start | bytes 2359304 | tf_op jit(solution)/shard_map/ppermute | solution.py:379
  372.6 20.1 %collective-permute-start.49 = (bf16[192,2048]{1,0:T(8,128)(2,1)S(1)}, bf16[192,2048]{1,0:T(8,128)(2,1)S(1)}, u32[]{:S(2)}, u32[]{:S(2)}) collective-permute-start(bf16[192,2048]{1,0:T(8,128)(2,1)S(1)} %pad_maximum_fusion.12), channel_id=1, source_target_pairs={{0,8},{8,0},{1,9},{9,1},{2,10},{10,2},{3,11},{11,3},{4,12},{12,4},... | collective-permute-start | bytes 2359304 | tf_op jit(solution)/shard_map/ppermute | solution.py:379
  398.5 42.2 %collective-permute-start.52 = (bf16[2,4,128,2048]{3,2,1,0:T(8,128)(2,1)}, bf16[2,4,128,2048]{3,2,1,0:T(8,128)(2,1)}, u32[]{:S(2)}, u32[]{:S(2)}) collective-permute-start(bf16[2,4,128,2048]{3,2,1,0:T(8,128)(2,1)} %dynamic-slice_bitcast_fusion), channel_id=1, source_target_pairs={{0,4},{4,0},{1,5},{5,1},{2,6},{6,2},{3,7},{7,3},{8,12},{12,8},{9,1... | collective-permute-start | bytes 12582920 | tf_op jit(solution)/shard_map/ppermute | solution.py:379
  398.6 161.0 %reduce-scatter.5.cloned.1.call-start = ((), (), s32[]{:S(2)}) async-start(), calls=%async_computation.6 | async-start | bytes 6291456 | tf_op jit(solution)/shard_map/reduce_scatter | solution.py:1102
  400.9 33.6 %collective-permute-start.51 = (bf16[192,2048]{1,0:T(8,128)(2,1)S(1)}, bf16[192,2048]{1,0:T(8,128)(2,1)S(1)}, u32[]{:S(2)}, u32[]{:S(2)}) collective-permute-start(bf16[192,2048]{1,0:T(8,128)(2,1)S(1)} %add_convert_fusion.2), channel_id=1, source_target_pairs={{0,1},{1,0},{2,3},{3,2},{4,5},{5,4},{6,7},{7,6},{8,9},{9,8},{10,11... | collective-permute-start | bytes 2359304 | tf_op jit(solution)/shard_map/ppermute | solution.py:379
  410.6 37.9 %collective-permute-start.56 = (bf16[192,2048]{1,0:T(8,128)(2,1)S(1)}, bf16[192,2048]{1,0:T(8,128)(2,1)S(1)}, u32[]{:S(2)}, u32[]{:S(2)}) collective-permute-start(bf16[192,2048]{1,0:T(8,128)(2,1)S(1)} %pad_maximum_fusion.15), channel_id=1, source_target_pairs={{0,16},{16,0},{1,17},{17,1},{2,18},{18,2},{3,19},{19,3},{4,20},{20... | collective-permute-start | bytes 2359304 | tf_op jit(solution)/shard_map/ppermute | solution.py:379
  411.4 37.1 %collective-permute-start.54 = (bf16[192,2048]{1,0:T(8,128)(2,1)S(1)}, bf16[192,2048]{1,0:T(8,128)(2,1)S(1)}, u32[]{:S(2)}, u32[]{:S(2)}) collective-permute-start(bf16[192,2048]{1,0:T(8,128)(2,1)S(1)} %pad_maximum_fusion.14), channel_id=1, source_target_pairs={{0,8},{8,0},{1,9},{9,1},{2,10},{10,2},{3,11},{11,3},{4,12},{12,4},... | collective-permute-start | bytes 2359304 | tf_op jit(solution)/shard_map/ppermute | solution.py:379
  471.3 42.2 %collective-permute-start.65 = (bf16[256,2048]{1,0:T(8,128)(2,1)}, bf16[256,2048]{1,0:T(8,128)(2,1)S(1)}, u32[]{:S(2)}, u32[]{:S(2)}) collective-permute-start(bf16[256,2048]{1,0:T(8,128)(2,1)} %bitcast.174), channel_id=1, source_target_pairs={{0,16},{16,0},{1,17},{17,1},{2,18},{18,2},{3,19},{19,3},{4,20},{20... | collective-permute-start | bytes 3145736 | tf_op jit(solution)/shard_map/ppermute | solution.py:379
  487.5 21.6 %collective-permute-start.61 = (bf16[384,1024]{1,0:T(8,128)(2,1)}, bf16[384,1024]{1,0:T(8,128)(2,1)S(1)}, u32[]{:S(2)}, u32[]{:S(2)}) collective-permute-start(bf16[384,1024]{1,0:T(8,128)(2,1)} %get-tuple-element.412), channel_id=1, source_target_pairs={{0,4},{4,0},{1,5},{5,1},{2,6},{6,2},{3,7},{7,3},{8,12},{12,8},{9,1... | collective-permute-start | bytes 2359304 | tf_op jit(solution)/shard_map/ppermute | solution.py:379
  533.3 20.3 %collective-permute-start.70 = (bf16[192,2048]{1,0:T(8,128)(2,1)}, bf16[192,2048]{1,0:T(8,128)(2,1)}, u32[]{:S(2)}, u32[]{:S(2)}) collective-permute-start(bf16[192,2048]{1,0:T(8,128)(2,1)} %pad_maximum_fusion.17), channel_id=1, source_target_pairs={{0,16},{16,0},{1,17},{17,1},{2,18},{18,2},{3,19},{19,3},{4,20},{20... | collective-permute-start | bytes 2359304 | tf_op jit(solution)/shard_map/ppermute | solution.py:379
  535.9 20.0 %collective-permute-start.69 = (bf16[192,2048]{1,0:T(8,128)(2,1)}, bf16[192,2048]{1,0:T(8,128)(2,1)}, u32[]{:S(2)}, u32[]{:S(2)}) collective-permute-start(bf16[192,2048]{1,0:T(8,128)(2,1)} %pad_maximum_fusion.16), channel_id=1, source_target_pairs={{0,8},{8,0},{1,9},{9,1},{2,10},{10,2},{3,11},{11,3},{4,12},{12,4},... | collective-permute-start | bytes 2359304 | tf_op jit(solution)/shard_map/ppermute | solution.py:379
  559.6 23.4 %collective-permute-start.74 = (bf16[96,2048]{1,0:T(8,128)(2,1)}, bf16[96,2048]{1,0:T(8,128)(2,1)S(1)}, u32[]{:S(2)}, u32[]{:S(2)}) collective-permute-start(bf16[96,2048]{1,0:T(8,128)(2,1)} %get-tuple-element.439), channel_id=1, source_target_pairs={{0,8},{8,0},{1,9},{9,1},{2,10},{10,2},{3,11},{11,3},{4,12},{12,4},... | collective-permute-start | bytes 1179656 | tf_op jit(solution)/shard_map/ppermute | solution.py:379
  561.0 49.2 %all-to-all-start.1 = ((bf16[4,128,2048]{2,1,0:T(8,128)(2,1)}), bf16[4,128,2048]{2,1,0:T(8,128)(2,1)S(1)}, u32[]{:S(2)}, u32[]{:S(2)}) async-start(bf16[4,128,2048]{2,1,0:T(8,128)(2,1)} %bitcast.181), calls=%async_computation.3 | async-start | bytes 4194304 | tf_op jit(solution)/shard_map/all_to_all | solution.py:479
  566.7 19.8 %collective-permute-start.76 = (bf16[256,2048]{1,0:T(8,128)(2,1)S(1)}, bf16[256,2048]{1,0:T(8,128)(2,1)S(1)}, u32[]{:S(2)}, u32[]{:S(2)}) collective-permute-start(bf16[256,2048]{1,0:T(8,128)(2,1)S(1)} %broadcast_select_fusion.4), channel_id=1, source_target_pairs={{0,4},{4,0},{1,5},{5,1},{2,6},{6,2},{3,7},{7,3},{8,12},{12,8},{9,1... | collective-permute-start | bytes 3145736 | tf_op jit(solution)/shard_map/ppermute | solution.py:379
  570.1 37.8 %collective-permute-start.71 = (bf16[256,1536]{1,0:T(8,128)(2,1)S(1)}, bf16[256,1536]{1,0:T(8,128)(2,1)S(1)}, u32[]{:S(2)}, u32[]{:S(2)}) collective-permute-start(bf16[256,1536]{1,0:T(8,128)(2,1)S(1)} %get-tuple-element.474), channel_id=1, source_target_pairs={{0,1},{1,0},{2,3},{3,2},{4,5},{5,4},{6,7},{7,6},{8,9},{9,8},{10,11... | collective-permute-start | bytes 2359304 | tf_op jit(solution)/shard_map/ppermute | solution.py:379
  583.2 24.7 %collective-permute-start.75 = (bf16[192,2048]{1,0:T(8,128)(2,1)S(1)}, bf16[192,2048]{1,0:T(8,128)(2,1)S(1)}, u32[]{:S(2)}, u32[]{:S(2)}) collective-permute-start(bf16[192,2048]{1,0:T(8,128)(2,1)S(1)} %pad_maximum_fusion.19), channel_id=1, source_target_pairs={{0,16},{16,0},{1,17},{17,1},{2,18},{18,2},{3,19},{19,3},{4,20},{20... | collective-permute-start | bytes 2359304 | tf_op jit(solution)/shard_map/ppermute | solution.py:379
  584.9 25.4 %collective-permute-start.73 = (bf16[192,2048]{1,0:T(8,128)(2,1)S(1)}, bf16[192,2048]{1,0:T(8,128)(2,1)}, u32[]{:S(2)}, u32[]{:S(2)}) collective-permute-start(bf16[192,2048]{1,0:T(8,128)(2,1)S(1)} %pad_maximum_fusion.18), channel_id=1, source_target_pairs={{0,8},{8,0},{1,9},{9,1},{2,10},{10,2},{3,11},{11,3},{4,12},{12,4},... | collective-permute-start | bytes 2359304 | tf_op jit(solution)/shard_map/ppermute | solution.py:379
  589.2 41.4 %collective-permute-start.78 = (bf16[256,1536]{1,0:T(8,128)(2,1)}, bf16[256,1536]{1,0:T(8,128)(2,1)}, u32[]{:S(2)}, u32[]{:S(2)}) collective-permute-start(bf16[256,1536]{1,0:T(8,128)(2,1)} %get-tuple-element.473), channel_id=1, source_target_pairs={{0,1},{1,0},{2,3},{3,2},{4,5},{5,4},{6,7},{7,6},{8,9},{9,8},{10,11... | collective-permute-start | bytes 2359304 | tf_op jit(solution)/shard_map/ppermute | solution.py:379
  613.5 36.8 %collective-permute-start.77 = (bf16[256,1536]{1,0:T(8,128)(2,1)}, bf16[256,1536]{1,0:T(8,128)(2,1)}, u32[]{:S(2)}, u32[]{:S(2)}) collective-permute-start(bf16[256,1536]{1,0:T(8,128)(2,1)} %fusion.4), channel_id=1, source_target_pairs={{0,2},{2,0},{1,3},{3,1},{4,6},{6,4},{5,7},{7,5},{8,10},{10,8},{9,1... | collective-permute-start | bytes 2359304 | tf_op jit(solution)/shard_map/ppermute | solution.py:379
  613.5 52.4 %collective-permute-start.84 = (bf16[4,128,2048]{2,1,0:T(8,128)(2,1)S(1)}, bf16[4,128,2048]{2,1,0:T(8,128)(2,1)}, u32[]{:S(2)}, u32[]{:S(2)}) collective-permute-start(bf16[4,128,2048]{2,1,0:T(8,128)(2,1)S(1)} %all-to-all-done.1), channel_id=1, source_target_pairs={{0,16},{16,0},{1,17},{17,1},{2,18},{18,2},{3,19},{19,3},{4,20},{20... | collective-permute-start | bytes 6291464 | tf_op jit(solution)/shard_map/ppermute | solution.py:379
  653.7 24.3 %collective-permute-start.79 = (bf16[128,1536]{1,0:T(8,128)(2,1)S(1)}, bf16[128,1536]{1,0:T(8,128)(2,1)}, u32[]{:S(2)}, u32[]{:S(2)}) collective-permute-start(bf16[128,1536]{1,0:T(8,128)(2,1)S(1)} %get-tuple-element.459), channel_id=1, source_target_pairs={{0,16},{16,0},{1,17},{17,1},{2,18},{18,2},{3,19},{19,3},{4,20},{20... | collective-permute-start | bytes 1179656 | tf_op jit(solution)/shard_map/ppermute | solution.py:379
  (130 other events, 1265.9 us)
Sparse Core Ops, SparseCore 0:
  175.1 103.3 all-gather.1
  398.7 54.4 reduce-scatter.2
  456.2 99.2 reduce-scatter.4

commit v5 on v4

--- a/solution.py
+++ b/solution.py
@@ -1094,6 +1094,7 @@
     across = return_across(db2[0], *far_along)
     near_y_along = return_along(y0[1], y1[0], *return_halves(*y1[1:]))
     gate_up_sums = add_core(place, gate_up_terms.reshape(2, 2, 4, rows, -1), 0)
+    across, gate_up_sums = fence([across, gate_up_sums], [])
     dh, dh_low = on_rows(
         close_hidden_kernel, "close_hidden", [dy_own, hidden, near0, *near_along, across], [F32, BF16]
     )
@@ -1142,7 +1143,8 @@
 
     qkv_zl = swap(part(qkv_sums, 1, 1), "zl")
     gate_up_near = share_columns(gate_up_near)
-    sums = return_along(term_x, term_s, *return_halves(*term_o))
+    by_seq = jnp.concatenate([swap(half, "seq") for half in term_o])
+    sums = [swap(add_low(term_x, by_seq).astype(BF16), "x"), swap(term_s, "seq")]
     down_grad = own_rows(place, down_total, down_other)
     qkv_zl, gate_up_near, sums, out_zl = fence([qkv_zl, gate_up_near, sums, out_zl], [down_grad])
 
@@ -1162,19 +1164,19 @@
         place, *[v.reshape(2, 2, rows, -1) for v in (gate_up_near, gate_up_far)], [gate_weight, up_weight], ff_gain,
         hidden_rows, True,
     )
-    kept, kept_far, received, received_far, out_zh, out_zl, far_y_along = fence(
-        [kept, kept_far, received, received_far, out_zh, out_zl, far_y_along], [ff_gain_grad]
-    )
-
     y_across = return_across(y2[0], *far_y_along)
+    kept, kept_far, received, received_far, out_zl = fence(
+        [kept, kept_far, received, received_far, out_zl], [ff_gain_grad]
+    )
+
     out_total = add_low(part(out_sums, 0, 0), out_zl, out_zh).astype(BF16)
     out_other = swap(out_total, "seq")
-    output_grad = own_rows(place, out_total, out_other)
-
     (query_grad, key_grad, value_grad), attn_gain_grad = finish_columns(
         place, in_order(kept, received, place.x), in_order(kept_far, received_far, place.x),
         [query_weight, key_weight, value_weight], attn_gain, rows, False,
     )
+    (out_other,) = fence([out_other], [attn_gain_grad])
+    output_grad = own_rows(place, out_total, out_other)
     layer_output = add_low(hidden, y0[0], *near_y_along, y_across).astype(BF16)
     return (
         layer_output[None], input_grad[None], attn_gain_grad, query_grad, key_grad, value_grad, output_grad,

time: 719 us -> 711 us (0.989)
  waiting for transfers between devices: 255 us -> 242 us
    ppermute x86, waiting for transfers between devices: 255 us -> 242 us  [swap(): return lax.ppermute(value, axis, [(0, 1), (1, 0)])]
    unnamed x175 -> x165, local copies, waits for them, and re-layouts: 20.9 us -> 19.8 us
  transfers between devices with their start and end apart: 93 -> 93, of which waited for: 31 -> 32; matrix products, arithmetic and copies ran while one was open for 18% -> 19% of each run, Pallas kernels for 26% -> 26%
where the time goes in v5:
time: 711 us; the launch traced here: 700 us
  waiting for transfers between devices  242 us (34%)
  Pallas kernels  185 us (26%)
  starting transfers between devices  98.9 us (14%)
  other arithmetic  70.5 us (10%)
  local copies, waits for them, and re-layouts  51.2 us (7%)
  matrix products  37 us (5%)
  between operations  15.3 us (2%)
    ppermute x86, waiting for transfers between devices, swap(): return lax.ppermute(value, axis, [(0, 1), (1, 0)])  242 us
    pallas_call x11, Pallas kernels, into(): pl.pallas_call(body, grid=grid, in_specs=in_specs + [pl.BlockSpec(memory_...  134 us
    ppermute x86, starting transfers between devices, swap(): return lax.ppermute(value, axis, [(0, 1), (1, 0)])  84.8 us
    dot_general x4, matrix products, dot_low(): lax.dot_general(left, right, (((left_dim,), (right_dim,)), ((), ())), pre...  37 us
    unnamed x165, local copies, waits for them, and re-layouts  19.8 us
    pallas_call x2, Pallas kernels, finish_columns(): pl.pallas_call(functools.partial(finish_kernel, count), grid_spec=pltpu.P...  17.5 us
    pallas_call x4, Pallas kernels, on_rows(): pl.pallas_call(kernel, grid=(3,), in_specs=[tile] * len(operands), out_sp...  16.8 us
    convert_element_type x4, other arithmetic, add_core(): add_low(lax.dynamic_index_in_dim(parts, place.core, axis, False), received)  14.7 us
  transfers between devices with their start and end apart: 93, of which 32 were waited for; matrix products, arithmetic and copies ran while one was open for 19% of the time, Pallas kernels for 26%

profile of v5, /device:TPU:0, one launch (start us, length us, event | category | flops | bytes accessed | tf_op | source)
XLA Modules:
  0.0 700.5 jit_solution(9296612576263216028)
XLA Ops:
  17.2 3.2 column_slices.2
  28.2 3.2 collective-permute-start.4
  44.3 4.7 collective-permute-done.2
  54.2 4.2 column_slices.3
  60.3 30.8 %collective-permute-done.11 = bf16[64,2048]{1,0:T(8,128)(2,1)S(1)} collective-permute-done((bf16[64,2048]{1,0:T(8,128)(2,1)S(1)}, bf16[64,2048]{1,0:T(8,128)(2,1)S(1)}, u32[]{:S(2)}, u32[]{:S(2)}) %collective-permute-start.11) | collective-permute-done | bytes 262176 | tf_op jit(solution)/shard_map/ppermute | solution.py:379
  104.4 9.3 %collective-permute-done.12 = bf16[2,128,1536]{2,1,0:T(8,128)(2,1)S(1)} collective-permute-done((bf16[2,128,1536]{2,1,0:T(8,128)(2,1)S(1)}, bf16[2,128,1536]{2,1,0:T(8,128)(2,1)S(1)}, u32[]{:S(2)}, u32[]{:S(2)}) %collective-permute-start.12) | collective-permute-done | bytes 786464 | tf_op jit(solution)/shard_map/ppermute | solution.py:379
  116.1 4.4 all-to-all-start
  128.8 30.8 %collective-permute-done.16 = bf16[192,2048]{1,0:T(8,128)(2,1)} collective-permute-done((bf16[192,2048]{1,0:T(8,128)(2,1)}, bf16[192,2048]{1,0:T(8,128)(2,1)}, u32[]{:S(2)}, u32[]{:S(2)}) %collective-permute-start.16) | collective-permute-done | bytes 786464 | tf_op jit(solution)/shard_map/ppermute | solution.py:379
  160.5 3.4 collective-permute-start.17
  165.5 9.5 %project.1 = (bf16[768,512]{1,0:T(8,128)(2,1)}, bf16[768,1024]{1,0:T(8,128)(2,1)}) custom-call(s32[1]{0:T(128)} %bitcast.20.core_ref.refs_3_, bf16[768,2048]{1,0:T(8,128)(2,1)} %constant_dynamic-update-slice_fusion.a_ref.a2_ref, bf16[768,2048]{1,0:T(8,128)(2,1)} %constant_dynamic-update-slice_fusion.a_ref.a2_ref, bf16[1024,1536]{1,0:T(8,128)(2,1)} %bitcast.151, ...), custom_call_target="tpu_custom_call" | custom-call | bytes 1000000 | tf_op jit(solution)/shard_map/project/pallas_call | solution.py:618
  186.6 9.0 %attend.2 = (bf16[768,512]{1,0:T(8,128)(2,1)}, bf16[192,2048]{1,0:T(8,128)(2,1)}, bf16[96,2048]{1,0:T(8,128)(2,1)}, bf16[96,2048]{1,0:T(8,128)(2,1)}) custom-call(bf16[768,512]{1,0:T(8,128)(2,1)} %get-tuple-element.280.refs_0_.refs_3_.refs_4_, bf16[768,1024]{1,0:T(8,128)(2,1)} %get-tuple-element.281.refs_1_.refs_4_.refs_5_, bf16[768,1024]{1,0:T(8,128)(2,1)} %copy-done.4, ...), custom_call_target="tpu_custom_call" | custom-call | bytes 1000000 | tf_op jit(solution)/shard_map/attend/pallas_call | solution.py:740
  203.0 9.3 %attend.3 = (bf16[768,512]{1,0:T(8,128)(2,1)}, bf16[192,2048]{1,0:T(8,128)(2,1)}, bf16[192,2048]{1,0:T(8,128)(2,1)}) custom-call(bf16[768,512]{1,0:T(8,128)(2,1)} %get-tuple-element.280.refs_0_.refs_3_.refs_4_, bf16[768,1024]{1,0:T(8,128)(2,1)} %get-tuple-element.281.refs_1_.refs_4_.refs_5_, ...), custom_call_target="tpu_custom_call", output_to_operand_aliasing={{0}: (7, {})} | custom-call | bytes 1000000 | tf_op jit(solution)/shard_map/attend/pallas_call | solution.py:740
  215.4 16.2 %collective-permute-done.28.refs_2_ = bf16[192,2048]{1,0:T(8,128)(2,1)S(1)} collective-permute-done((bf16[192,2048]{1,0:T(8,128)(2,1)S(1)}, bf16[192,2048]{1,0:T(8,128)(2,1)S(1)}, u32[]{:S(2)}, u32[]{:S(2)}) %collective-permute-start.28) | collective-permute-done | bytes 786464 | tf_op jit(solution)/shard_map/ppermute | solution.py:379
  233.4 4.2 close_attention.1
  242.3 16.0 %collective-permute-done.29.refs_1_ = bf16[192,2048]{1,0:T(8,128)(2,1)S(1)} collective-permute-done((bf16[192,2048]{1,0:T(8,128)(2,1)}, bf16[192,2048]{1,0:T(8,128)(2,1)S(1)}, u32[]{:S(2)}, u32[]{:S(2)}) %collective-permute-start.29) | collective-permute-done | bytes 786464 | tf_op jit(solution)/shard_map/ppermute | solution.py:379
  259.5 12.8 %collective-permute-done.31.refs_3_ = bf16[192,2048]{1,0:T(8,128)(2,1)S(1)} collective-permute-done((bf16[192,2048]{1,0:T(8,128)(2,1)}, bf16[192,2048]{1,0:T(8,128)(2,1)S(1)}, u32[]{:S(2)}, u32[]{:S(2)}) %collective-permute-start.31) | collective-permute-done | bytes 786464 | tf_op jit(solution)/shard_map/ppermute | solution.py:379
  280.7 17.1 %hidden_units.4 = (bf16[1536,1024]{1,0:T(8,128)(2,1)}, bf16[1536,2048]{1,0:T(8,128)(2,1)}, bf16[1536,2048]{1,0:T(8,128)(2,1)}, bf16[1536,2048]{1,0:T(8,128)(2,1)...) custom-call(bf16[192,2048]{1,0:T(8,128)(2,1)} %get-tuple-element.309, ...), custom_call_target="tpu_custom_call" | custom-call | bytes 1000000 | tf_op jit(solution)/shard_map/hidden_units/pallas_call | solution.py:740
  299.6 17.2 %hidden_units.5 = (bf16[1536,1024]{1,0:T(8,128)(2,1)}, bf16[1536,2048]{1,0:T(8,128)(2,1)}, bf16[1536,2048]{1,0:T(8,128)(2,1)}, bf16[1536,2048]{1,0:T(8,128)(2,1)...) custom-call(bf16[192,2048]{1,0:T(8,128)(2,1)} %copy-done.24, ...), custom_call_target="tpu_custom_call", output_to_operand_aliasing={{0}: (8, {}), {1}: (9, {}), {2}: (10, {}), {3}: (11, {})} | custom-call | bytes 1000000 | tf_op jit(solution)/shard_map/hidden_units/pallas_call | solution.py:740
  321.3 17.3 %hidden_units.6 = (bf16[1536,1024]{1,0:T(8,128)(2,1)}, bf16[1536,2048]{1,0:T(8,128)(2,1)}, bf16[1536,2048]{1,0:T(8,128)(2,1)}, bf16[1536,2048]{1,0:T(8,128)(2,1)...) custom-call(bf16[192,2048]{1,0:T(8,128)(2,1)} %collective-permute-do, ...), custom_call_target="tpu_custom_call", output_to_operand_aliasing={{0}: (6, {}), {1}: (7, {}), {2}: (8, {}), {3}: (9, {})} | custom-call | bytes 1000000 | tf_op jit(solution)/shard_map/hidden_units/pallas_call | solution.py:740
  341.4 17.1 %hidden_units.7 = (bf16[1536,1024]{1,0:T(8,128)(2,1)}, bf16[1536,2048]{1,0:T(8,128)(2,1)}, bf16[1536,2048]{1,0:T(8,128)(2,1)}, bf16[1536,2048]{1,0:T(8,128)(2,1)...) custom-call(bf16[192,2048]{1,0:T(8,128)(2,1)} %copy-done.23, ...), custom_call_target="tpu_custom_call", output_to_operand_aliasing={{0}: (8, {}), {1}: (9, {}), {2}: (10, {}), {3}: (11, {})} | custom-call | bytes 1000000 | tf_op jit(solution)/shard_map/hidden_units/pallas_call | solution.py:740
  360.4 10.4 %convolution_convert_fusion.2 = bf16[1024,2048]{1,0:T(8,128)(2,1)S(1)} fusion(bf16[1536,1024]{1,0:T(8,128)(2,1)} %get-tuple-element.364, bf16[1536,2048]{1,0:T(8,128)(2,1)} %get-tuple-element.365), kind=kOutput, calls=%fused_computation.10 | convolution fusion | flops 6444548096 | bytes 13631488 | tf_op jit(solution)/shard_map/dot_general | solution.py:946
  375.4 15.4 %convolution_convert_fusion.1 = bf16[2048,2048]{1,0:T(8,128)(2,1)} fusion(bf16[1536,2048]{1,0:T(8,128)(2,1)S(1)} %copy-done.1, bf16[1536,2048]{1,0:T(8,128)(2,1)S(1)} %copy-done), kind=kOutput, calls=%fused_computation.3 | convolution fusion | flops 12889096192 | bytes 20971520 | tf_op jit(solution)/shard_map/dot_general | solution.py:946
  393.8 4.8 dynamic-slice_bitcast_fusion
  402.5 8.1 %collective-permute-done.55 = bf16[96,2048]{1,0:T(8,128)(2,1)S(1)} collective-permute-done((bf16[96,2048]{1,0:T(8,128)(2,1)}, bf16[96,2048]{1,0:T(8,128)(2,1)S(1)}, u32[]{:S(2)}, u32[]{:S(2)}) %collective-permute-start.55) | collective-permute-done | bytes 393248 | tf_op jit(solution)/shard_map/ppermute | solution.py:379
  412.7 7.8 %fusion = bf16[2,4,128,2048]{3,2,1,0:T(8,128)(2,1)} fusion(bf16[2,4,128,2048]{3,2,1,0:T(8,128)(2,1)} %collective-permute-done.52, bf16[2,2,4,128,2048]{4,3,2,1,0:T(8,128)(2,1)} %bitcast.158, s32[]{:T(128)S(6)} %select_n.339), kind=kLoop, calls=%fused_computation.1 | loop fusion | flops 8388608 | bytes 12582916 | tf_op jit(solution)/shard_map/convert_element_type | solution.py:499
  420.5 16.4 %collective-permute-done.51.refs_3_ = bf16[192,2048]{1,0:T(8,128)(2,1)} collective-permute-done((bf16[192,2048]{1,0:T(8,128)(2,1)}, bf16[192,2048]{1,0:T(8,128)(2,1)}, u32[]{:S(2)}, u32[]{:S(2)}) %collective-permute-start.51) | collective-permute-done | bytes 786464 | tf_op jit(solution)/shard_map/ppermute | solution.py:379
  436.9 5.3 close_hidden.1
  446.3 16.2 %collective-permute-done.57.refs_1_ = bf16[192,2048]{1,0:T(8,128)(2,1)S(1)} collective-permute-done((bf16[192,2048]{1,0:T(8,128)(2,1)S(1)}, bf16[192,2048]{1,0:T(8,128)(2,1)S(1)}, u32[]{:S(2)}, u32[]{:S(2)}) %collective-permute-start.57) | collective-permute-done | bytes 786464 | tf_op jit(solution)/shard_map/ppermute | solution.py:379
  466.4 14.5 %attend_back.2 = (bf16[768,2048]{1,0:T(8,128)(2,1)}, bf16[384,512]{1,0:T(8,128)(2,1)}, f32[384,1024]{1,0:T(8,128)}, bf16[384,1024]{1,0:T(8,128)(2,1)}) custom-call(bf16[192,2048]{1,0:T(8,128)(2,1)} %get-tuple-element.398.refs_0_, bf16[192,2048]{1,0:T(8,128)(2,1)} %copy-done.20, bf16[512,2048]{1,0:T(8,128)(2,1)} %bitcast.148, ...), custom_call_target="tpu_custom_call" | custom-call | bytes 1000000 | tf_op jit(solution)/shard_map/attend_back/pallas_call | solution.py:740
  481.8 14.9 %attend_back.3 = (bf16[768,2048]{1,0:T(8,128)(2,1)}, bf16[384,512]{1,0:T(8,128)(2,1)}, f32[384,1024]{1,0:T(8,128)}, bf16[384,1024]{1,0:T(8,128)(2,1)}) custom-call(bf16[192,2048]{1,0:T(8,128)(2,1)} %copy-done.19, bf16[96,2048]{1,0:T(8,128)(2,1)} %copy-done.62, bf16[96,2048]{1,0:T(8,128)(2,1)} %copy-done.63, ...), custom_call_target="tpu_custom_call", output_to_operand_aliasing={{0}: (12, {})} | custom-call | bytes 1000000 | tf_op jit(solution)/shard_map/attend_back/pallas_call | solution.py:740
  498.6 3.7 convolution_convert_fusion.3
  503.2 3.5 join_grads.2.refs_5_
  509.2 3.8 join_grads.3.refs_0_
  513.0 7.5 %convolution_convert_fusion = bf16[2048,1536]{1,0:T(8,128)(2,1)S(1)} fusion(bf16[768,2048]{1,0:T(8,128)(2,1)} %constant_dynamic-update-slice_fusion.a_ref.a2_ref, bf16[768,1536]{1,0:T(8,128)(2,1)} %join_grads.3.refs_0_), kind=kOutput, calls=%fused_computation.2 | convolution fusion | flops 4834983936 | bytes 11796480 | tf_op jit(solution)/shard_map/dot_general | solution.py:946
  530.6 10.6 %input_terms.1 = (bf16[192,2048]{1,0:T(8,128)(2,1)}, bf16[192,2048]{1,0:T(8,128)(2,1)}, bf16[192,2048]{1,0:T(8,128)(2,1)}, bf16[96,2048]{1,0:T(8,128)(2,1)}, bf16[96,2048]{1,0:T(8,128)(2,1)}) custom-call(bf16[768,1536]{1,0:T(8,128)(2,1)} %join_grads.3.refs_0_, bf16[1024,1536]{1,0:T(8,128)(2,1)} %bitcast.152, ...), custom_call_target="tpu_custom_call" | custom-call | bytes 1000000 | tf_op jit(solution)/shard_map/input_terms/pallas_call | solution.py:740
  542.6 4.4 fusion.1
  549.7 9.8 %collective-permute-done.68 = bf16[64,2048]{1,0:T(8,128)(2,1)S(1)} collective-permute-done((bf16[64,2048]{1,0:T(8,128)(2,1)S(1)}, bf16[64,2048]{1,0:T(8,128)(2,1)S(1)}, u32[]{:S(2)}, u32[]{:S(2)}) %collective-permute-start.68) | collective-permute-done | bytes 262176 | tf_op jit(solution)/shard_map/ppermute | solution.py:379
  560.2 3.8 all-to-all-start.1
  574.3 4.5 collective-permute-done.73
  578.8 8.5 %collective-permute-done.74 = bf16[96,2048]{1,0:T(8,128)(2,1)} collective-permute-done((bf16[96,2048]{1,0:T(8,128)(2,1)}, bf16[96,2048]{1,0:T(8,128)(2,1)}, u32[]{:S(2)}, u32[]{:S(2)}) %collective-permute-start.74) | collective-permute-done | bytes 393248 | tf_op jit(solution)/shard_map/ppermute | solution.py:379
  596.1 7.6 %collective-permute-done.76.refs_2_ = bf16[192,2048]{1,0:T(8,128)(2,1)S(1)} collective-permute-done((bf16[192,2048]{1,0:T(8,128)(2,1)}, bf16[192,2048]{1,0:T(8,128)(2,1)S(1)}, u32[]{:S(2)}, u32[]{:S(2)}) %collective-permute-start.76) | collective-permute-done | bytes 786464 | tf_op jit(solution)/shard_map/ppermute | solution.py:379
  603.7 3.4 collective-permute-done.72
  608.0 3.2 fusion.4
  613.2 4.3 close_input.1
  617.6 15.0 %collective-permute-done.79 = bf16[256,1536]{1,0:T(8,128)(2,1)} collective-permute-done((bf16[256,1536]{1,0:T(8,128)(2,1)}, bf16[256,1536]{1,0:T(8,128)(2,1)}, u32[]{:S(2)}, u32[]{:S(2)}) %collective-permute-start.79) | collective-permute-done | bytes 786464 | tf_op jit(solution)/shard_map/ppermute | solution.py:379
  632.6 14.6 %collective-permute-done.78 = bf16[256,1536]{1,0:T(8,128)(2,1)} collective-permute-done((bf16[256,1536]{1,0:T(8,128)(2,1)}, bf16[256,1536]{1,0:T(8,128)(2,1)}, u32[]{:S(2)}, u32[]{:S(2)}) %collective-permute-start.78) | collective-permute-done | bytes 786464 | tf_op jit(solution)/shard_map/ppermute | solution.py:379
  662.0 10.4 %finish_columns.2 = (f32[128,8192]{1,0:T(8,128)}, f32[128,8192]{1,0:T(8,128)}, f32[128,1024]{1,0:T(8,128)}) custom-call(s32[1]{0:T(128)} %bitcast.1.table_ref.seq_ref, bf16[2,2,128,2048]{3,2,1,0:T(8,128)(2,1)} %bitcast.153, bf16[2,2,128,2048]{3,2,1,0:T(8,128)(2,1)} %bitcast.154, bf16[2,2,128,2048]{3,2,1,0:T(8,128)(2,1)} %bitcast.63.refs_2_.refs_3_, ...), custom_call_target="tpu_custom_call" | custom-call | bytes 1000000 | tf_op jit(solution)/shard_map/finish_columns/pallas_call | solution.py:551
  680.1 7.1 %finish_columns.3 = (f32[128,2048]{1,0:T(8,128)}, f32[128,2048]{1,0:T(8,128)}, f32[128,2048]{1,0:T(8,128)}, f32[128,256]{1,0:T(8,128)}) custom-call(s32[1]{0:T(128)} %bitcast.1.table_ref.seq_ref, bf16[2,128,1536]{2,1,0:T(8,128)(2,1)} %pad_maximum_fusion.18.refs_0_.refs_1_.refs_2_, bf16[2,128,1536]{2,1,0:T(8,128)(2,1)} %pad_maximum_fusion.18.refs_0_.refs_1_.refs_2_, ...), custom_call_target="tpu_custom_call" | custom-call | bytes 1000000 | tf_op jit(solution)/shard_map/finish_columns/pallas_call | solution.py:551
  (457 shorter events, 206.1 us)
Async XLA Ops:
  10.5 39.8 %collective-permute-start.5 = (bf16[192,2048]{1,0:T(8,128)(2,1)}, bf16[192,2048]{1,0:T(8,128)(2,1)}, u32[]{:S(2)}, u32[]{:S(2)}) collective-permute-start(bf16[192,2048]{1,0:T(8,128)(2,1)} %bitcast.176), channel_id=1, source_target_pairs={{0,1},{1,0},{2,3},{3,2},{4,5},{5,4},{6,7},{7,6},{8,9},{9,8},{10,11... | collective-permute-start | bytes 2359304 | tf_op jit(solution)/shard_map/ppermute | solution.py:379
  14.1 20.8 %collective-permute-start.6 = (s32[768]{0:T(1024)S(1)}, s32[768]{0:T(1024)}, u32[]{:S(2)}, u32[]{:S(2)}) collective-permute-start(s32[768]{0:T(1024)S(1)} %convert_reduce_fusion), channel_id=1, source_target_pairs={{0,16},{16,0},{1,17},{17,1},{2,18},{18,2},{3,19},{19,3},{4,20},{20... | collective-permute-start | bytes 9224 | tf_op jit(solution)/shard_map/ppermute | solution.py:379
  50.3 40.7 %collective-permute-start.7 = (bf16[2,128,1536]{2,1,0:T(8,128)(2,1)S(1)}, bf16[2,128,1536]{2,1,0:T(8,128)(2,1)S(1)}, u32[]{:S(2)}, u32[]{:S(2)}) collective-permute-start(bf16[2,128,1536]{2,1,0:T(8,128)(2,1)S(1)} %pad_maximum_fusion.7), channel_id=1, source_target_pairs={{0,2},{2,0},{1,3},{3,1},{4,6},{6,4},{5,7},{7,5},{8,10},{10,8},{9,1... | collective-permute-start | bytes 2359304 | tf_op jit(solution)/shard_map/ppermute | solution.py:379
  50.3 40.7 %collective-permute-start.8 = (bf16[2,128,1536]{2,1,0:T(8,128)(2,1)S(1)}, bf16[2,128,1536]{2,1,0:T(8,128)(2,1)S(1)}, u32[]{:S(2)}, u32[]{:S(2)}) collective-permute-start(bf16[2,128,1536]{2,1,0:T(8,128)(2,1)S(1)} %pad_maximum_fusion.7), channel_id=1, source_target_pairs={{0,1},{1,0},{2,3},{3,2},{4,5},{5,4},{6,7},{7,6},{8,9},{9,8},{10,11... | collective-permute-start | bytes 2359304 | tf_op jit(solution)/shard_map/ppermute | solution.py:379
  52.2 38.9 %collective-permute-start.10 = (bf16[192,2048]{1,0:T(8,128)(2,1)S(1)}, bf16[192,2048]{1,0:T(8,128)(2,1)S(1)}, u32[]{:S(2)}, u32[]{:S(2)}) collective-permute-start(bf16[192,2048]{1,0:T(8,128)(2,1)S(1)} %copy-done.16), channel_id=1, source_target_pairs={{0,16},{16,0},{1,17},{17,1},{2,18},{18,2},{3,19},{19,3},{4,20},{20... | collective-permute-start | bytes 2359304 | tf_op jit(solution)/shard_map/ppermute | solution.py:379
  52.8 38.3 %collective-permute-start.9 = (bf16[192,2048]{1,0:T(8,128)(2,1)S(1)}, bf16[192,2048]{1,0:T(8,128)(2,1)S(1)}, u32[]{:S(2)}, u32[]{:S(2)}) collective-permute-start(bf16[192,2048]{1,0:T(8,128)(2,1)S(1)} %copy-done.16), channel_id=1, source_target_pairs={{0,8},{8,0},{1,9},{9,1},{2,10},{10,2},{3,11},{11,3},{4,12},{12,4},... | collective-permute-start | bytes 2359304 | tf_op jit(solution)/shard_map/ppermute | solution.py:379
  58.5 32.6 %collective-permute-start.11 = (bf16[64,2048]{1,0:T(8,128)(2,1)S(1)}, bf16[64,2048]{1,0:T(8,128)(2,1)S(1)}, u32[]{:S(2)}, u32[]{:S(2)}) collective-permute-start(bf16[64,2048]{1,0:T(8,128)(2,1)S(1)} %copy-done.67), channel_id=1, source_target_pairs={{0,1},{1,0},{2,3},{3,2},{4,5},{5,4},{6,7},{7,6},{8,9},{9,8},{10,11... | collective-permute-start | bytes 786440 | tf_op jit(solution)/shard_map/ppermute | solution.py:379
  114.5 45.1 %collective-permute-start.15 = (bf16[1024,1536]{1,0:T(8,128)(2,1)S(1)}, bf16[1024,1536]{1,0:T(8,128)(2,1)}, u32[]{:S(2)}, u32[]{:S(2)}) collective-permute-start(bf16[1024,1536]{1,0:T(8,128)(2,1)S(1)} %bitcast.150), channel_id=1, source_target_pairs={{0,4},{4,0},{1,5},{5,1},{2,6},{6,2},{3,7},{7,3},{8,12},{12,8},{9,1... | collective-permute-start | bytes 9437192 | tf_op jit(solution)/shard_map/ppermute | solution.py:379
  116.1 58.9 %all-to-all-start = ((bf16[4,128,2048]{2,1,0:T(8,128)(2,1)}), bf16[4,128,2048]{2,1,0:T(8,128)(2,1)}, u32[]{:S(2)}, u32[]{:S(2)}) async-start(bf16[4,128,2048]{2,1,0:T(8,128)(2,1)} %column_slices.3), calls=%async_computation | async-start | bytes 4194304 | tf_op jit(solution)/shard_map/all_to_all | solution.py:479
  120.6 160.1 %all-gather.2.cloned.1.call-start = ((), (), s32[]{:S(2)}) async-start(), calls=%async_computation.4 | async-start | bytes 10485760 | tf_op jit(solution)/shard_map/all_gather | solution.py:1042
  122.8 36.7 %collective-permute-start.16 = (bf16[192,2048]{1,0:T(8,128)(2,1)}, bf16[192,2048]{1,0:T(8,128)(2,1)}, u32[]{:S(2)}, u32[]{:S(2)}) collective-permute-start(bf16[192,2048]{1,0:T(8,128)(2,1)} %slice.104), channel_id=1, source_target_pairs={{0,2},{2,0},{1,3},{3,1},{4,6},{6,4},{5,7},{7,5},{8,10},{10,8},{9,1... | collective-permute-start | bytes 2359304 | tf_op jit(solution)/shard_map/ppermute | solution.py:379
  125.0 50.0 %collective-permute-start.18 = (bf16[192,2048]{1,0:T(8,128)(2,1)}, bf16[192,2048]{1,0:T(8,128)(2,1)}, u32[]{:S(2)}, u32[]{:S(2)}) collective-permute-start(bf16[192,2048]{1,0:T(8,128)(2,1)} %bitcast.177), channel_id=1, source_target_pairs={{0,8},{8,0},{1,9},{9,1},{2,10},{10,2},{3,11},{11,3},{4,12},{12,4},... | collective-permute-start | bytes 2359304 | tf_op jit(solution)/shard_map/ppermute | solution.py:379
  126.8 48.2 %collective-permute-start.19 = (bf16[192,2048]{1,0:T(8,128)(2,1)}, bf16[192,2048]{1,0:T(8,128)(2,1)}, u32[]{:S(2)}, u32[]{:S(2)}) collective-permute-start(bf16[192,2048]{1,0:T(8,128)(2,1)} %bitcast.178), channel_id=1, source_target_pairs={{0,16},{16,0},{1,17},{17,1},{2,18},{18,2},{3,19},{19,3},{4,20},{20... | collective-permute-start | bytes 2359304 | tf_op jit(solution)/shard_map/ppermute | solution.py:379
  175.0 290.0 %reduce-scatter.3.cloned.1.call-start = ((), (), s32[]{:S(2)}) async-start(), calls=%async_computation.5 | async-start | bytes 3145728 | tf_op jit(solution)/shard_map/reduce_scatter | solution.py:1093
  237.6 20.7 %collective-permute-start.29 = (bf16[192,2048]{1,0:T(8,128)(2,1)}, bf16[192,2048]{1,0:T(8,128)(2,1)S(1)}, u32[]{:S(2)}, u32[]{:S(2)}) collective-permute-start(bf16[192,2048]{1,0:T(8,128)(2,1)} %get-tuple-element.309.refs_0_), channel_id=1, source_target_pairs={{0,8},{8,0},{1,9},{9,1},{2,10},{10,2},{3,11},{11,3},{4,12},{12,4},... | collective-permute-start | bytes 2359304 | tf_op jit(solution)/shard_map/ppermute | solution.py:379
  238.8 20.7 %collective-permute-start.30 = (bf16[192,2048]{1,0:T(8,128)(2,1)}, bf16[192,2048]{1,0:T(8,128)(2,1)S(1)}, u32[]{:S(2)}, u32[]{:S(2)}) collective-permute-start(bf16[192,2048]{1,0:T(8,128)(2,1)} %get-tuple-element.309.refs_0_), channel_id=1, source_target_pairs={{0,16},{16,0},{1,17},{17,1},{2,18},{18,2},{3,19},{19,3},{4,20},{20... | collective-permute-start | bytes 2359304 | tf_op jit(solution)/shard_map/ppermute | solution.py:379
  239.7 32.6 %collective-permute-start.31 = (bf16[192,2048]{1,0:T(8,128)(2,1)}, bf16[192,2048]{1,0:T(8,128)(2,1)S(1)}, u32[]{:S(2)}, u32[]{:S(2)}) collective-permute-start(bf16[192,2048]{1,0:T(8,128)(2,1)} %collective-permute-done.5.refs_2_), channel_id=1, source_target_pairs={{0,8},{8,0},{1,9},{9,1},{2,10},{10,2},{3,11},{11,3},{4,12},{12,4},... | collective-permute-start | bytes 2359304 | tf_op jit(solution)/shard_map/ppermute | solution.py:379
  240.8 32.7 %collective-permute-start.32 = (bf16[192,2048]{1,0:T(8,128)(2,1)}, bf16[192,2048]{1,0:T(8,128)(2,1)S(1)}, u32[]{:S(2)}, u32[]{:S(2)}) collective-permute-start(bf16[192,2048]{1,0:T(8,128)(2,1)} %collective-permute-done.5.refs_2_), channel_id=1, source_target_pairs={{0,16},{16,0},{1,17},{17,1},{2,18},{18,2},{3,19},{19,3},{4,20},{20... | collective-permute-start | bytes 2359304 | tf_op jit(solution)/shard_map/ppermute | solution.py:379
  241.7 56.1 %collective-permute-start.35 = (bf16[192,2048]{1,0:T(8,128)(2,1)}, bf16[192,2048]{1,0:T(8,128)(2,1)}, u32[]{:S(2)}, u32[]{:S(2)}) collective-permute-start(bf16[192,2048]{1,0:T(8,128)(2,1)} %get-tuple-element.309.refs_0_), channel_id=1, source_target_pairs={{0,1},{1,0},{2,3},{3,2},{4,5},{5,4},{6,7},{7,6},{8,9},{9,8},{10,11... | collective-permute-start | bytes 2359304 | tf_op jit(solution)/shard_map/ppermute | solution.py:379
  274.3 23.5 %collective-permute-start.33 = (bf16[96,2048]{1,0:T(8,128)(2,1)}, bf16[96,2048]{1,0:T(8,128)(2,1)}, u32[]{:S(2)}, u32[]{:S(2)}) collective-permute-start(bf16[96,2048]{1,0:T(8,128)(2,1)} %slice.112), channel_id=1, source_target_pairs={{0,8},{8,0},{1,9},{9,1},{2,10},{10,2},{3,11},{11,3},{4,12},{12,4},... | collective-permute-start | bytes 1179656 | tf_op jit(solution)/shard_map/ppermute | solution.py:379
  275.7 22.2 %collective-permute-start.34 = (bf16[96,2048]{1,0:T(8,128)(2,1)}, bf16[96,2048]{1,0:T(8,128)(2,1)}, u32[]{:S(2)}, u32[]{:S(2)}) collective-permute-start(bf16[96,2048]{1,0:T(8,128)(2,1)} %slice.113), channel_id=1, source_target_pairs={{0,16},{16,0},{1,17},{17,1},{2,18},{18,2},{3,19},{19,3},{4,20},{20... | collective-permute-start | bytes 1179656 | tf_op jit(solution)/shard_map/ppermute | solution.py:379
  277.5 20.3 %collective-permute-start.36 = (bf16[96,2048]{1,0:T(8,128)(2,1)}, bf16[96,2048]{1,0:T(8,128)(2,1)S(1)}, u32[]{:S(2)}, u32[]{:S(2)}) collective-permute-start(bf16[96,2048]{1,0:T(8,128)(2,1)} %slice.114), channel_id=1, source_target_pairs={{0,8},{8,0},{1,9},{9,1},{2,10},{10,2},{3,11},{11,3},{4,12},{12,4},... | collective-permute-start | bytes 1179656 | tf_op jit(solution)/shard_map/ppermute | solution.py:379
  317.0 21.6 %collective-permute-start.40 = (bf16[96,2048]{1,0:T(8,128)(2,1)S(1)}, bf16[96,2048]{1,0:T(8,128)(2,1)S(1)}, u32[]{:S(2)}, u32[]{:S(2)}) collective-permute-start(bf16[96,2048]{1,0:T(8,128)(2,1)S(1)} %slice.116), channel_id=1, source_target_pairs={{0,8},{8,0},{1,9},{9,1},{2,10},{10,2},{3,11},{11,3},{4,12},{12,4},... | collective-permute-start | bytes 1179656 | tf_op jit(solution)/shard_map/ppermute | solution.py:379
  318.2 20.4 %collective-permute-start.41 = (bf16[96,2048]{1,0:T(8,128)(2,1)S(1)}, bf16[96,2048]{1,0:T(8,128)(2,1)S(1)}, u32[]{:S(2)}, u32[]{:S(2)}) collective-permute-start(bf16[96,2048]{1,0:T(8,128)(2,1)S(1)} %slice.117), channel_id=1, source_target_pairs={{0,16},{16,0},{1,17},{17,1},{2,18},{18,2},{3,19},{19,3},{4,20},{20... | collective-permute-start | bytes 1179656 | tf_op jit(solution)/shard_map/ppermute | solution.py:379
  319.4 19.2 %collective-permute-start.42 = (bf16[96,2048]{1,0:T(8,128)(2,1)}, bf16[96,2048]{1,0:T(8,128)(2,1)S(1)}, u32[]{:S(2)}, u32[]{:S(2)}) collective-permute-start(bf16[96,2048]{1,0:T(8,128)(2,1)} %get-tuple-element.345), channel_id=1, source_target_pairs={{0,8},{8,0},{1,9},{9,1},{2,10},{10,2},{3,11},{11,3},{4,12},{12,4},... | collective-permute-start | bytes 1179656 | tf_op jit(solution)/shard_map/ppermute | solution.py:379
  338.8 19.7 %collective-permute-start.45 = (bf16[192,2048]{1,0:T(8,128)(2,1)S(1)}, bf16[192,2048]{1,0:T(8,128)(2,1)S(1)}, u32[]{:S(2)}, u32[]{:S(2)}) collective-permute-start(bf16[192,2048]{1,0:T(8,128)(2,1)S(1)} %pad_maximum_fusion.11), channel_id=1, source_target_pairs={{0,16},{16,0},{1,17},{17,1},{2,18},{18,2},{3,19},{19,3},{4,20},{20... | collective-permute-start | bytes 2359304 | tf_op jit(solution)/shard_map/ppermute | solution.py:379
  371.1 21.9 %collective-permute-start.50 = (bf16[192,2048]{1,0:T(8,128)(2,1)S(1)}, bf16[192,2048]{1,0:T(8,128)(2,1)S(1)}, u32[]{:S(2)}, u32[]{:S(2)}) collective-permute-start(bf16[192,2048]{1,0:T(8,128)(2,1)S(1)} %pad_maximum_fusion.13), channel_id=1, source_target_pairs={{0,16},{16,0},{1,17},{17,1},{2,18},{18,2},{3,19},{19,3},{4,20},{20... | collective-permute-start | bytes 2359304 | tf_op jit(solution)/shard_map/ppermute | solution.py:379
  372.8 20.1 %collective-permute-start.49 = (bf16[192,2048]{1,0:T(8,128)(2,1)S(1)}, bf16[192,2048]{1,0:T(8,128)(2,1)S(1)}, u32[]{:S(2)}, u32[]{:S(2)}) collective-permute-start(bf16[192,2048]{1,0:T(8,128)(2,1)S(1)} %pad_maximum_fusion.12), channel_id=1, source_target_pairs={{0,8},{8,0},{1,9},{9,1},{2,10},{10,2},{3,11},{11,3},{4,12},{12,4},... | collective-permute-start | bytes 2359304 | tf_op jit(solution)/shard_map/ppermute | solution.py:379
  398.7 160.8 %reduce-scatter.5.cloned.1.call-start = ((), (), s32[]{:S(2)}) async-start(), calls=%async_computation.6 | async-start | bytes 6291456 | tf_op jit(solution)/shard_map/reduce_scatter | solution.py:1103
  401.9 35.0 %collective-permute-start.51 = (bf16[192,2048]{1,0:T(8,128)(2,1)}, bf16[192,2048]{1,0:T(8,128)(2,1)}, u32[]{:S(2)}, u32[]{:S(2)}) collective-permute-start(bf16[192,2048]{1,0:T(8,128)(2,1)} %add_convert_fusion.3), channel_id=1, source_target_pairs={{0,1},{1,0},{2,3},{3,2},{4,5},{5,4},{6,7},{7,6},{8,9},{9,8},{10,11... | collective-permute-start | bytes 2359304 | tf_op jit(solution)/shard_map/ppermute | solution.py:379
  410.7 31.5 %collective-permute-start.56 = (bf16[192,2048]{1,0:T(8,128)(2,1)S(1)}, bf16[192,2048]{1,0:T(8,128)(2,1)S(1)}, u32[]{:S(2)}, u32[]{:S(2)}) collective-permute-start(bf16[192,2048]{1,0:T(8,128)(2,1)S(1)} %pad_maximum_fusion.15), channel_id=1, source_target_pairs={{0,16},{16,0},{1,17},{17,1},{2,18},{18,2},{3,19},{19,3},{4,20},{20... | collective-permute-start | bytes 2359304 | tf_op jit(solution)/shard_map/ppermute | solution.py:379
  411.5 30.7 %collective-permute-start.54 = (bf16[192,2048]{1,0:T(8,128)(2,1)S(1)}, bf16[192,2048]{1,0:T(8,128)(2,1)S(1)}, u32[]{:S(2)}, u32[]{:S(2)}) collective-permute-start(bf16[192,2048]{1,0:T(8,128)(2,1)S(1)} %pad_maximum_fusion.14), channel_id=1, source_target_pairs={{0,8},{8,0},{1,9},{9,1},{2,10},{10,2},{3,11},{11,3},{4,12},{12,4},... | collective-permute-start | bytes 2359304 | tf_op jit(solution)/shard_map/ppermute | solution.py:379
  465.0 41.7 %collective-permute-start.65 = (bf16[256,2048]{1,0:T(8,128)(2,1)}, bf16[256,2048]{1,0:T(8,128)(2,1)S(1)}, u32[]{:S(2)}, u32[]{:S(2)}) collective-permute-start(bf16[256,2048]{1,0:T(8,128)(2,1)} %bitcast.174), channel_id=1, source_target_pairs={{0,16},{16,0},{1,17},{17,1},{2,18},{18,2},{3,19},{19,3},{4,20},{20... | collective-permute-start | bytes 3145736 | tf_op jit(solution)/shard_map/ppermute | solution.py:379
  481.0 21.4 %collective-permute-start.61 = (bf16[384,1024]{1,0:T(8,128)(2,1)}, bf16[384,1024]{1,0:T(8,128)(2,1)S(1)}, u32[]{:S(2)}, u32[]{:S(2)}) collective-permute-start(bf16[384,1024]{1,0:T(8,128)(2,1)} %get-tuple-element.414), channel_id=1, source_target_pairs={{0,4},{4,0},{1,5},{5,1},{2,6},{6,2},{3,7},{7,3},{8,12},{12,8},{9,1... | collective-permute-start | bytes 2359304 | tf_op jit(solution)/shard_map/ppermute | solution.py:379
  527.2 20.3 %collective-permute-start.70 = (bf16[192,2048]{1,0:T(8,128)(2,1)}, bf16[192,2048]{1,0:T(8,128)(2,1)}, u32[]{:S(2)}, u32[]{:S(2)}) collective-permute-start(bf16[192,2048]{1,0:T(8,128)(2,1)} %pad_maximum_fusion.17), channel_id=1, source_target_pairs={{0,16},{16,0},{1,17},{17,1},{2,18},{18,2},{3,19},{19,3},{4,20},{20... | collective-permute-start | bytes 2359304 | tf_op jit(solution)/shard_map/ppermute | solution.py:379
  529.8 20.0 %collective-permute-start.69 = (bf16[192,2048]{1,0:T(8,128)(2,1)}, bf16[192,2048]{1,0:T(8,128)(2,1)}, u32[]{:S(2)}, u32[]{:S(2)}) collective-permute-start(bf16[192,2048]{1,0:T(8,128)(2,1)} %pad_maximum_fusion.16), channel_id=1, source_target_pairs={{0,8},{8,0},{1,9},{9,1},{2,10},{10,2},{3,11},{11,3},{4,12},{12,4},... | collective-permute-start | bytes 2359304 | tf_op jit(solution)/shard_map/ppermute | solution.py:379
  560.2 47.8 %all-to-all-start.1 = ((bf16[4,128,2048]{2,1,0:T(8,128)(2,1)}), bf16[4,128,2048]{2,1,0:T(8,128)(2,1)S(1)}, u32[]{:S(2)}, u32[]{:S(2)}) async-start(bf16[4,128,2048]{2,1,0:T(8,128)(2,1)} %bitcast.181), calls=%async_computation.3 | async-start | bytes 4194304 | tf_op jit(solution)/shard_map/all_to_all | solution.py:479
  566.7 24.0 %collective-permute-start.77 = (bf16[256,2048]{1,0:T(8,128)(2,1)}, bf16[256,2048]{1,0:T(8,128)(2,1)}, u32[]{:S(2)}, u32[]{:S(2)}) collective-permute-start(bf16[256,2048]{1,0:T(8,128)(2,1)} %broadcast_select_fusion.4), channel_id=1, source_target_pairs={{0,4},{4,0},{1,5},{5,1},{2,6},{6,2},{3,7},{7,3},{8,12},{12,8},{9,1... | collective-permute-start | bytes 3145736 | tf_op jit(solution)/shard_map/ppermute | solution.py:379
  568.7 35.0 %collective-permute-start.76 = (bf16[192,2048]{1,0:T(8,128)(2,1)}, bf16[192,2048]{1,0:T(8,128)(2,1)S(1)}, u32[]{:S(2)}, u32[]{:S(2)}) collective-permute-start(bf16[192,2048]{1,0:T(8,128)(2,1)} %get-tuple-element.445), channel_id=1, source_target_pairs={{0,16},{16,0},{1,17},{17,1},{2,18},{18,2},{3,19},{19,3},{4,20},{20... | collective-permute-start | bytes 2359304 | tf_op jit(solution)/shard_map/ppermute | solution.py:379
  572.5 34.6 %collective-permute-start.72 = (bf16[256,1536]{1,0:T(8,128)(2,1)S(1)}, bf16[256,1536]{1,0:T(8,128)(2,1)S(1)}, u32[]{:S(2)}, u32[]{:S(2)}) collective-permute-start(bf16[256,1536]{1,0:T(8,128)(2,1)S(1)} %get-tuple-element.474), channel_id=1, source_target_pairs={{0,1},{1,0},{2,3},{3,2},{4,5},{5,4},{6,7},{7,6},{8,9},{9,8},{10,11... | collective-permute-start | bytes 2359304 | tf_op jit(solution)/shard_map/ppermute | solution.py:379
  588.6 19.4 %collective-permute-start.75 = (bf16[192,2048]{1,0:T(8,128)(2,1)S(1)}, bf16[192,2048]{1,0:T(8,128)(2,1)}, u32[]{:S(2)}, u32[]{:S(2)}) collective-permute-start(bf16[192,2048]{1,0:T(8,128)(2,1)S(1)} %add_convert_fusion), channel_id=1, source_target_pairs={{0,8},{8,0},{1,9},{9,1},{2,10},{10,2},{3,11},{11,3},{4,12},{12,4},... | collective-permute-start | bytes 2359304 | tf_op jit(solution)/shard_map/ppermute | solution.py:379
  594.6 38.0 %collective-permute-start.79 = (bf16[256,1536]{1,0:T(8,128)(2,1)}, bf16[256,1536]{1,0:T(8,128)(2,1)}, u32[]{:S(2)}, u32[]{:S(2)}) collective-permute-start(bf16[256,1536]{1,0:T(8,128)(2,1)} %get-tuple-element.473), channel_id=1, source_target_pairs={{0,1},{1,0},{2,3},{3,2},{4,5},{5,4},{6,7},{7,6},{8,9},{9,8},{10,11... | collective-permute-start | bytes 2359304 | tf_op jit(solution)/shard_map/ppermute | solution.py:379
  611.2 36.0 %collective-permute-start.78 = (bf16[256,1536]{1,0:T(8,128)(2,1)}, bf16[256,1536]{1,0:T(8,128)(2,1)}, u32[]{:S(2)}, u32[]{:S(2)}) collective-permute-start(bf16[256,1536]{1,0:T(8,128)(2,1)} %fusion.4), channel_id=1, source_target_pairs={{0,2},{2,0},{1,3},{3,1},{4,6},{6,4},{5,7},{7,5},{8,10},{10,8},{9,1... | collective-permute-start | bytes 2359304 | tf_op jit(solution)/shard_map/ppermute | solution.py:379
  611.8 50.1 %collective-permute-start.84 = (bf16[4,128,2048]{2,1,0:T(8,128)(2,1)S(1)}, bf16[4,128,2048]{2,1,0:T(8,128)(2,1)}, u32[]{:S(2)}, u32[]{:S(2)}) collective-permute-start(bf16[4,128,2048]{2,1,0:T(8,128)(2,1)S(1)} %all-to-all-done.1), channel_id=1, source_target_pairs={{0,16},{16,0},{1,17},{17,1},{2,18},{18,2},{3,19},{19,3},{4,20},{20... | collective-permute-start | bytes 6291464 | tf_op jit(solution)/shard_map/ppermute | solution.py:379
  651.5 23.0 %collective-permute-start.85 = (bf16[64,2048]{1,0:T(8,128)(2,1)}, bf16[64,2048]{1,0:T(8,128)(2,1)}, u32[]{:S(2)}, u32[]{:S(2)}) collective-permute-start(bf16[64,2048]{1,0:T(8,128)(2,1)} %fusion.8), channel_id=1, source_target_pairs={{0,2},{2,0},{1,3},{3,1},{4,6},{6,4},{5,7},{7,5},{8,10},{10,8},{9,1... | collective-permute-start | bytes 786440 | tf_op jit(solution)/shard_map/ppermute | solution.py:379
  651.5 22.5 %collective-permute-start.80 = (bf16[128,1536]{1,0:T(8,128)(2,1)S(1)}, bf16[128,1536]{1,0:T(8,128)(2,1)}, u32[]{:S(2)}, u32[]{:S(2)}) collective-permute-start(bf16[128,1536]{1,0:T(8,128)(2,1)S(1)} %get-tuple-element.458), channel_id=1, source_target_pairs={{0,16},{16,0},{1,17},{17,1},{2,18},{18,2},{3,19},{19,3},{4,20},{20... | collective-permute-start | bytes 1179656 | tf_op jit(solution)/shard_map/ppermute | solution.py:379
  653.6 20.5 %collective-permute-start.83 = (bf16[64,2048]{1,0:T(8,128)(2,1)}, bf16[64,2048]{1,0:T(8,128)(2,1)}, u32[]{:S(2)}, u32[]{:S(2)}) collective-permute-start(bf16[64,2048]{1,0:T(8,128)(2,1)} %dynamic-slice_bitcast_fusion.8), channel_id=1, source_target_pairs={{0,1},{1,0},{2,3},{3,2},{4,5},{5,4},{6,7},{7,6},{8,9},{9,8},{10,11... | collective-permute-start | bytes 786440 | tf_op jit(solution)/shard_map/ppermute | solution.py:379
  661.9 27.9 %collective-permute-start.71 = (bf16[192,2048]{1,0:T(8,128)(2,1)}, bf16[192,2048]{1,0:T(8,128)(2,1)}, u32[]{:S(2)}, u32[]{:S(2)}) collective-permute-start(bf16[192,2048]{1,0:T(8,128)(2,1)} %add_convert_fusion.2), channel_id=1, source_target_pairs={{0,1},{1,0},{2,3},{3,2},{4,5},{5,4},{6,7},{7,6},{8,9},{9,8},{10,11... | collective-permute-start | bytes 2359304 | tf_op jit(solution)/shard_map/ppermute | solution.py:379
  (125 other events, 1317.9 us)
Sparse Core Ops, SparseCore 0:
  175.2 103.3 all-gather.1
  398.8 54.2 reduce-scatter.2
  456.1 99.2 reduce-scatter.4
